TPU v7x, 32 devices: a whole 2x2x4 slice. The times are simulated.
32 devices in a mesh: req: 4 (over y, core), tp: 8 (over z, x).
Axes of the slice: x: 2, y: 2, z: 4, core: 2. Of those that a mesh axis runs over, the one named last changes fastest.
Arguments:
- patches: bfloat16 [4, 512, 1664], P('req', 'tp'), may hold values from -6 to 6
- vis_gain: float32 [1664], replicated, may hold values from 0.1 to 1.9
- w_fc1: bfloat16 [1664, 8192], P(None, 'tp'), may hold values from -0.15625 to 0.15625
- w_fc2: bfloat16 [8192, 1664], P('tp'), may hold values from -0.125 to 0.125
- merge_gain: float32 [1664], replicated, may hold values from 0.1 to 1.9
- w_merge: bfloat16 [6656, 1664], P('tp'), may hold values from -0.078125 to 0.078125
- slots: int32 [4, 128], P('req'), may hold values from 0 to 1535, as said below
- text: bfloat16 [4, 1536, 1664], P('req', 'tp'), may hold values from -6 to 6
- docs: int32 [4, 1536], P('req'), may hold values from 0 to 7, never falling along the last dimension, each value on 1 to 384 neighbouring positions
- dec_gain: float32 [1664], replicated, may hold values from 0.1 to 1.9
- w_qkv: bfloat16 [1664, 4992], P(None, 'tp'), may hold values from -0.2773501 to 0.2773501
- w_out: bfloat16 [1664, 1664], P('tp'), may hold values from -0.625 to 0.625
Outputs:
- decoded: bfloat16 [4, 1536, 1664], P('req', 'tp')
Inputs may be any that keep to these rules, and one draw needn't show every extreme that they name: `slots`: positions in a group are distinct; each image's 64 merged rows take consecutive positions in order, and image k lies within positions j * 768 to (j + 1) * 768 - 1 with j = (k + 1) mod 2; the image with j = 1 takes the last 64 positions of the prompt. `docs`: request numbers never fall along a prompt; each request spans 1 to 384 positions.
All inputs are finite; a program needn't handle non-finite values.
Results may differ from a plain program's by a relative error of at most 0.033.
Values may be sent and summed in bfloat16 or wider, within the bound.
No kernel may reach another device: no remote copies, remote signals or barrier semaphores. Data moves between devices by JAX's collectives and lax.ppermute only.
A program may use at most 64 MiB of HBM per device.

v0:
```python
import math

import jax
import jax.numpy as jnp
from jax import lax
from jax.sharding import PartitionSpec as P

HD = 104


EPSILON = 1e-06


def layer_norm(values, gains):
    average = jnp.mean(values, axis=-1, keepdims=True)
    centred = values - average
    variance = jnp.mean(centred * centred, axis=-1, keepdims=True)
    return centred * lax.rsqrt(variance + EPSILON) * gains


def rms_norm(values, gains):
    return values * lax.rsqrt(jnp.mean(values * values, axis=-1, keepdims=True) + EPSILON) * gains


def attend(qkv_rows, doc_row, heads_here):
    seq_len = qkv_rows.shape[0]
    block_rows = min(512, seq_len)
    shaped = qkv_rows.reshape(seq_len, heads_here, 3, HD)
    queries = shaped[:, :, 0]
    key_rows = shaped[:, :, 1]
    value_rows = shaped[:, :, 2]
    key_pos = jnp.arange(seq_len)

    def one_block(block_index):
        offset = block_index * block_rows
        query_block = lax.dynamic_slice_in_dim(queries, offset, block_rows, 0)
        query_pos = offset + jnp.arange(block_rows)
        query_docs = lax.dynamic_slice_in_dim(doc_row, offset, block_rows, 0)
        scores = jnp.einsum(
            "qhe,khe->hqk", query_block, key_rows, preferred_element_type=jnp.float32
        ) / math.sqrt(HD)
        allowed = (key_pos[None, :] <= query_pos[:, None]) & (
            doc_row[None, :] == query_docs[:, None]
        )
        scores = jnp.where(allowed[None], scores, -1e30)
        largest = jnp.max(scores, axis=-1, keepdims=True)
        raised = jnp.where(allowed[None], jnp.exp(scores - largest), 0.0)
        weights = (raised / jnp.sum(raised, axis=-1, keepdims=True)).astype(jnp.bfloat16)
        blended = jnp.einsum(
            "hqk,khe->qhe", weights, value_rows, preferred_element_type=jnp.float32
        )
        return blended.astype(jnp.bfloat16).reshape(block_rows, heads_here * HD)

    blocks = lax.map(one_block, jnp.arange(seq_len // block_rows))
    return blocks.reshape(seq_len, heads_here * HD)


def shards(
    patches, vis_gain, w_fc1, w_fc2, merge_gain, w_merge, slots, text, docs, dec_gain, w_qkv, w_out
):
    patch_rows = patches[0]
    slot_row = slots[0]
    text_rows = text[0]
    doc_row = docs[0]
    width = patch_rows.shape[1]
    local_rows = patch_rows.shape[0]
    seq_here = text_rows.shape[0]
    wide_in = patch_rows.astype(jnp.float32)
    normed_in = layer_norm(wide_in, vis_gain).astype(jnp.bfloat16)
    hidden = jax.nn.gelu(
        jnp.dot(
            lax.all_gather(normed_in, "tp", axis=0, tiled=True),
            w_fc1,
            preferred_element_type=jnp.float32,
        ),
        approximate=False,
    ).astype(jnp.bfloat16)
    mlp_sum = lax.psum_scatter(
        jnp.dot(hidden, w_fc2, preferred_element_type=jnp.float32).astype(jnp.bfloat16),
        "tp",
        scatter_dimension=0,
        tiled=True,
    ).astype(jnp.float32)
    normed_out = layer_norm(wide_in + mlp_sum, merge_gain).astype(jnp.bfloat16)
    merge_in = normed_out.reshape(local_rows // 4, 4 * width)
    features = lax.all_to_all(merge_in, "tp", split_axis=1, concat_axis=0, tiled=True)
    merge_term = jnp.dot(features, w_merge, preferred_element_type=jnp.float32)
    merged_share = lax.psum_scatter(
        merge_term.astype(jnp.bfloat16), "tp", scatter_dimension=0, tiled=True
    )
    merged = lax.all_gather(merged_share, "tp", axis=0, tiled=True)
    positions = lax.axis_index("tp") * seq_here + jnp.arange(seq_here, dtype=jnp.int32)
    matches = slot_row[None, :] == positions[:, None]
    placed = jnp.dot(
        matches.astype(jnp.bfloat16), merged, preferred_element_type=jnp.float32
    ).astype(jnp.bfloat16)
    embedded = jnp.where(jnp.any(matches, axis=1)[:, None], placed, text_rows)
    dec_in = rms_norm(embedded.astype(jnp.float32), dec_gain).astype(jnp.bfloat16)
    qkv_rows = jnp.dot(
        lax.all_gather(dec_in, "tp", axis=0, tiled=True), w_qkv, preferred_element_type=jnp.float32
    ).astype(jnp.bfloat16)
    heads_here = qkv_rows.shape[1] // (3 * HD)
    attended = attend(qkv_rows, doc_row, heads_here)
    out_sum = lax.psum_scatter(
        jnp.dot(attended, w_out, preferred_element_type=jnp.float32).astype(jnp.bfloat16),
        "tp",
        scatter_dimension=0,
        tiled=True,
    ).astype(jnp.float32)
    decoded = (embedded.astype(jnp.float32) + out_sum).astype(jnp.bfloat16)
    return decoded[None]


def solution(mesh):
    placed = (
        P("req", "tp", None),
        P(),
        P(None, "tp"),
        P("tp", None),
        P(),
        P("tp", None),
        P("req", None),
        P("req", "tp", None),
        P("req", None),
        P(),
        P(None, "tp"),
        P("tp", None),
    )
    return jax.shard_map(
        shards, mesh=mesh, in_specs=placed, out_specs=P("req", "tp", None), check_vma=False
    )
```

profile of v0, /device:TPU:0, one launch (start us, length us, event | category | flops | bytes accessed | tf_op | source)
XLA Modules:
  0.0 499.7 jit_solution(9596321177010557180)
XLA Ops:
  6.5 1.2 convert_reduce_fusion
  7.8 1.2 fusion.71
  8.9 1.8 fusion.73
  10.8 48.1 %all-gather.3.cloned.1.call-done = bf16[512,1664]{1,0:T(8,128)(2,1)} async-done(((bf16[64,1664]{1,0:T(8,128)(2,1)}), bf16[512,1664]{1,0:T(8,128)(2,1)}) %all-gather.3.cloned.1.call-update) | async-done | bytes 1703952 | tf_op jit(solution)/shard_map/all_gather | solution.py:72
  58.9 11.6 %convolution_convert_fusion.2 = bf16[512,1664]{1,0:T(8,128)(2,1)} fusion(bf16[1024,1664]{1,0:T(8,128)(2,1)S(1)} %copy-done, bf16[512,1664]{1,0:T(8,128)(2,1)} %all-gather.3.cloned.1.call-done, bf16[1664,1024]{1,0:T(8,128)(2,1)} %param.16), kind=kOutput, calls=%fused_computation.26 | convolution fusion | flops 3524591616 | bytes 10223616 | tf_op jit(solution)/shard_map/dot_general | solution.py:79
  70.5 0.0 reduce-scatter.6.cloned.1.call-start
  70.5 64.9 %reduce-scatter.4.cloned.1.call-done = bf16[64,1664]{1,0:T(8,128)(2,1)} async-done(((bf16[512,1664]{1,0:T(8,128)(2,1)}), bf16[64,1664]{1,0:T(8,128)(2,1)}) %reduce-scatter.4.cloned.1.call-update) | async-done | bytes 213008 | tf_op jit(solution)/shard_map/reduce_scatter | solution.py:78
  135.4 1.2 fusion.75
  136.6 1.3 multiply_reduce_fusion.1
  137.9 1.8 multiply_convert_fusion.1
  139.7 1.8 all_to_all.14
  141.5 1.0 copy.21
  142.5 11.3 %all_to_all.19 = bf16[16,8,832]{2,0,1:T(8,128)(2,1)S(1)} all-to-all(bf16[16,8,832]{2,0,1:T(8,128)(2,1)S(1)} %copy.21), channel_id=1, replica_groups=mesh['req'=4,'tp'=8] {'tp'}, dimensions={1} | all-to-all | bytes 425984 | tf_op jit(solution)/shard_map/all_to_all | solution.py:86
  153.9 3.2 convolution_convert_fusion.4
  157.0 0.0 all-gather.5.cloned.1.call-start
  157.1 0.2 compare_reduce_fusion
  157.3 53.5 %reduce-scatter.6.cloned.1.call-done = bf16[16,1664]{1,0:T(8,128)(2,1)} async-done(((bf16[128,1664]{1,0:T(8,128)(2,1)}), bf16[16,1664]{1,0:T(8,128)(2,1)}) %reduce-scatter.6.cloned.1.call-update) | async-done | bytes 53264 | tf_op jit(solution)/shard_map/reduce_scatter | solution.py:88
  210.8 31.3 %all_gather.10 = bf16[128,1664]{1,0:T(8,128)(2,1)S(1)} all-gather(bf16[16,1664]{1,0:T(8,128)(2,1)} %reduce-scatter.6.cloned.1.call-done), channel_id=1, replica_groups=mesh['req'=4,'tp'=8] {'tp'}, dimensions={0}, use_global_device_ids=true | all-gather | bytes 479232 | tf_op jit(solution)/shard_map/all_gather | solution.py:91
  242.1 1.6 multiply_reduce_fusion
  243.7 1.1 copy-done.1
  244.8 1.0 multiply_convert_fusion
  245.8 0.2 reduce-scatter.8.cloned.1.call-start
  246.1 83.8 %all-gather.5.cloned.1.call-done = bf16[1536,1664]{1,0:T(8,128)(2,1)} async-done(((bf16[192,1664]{1,0:T(8,128)(2,1)}), bf16[1536,1664]{1,0:T(8,128)(2,1)}) %all-gather.5.cloned.1.call-update) | async-done | bytes 5111824 | tf_op jit(solution)/shard_map/all_gather | solution.py:100
  329.9 6.8 %convolution_convert_fusion.1 = bf16[1536,624]{0,1:T(8,128)(2,1)S(1)} fusion(bf16[1536,1664]{1,0:T(8,128)(2,1)} %all-gather.5.cloned.1.call-done, bf16[1664,624]{0,1:T(8,128)(2,1)} %param.24), kind=kOutput, calls=%fused_computation.24 | convolution fusion | flops 3190726656 | bytes 9105408 | tf_op jit(solution)/shard_map/dot_general | solution.py:99
  336.7 1.4 slice_bitcast_fusion
  338.1 45.8 %while.11 = (s32[]{:T(128)}, bf16[3,512,208]{1,2,0:T(8,128)(2,1)}, s32[3]{0:T(128)S(1)}, s32[1,1536]{1,0:T(1,128)S(1)}, s32[1536]{0:T(1024)S(1)}, /*index=5*/bf1...) while((s32[]{:T(128)}, bf16[3,512,208]{1,2,0:T(8,128)(2,1)}, ...), condition=%wide.region_11.12_spmd.clone, body=%wide.region_8.11_spmd.clone.sunk | while | flops 667789312 | bytes 17109696 | solution.py:54
  338.1 0.7 dynamic_slice.26
  339.5 0.1 dynamic_slice.27
  339.6 1.7 fusion.135
  341.2 7.3 %fusion.136 = (f32[2,512]{1,0:T(2,128)S(1)}, f32[2,512,1536]{2,1,0:T(8,128)}) fusion(pred[512,1536]{1,0:T(8,128)(4,1)} %fusion.135, bf16[1536,2,104]{0,2,1:T(8,128)(2,1)} %get-tuple-element.177, bf16[1536,2,104]{0,2,1:T(8,128)(2,1)} %get-tuple-element.176, s32[]{:T(128)S(6)} %select_n.32), kind=kOutput, calls=%fused_computation.139.clone.1 | convolution fusion | flops 335021568 | bytes 8720388 | tf_op jit(solution)/shard_map/while/body/eval_jaxpr/sub | solution.py:47
  348.6 4.1 fusion.137
  352.7 0.7 bitcast_dynamic-update-slice_fusion.2
  353.4 0.7 dynamic_slice.26
  354.7 0.1 dynamic_slice.27
  354.8 1.7 fusion.135
  356.5 7.3 %fusion.136 = (f32[2,512]{1,0:T(2,128)S(1)}, f32[2,512,1536]{2,1,0:T(8,128)}) fusion(pred[512,1536]{1,0:T(8,128)(4,1)} %fusion.135, bf16[1536,2,104]{0,2,1:T(8,128)(2,1)} %get-tuple-element.177, bf16[1536,2,104]{0,2,1:T(8,128)(2,1)} %get-tuple-element.176, s32[]{:T(128)S(6)} %select_n.32), kind=kOutput, calls=%fused_computation.139.clone.1 | convolution fusion | flops 335021568 | bytes 8720388 | tf_op jit(solution)/shard_map/while/body/eval_jaxpr/sub | solution.py:47
  363.8 4.1 fusion.137
  367.9 0.7 bitcast_dynamic-update-slice_fusion.2
  368.6 0.7 dynamic_slice.26
  370.0 0.1 dynamic_slice.27
  370.1 1.7 fusion.135
  371.8 7.3 %fusion.136 = (f32[2,512]{1,0:T(2,128)S(1)}, f32[2,512,1536]{2,1,0:T(8,128)}) fusion(pred[512,1536]{1,0:T(8,128)(4,1)} %fusion.135, bf16[1536,2,104]{0,2,1:T(8,128)(2,1)} %get-tuple-element.177, bf16[1536,2,104]{0,2,1:T(8,128)(2,1)} %get-tuple-element.176, s32[]{:T(128)S(6)} %select_n.32), kind=kOutput, calls=%fused_computation.139.clone.1 | convolution fusion | flops 335021568 | bytes 8720388 | tf_op jit(solution)/shard_map/while/body/eval_jaxpr/sub | solution.py:47
  379.1 4.1 fusion.137
  383.2 0.7 bitcast_dynamic-update-slice_fusion.2
  383.9 2.2 copy.25
  386.1 5.2 %convolution_convert_fusion = bf16[1536,1664]{1,0:T(8,128)(2,1)} fusion(bf16[1536,208]{1,0:T(8,128)(2,1)} %bitcast.73, bf16[208,1664]{1,0:T(8,128)(2,1)} %param.25), kind=kOutput, calls=%fused_computation.23 | convolution fusion | flops 1065811968 | bytes 6443008 | tf_op jit(solution)/shard_map/dot_general | solution.py:105
  391.3 99.5 %reduce-scatter.8.cloned.1.call-done = bf16[192,1664]{1,0:T(8,128)(2,1)} async-done(((bf16[1536,1664]{1,0:T(8,128)(2,1)}), bf16[192,1664]{1,0:T(8,128)(2,1)}) %reduce-scatter.8.cloned.1.call-update) | async-done | bytes 638992 | tf_op jit(solution)/shard_map/reduce_scatter | solution.py:104
  490.8 2.4 fusion.66
  (33 shorter events, 0.3 us)
Async XLA Ops:
  6.5 52.3 %copy-start = (bf16[1024,1664]{1,0:T(8,128)(2,1)S(1)}, bf16[1024,1664]{1,0:T(8,128)(2,1)}, u32[]{:S(2)}) copy-start(bf16[1024,1664]{1,0:T(8,128)(2,1)} %param.17) | copy-start | bytes 10223620
  6.5 52.3 %all-gather.3.cloned.1.call-start = ((), (), s32[]{:S(2)}) async-start(), calls=%async_computation.4 | async-start | bytes 1916928 | tf_op jit(solution)/shard_map/all_gather | solution.py:72
  10.7 124.7 %reduce-scatter.4.cloned.1.call-start = ((), (), s32[]{:S(2)}) async-start(), calls=%async_computation.5 | async-start | bytes 1916928 | tf_op jit(solution)/shard_map/reduce_scatter | solution.py:78
  70.4 67.5 %copy-start.3 = (f32[1664]{0:T(1024)S(1)}, f32[1664]{0:T(1024)}, u32[]{:S(2)}) copy-start(f32[1664]{0:T(1024)} %param.18) | copy-start | bytes 19972
  70.5 140.3 %reduce-scatter.6.cloned.1.call-start = ((), (), s32[]{:S(2)}) async-start(), calls=%async_computation.6 | async-start | bytes 479232 | tf_op jit(solution)/shard_map/reduce_scatter | solution.py:88
  142.5 14.6 %copy-start.5 = (s32[1,128]{1,0:T(1,128)S(1)}, s32[1,128]{1,0:T(1,128)}, u32[]{:S(2)}) copy-start(s32[1,128]{1,0:T(1,128)} %param.20) | copy-start | bytes 1540
  157.0 87.7 %copy-start.4 = (f32[1664]{0:T(1024)S(1)}, f32[1664]{0:T(1024)}, u32[]{:S(2)}) copy-start(f32[1664]{0:T(1024)} %param.23) | copy-start | bytes 19972
  157.0 172.9 %all-gather.5.cloned.1.call-start = ((), (), s32[]{:S(2)}) async-start(), calls=%async_computation.7 | async-start | bytes 5750784 | tf_op jit(solution)/shard_map/all_gather | solution.py:100
  242.1 4.0 copy-start.2
  243.7 1.1 copy-start.1
  245.8 245.0 %reduce-scatter.8.cloned.1.call-start = ((), (), s32[]{:S(2)}) async-start(), calls=%async_computation.8 | async-start | bytes 5750784 | tf_op jit(solution)/shard_map/reduce_scatter | solution.py:104
Sparse Core Ops, SparseCore 0:
  10.9 47.9 all-gather.2
  70.6 64.7 reduce-scatter.3
  157.2 53.5 reduce-scatter.5
  245.9 83.9 all-gather.4
  391.5 99.2 reduce-scatter.7
where the time goes:
time: 500 us
  waiting for transfers between devices  350 us (70%)
  matrix products  62.5 us (12%)
  blocking collectives  42.7 us (9%)
  other arithmetic  17.2 us (3%)
  between operations  13.3 us (3%)
  local copies, waits for them, and re-layouts  11.8 us (2%)
    reduce_scatter x1, waiting for transfers between devices, shards(): lax.psum_scatter(jnp.dot(attended, w_out, preferred_element_type=jnp.floa...  99.5 us
    all_gather x1, waiting for transfers between devices, shards(): lax.all_gather(dec_in, 'tp', axis=0, tiled=True)  83.8 us
    reduce_scatter x1, waiting for transfers between devices, shards(): lax.psum_scatter(jnp.dot(hidden, w_fc2, preferred_element_type=jnp.float3...  64.9 us
    reduce_scatter x1, waiting for transfers between devices, shards(): lax.psum_scatter(merge_term.astype(jnp.bfloat16), 'tp', scatter_dimension...  53.5 us
    all_gather x1, waiting for transfers between devices, shards(): lax.all_gather(normed_in, 'tp', axis=0, tiled=True)  48.1 us
    all_gather x1, blocking collectives, shards(): merged = lax.all_gather(merged_share, 'tp', axis=0, tiled=True)  31.3 us
    sub x3, matrix products, one_block(): raised = jnp.where(allowed[None], jnp.exp(scores - largest), 0.0)  22 us
    dot_general x3, matrix products, one_block(): jnp.einsum('hqk,khe->qhe', weights, value_rows, preferred_element_type=jn...  12.2 us
  transfers between devices with their start and end apart: 5, of which 5 were waited for; matrix products, arithmetic and copies ran while one was open for 0% of the time, Pallas kernels for 0%

commit v1 on v0

--- a/solution.py
+++ b/solution.py
@@ -55,6 +55,23 @@
     return blocks.reshape(seq_len, heads_here * HD)
 
 
+def pair_steps(tp_size):
+    return [(i, i ^ 1) for i in range(tp_size)]
+
+
+def turn_steps(tp_size, turn):
+    lines = tp_size // 2
+    return [(a * 2 + b, ((a + turn) % lines) * 2 + b) for a in range(lines) for b in range(2)]
+
+
+def swap_pair(values, tp_size):
+    return lax.ppermute(values, "tp", pair_steps(tp_size))
+
+
+def turned(values, tp_size, turn):
+    return lax.ppermute(values, "tp", turn_steps(tp_size, turn))
+
+
 def shards(
     patches, vis_gain, w_fc1, w_fc2, merge_gain, w_merge, slots, text, docs, dec_gain, w_qkv, w_out
 ):
@@ -66,29 +83,62 @@
     local_rows = patch_rows.shape[0]
     seq_here = text_rows.shape[0]
     wide_in = patch_rows.astype(jnp.float32)
-    normed_in = layer_norm(wide_in, vis_gain).astype(jnp.bfloat16)
+    tp_size = lax.axis_size("tp")
+    lines = tp_size // 2
+    line = lax.axis_index("tp") // 2
+    side = lax.axis_index("tp") % 2
+    mine = [patch_rows] + [turned(patch_rows, tp_size, k) for k in range(1, lines)]
+    other = [swap_pair(block, tp_size) for block in mine]
+    rows = jnp.concatenate([part for k in range(lines) for part in (mine[k], other[k])], axis=0)
+    normed_in = layer_norm(rows.astype(jnp.float32), vis_gain).astype(jnp.bfloat16)
     hidden = jax.nn.gelu(
-        jnp.dot(
-            lax.all_gather(normed_in, "tp", axis=0, tiled=True),
-            w_fc1,
-            preferred_element_type=jnp.float32,
-        ),
-        approximate=False,
+        jnp.dot(normed_in, w_fc1, preferred_element_type=jnp.float32), approximate=False
     ).astype(jnp.bfloat16)
-    mlp_sum = lax.psum_scatter(
-        jnp.dot(hidden, w_fc2, preferred_element_type=jnp.float32).astype(jnp.bfloat16),
-        "tp",
-        scatter_dimension=0,
-        tiled=True,
-    ).astype(jnp.float32)
+    part = jnp.dot(hidden, w_fc2, preferred_element_type=jnp.float32).astype(jnp.bfloat16)
+    part = part.reshape(lines, 2, local_rows, width)
+    mlp_sum = jnp.zeros((local_rows, width), jnp.float32)
+    for k in range(lines):
+        pair = part[k, 0].astype(jnp.float32) + swap_pair(part[k, 1], tp_size).astype(jnp.float32)
+        if k:
+            pair = turned(pair.astype(jnp.bfloat16), tp_size, lines - k).astype(jnp.float32)
+        mlp_sum = mlp_sum + pair
     normed_out = layer_norm(wide_in + mlp_sum, merge_gain).astype(jnp.bfloat16)
-    merge_in = normed_out.reshape(local_rows // 4, 4 * width)
-    features = lax.all_to_all(merge_in, "tp", split_axis=1, concat_axis=0, tiled=True)
+    quads = local_rows // 4
+    blocks = normed_out.reshape(quads, lines, 2, 4 * width // tp_size)
+    kept = lax.dynamic_index_in_dim(blocks, side, 2, keepdims=False)
+    given = swap_pair(lax.dynamic_index_in_dim(blocks, 1 - side, 2, keepdims=False), tp_size)
+    both = jnp.where(side == 0, jnp.stack([kept, given]), jnp.stack([given, kept]))
+    features = jnp.zeros((lines, 2, quads, both.shape[3]), jnp.bfloat16)
+    for k in range(lines):
+        target = (line + k) % lines
+        block = lax.dynamic_index_in_dim(both, target, 2, keepdims=False)
+        if k:
+            block = turned(block, tp_size, k)
+        source = (line + lines - k) % lines
+        features = lax.dynamic_update_index_in_dim(features, block, source, 0)
+    features = features.reshape(lines * 2 * quads, both.shape[3])
     merge_term = jnp.dot(features, w_merge, preferred_element_type=jnp.float32)
-    merged_share = lax.psum_scatter(
-        merge_term.astype(jnp.bfloat16), "tp", scatter_dimension=0, tiled=True
+    half = merge_term.shape[1] // 2
+    low, high = merge_term[:, :half], merge_term[:, half:]
+    sent = jnp.where(side == 0, high, low).astype(jnp.bfloat16)
+    summed = jnp.where(side == 0, low, high) + swap_pair(sent, tp_size).astype(jnp.float32)
+    share = summed.reshape(lines, -1, half).astype(jnp.bfloat16)
+    total = lax.dynamic_index_in_dim(share, line, 0, keepdims=False).astype(jnp.float32)
+    for k in range(1, lines):
+        block = lax.dynamic_index_in_dim(share, (line + k) % lines, 0, keepdims=False)
+        total = total + turned(block, tp_size, k).astype(jnp.float32)
+    total = total.astype(jnp.bfloat16)
+    gathered = jnp.zeros((lines,) + total.shape, jnp.bfloat16)
+    for k in range(lines):
+        block = turned(total, tp_size, k) if k else total
+        gathered = lax.dynamic_update_index_in_dim(gathered, block, (line + lines - k) % lines, 0)
+    gathered = gathered.reshape(-1, half)
+    far = swap_pair(gathered, tp_size)
+    merged = jnp.where(
+        side == 0,
+        jnp.concatenate([gathered, far], axis=1),
+        jnp.concatenate([far, gathered], axis=1),
     )
-    merged = lax.all_gather(merged_share, "tp", axis=0, tiled=True)
     positions = lax.axis_index("tp") * seq_here + jnp.arange(seq_here, dtype=jnp.int32)
     matches = slot_row[None, :] == positions[:, None]
     placed = jnp.dot(

time: 500 us -> 406 us (0.81)
  waiting for transfers between devices: 350 us -> 247 us
  blocking collectives: 42.7 us -> 0 us
  starting transfers between devices: 0.35 us -> 40.7 us
  local copies, waits for them, and re-layouts: 11.8 us -> 22.7 us
    reduce_scatter x2 -> x0, waiting for transfers between devices: 118 us -> none  [the longest x1 64.9 us: shards(): lax.psum_scatter(jnp.dot(hidden, w_fc2, preferred_element_type=jnp.float3...]
    ppermute x0 -> x26, waiting for transfers between devices: none -> 63.8 us  [the longest x11 34.2 us: swap_pair(): return lax.ppermute(values, 'tp', pair_steps(tp_size))]
    all_gather x1 -> x0, waiting for transfers between devices: 48.1 us -> none  [shards(): lax.all_gather(normed_in, 'tp', axis=0, tiled=True)]
    ppermute x0 -> x26, starting transfers between devices: none -> 40.5 us  [the longest x15 26.6 us: turned(): return lax.ppermute(values, 'tp', turn_steps(tp_size, turn))]
    all_gather x1 -> x0, blocking collectives: 31.3 us -> none  [shards(): merged = lax.all_gather(merged_share, 'tp', axis=0, tiled=True)]
    all_to_all x1 -> x0, blocking collectives: 11.3 us -> none  [shards(): lax.all_to_all(merge_in, 'tp', split_axis=1, concat_axis=0, tiled=True)]
  transfers between devices with their start and end apart: 5 -> 28, of which waited for: 5 -> 20; matrix products, arithmetic and copies ran while one was open for 0% -> 1% of each run, Pallas kernels for 0% -> 0%
where the time goes in v1:
time: 406 us; the launch traced here: 405 us
  waiting for transfers between devices  247 us (61%)
  matrix products  62.6 us (15%)
  starting transfers between devices  40.7 us (10%)
  local copies, waits for them, and re-layouts  22.7 us (6%)
  other arithmetic  16.4 us (4%)
  between operations  13.6 us (3%)
    reduce_scatter x1, waiting for transfers between devices, shards(): lax.psum_scatter(jnp.dot(attended, w_out, preferred_element_type=jnp.floa...  99.1 us
    all_gather x1, waiting for transfers between devices, shards(): lax.all_gather(dec_in, 'tp', axis=0, tiled=True)  84.3 us
    ppermute x11, waiting for transfers between devices, swap_pair(): return lax.ppermute(values, 'tp', pair_steps(tp_size))  34.2 us
    ppermute x15, waiting for transfers between devices, turned(): return lax.ppermute(values, 'tp', turn_steps(tp_size, turn))  29.6 us
    ppermute x15, starting transfers between devices, turned(): return lax.ppermute(values, 'tp', turn_steps(tp_size, turn))  26.6 us
    sub x3, matrix products, one_block(): raised = jnp.where(allowed[None], jnp.exp(scores - largest), 0.0)  22.3 us
    ppermute x11, starting transfers between devices, swap_pair(): return lax.ppermute(values, 'tp', pair_steps(tp_size))  13.9 us
    dot_general x3, matrix products, one_block(): jnp.einsum('hqk,khe->qhe', weights, value_rows, preferred_element_type=jn...  12.2 us
  transfers between devices with their start and end apart: 28, of which 20 were waited for; matrix products, arithmetic and copies ran while one was open for 1% of the time, Pallas kernels for 0%

profile of v1, /device:TPU:0, one launch (start us, length us, event | category | flops | bytes accessed | tf_op | source)
XLA Modules:
  0.0 405.5 jit_solution(15090845539255738892)
XLA Ops:
  6.5 3.0 collective-permute-start.1
  11.1 2.6 collective-permute-start.3
  16.0 2.0 collective-permute-done.1
  18.0 1.7 collective-permute-start.2
  19.7 6.5 %collective-permute-done.3 = bf16[64,1664]{1,0:T(8,128)(2,1)S(1)} collective-permute-done((bf16[64,1664]{1,0:T(8,128)(2,1)}, bf16[64,1664]{1,0:T(8,128)(2,1)S(1)}, u32[]{:S(2)}, u32[]{:S(2)}) %collective-permute-start.3) | collective-permute-done | bytes 213024 | tf_op jit(solution)/shard_map/ppermute | solution.py:72
  28.4 6.0 %collective-permute-done.4 = bf16[64,1664]{1,0:T(8,128)(2,1)S(1)} collective-permute-done((bf16[64,1664]{1,0:T(8,128)(2,1)S(1)}, bf16[64,1664]{1,0:T(8,128)(2,1)S(1)}, u32[]{:S(2)}, u32[]{:S(2)}) %collective-permute-start.4) | collective-permute-done | bytes 213024 | tf_op jit(solution)/shard_map/ppermute | solution.py:68
  34.5 3.5 collective-permute-done.6
  39.7 11.9 %convolution_convert_fusion.2 = bf16[512,1664]{1,0:T(8,128)(2,1)} fusion(bf16[1024,1664]{1,0:T(8,128)(2,1)S(1)} %copy-done, bf16[1664,1024]{1,0:T(8,128)(2,1)} %param.16, bf16[512,1664]{1,0:T(8,128)(2,1)} %copy-done.1, f32[1664]{0:T(1024)S(1)} %copy-done.9, f32[512]{0:T(512)S(1)} %add_rsqrt_fusion, f32[512]{0:T(512)S(1)} %broadcast_multiply_fusion), kind=kOutput, calls=%fused_computation.33 | convolution fusion | flops 3528851456 | bytes 10234368 | tf_op jit(solution)/shard_map/dot_general | solution.py:97
  51.6 2.0 slice_bitcast_fusion.9
  57.7 4.1 %collective-permute-done.10 = bf16[64,1664]{1,0:T(8,128)(2,1)S(1)} collective-permute-done((bf16[64,1664]{1,0:T(8,128)(2,1)S(1)}, bf16[64,1664]{1,0:T(8,128)(2,1)S(1)}, u32[]{:S(2)}, u32[]{:S(2)}) %collective-permute-start.10) | collective-permute-done | bytes 213024 | tf_op jit(solution)/shard_map/ppermute | solution.py:68
  61.8 4.6 %collective-permute-done.12 = bf16[64,1664]{1,0:T(8,128)(2,1)S(1)} collective-permute-done((bf16[64,1664]{1,0:T(8,128)(2,1)S(1)}, bf16[64,1664]{1,0:T(8,128)(2,1)S(1)}, u32[]{:S(2)}, u32[]{:S(2)}) %collective-permute-start.12) | collective-permute-done | bytes 213024 | tf_op jit(solution)/shard_map/ppermute | solution.py:68
  66.4 4.6 %collective-permute-done.8 = bf16[64,1664]{1,0:T(8,128)(2,1)S(1)} collective-permute-done((bf16[64,1664]{1,0:T(8,128)(2,1)S(1)}, bf16[64,1664]{1,0:T(8,128)(2,1)S(1)}, u32[]{:S(2)}, u32[]{:S(2)}) %collective-permute-start.8) | collective-permute-done | bytes 213024 | tf_op jit(solution)/shard_map/ppermute | solution.py:68
  70.9 2.1 fusion.87
  74.0 4.0 collective-permute-start.13
  78.7 10.4 %collective-permute-done.11 = bf16[64,1664]{1,0:T(8,128)(2,1)} collective-permute-done((bf16[64,1664]{1,0:T(8,128)(2,1)}, bf16[64,1664]{1,0:T(8,128)(2,1)}, u32[]{:S(2)}, u32[]{:S(2)}) %collective-permute-start.11) | collective-permute-done | bytes 213024 | tf_op jit(solution)/shard_map/ppermute | solution.py:72
  89.1 1.6 fusion.131
  91.8 1.8 reshape.140
  93.6 2.2 constant_dynamic-slice_fusion.1
  98.9 2.6 collective-permute-done.14
  101.6 2.9 collective-permute-start.15
  104.5 2.5 collective-permute-start.17
  107.6 2.1 collective-permute-done.16
  109.7 2.4 fusion.136
  112.3 1.6 collective-permute-start.18
  113.9 4.5 %collective-permute-done.18 = bf16[128,832]{1,0:T(8,128)(2,1)S(1)} collective-permute-done((bf16[128,832]{1,0:T(8,128)(2,1)S(1)}, bf16[128,832]{1,0:T(8,128)(2,1)S(1)}, u32[]{:S(2)}, u32[]{:S(2)}) %collective-permute-start.18) | collective-permute-done | bytes 213024 | tf_op jit(solution)/shard_map/ppermute | solution.py:68
  121.1 2.6 collective-permute-start.20
  126.2 1.6 collective-permute-done.20
  127.8 2.1 collective-permute-done.21
  134.2 1.8 collective-permute-start.24
  135.9 2.3 collective-permute-done.22
  142.3 4.5 %collective-permute-done.25 = bf16[128,832]{1,0:T(8,128)(2,1)S(1)} collective-permute-done((bf16[128,832]{1,0:T(8,128)(2,1)}, bf16[128,832]{1,0:T(8,128)(2,1)S(1)}, u32[]{:S(2)}, u32[]{:S(2)}) %collective-permute-start.25) | collective-permute-done | bytes 213024 | tf_op jit(solution)/shard_map/ppermute | solution.py:68
  146.8 1.9 multiply_reduce_fusion
  151.1 84.3 %all-gather.2.cloned.1.call-done = bf16[1536,1664]{1,0:T(8,128)(2,1)} async-done(((bf16[192,1664]{1,0:T(8,128)(2,1)}), bf16[1536,1664]{1,0:T(8,128)(2,1)}) %all-gather.2.cloned.1.call-update) | async-done | bytes 5111824 | tf_op jit(solution)/shard_map/all_gather | solution.py:150
  235.4 6.8 %convolution_convert_fusion.1 = bf16[1536,624]{0,1:T(8,128)(2,1)S(1)} fusion(bf16[1536,1664]{1,0:T(8,128)(2,1)} %all-gather.2.cloned.1.call-done, bf16[1664,624]{0,1:T(8,128)(2,1)} %param.24), kind=kOutput, calls=%fused_computation.31 | convolution fusion | flops 3190726656 | bytes 9105408 | tf_op jit(solution)/shard_map/dot_general | solution.py:149
  243.5 46.2 %while.11 = (s32[]{:T(128)}, bf16[3,512,208]{1,2,0:T(8,128)(2,1)}, s32[3]{0:T(128)S(1)}, s32[1,1536]{1,0:T(1,128)S(1)}, s32[1536]{0:T(1024)S(1)}, /*index=5*/bf1...) while((s32[]{:T(128)}, bf16[3,512,208]{1,2,0:T(8,128)(2,1)}, ...), condition=%wide.region_9.10_spmd.clone, body=%wide.region_6.9_spmd.clone.sunk | while | flops 667789312 | bytes 17109696 | solution.py:54
  244.9 1.7 fusion.156
  246.7 7.4 %fusion.157 = (f32[2,512]{1,0:T(2,128)S(1)}, f32[2,512,1536]{2,1,0:T(8,128)}) fusion(pred[512,1536]{1,0:T(8,128)(4,1)} %fusion.156, bf16[1536,2,104]{0,2,1:T(8,128)(2,1)} %get-tuple-element.196, bf16[1536,2,104]{0,2,1:T(8,128)(2,1)} %get-tuple-element.195, s32[]{:T(128)S(6)} %select_n.188), kind=kOutput, calls=%fused_computation.199.clone.1 | convolution fusion | flops 335021568 | bytes 8720388 | tf_op jit(solution)/shard_map/while/body/eval_jaxpr/sub | solution.py:47
  254.1 4.1 %fusion.158 = bf16[2,512,104]{1,2,0:T(8,128)(2,1)S(1)} fusion(bf16[1536,2,104]{0,2,1:T(8,128)(2,1)} %get-tuple-element.197, f32[2,512,1536]{2,1,0:T(8,128)} %get-tuple-element.164, f32[2,512]{1,0:T(2,128)S(1)} %get-tuple-element.165), kind=kOutput, calls=%fused_computation.12.clone.1 | convolution fusion | flops 330407936 | bytes 7147520 | tf_op jit(solution)/shard_map/while/body/eval_jaxpr/hqk,khe->qhe/dot_general | solution.py:49
  260.3 1.7 fusion.156
  262.1 7.4 %fusion.157 = (f32[2,512]{1,0:T(2,128)S(1)}, f32[2,512,1536]{2,1,0:T(8,128)}) fusion(pred[512,1536]{1,0:T(8,128)(4,1)} %fusion.156, bf16[1536,2,104]{0,2,1:T(8,128)(2,1)} %get-tuple-element.196, bf16[1536,2,104]{0,2,1:T(8,128)(2,1)} %get-tuple-element.195, s32[]{:T(128)S(6)} %select_n.188), kind=kOutput, calls=%fused_computation.199.clone.1 | convolution fusion | flops 335021568 | bytes 8720388 | tf_op jit(solution)/shard_map/while/body/eval_jaxpr/sub | solution.py:47
  269.5 4.1 %fusion.158 = bf16[2,512,104]{1,2,0:T(8,128)(2,1)S(1)} fusion(bf16[1536,2,104]{0,2,1:T(8,128)(2,1)} %get-tuple-element.197, f32[2,512,1536]{2,1,0:T(8,128)} %get-tuple-element.164, f32[2,512]{1,0:T(2,128)S(1)} %get-tuple-element.165), kind=kOutput, calls=%fused_computation.12.clone.1 | convolution fusion | flops 330407936 | bytes 7147520 | tf_op jit(solution)/shard_map/while/body/eval_jaxpr/hqk,khe->qhe/dot_general | solution.py:49
  275.7 1.7 fusion.156
  277.4 7.4 %fusion.157 = (f32[2,512]{1,0:T(2,128)S(1)}, f32[2,512,1536]{2,1,0:T(8,128)}) fusion(pred[512,1536]{1,0:T(8,128)(4,1)} %fusion.156, bf16[1536,2,104]{0,2,1:T(8,128)(2,1)} %get-tuple-element.196, bf16[1536,2,104]{0,2,1:T(8,128)(2,1)} %get-tuple-element.195, s32[]{:T(128)S(6)} %select_n.188), kind=kOutput, calls=%fused_computation.199.clone.1 | convolution fusion | flops 335021568 | bytes 8720388 | tf_op jit(solution)/shard_map/while/body/eval_jaxpr/sub | solution.py:47
  284.9 4.1 %fusion.158 = bf16[2,512,104]{1,2,0:T(8,128)(2,1)S(1)} fusion(bf16[1536,2,104]{0,2,1:T(8,128)(2,1)} %get-tuple-element.197, f32[2,512,1536]{2,1,0:T(8,128)} %get-tuple-element.164, f32[2,512]{1,0:T(2,128)S(1)} %get-tuple-element.165), kind=kOutput, calls=%fused_computation.12.clone.1 | convolution fusion | flops 330407936 | bytes 7147520 | tf_op jit(solution)/shard_map/while/body/eval_jaxpr/hqk,khe->qhe/dot_general | solution.py:49
  289.6 2.3 copy.31
  291.9 5.2 %convolution_convert_fusion = bf16[1536,1664]{1,0:T(8,128)(2,1)} fusion(bf16[1536,208]{1,0:T(8,128)(2,1)} %bitcast.120, bf16[208,1664]{1,0:T(8,128)(2,1)} %param.25), kind=kOutput, calls=%fused_computation.23 | convolution fusion | flops 1065811968 | bytes 6443008 | tf_op jit(solution)/shard_map/dot_general | solution.py:155
  297.1 99.1 %reduce-scatter.2.cloned.1.call-done = bf16[192,1664]{1,0:T(8,128)(2,1)} async-done(((bf16[1536,1664]{1,0:T(8,128)(2,1)}), bf16[192,1664]{1,0:T(8,128)(2,1)}) %reduce-scatter.2.cloned.1.call-update) | async-done | bytes 638992 | tf_op jit(solution)/shard_map/reduce_scatter | solution.py:154
  396.2 2.4 fusion.79
  (108 shorter events, 40.3 us)
Async XLA Ops:
  6.5 33.2 %copy-start = (bf16[1024,1664]{1,0:T(8,128)(2,1)S(1)}, bf16[1024,1664]{1,0:T(8,128)(2,1)}, u32[]{:S(2)}) copy-start(bf16[1024,1664]{1,0:T(8,128)(2,1)} %param.17) | copy-start | bytes 10223620
  6.5 228.8 %all-gather.2.cloned.1.call-start = ((), (), s32[]{:S(2)}) async-start(), calls=%async_computation.1 | async-start | bytes 5750784 | tf_op jit(solution)/shard_map/all_gather | solution.py:150
  6.5 11.4 %collective-permute-start.1 = (bf16[64,1664]{1,0:T(8,128)(2,1)}, bf16[64,1664]{1,0:T(8,128)(2,1)S(1)}, u32[]{:S(2)}, u32[]{:S(2)}) collective-permute-start(bf16[64,1664]{1,0:T(8,128)(2,1)} %bitcast.128), channel_id=1, source_target_pairs={{0,2},{1,3},{2,4},{3,5},{4,6},{5,7},{6,0},{7,1},{8,10},{9,11},{10,... | collective-permute-start | bytes 638984 | tf_op jit(solution)/shard_map/ppermute | solution.py:72
  9.6 18.7 %collective-permute-start = (bf16[64,1664]{1,0:T(8,128)(2,1)}, bf16[64,1664]{1,0:T(8,128)(2,1)S(1)}, u32[]{:S(2)}, u32[]{:S(2)}) collective-permute-start(bf16[64,1664]{1,0:T(8,128)(2,1)} %bitcast.129), channel_id=1, source_target_pairs={{0,1},{1,0},{2,3},{3,2},{4,5},{5,4},{6,7},{7,6},{8,9},{9,8},{10,11... | collective-permute-start | bytes 638984 | tf_op jit(solution)/shard_map/ppermute | solution.py:68
  11.1 15.2 %collective-permute-start.3 = (bf16[64,1664]{1,0:T(8,128)(2,1)}, bf16[64,1664]{1,0:T(8,128)(2,1)S(1)}, u32[]{:S(2)}, u32[]{:S(2)}) collective-permute-start(bf16[64,1664]{1,0:T(8,128)(2,1)} %bitcast.130), channel_id=1, source_target_pairs={{0,4},{1,5},{2,6},{3,7},{4,0},{5,1},{6,2},{7,3},{8,12},{9,13},{10,... | collective-permute-start | bytes 638984 | tf_op jit(solution)/shard_map/ppermute | solution.py:72
  13.6 14.1 %collective-permute-start.5 = (bf16[64,1664]{1,0:T(8,128)(2,1)}, bf16[64,1664]{1,0:T(8,128)(2,1)S(1)}, u32[]{:S(2)}, u32[]{:S(2)}) collective-permute-start(bf16[64,1664]{1,0:T(8,128)(2,1)} %bitcast.131), channel_id=1, source_target_pairs={{0,6},{1,7},{2,0},{3,1},{4,2},{5,3},{6,4},{7,5},{8,14},{9,15},{10,... | collective-permute-start | bytes 638984 | tf_op jit(solution)/shard_map/ppermute | solution.py:72
  18.0 10.4 %collective-permute-start.2 = (bf16[64,1664]{1,0:T(8,128)(2,1)S(1)}, bf16[64,1664]{1,0:T(8,128)(2,1)S(1)}, u32[]{:S(2)}, u32[]{:S(2)}) collective-permute-start(bf16[64,1664]{1,0:T(8,128)(2,1)S(1)} %collective-permute-done.1), channel_id=1, source_target_pairs={{0,1},{1,0},{2,3},{3,2},{4,5},{5,4},{6,7},{7,6},{8,9},{9,8},{10,11... | collective-permute-start | bytes 638984 | tf_op jit(solution)/shard_map/ppermute | solution.py:68
  26.3 8.1 %collective-permute-start.4 = (bf16[64,1664]{1,0:T(8,128)(2,1)S(1)}, bf16[64,1664]{1,0:T(8,128)(2,1)S(1)}, u32[]{:S(2)}, u32[]{:S(2)}) collective-permute-start(bf16[64,1664]{1,0:T(8,128)(2,1)S(1)} %collective-permute-done.3), channel_id=1, source_target_pairs={{0,1},{1,0},{2,3},{3,2},{4,5},{5,4},{6,7},{7,6},{8,9},{9,8},{10,11... | collective-permute-start | bytes 638984 | tf_op jit(solution)/shard_map/ppermute | solution.py:68
  27.8 10.1 %collective-permute-start.6 = (bf16[64,1664]{1,0:T(8,128)(2,1)S(1)}, bf16[64,1664]{1,0:T(8,128)(2,1)S(1)}, u32[]{:S(2)}, u32[]{:S(2)}) collective-permute-start(bf16[64,1664]{1,0:T(8,128)(2,1)S(1)} %collective-permute-done.5), channel_id=1, source_target_pairs={{0,1},{1,0},{2,3},{3,2},{4,5},{5,4},{6,7},{7,6},{8,9},{9,8},{10,11... | collective-permute-start | bytes 638984 | tf_op jit(solution)/shard_map/ppermute | solution.py:68
  34.4 5.3 %copy-start.9 = (f32[1664]{0:T(1024)S(1)}, f32[1664]{0:T(1024)}, u32[]{:S(2)}) copy-start(f32[1664]{0:T(1024)} %param.15) | copy-start | bytes 19972
  37.9 1.2 copy-start.1
  53.6 37.4 %copy-start.6 = (f32[1664]{0:T(1024)S(1)}, f32[1664]{0:T(1024)}, u32[]{:S(2)}) copy-start(f32[1664]{0:T(1024)} %param.18) | copy-start | bytes 19972
  53.6 8.2 %collective-permute-start.10 = (bf16[64,1664]{1,0:T(8,128)(2,1)S(1)}, bf16[64,1664]{1,0:T(8,128)(2,1)S(1)}, u32[]{:S(2)}, u32[]{:S(2)}) collective-permute-start(bf16[64,1664]{1,0:T(8,128)(2,1)S(1)} %get-tuple-element.98), channel_id=1, source_target_pairs={{0,1},{1,0},{2,3},{3,2},{4,5},{5,4},{6,7},{7,6},{8,9},{9,8},{10,11... | collective-permute-start | bytes 638984 | tf_op jit(solution)/shard_map/ppermute | solution.py:68
  55.1 11.3 %collective-permute-start.12 = (bf16[64,1664]{1,0:T(8,128)(2,1)S(1)}, bf16[64,1664]{1,0:T(8,128)(2,1)S(1)}, u32[]{:S(2)}, u32[]{:S(2)}) collective-permute-start(bf16[64,1664]{1,0:T(8,128)(2,1)S(1)} %get-tuple-element.97), channel_id=1, source_target_pairs={{0,1},{1,0},{2,3},{3,2},{4,5},{5,4},{6,7},{7,6},{8,9},{9,8},{10,11... | collective-permute-start | bytes 638984 | tf_op jit(solution)/shard_map/ppermute | solution.py:68
  55.6 15.3 %collective-permute-start.8 = (bf16[64,1664]{1,0:T(8,128)(2,1)S(1)}, bf16[64,1664]{1,0:T(8,128)(2,1)S(1)}, u32[]{:S(2)}, u32[]{:S(2)}) collective-permute-start(bf16[64,1664]{1,0:T(8,128)(2,1)S(1)} %get-tuple-element.99), channel_id=1, source_target_pairs={{0,1},{1,0},{2,3},{3,2},{4,5},{5,4},{6,7},{7,6},{8,9},{9,8},{10,11... | collective-permute-start | bytes 638984 | tf_op jit(solution)/shard_map/ppermute | solution.py:68
  57.1 21.5 %collective-permute-start.7 = (bf16[64,1664]{1,0:T(8,128)(2,1)}, bf16[64,1664]{1,0:T(8,128)(2,1)}, u32[]{:S(2)}, u32[]{:S(2)}) collective-permute-start(bf16[64,1664]{1,0:T(8,128)(2,1)} %get-tuple-element.96), channel_id=1, source_target_pairs={{0,1},{1,0},{2,3},{3,2},{4,5},{5,4},{6,7},{7,6},{8,9},{9,8},{10,11... | collective-permute-start | bytes 638984 | tf_op jit(solution)/shard_map/ppermute | solution.py:68
  73.0 16.1 %collective-permute-start.11 = (bf16[64,1664]{1,0:T(8,128)(2,1)}, bf16[64,1664]{1,0:T(8,128)(2,1)}, u32[]{:S(2)}, u32[]{:S(2)}) collective-permute-start(bf16[64,1664]{1,0:T(8,128)(2,1)} %get-tuple-element.102), channel_id=1, source_target_pairs={{0,4},{1,5},{2,6},{3,7},{4,0},{5,1},{6,2},{7,3},{8,12},{9,13},{10,... | collective-permute-start | bytes 638984 | tf_op jit(solution)/shard_map/ppermute | solution.py:72
  74.0 15.1 %collective-permute-start.13 = (bf16[64,1664]{1,0:T(8,128)(2,1)}, bf16[64,1664]{1,0:T(8,128)(2,1)}, u32[]{:S(2)}, u32[]{:S(2)}) collective-permute-start(bf16[64,1664]{1,0:T(8,128)(2,1)} %get-tuple-element.101), channel_id=1, source_target_pairs={{0,2},{1,3},{2,4},{3,5},{4,6},{5,7},{6,0},{7,1},{8,10},{9,11},{10,... | collective-permute-start | bytes 638984 | tf_op jit(solution)/shard_map/ppermute | solution.py:72
  78.0 11.1 %collective-permute-start.9 = (bf16[64,1664]{1,0:T(8,128)(2,1)}, bf16[64,1664]{1,0:T(8,128)(2,1)}, u32[]{:S(2)}, u32[]{:S(2)}) collective-permute-start(bf16[64,1664]{1,0:T(8,128)(2,1)} %get-tuple-element.100), channel_id=1, source_target_pairs={{0,6},{1,7},{2,0},{3,1},{4,2},{5,3},{6,4},{7,5},{8,14},{9,15},{10,... | collective-permute-start | bytes 638984 | tf_op jit(solution)/shard_map/ppermute | solution.py:72
  96.5 5.0 %collective-permute-start.14 = (bf16[16,4,832]{2,0,1:T(8,128)(2,1)}, bf16[16,4,832]{2,0,1:T(8,128)(2,1)S(1)}, u32[]{:S(2)}, u32[]{:S(2)}) collective-permute-start(bf16[16,4,832]{2,0,1:T(8,128)(2,1)} %bitcast.109), channel_id=1, source_target_pairs={{0,1},{1,0},{2,3},{3,2},{4,5},{5,4},{6,7},{7,6},{8,9},{9,8},{10,11... | collective-permute-start | bytes 319496 | tf_op jit(solution)/shard_map/ppermute | solution.py:68
  101.6 6.0 %collective-permute-start.15 = (bf16[2,16,832]{2,1,0:T(8,128)(2,1)S(1)}, bf16[2,16,832]{2,1,0:T(8,128)(2,1)S(1)}, u32[]{:S(2)}, u32[]{:S(2)}) collective-permute-start(bf16[2,16,832]{2,1,0:T(8,128)(2,1)S(1)} %get-tuple-element.108), channel_id=1, source_target_pairs={{0,2},{1,3},{2,4},{3,5},{4,6},{5,7},{6,0},{7,1},{8,10},{9,11},{10,... | collective-permute-start | bytes 159752 | tf_op jit(solution)/shard_map/ppermute | solution.py:72
  104.5 5.2 %collective-permute-start.16 = (bf16[2,16,832]{2,1,0:T(8,128)(2,1)S(1)}, bf16[2,16,832]{2,1,0:T(8,128)(2,1)S(1)}, u32[]{:S(2)}, u32[]{:S(2)}) collective-permute-start(bf16[2,16,832]{2,1,0:T(8,128)(2,1)S(1)} %get-tuple-element.107), channel_id=1, source_target_pairs={{0,4},{1,5},{2,6},{3,7},{4,0},{5,1},{6,2},{7,3},{8,12},{9,13},{10,... | collective-permute-start | bytes 159752 | tf_op jit(solution)/shard_map/ppermute | solution.py:72
  104.5 5.2 %collective-permute-start.17 = (bf16[2,16,832]{2,1,0:T(8,128)(2,1)S(1)}, bf16[2,16,832]{2,1,0:T(8,128)(2,1)S(1)}, u32[]{:S(2)}, u32[]{:S(2)}) collective-permute-start(bf16[2,16,832]{2,1,0:T(8,128)(2,1)S(1)} %get-tuple-element.106), channel_id=1, source_target_pairs={{0,6},{1,7},{2,0},{3,1},{4,2},{5,3},{6,4},{7,5},{8,14},{9,15},{10,... | collective-permute-start | bytes 159752 | tf_op jit(solution)/shard_map/ppermute | solution.py:72
  112.2 30.0 %copy-start.8 = (s32[1,128]{1,0:T(1,128)S(1)}, s32[1,128]{1,0:T(1,128)}, u32[]{:S(2)}) copy-start(s32[1,128]{1,0:T(1,128)} %param.20) | copy-start | bytes 1540
  112.3 6.1 %collective-permute-start.18 = (bf16[128,832]{1,0:T(8,128)(2,1)S(1)}, bf16[128,832]{1,0:T(8,128)(2,1)S(1)}, u32[]{:S(2)}, u32[]{:S(2)}) collective-permute-start(bf16[128,832]{1,0:T(8,128)(2,1)S(1)} %select_convert_fusion), channel_id=1, source_target_pairs={{0,1},{1,0},{2,3},{3,2},{4,5},{5,4},{6,7},{7,6},{8,9},{9,8},{10,11... | collective-permute-start | bytes 638984 | tf_op jit(solution)/shard_map/ppermute | solution.py:68
  118.6 0.7 copy-start.3
  119.9 29.8 %copy-start.7 = (f32[1664]{0:T(1024)S(1)}, f32[1664]{0:T(1024)}, u32[]{:S(2)}) copy-start(f32[1664]{0:T(1024)} %param.23) | copy-start | bytes 19972
  119.9 6.2 %collective-permute-start.19 = (bf16[32,832]{1,0:T(8,128)(2,1)}, bf16[32,832]{1,0:T(8,128)(2,1)S(1)}, u32[]{:S(2)}, u32[]{:S(2)}) collective-permute-start(bf16[32,832]{1,0:T(8,128)(2,1)} %get-tuple-element.103), channel_id=1, source_target_pairs={{0,2},{1,3},{2,4},{3,5},{4,6},{5,7},{6,0},{7,1},{8,10},{9,11},{10,... | collective-permute-start | bytes 159752 | tf_op jit(solution)/shard_map/ppermute | solution.py:72
  121.1 6.7 %collective-permute-start.20 = (bf16[32,832]{1,0:T(8,128)(2,1)}, bf16[32,832]{1,0:T(8,128)(2,1)S(1)}, u32[]{:S(2)}, u32[]{:S(2)}) collective-permute-start(bf16[32,832]{1,0:T(8,128)(2,1)} %get-tuple-element.105), channel_id=1, source_target_pairs={{0,4},{1,5},{2,6},{3,7},{4,0},{5,1},{6,2},{7,3},{8,12},{9,13},{10,... | collective-permute-start | bytes 159752 | tf_op jit(solution)/shard_map/ppermute | solution.py:72
  123.7 6.2 %collective-permute-start.21 = (bf16[32,832]{1,0:T(8,128)(2,1)}, bf16[32,832]{1,0:T(8,128)(2,1)}, u32[]{:S(2)}, u32[]{:S(2)}) collective-permute-start(bf16[32,832]{1,0:T(8,128)(2,1)} %get-tuple-element.104), channel_id=1, source_target_pairs={{0,6},{1,7},{2,0},{3,1},{4,2},{5,3},{6,4},{7,5},{8,14},{9,15},{10,... | collective-permute-start | bytes 159752 | tf_op jit(solution)/shard_map/ppermute | solution.py:72
  127.8 2.1 copy-start.5
  132.1 6.1 %collective-permute-start.22 = (bf16[32,832]{1,0:T(8,128)(2,1)S(1)}, bf16[32,832]{1,0:T(8,128)(2,1)S(1)}, u32[]{:S(2)}, u32[]{:S(2)}) collective-permute-start(bf16[32,832]{1,0:T(8,128)(2,1)S(1)} %get-tuple-element.88), channel_id=1, source_target_pairs={{0,2},{1,3},{2,4},{3,5},{4,6},{5,7},{6,0},{7,1},{8,10},{9,11},{10,... | collective-permute-start | bytes 159752 | tf_op jit(solution)/shard_map/ppermute | solution.py:72
  133.0 6.3 %collective-permute-start.23 = (bf16[32,832]{1,0:T(8,128)(2,1)S(1)}, bf16[32,832]{1,0:T(8,128)(2,1)S(1)}, u32[]{:S(2)}, u32[]{:S(2)}) collective-permute-start(bf16[32,832]{1,0:T(8,128)(2,1)S(1)} %get-tuple-element.88), channel_id=1, source_target_pairs={{0,4},{1,5},{2,6},{3,7},{4,0},{5,1},{6,2},{7,3},{8,12},{9,13},{10,... | collective-permute-start | bytes 159752 | tf_op jit(solution)/shard_map/ppermute | solution.py:72
  134.2 5.7 %collective-permute-start.24 = (bf16[32,832]{1,0:T(8,128)(2,1)S(1)}, bf16[32,832]{1,0:T(8,128)(2,1)S(1)}, u32[]{:S(2)}, u32[]{:S(2)}) collective-permute-start(bf16[32,832]{1,0:T(8,128)(2,1)S(1)} %get-tuple-element.88), channel_id=1, source_target_pairs={{0,6},{1,7},{2,0},{3,1},{4,2},{5,3},{6,4},{7,5},{8,14},{9,15},{10,... | collective-permute-start | bytes 159752 | tf_op jit(solution)/shard_map/ppermute | solution.py:72
  140.6 6.2 %collective-permute-start.25 = (bf16[128,832]{1,0:T(8,128)(2,1)}, bf16[128,832]{1,0:T(8,128)(2,1)S(1)}, u32[]{:S(2)}, u32[]{:S(2)}) collective-permute-start(bf16[128,832]{1,0:T(8,128)(2,1)} %bitcast.31), channel_id=1, source_target_pairs={{0,1},{1,0},{2,3},{3,2},{4,5},{5,4},{6,7},{7,6},{8,9},{9,8},{10,11... | collective-permute-start | bytes 638984 | tf_op jit(solution)/shard_map/ppermute | solution.py:68
  142.3 8.7 %copy-start.4 = (s32[1,1536]{1,0:T(1,128)S(1)}, s32[1,1536]{1,0:T(1,128)}, u32[]{:S(2)}) copy-start(s32[1,1536]{1,0:T(1,128)} %param.22) | copy-start | bytes 18436
  148.7 1.1 copy-start.2
  150.8 245.4 %reduce-scatter.2.cloned.1.call-start = ((), (), s32[]{:S(2)}) async-start(), calls=%async_computation.2 | async-start | bytes 5750784 | tf_op jit(solution)/shard_map/reduce_scatter | solution.py:154
Sparse Core Ops, SparseCore 0:
  150.9 84.4 all-gather.1
  297.3 98.9 reduce-scatter.1

commit v2 on v1

--- a/solution.py
+++ b/solution.py
@@ -1,8 +1,11 @@
+import functools
 import math
 
 import jax
 import jax.numpy as jnp
 from jax import lax
+from jax.experimental import pallas as pl
+from jax.experimental.pallas import tpu as pltpu
 from jax.sharding import PartitionSpec as P
 
 HD = 104
@@ -22,39 +25,6 @@
     return values * lax.rsqrt(jnp.mean(values * values, axis=-1, keepdims=True) + EPSILON) * gains
 
 
-def attend(qkv_rows, doc_row, heads_here):
-    seq_len = qkv_rows.shape[0]
-    block_rows = min(512, seq_len)
-    shaped = qkv_rows.reshape(seq_len, heads_here, 3, HD)
-    queries = shaped[:, :, 0]
-    key_rows = shaped[:, :, 1]
-    value_rows = shaped[:, :, 2]
-    key_pos = jnp.arange(seq_len)
-
-    def one_block(block_index):
-        offset = block_index * block_rows
-        query_block = lax.dynamic_slice_in_dim(queries, offset, block_rows, 0)
-        query_pos = offset + jnp.arange(block_rows)
-        query_docs = lax.dynamic_slice_in_dim(doc_row, offset, block_rows, 0)
-        scores = jnp.einsum(
-            "qhe,khe->hqk", query_block, key_rows, preferred_element_type=jnp.float32
-        ) / math.sqrt(HD)
-        allowed = (key_pos[None, :] <= query_pos[:, None]) & (
-            doc_row[None, :] == query_docs[:, None]
-        )
-        scores = jnp.where(allowed[None], scores, -1e30)
-        largest = jnp.max(scores, axis=-1, keepdims=True)
-        raised = jnp.where(allowed[None], jnp.exp(scores - largest), 0.0)
-        weights = (raised / jnp.sum(raised, axis=-1, keepdims=True)).astype(jnp.bfloat16)
-        blended = jnp.einsum(
-            "hqk,khe->qhe", weights, value_rows, preferred_element_type=jnp.float32
-        )
-        return blended.astype(jnp.bfloat16).reshape(block_rows, heads_here * HD)
-
-    blocks = lax.map(one_block, jnp.arange(seq_len // block_rows))
-    return blocks.reshape(seq_len, heads_here * HD)
-
-
 def pair_steps(tp_size):
     return [(i, i ^ 1) for i in range(tp_size)]
 
@@ -70,6 +40,125 @@
 
 def turned(values, tp_size, turn):
     return lax.ppermute(values, "tp", turn_steps(tp_size, turn))
+
+
+NT = (((1,), (1,)), ((), ()))
+TN = (((0,), (0,)), ((), ()))
+
+
+def put_quarters(whole, own, ours, theirs, starts, offset):
+    step = pl.program_id(0)
+
+    @pl.when(step == 0)
+    def _():
+        whole[...] = own[...]
+
+    @pl.when(step > 0)
+    def _():
+        size = ours.shape[2]
+        for index in range(4):
+            quarter = ours[index // 2, 0] if index % 2 == 0 else theirs[index // 2, 0]
+            start = pl.multiple_of(starts[offset + index], 16)
+            whole[pl.ds(start, size), :] = quarter
+
+
+def text_kernel(starts, rows, own, ours, theirs, out, whole):
+    put_quarters(whole, own, ours, theirs, starts, 0)
+    out[0] = lax.dot_general(
+        whole[...], rows[...], NT, preferred_element_type=jnp.float32
+    ).astype(jnp.bfloat16)
+
+
+def late_kernel(
+    blk, longest, starts, merged, gain, slots, key_docs, query_docs, text_part,
+    own, ours, theirs, own_out, ours_out, theirs_out,
+    out, whole, whole_out, image_rows, spread, hits, bias, total,
+):
+    step = pl.program_id(0)
+    window = text_part.shape[2]
+    ahead = window - blk
+    reach = longest + 128
+    shift = ahead - longest
+
+    @pl.when(step == 0)
+    def _():
+        wide = merged[...].astype(jnp.float32)
+        scale = lax.rsqrt(jnp.mean(wide * wide, axis=-1, keepdims=True) + EPSILON)
+        image_rows[...] = (wide * scale * gain[...]).astype(jnp.bfloat16)
+        position = starts[8] + lax.broadcasted_iota(jnp.int32, spread.shape, 1)
+        match = jnp.where(slots[...] == position, 1.0, 0.0)
+        spread[...] = match.astype(jnp.bfloat16)
+        hits[...] = jnp.broadcast_to(jnp.max(match, axis=0, keepdims=True), hits.shape)
+        for block in range(blk // 128):
+            first = shift + block * 128
+            key_place = first + lax.broadcasted_iota(jnp.int32, (reach, 128), 0)
+            query_place = ahead + block * 128 + lax.broadcasted_iota(jnp.int32, (reach, 128), 1)
+            allowed = (key_place <= query_place) & (
+                key_docs[pl.ds(first, reach), :] == query_docs[:, pl.ds(block * 128, 128)]
+            )
+            bias[block] = jnp.where(allowed, 0.0, -1e30)
+        total[...] = jnp.zeros_like(total)
+
+    put_quarters(whole, own, ours, theirs, starts, 0)
+    put_quarters(whole_out, own_out, ours_out, theirs_out, starts, 4)
+    image_part = lax.dot_general(
+        whole[...], image_rows[...], NT, preferred_element_type=jnp.float32
+    ).astype(jnp.bfloat16)
+    placed = jnp.dot(image_part, spread[...], preferred_element_type=jnp.float32)
+    qkv = jnp.where(hits[0:1, :] > 0.5, placed, text_part[0].astype(jnp.float32))
+    factor = math.log2(math.e) / math.sqrt(HD)
+    heads = []
+    for head in range(qkv.shape[0] // (3 * HD)):
+        base = head * 3 * HD
+        queries = (qkv[base : base + HD, ahead:] * factor).astype(jnp.bfloat16)
+        keys = qkv[base + HD : base + 2 * HD].T.astype(jnp.bfloat16)
+        values = qkv[base + 2 * HD : base + 3 * HD].astype(jnp.bfloat16)
+        blocks = []
+        for block in range(blk // 128):
+            first = shift + block * 128
+            scores = jnp.dot(
+                keys[first : first + reach],
+                queries[:, block * 128 : block * 128 + 128],
+                preferred_element_type=jnp.float32,
+            ) + bias[block]
+            raised = jnp.exp2(scores - jnp.max(scores, axis=0, keepdims=True))
+            blended = jnp.dot(
+                values[:, first : first + reach],
+                raised.astype(jnp.bfloat16),
+                preferred_element_type=jnp.float32,
+            )
+            blocks.append(blended / jnp.sum(raised, axis=0, keepdims=True))
+        heads.append(jnp.concatenate(blocks, axis=1))
+    attended = jnp.concatenate(heads, axis=0).T.astype(jnp.bfloat16)
+    depth = attended.shape[1]
+    total[...] += jnp.dot(attended, whole_out[:depth], preferred_element_type=jnp.float32)
+
+    @pl.when(step == pl.num_programs(0) - 1)
+    def _():
+        out[...] = total[...].astype(jnp.bfloat16)
+
+
+def quarter_size(rows):
+    return -(-rows // 64) * 16
+
+
+def quarter_start(rows, index):
+    return jnp.minimum(index * quarter_size(rows), rows - quarter_size(rows))
+
+
+def gather_lines(weights, tp_size, first_after):
+    lines = tp_size // 2
+    copies = lax.axis_size("req")
+    weights = jnp.pad(weights, ((0, -weights.shape[0] % 16), (0, 0)))
+    place = lax.axis_index("req") % 4
+    size = quarter_size(weights.shape[0])
+    quarter = lax.dynamic_slice_in_dim(weights, quarter_start(weights.shape[0], place), size, 0)
+    quarter = lax.optimization_barrier((quarter, first_after))[0]
+    near = jnp.stack([turned(quarter, tp_size, k) for k in range(1, lines)])
+    far = lax.ppermute(near, "req", [(i, i ^ 2) for i in range(copies)])
+    ours = jnp.stack([near, far])
+    theirs = lax.ppermute(ours, "req", [(i, i ^ 1) for i in range(copies)])
+    return weights, ours, theirs
 
 
 def shards(
@@ -90,6 +179,20 @@
     mine = [patch_rows] + [turned(patch_rows, tp_size, k) for k in range(1, lines)]
     other = [swap_pair(block, tp_size) for block in mine]
     rows = jnp.concatenate([part for k in range(lines) for part in (mine[k], other[k])], axis=0)
+    blk = 2 * seq_here
+    longest = seq_here * tp_size // 4
+    halo = -(-longest // blk)
+    ahead = halo * blk
+    early_text = lax.optimization_barrier((text_rows, rows))[0]
+    pieces = []
+    for back in range(halo, -1, -1):
+        steps = [(i, i + 2 * back) for i in range(tp_size - 2 * back)]
+        ours = lax.ppermute(early_text, "tp", steps) if back else early_text
+        theirs = swap_pair(ours, tp_size)
+        pieces += [jnp.where(side == 0, ours, theirs), jnp.where(side == 0, theirs, ours)]
+    text_normed = rms_norm(jnp.concatenate(pieces).astype(jnp.float32), dec_gain).astype(jnp.bfloat16)
+    qkv_weights = gather_lines(w_qkv.T, tp_size, rows)
+    out_weights = gather_lines(w_out, tp_size, qkv_weights[1])
     normed_in = layer_norm(rows.astype(jnp.float32), vis_gain).astype(jnp.bfloat16)
     hidden = jax.nn.gelu(
         jnp.dot(normed_in, w_fc1, preferred_element_type=jnp.float32), approximate=False
@@ -145,18 +248,85 @@
         matches.astype(jnp.bfloat16), merged, preferred_element_type=jnp.float32
     ).astype(jnp.bfloat16)
     embedded = jnp.where(jnp.any(matches, axis=1)[:, None], placed, text_rows)
-    dec_in = rms_norm(embedded.astype(jnp.float32), dec_gain).astype(jnp.bfloat16)
-    qkv_rows = jnp.dot(
-        lax.all_gather(dec_in, "tp", axis=0, tiled=True), w_qkv, preferred_element_type=jnp.float32
-    ).astype(jnp.bfloat16)
-    heads_here = qkv_rows.shape[1] // (3 * HD)
-    attended = attend(qkv_rows, doc_row, heads_here)
-    out_sum = lax.psum_scatter(
-        jnp.dot(attended, w_out, preferred_element_type=jnp.float32).astype(jnp.bfloat16),
-        "tp",
-        scatter_dimension=0,
-        tiled=True,
-    ).astype(jnp.float32)
+
+    count = merged.shape[0]
+    columns = qkv_weights[0].shape[0]
+    depth = out_weights[0].shape[0]
+    size, size_out = quarter_size(columns), quarter_size(depth)
+    place = lax.axis_index("req") % 4
+    starts = jnp.stack(
+        [quarter_start(columns, place ^ i) for i in (0, 1, 2, 3)]
+        + [quarter_start(depth, place ^ i) for i in (0, 1, 2, 3)]
+        + [line * blk - ahead]
+    ).astype(jnp.int32)
+    smem = pl.BlockSpec(memory_space=pltpu.SMEM)
+
+    def fixed(shape):
+        return pl.BlockSpec(shape, lambda k: (0,) * len(shape))
+
+    def moving(size):
+        return pl.BlockSpec((2, 1, size, width), lambda k: (0, jnp.maximum(k - 1, 0), 0, 0))
+
+    window = ahead + blk
+    text_part = pl.pallas_call(
+        text_kernel,
+        grid=(lines,),
+        in_specs=[smem, fixed((window, width)), fixed((columns, width)), moving(size), moving(size)],
+        out_specs=pl.BlockSpec((1, columns, window), lambda k: (k, 0, 0)),
+        out_shape=jax.ShapeDtypeStruct((lines, columns, window), jnp.bfloat16),
+        scratch_shapes=[pltpu.VMEM((columns, width), jnp.bfloat16)],
+        compiler_params=pltpu.CompilerParams(vmem_limit_bytes=40 << 20),
+        cost_estimate=pl.CostEstimate(
+            flops=2 * lines * columns * window * width,
+            bytes_accessed=2 * lines * columns * (window + width),
+            transcendentals=0,
+        ),
+        name="text_qkv",
+    )(starts, text_normed, *qkv_weights)
+
+    doc_window = lax.dynamic_slice_in_dim(
+        jnp.concatenate([jnp.full((ahead,), -1, jnp.int32), doc_row]), line * blk, window, 0
+    )
+    out_part = pl.pallas_call(
+        functools.partial(late_kernel, blk, longest),
+        grid=(lines,),
+        in_specs=[
+            smem,
+            fixed((count, width)),
+            fixed((1, width)),
+            fixed((count, 1)),
+            fixed((window, 1)),
+            fixed((1, blk)),
+            pl.BlockSpec((1, columns, window), lambda k: (k, 0, 0)),
+            fixed((columns, width)), moving(size), moving(size),
+            fixed((depth, width)), moving(size_out), moving(size_out),
+        ],
+        out_specs=fixed((blk, width)),
+        out_shape=jax.ShapeDtypeStruct((blk, width), jnp.bfloat16),
+        scratch_shapes=[
+            pltpu.VMEM((columns, width), jnp.bfloat16),
+            pltpu.VMEM((depth, width), jnp.bfloat16),
+            pltpu.VMEM((count, width), jnp.bfloat16),
+            pltpu.VMEM((count, window), jnp.bfloat16),
+            pltpu.VMEM((8, window), jnp.float32),
+            pltpu.VMEM((blk // 128, longest + 128, 128), jnp.float32),
+            pltpu.VMEM((blk, width), jnp.float32),
+        ],
+        compiler_params=pltpu.CompilerParams(vmem_limit_bytes=48 << 20),
+        cost_estimate=pl.CostEstimate(
+            flops=2 * lines * columns * (count + 2 * blk) * width,
+            bytes_accessed=2 * lines * columns * (window + width),
+            transcendentals=lines * columns // (3 * HD) * blk * (longest + 128),
+        ),
+        name="late_attention",
+    )(
+        starts, merged, dec_gain[None], slot_row[:, None], doc_window[:, None],
+        doc_window[None, ahead:], text_part, *qkv_weights, *out_weights,
+    )
+    halves = out_part.reshape(2, seq_here, width)
+    kept = lax.dynamic_index_in_dim(halves, side, 0, keepdims=False)
+    given = swap_pair(lax.dynamic_index_in_dim(halves, 1 - side, 0, keepdims=False), tp_size)
+    out_sum = kept.astype(jnp.float32) + given.astype(jnp.float32)
     decoded = (embedded.astype(jnp.float32) + out_sum).astype(jnp.bfloat16)
     return decoded[None]
 

time: 406 us -> 275 us (0.68)
  waiting for transfers between devices: 247 us -> 97.4 us
  matrix products: 62.6 us -> 15.3 us
  starting transfers between devices: 40.7 us -> 82.8 us
  Pallas kernels: 0 us -> 30.8 us
  between operations: 13.6 us -> 0.46 us
  other arithmetic: 16.4 us -> 24.1 us
    reduce_scatter x1 -> x0, waiting for transfers between devices: 99.1 us -> none  [shards(): lax.psum_scatter(jnp.dot(attended, w_out, preferred_element_type=jnp.floa...]
    all_gather x1 -> x0, waiting for transfers between devices: 84.3 us -> none  [shards(): lax.all_gather(dec_in, 'tp', axis=0, tiled=True)]
    ppermute x15 -> x21, starting transfers between devices: 26.6 us -> 63 us  [turned(): return lax.ppermute(values, 'tp', turn_steps(tp_size, turn))]
    pallas_call x0 -> x2, Pallas kernels: none -> 30.8 us  [the longest x1 20.4 us: shards(): pl.pallas_call(functools.partial(late_kernel, blk, longest), grid=(lines,...]
    ppermute x11 -> x14, waiting for transfers between devices: 34.2 us -> 61.2 us  [swap_pair(): return lax.ppermute(values, 'tp', pair_steps(tp_size))]
    dot_general x5 -> x0, matrix products: 24.2 us -> none  [the longest x3 12.2 us: one_block(): jnp.einsum('hqk,khe->qhe', weights, value_rows, preferred_element_type=jn...]
    sub x3 -> x0, matrix products: 22.3 us -> none  [one_block(): raised = jnp.where(allowed[None], jnp.exp(scores - largest), 0.0)]
    ppermute x0 -> x5, waiting for transfers between devices: none -> 6.89 us  [the longest x2 6.88 us: gather_lines(): far = lax.ppermute(near, 'req', [(i, i ^ 2) for i in range(copies)])]
  transfers between devices with their start and end apart: 28 -> 40, of which waited for: 20 -> 19; matrix products, arithmetic and copies ran while one was open for 1% -> 15% of each run, Pallas kernels for 0% -> 4%
where the time goes in v2:
time: 275 us; the launch traced here: 274 us
  waiting for transfers between devices  97.4 us (35%)
  starting transfers between devices  82.8 us (30%)
  Pallas kernels  30.8 us (11%)
  other arithmetic  24.1 us (9%)
  local copies, waits for them, and re-layouts  23.5 us (9%)
  matrix products  15.3 us (6%)
    ppermute x21, starting transfers between devices, turned(): return lax.ppermute(values, 'tp', turn_steps(tp_size, turn))  63 us
    ppermute x14, waiting for transfers between devices, swap_pair(): return lax.ppermute(values, 'tp', pair_steps(tp_size))  61.2 us
    ppermute x21, waiting for transfers between devices, turned(): return lax.ppermute(values, 'tp', turn_steps(tp_size, turn))  29.3 us
    pallas_call x1, Pallas kernels, shards(): pl.pallas_call(functools.partial(late_kernel, blk, longest), grid=(lines,...  20.4 us
    ppermute x14, starting transfers between devices, swap_pair(): return lax.ppermute(values, 'tp', pair_steps(tp_size))  15.4 us
    dot_general x1, matrix products, shards(): jnp.dot(hidden, w_fc2, preferred_element_type=jnp.float32)  11.8 us
    pallas_call x1, Pallas kernels, shards(): pl.pallas_call(text_kernel, grid=(lines,), in_specs=[smem, fixed((window,...  10.4 us
    ppermute x2, waiting for transfers between devices, gather_lines(): far = lax.ppermute(near, 'req', [(i, i ^ 2) for i in range(copies)])  6.88 us
  transfers between devices with their start and end apart: 40, of which 19 were waited for; matrix products, arithmetic and copies ran while one was open for 15% of the time, Pallas kernels for 4%

profile of v2, /device:TPU:0, one launch (start us, length us, event | category | flops | bytes accessed | tf_op | source)
XLA Modules:
  0.0 274.4 jit_solution(12561878842603634535)
XLA Ops:
  0.0 2.9 %collective-permute-start = (bf16[64,1664]{1,0:T(8,128)(2,1)}, bf16[64,1664]{1,0:T(8,128)(2,1)S(1)}, u32[]{:S(2)}, u32[]{:S(2)}) collective-permute-start(bf16[64,1664]{1,0:T(8,128)(2,1)} %bitcast.130), channel_id=1, source_target_pairs={{0,1},{1,0},{2,3},{3,2},{4,5},{5,4},{6,7},{7,6},{8,9},{9,8},{10,11... | collective-permute-start | bytes 638984 | tf_op jit(solution)/shard_map/ppermute | solution.py:38
  2.9 1.6 collective-permute-start.1
  4.5 2.6 collective-permute-start.3
  9.4 3.8 %collective-permute-done.1 = bf16[64,1664]{1,0:T(8,128)(2,1)S(1)} collective-permute-done((bf16[64,1664]{1,0:T(8,128)(2,1)}, bf16[64,1664]{1,0:T(8,128)(2,1)S(1)}, u32[]{:S(2)}, u32[]{:S(2)}) %collective-permute-start.1) | collective-permute-done | bytes 213024 | tf_op jit(solution)/shard_map/ppermute | solution.py:42
  13.6 7.4 %collective-permute-done.3 = bf16[64,1664]{1,0:T(8,128)(2,1)S(1)} collective-permute-done((bf16[64,1664]{1,0:T(8,128)(2,1)}, bf16[64,1664]{1,0:T(8,128)(2,1)S(1)}, u32[]{:S(2)}, u32[]{:S(2)}) %collective-permute-start.3) | collective-permute-done | bytes 213024 | tf_op jit(solution)/shard_map/ppermute | solution.py:42
  21.5 1.5 collective-permute-start.6
  23.1 6.0 %collective-permute-done.4 = bf16[64,1664]{1,0:T(8,128)(2,1)S(1)} collective-permute-done((bf16[64,1664]{1,0:T(8,128)(2,1)S(1)}, bf16[64,1664]{1,0:T(8,128)(2,1)S(1)}, u32[]{:S(2)}, u32[]{:S(2)}) %collective-permute-start.4) | collective-permute-done | bytes 213024 | tf_op jit(solution)/shard_map/ppermute | solution.py:38
  29.2 3.5 %collective-permute-done.6 = bf16[64,1664]{1,0:T(8,128)(2,1)S(1)} collective-permute-done((bf16[64,1664]{1,0:T(8,128)(2,1)S(1)}, bf16[64,1664]{1,0:T(8,128)(2,1)S(1)}, u32[]{:S(2)}, u32[]{:S(2)}) %collective-permute-start.6) | collective-permute-done | bytes 213024 | tf_op jit(solution)/shard_map/ppermute | solution.py:38
  34.5 11.8 %convolution_convert_fusion = bf16[512,1664]{1,0:T(8,128)(2,1)} fusion(bf16[1024,1664]{1,0:T(8,128)(2,1)S(1)} %copy-done, bf16[1664,1024]{1,0:T(8,128)(2,1)} %param.14, bf16[512,1664]{1,0:T(8,128)(2,1)} %copy-done.8, f32[1664]{0:T(1024)S(1)} %copy-done.19, f32[512]{0:T(512)S(1)} %add_rsqrt_fusion.1, f32[512]{0:T(512)S(1)} %broadcast_multiply_fusion), kind=kOutput, calls=%fused_computation.14 | convolution fusion | flops 3528851456 | bytes 10234368 | tf_op jit(solution)/shard_map/dot_general | solution.py:200
  46.3 2.2 slice_bitcast_fusion.6
  52.5 4.4 %collective-permute-done.8 = bf16[64,1664]{1,0:T(8,128)(2,1)} collective-permute-done((bf16[64,1664]{1,0:T(8,128)(2,1)}, bf16[64,1664]{1,0:T(8,128)(2,1)}, u32[]{:S(2)}, u32[]{:S(2)}) %collective-permute-start.8) | collective-permute-done | bytes 213024 | tf_op jit(solution)/shard_map/ppermute | solution.py:38
  56.9 4.6 %collective-permute-done.12 = bf16[64,1664]{1,0:T(8,128)(2,1)} collective-permute-done((bf16[64,1664]{1,0:T(8,128)(2,1)}, bf16[64,1664]{1,0:T(8,128)(2,1)}, u32[]{:S(2)}, u32[]{:S(2)}) %collective-permute-start.12) | collective-permute-done | bytes 213024 | tf_op jit(solution)/shard_map/ppermute | solution.py:38
  61.5 4.6 %collective-permute-done.10 = bf16[64,1664]{1,0:T(8,128)(2,1)} collective-permute-done((bf16[64,1664]{1,0:T(8,128)(2,1)}, bf16[64,1664]{1,0:T(8,128)(2,1)}, u32[]{:S(2)}, u32[]{:S(2)}) %collective-permute-start.10) | collective-permute-done | bytes 213024 | tf_op jit(solution)/shard_map/ppermute | solution.py:38
  66.1 1.5 fusion.64
  67.6 3.5 %collective-permute-start.13 = (bf16[64,1664]{1,0:T(8,128)(2,1)S(1)}, bf16[64,1664]{1,0:T(8,128)(2,1)S(1)}, u32[]{:S(2)}, u32[]{:S(2)}) collective-permute-start(bf16[64,1664]{1,0:T(8,128)(2,1)S(1)} %get-tuple-element.20), channel_id=1, source_target_pairs={{0,2},{1,3},{2,4},{3,5},{4,6},{5,7},{6,0},{7,1},{8,10},{9,11},{10,... | collective-permute-start | bytes 638984 | tf_op jit(solution)/shard_map/ppermute | solution.py:42
  72.0 1.5 collective-permute-start.9
  73.5 2.0 dynamic-slice_bitcast_fusion.1
  75.5 1.9 collective-permute-start.31
  77.7 25.6 %collective-permute-start.29 = (bf16[160,1664]{1,0:T(8,128)(2,1)}, bf16[160,1664]{1,0:T(8,128)(2,1)}, u32[]{:S(2)}, u32[]{:S(2)}) collective-permute-start(bf16[160,1664]{1,0:T(8,128)(2,1)} %dynamic-slice_bitcast_fusion.1), channel_id=1, source_target_pairs={{0,2},{1,3},{2,4},{3,5},{4,6},{5,7},{6,0},{7,1},{8,10},{9,11},{10,... | collective-permute-start | bytes 1597448 | tf_op jit(solution)/shard_map/ppermute | solution.py:42
  105.6 1.9 reshape.72
  107.5 2.2 constant_dynamic-slice_fusion.2
  111.9 3.5 %collective-permute-done.14 = bf16[16,4,832]{2,0,1:T(8,128)(2,1)S(1)} collective-permute-done((bf16[16,4,832]{2,0,1:T(8,128)(2,1)}, bf16[16,4,832]{2,0,1:T(8,128)(2,1)S(1)}, u32[]{:S(2)}, u32[]{:S(2)}) %collective-permute-start.14) | collective-permute-done | bytes 106528 | tf_op jit(solution)/shard_map/ppermute | solution.py:38
  115.5 8.3 %collective-permute-start.15 = (bf16[2,16,832]{2,1,0:T(8,128)(2,1)S(1)}, bf16[2,16,832]{2,1,0:T(8,128)(2,1)S(1)}, u32[]{:S(2)}, u32[]{:S(2)}) collective-permute-start(bf16[2,16,832]{2,1,0:T(8,128)(2,1)S(1)} %get-tuple-element.35), channel_id=1, source_target_pairs={{0,2},{1,3},{2,4},{3,5},{4,6},{5,7},{6,0},{7,1},{8,10},{9,11},{10,... | collective-permute-start | bytes 159752 | tf_op jit(solution)/shard_map/ppermute | solution.py:42
  123.7 3.4 %collective-permute-start.16 = (bf16[2,16,832]{2,1,0:T(8,128)(2,1)S(1)}, bf16[2,16,832]{2,1,0:T(8,128)(2,1)S(1)}, u32[]{:S(2)}, u32[]{:S(2)}) collective-permute-start(bf16[2,16,832]{2,1,0:T(8,128)(2,1)S(1)} %get-tuple-element.34), channel_id=1, source_target_pairs={{0,4},{1,5},{2,6},{3,7},{4,0},{5,1},{6,2},{7,3},{8,12},{9,13},{10,... | collective-permute-start | bytes 159752 | tf_op jit(solution)/shard_map/ppermute | solution.py:42
  127.2 8.9 %collective-permute-done.30 = bf16[160,1664]{1,0:T(8,128)(2,1)} collective-permute-done((bf16[160,1664]{1,0:T(8,128)(2,1)}, bf16[160,1664]{1,0:T(8,128)(2,1)}, u32[]{:S(2)}, u32[]{:S(2)}) %collective-permute-start.30) | collective-permute-done | bytes 532512 | tf_op jit(solution)/shard_map/ppermute | solution.py:42
  136.0 3.4 %fusion.106 = (bf16[1,3,160,1664]{3,2,1,0:T(8,128)(2,1)}, bf16[3,160,1664]{2,1,0:T(8,128)(2,1)}) fusion(bf16[1,160,1664]{2,1,0:T(8,128)(2,1)} %bitcast.47, bf16[1,160,1664]{2,1,0:T(8,128)(2,1)} %bitcast.46, bf16[1,160,1664]{2,1,0:T(8,128)(2,1)} %bitcast.45), kind=kLoop, calls=%fused_computation.182 | loop fusion | flops 1597440 | bytes 4792320 | tf_op jit(solution)/shard_map/stack | solution.py:159
  139.5 1.5 collective-permute-start.32
  144.1 2.2 collective-permute-start.26
  146.3 3.6 %collective-permute-done.18 = bf16[128,832]{1,0:T(8,128)(2,1)} collective-permute-done((bf16[128,832]{1,0:T(8,128)(2,1)}, bf16[128,832]{1,0:T(8,128)(2,1)}, u32[]{:S(2)}, u32[]{:S(2)}) %collective-permute-start.18) | collective-permute-done | bytes 213024 | tf_op jit(solution)/shard_map/ppermute | solution.py:38
  153.1 2.0 collective-permute-start.19
  155.1 1.7 constant_dynamic-slice_fusion
  157.4 1.7 collective-permute-done.21
  161.1 1.5 bitcast_dynamic-update-slice_fusion.3
  162.6 2.5 collective-permute-start.22
  169.7 1.8 collective-permute-start.23
  171.5 2.2 collective-permute-start.24
  174.3 2.3 pad_maximum_fusion.ours
  179.7 5.5 %collective-permute-done.28 = bf16[192,1664]{1,0:T(8,128)(2,1)S(1)} collective-permute-done((bf16[192,1664]{1,0:T(8,128)(2,1)}, bf16[192,1664]{1,0:T(8,128)(2,1)S(1)}, u32[]{:S(2)}, u32[]{:S(2)}) %collective-permute-start.28) | collective-permute-done | bytes 639008 | tf_op jit(solution)/shard_map/ppermute | solution.py:38
  186.8 1.7 collective-permute-start.35
  188.5 10.2 %collective-permute-done.25 = bf16[128,832]{1,0:T(8,128)(2,1)S(1)} collective-permute-done((bf16[128,832]{1,0:T(8,128)(2,1)}, bf16[128,832]{1,0:T(8,128)(2,1)S(1)}, u32[]{:S(2)}, u32[]{:S(2)}) %collective-permute-start.25) | collective-permute-done | bytes 213024 | tf_op jit(solution)/shard_map/ppermute | solution.py:38
  200.3 6.1 %collective-permute-done.34 = bf16[64,1664]{1,0:T(8,128)(2,1)S(1)} collective-permute-done((bf16[64,1664]{1,0:T(8,128)(2,1)S(1)}, bf16[64,1664]{1,0:T(8,128)(2,1)S(1)}, u32[]{:S(2)}, u32[]{:S(2)}) %collective-permute-start.34) | collective-permute-done | bytes 213024 | tf_op jit(solution)/shard_map/ppermute | solution.py:42
  208.1 1.9 fusion
  210.0 6.9 %collective-permute-done.37 = bf16[3,64,1664]{2,1,0:T(8,128)(2,1)S(1)} collective-permute-done((bf16[3,64,1664]{2,1,0:T(8,128)(2,1)S(1)}, bf16[3,64,1664]{2,1,0:T(8,128)(2,1)S(1)}, u32[]{:S(2)}, u32[]{:S(2)}) %collective-permute-start.37) | collective-permute-done | bytes 639008 | tf_op jit(solution)/shard_map/ppermute | solution.py:158
  217.1 4.4 %fusion.2.rows = bf16[768,1664]{1,0:T(8,128)(2,1)S(1)} fusion(f32[1664]{0:T(1024)S(1)} %copy-done.15, f32[768]{0:T(1024)S(1)} %add_rsqrt_fusion, bf16[192,1664]{1,0:T(8,128)(2,1)S(1)} %get-tuple-element.27, bf16[192,1664]{1,0:T(8,128)(2,1)S(1)} %get-tuple-element.26, bf16[192,1664]{1,0:T(8,128)(2,1)S(1)} %get-tuple-element.25, ...), kind=kLoop, calls=%fused_computation.4 | loop fusion | flops 14057472 | bytes 5121536 | tf_op jit(solution)/shard_map/convert_element_type | solution.py:193
  221.6 10.4 %text_qkv.1.text_part = bf16[4,624,768]{2,1,0:T(8,128)(2,1)} custom-call(s32[9]{0:T(128)S(1)} %stack.99.starts, bf16[768,1664]{1,0:T(8,128)(2,1)S(1)} %fusion.2.rows, bf16[624,1664]{1,0:T(8,128)(2,1)S(1)} %bitcast.120, bf16[2,3,160,1664]{3,2,1,0:T(8,128)(2,1)S(1)} %pad_maximum_fusion.ours, bf16[2,3,160,1664]{3,2,1,0:T(8,128)(2,1)S(1)} %collective-permute-done.33.theirs), custom_call_target="tpu_custom_call" | custom-call | flops 6379536384 | bytes 12140544 | tf_op jit(solution)/shard_map/text_qkv/pallas_call | solution.py:271
  232.0 20.4 %late_attention.1 = bf16[384,1664]{1,0:T(8,128)(2,1)S(1)} custom-call(s32[9]{0:T(128)S(1)} %stack.99.starts, bf16[128,1664]{1,0:T(8,128)(2,1)S(1)} %maximum_select_fusion.merged, f32[1,1664]{1,0:T(1,128)S(1)} %broadcast_in_dim.74.gain, s32[128,1]{1,0:T(8,128)S(1)} %copy.22.slots, s32[768,1]{1,0:T(8,128)S(1)} %copy-done.4, ...), custom_call_target="tpu_custom_call" | custom-call | flops 7442792448 | bytes 12140544 | tf_op jit(solution)/shard_map/late_attention/pallas_call | solution.py:290
  256.1 15.4 %collective-permute-done.39 = bf16[192,1664]{1,0:T(8,128)(2,1)} collective-permute-done((bf16[192,1664]{1,0:T(8,128)(2,1)}, bf16[192,1664]{1,0:T(8,128)(2,1)}, u32[]{:S(2)}, u32[]{:S(2)}) %collective-permute-start.39) | collective-permute-done | bytes 639008 | tf_op jit(solution)/shard_map/ppermute | solution.py:38
  271.5 2.9 %fusion.12 = bf16[1,192,1664]{2,1,0:T(8,128)(2,1)} fusion(bf16[128,1664]{1,0:T(8,128)(2,1)} %copy-done.2, bf16[192,1664]{1,0:T(8,128)(2,1)} %collective-permute-done.39, bf16[2,192,1664]{2,1,0:T(8,128)(2,1)} %bitcast.118, s32[]{:T(128)S(6)} %select_n.166, pred[192]{0:T(512)(128)(4,1)S(1)} %compare_reduce_fusion, s32[128]{0:T(128)S(1)} %bitcast.142, ...), kind=kOutput, calls=%fused_computation.21 | convolution fusion | flops 84369408 | bytes 2983364 | tf_op jit(solution)/shard_map/dot_general | solution.py:247
  (138 shorter events, 40.9 us)
Async XLA Ops:
  0.0 34.4 %copy-start = (bf16[1024,1664]{1,0:T(8,128)(2,1)S(1)}, bf16[1024,1664]{1,0:T(8,128)(2,1)}, u32[]{:S(2)}) copy-start(bf16[1024,1664]{1,0:T(8,128)(2,1)} %param.15) | copy-start | bytes 10223620
  0.0 23.0 %collective-permute-start = (bf16[64,1664]{1,0:T(8,128)(2,1)}, bf16[64,1664]{1,0:T(8,128)(2,1)S(1)}, u32[]{:S(2)}, u32[]{:S(2)}) collective-permute-start(bf16[64,1664]{1,0:T(8,128)(2,1)} %bitcast.130), channel_id=1, source_target_pairs={{0,1},{1,0},{2,3},{3,2},{4,5},{5,4},{6,7},{7,6},{8,9},{9,8},{10,11... | collective-permute-start | bytes 638984 | tf_op jit(solution)/shard_map/ppermute | solution.py:38
  2.9 10.3 %collective-permute-start.1 = (bf16[64,1664]{1,0:T(8,128)(2,1)}, bf16[64,1664]{1,0:T(8,128)(2,1)S(1)}, u32[]{:S(2)}, u32[]{:S(2)}) collective-permute-start(bf16[64,1664]{1,0:T(8,128)(2,1)} %bitcast.131), channel_id=1, source_target_pairs={{0,2},{1,3},{2,4},{3,5},{4,6},{5,7},{6,0},{7,1},{8,10},{9,11},{10,... | collective-permute-start | bytes 638984 | tf_op jit(solution)/shard_map/ppermute | solution.py:42
  4.5 16.5 %collective-permute-start.3 = (bf16[64,1664]{1,0:T(8,128)(2,1)}, bf16[64,1664]{1,0:T(8,128)(2,1)S(1)}, u32[]{:S(2)}, u32[]{:S(2)}) collective-permute-start(bf16[64,1664]{1,0:T(8,128)(2,1)} %bitcast.132), channel_id=1, source_target_pairs={{0,4},{1,5},{2,6},{3,7},{4,0},{5,1},{6,2},{7,3},{8,12},{9,13},{10,... | collective-permute-start | bytes 638984 | tf_op jit(solution)/shard_map/ppermute | solution.py:42
  7.1 14.4 %collective-permute-start.5 = (bf16[64,1664]{1,0:T(8,128)(2,1)}, bf16[64,1664]{1,0:T(8,128)(2,1)S(1)}, u32[]{:S(2)}, u32[]{:S(2)}) collective-permute-start(bf16[64,1664]{1,0:T(8,128)(2,1)} %bitcast.133), channel_id=1, source_target_pairs={{0,6},{1,7},{2,0},{3,1},{4,2},{5,3},{6,4},{7,5},{8,14},{9,15},{10,... | collective-permute-start | bytes 638984 | tf_op jit(solution)/shard_map/ppermute | solution.py:42
  13.2 9.9 %collective-permute-start.2 = (bf16[64,1664]{1,0:T(8,128)(2,1)S(1)}, bf16[64,1664]{1,0:T(8,128)(2,1)S(1)}, u32[]{:S(2)}, u32[]{:S(2)}) collective-permute-start(bf16[64,1664]{1,0:T(8,128)(2,1)S(1)} %collective-permute-done.1), channel_id=1, source_target_pairs={{0,1},{1,0},{2,3},{3,2},{4,5},{5,4},{6,7},{7,6},{8,9},{9,8},{10,11... | collective-permute-start | bytes 638984 | tf_op jit(solution)/shard_map/ppermute | solution.py:38
  21.0 8.1 %collective-permute-start.4 = (bf16[64,1664]{1,0:T(8,128)(2,1)S(1)}, bf16[64,1664]{1,0:T(8,128)(2,1)S(1)}, u32[]{:S(2)}, u32[]{:S(2)}) collective-permute-start(bf16[64,1664]{1,0:T(8,128)(2,1)S(1)} %collective-permute-done.3), channel_id=1, source_target_pairs={{0,1},{1,0},{2,3},{3,2},{4,5},{5,4},{6,7},{7,6},{8,9},{9,8},{10,11... | collective-permute-start | bytes 638984 | tf_op jit(solution)/shard_map/ppermute | solution.py:38
  21.5 11.1 %collective-permute-start.6 = (bf16[64,1664]{1,0:T(8,128)(2,1)S(1)}, bf16[64,1664]{1,0:T(8,128)(2,1)S(1)}, u32[]{:S(2)}, u32[]{:S(2)}) collective-permute-start(bf16[64,1664]{1,0:T(8,128)(2,1)S(1)} %collective-permute-done.5), channel_id=1, source_target_pairs={{0,1},{1,0},{2,3},{3,2},{4,5},{5,4},{6,7},{7,6},{8,9},{9,8},{10,11... | collective-permute-start | bytes 638984 | tf_op jit(solution)/shard_map/ppermute | solution.py:38
  48.4 8.5 %collective-permute-start.8 = (bf16[64,1664]{1,0:T(8,128)(2,1)}, bf16[64,1664]{1,0:T(8,128)(2,1)}, u32[]{:S(2)}, u32[]{:S(2)}) collective-permute-start(bf16[64,1664]{1,0:T(8,128)(2,1)} %get-tuple-element.18), channel_id=1, source_target_pairs={{0,1},{1,0},{2,3},{3,2},{4,5},{5,4},{6,7},{7,6},{8,9},{9,8},{10,11... | collective-permute-start | bytes 638984 | tf_op jit(solution)/shard_map/ppermute | solution.py:38
  49.0 12.5 %collective-permute-start.12 = (bf16[64,1664]{1,0:T(8,128)(2,1)}, bf16[64,1664]{1,0:T(8,128)(2,1)}, u32[]{:S(2)}, u32[]{:S(2)}) collective-permute-start(bf16[64,1664]{1,0:T(8,128)(2,1)} %get-tuple-element.16), channel_id=1, source_target_pairs={{0,1},{1,0},{2,3},{3,2},{4,5},{5,4},{6,7},{7,6},{8,9},{9,8},{10,11... | collective-permute-start | bytes 638984 | tf_op jit(solution)/shard_map/ppermute | solution.py:38
  50.5 15.6 %collective-permute-start.10 = (bf16[64,1664]{1,0:T(8,128)(2,1)}, bf16[64,1664]{1,0:T(8,128)(2,1)}, u32[]{:S(2)}, u32[]{:S(2)}) collective-permute-start(bf16[64,1664]{1,0:T(8,128)(2,1)} %get-tuple-element.17), channel_id=1, source_target_pairs={{0,1},{1,0},{2,3},{3,2},{4,5},{5,4},{6,7},{7,6},{8,9},{9,8},{10,11... | collective-permute-start | bytes 638984 | tf_op jit(solution)/shard_map/ppermute | solution.py:38
  51.0 52.3 %copy-start.13 = (bf16[1,64,1664]{2,1,0:T(8,128)(2,1)S(1)}, bf16[1,64,1664]{2,1,0:T(8,128)(2,1)}, u32[]{:S(2)}) copy-start(bf16[1,64,1664]{2,1,0:T(8,128)(2,1)} %param.12) | copy-start | bytes 638980
  51.0 53.8 %copy-start.16 = (f32[1664]{0:T(1024)S(1)}, f32[1664]{0:T(1024)}, u32[]{:S(2)}) copy-start(f32[1664]{0:T(1024)} %param.16) | copy-start | bytes 19972
  51.0 26.4 %collective-permute-start.7 = (bf16[64,1664]{1,0:T(8,128)(2,1)}, bf16[64,1664]{1,0:T(8,128)(2,1)S(1)}, u32[]{:S(2)}, u32[]{:S(2)}) collective-permute-start(bf16[64,1664]{1,0:T(8,128)(2,1)} %get-tuple-element.15), channel_id=1, source_target_pairs={{0,1},{1,0},{2,3},{3,2},{4,5},{5,4},{6,7},{7,6},{8,9},{9,8},{10,11... | collective-permute-start | bytes 638984 | tf_op jit(solution)/shard_map/ppermute | solution.py:38
  67.6 10.1 %collective-permute-start.13 = (bf16[64,1664]{1,0:T(8,128)(2,1)S(1)}, bf16[64,1664]{1,0:T(8,128)(2,1)S(1)}, u32[]{:S(2)}, u32[]{:S(2)}) collective-permute-start(bf16[64,1664]{1,0:T(8,128)(2,1)S(1)} %get-tuple-element.20), channel_id=1, source_target_pairs={{0,2},{1,3},{2,4},{3,5},{4,6},{5,7},{6,0},{7,1},{8,10},{9,11},{10,... | collective-permute-start | bytes 638984 | tf_op jit(solution)/shard_map/ppermute | solution.py:42
  71.1 32.3 %collective-permute-start.11 = (bf16[64,1664]{1,0:T(8,128)(2,1)S(1)}, bf16[64,1664]{1,0:T(8,128)(2,1)S(1)}, u32[]{:S(2)}, u32[]{:S(2)}) collective-permute-start(bf16[64,1664]{1,0:T(8,128)(2,1)S(1)} %get-tuple-element.21), channel_id=1, source_target_pairs={{0,4},{1,5},{2,6},{3,7},{4,0},{5,1},{6,2},{7,3},{8,12},{9,13},{10,... | collective-permute-start | bytes 638984 | tf_op jit(solution)/shard_map/ppermute | solution.py:42
  72.0 31.4 %collective-permute-start.9 = (bf16[64,1664]{1,0:T(8,128)(2,1)S(1)}, bf16[64,1664]{1,0:T(8,128)(2,1)S(1)}, u32[]{:S(2)}, u32[]{:S(2)}) collective-permute-start(bf16[64,1664]{1,0:T(8,128)(2,1)S(1)} %get-tuple-element.19), channel_id=1, source_target_pairs={{0,6},{1,7},{2,0},{3,1},{4,2},{5,3},{6,4},{7,5},{8,14},{9,15},{10,... | collective-permute-start | bytes 638984 | tf_op jit(solution)/shard_map/ppermute | solution.py:42
  75.5 51.7 %collective-permute-start.31 = (bf16[160,1664]{1,0:T(8,128)(2,1)}, bf16[160,1664]{1,0:T(8,128)(2,1)}, u32[]{:S(2)}, u32[]{:S(2)}) collective-permute-start(bf16[160,1664]{1,0:T(8,128)(2,1)} %dynamic-slice_bitcast_fusion.1), channel_id=1, source_target_pairs={{0,6},{1,7},{2,0},{3,1},{4,2},{5,3},{6,4},{7,5},{8,14},{9,15},{10,... | collective-permute-start | bytes 1597448 | tf_op jit(solution)/shard_map/ppermute | solution.py:42
  77.4 58.6 %collective-permute-start.30 = (bf16[160,1664]{1,0:T(8,128)(2,1)}, bf16[160,1664]{1,0:T(8,128)(2,1)}, u32[]{:S(2)}, u32[]{:S(2)}) collective-permute-start(bf16[160,1664]{1,0:T(8,128)(2,1)} %dynamic-slice_bitcast_fusion.1), channel_id=1, source_target_pairs={{0,4},{1,5},{2,6},{3,7},{4,0},{5,1},{6,2},{7,3},{8,12},{9,13},{10,... | collective-permute-start | bytes 1597448 | tf_op jit(solution)/shard_map/ppermute | solution.py:42
  77.7 58.3 %collective-permute-start.29 = (bf16[160,1664]{1,0:T(8,128)(2,1)}, bf16[160,1664]{1,0:T(8,128)(2,1)}, u32[]{:S(2)}, u32[]{:S(2)}) collective-permute-start(bf16[160,1664]{1,0:T(8,128)(2,1)} %dynamic-slice_bitcast_fusion.1), channel_id=1, source_target_pairs={{0,2},{1,3},{2,4},{3,5},{4,6},{5,7},{6,0},{7,1},{8,10},{9,11},{10,... | collective-permute-start | bytes 1597448 | tf_op jit(solution)/shard_map/ppermute | solution.py:42
  110.4 5.0 %collective-permute-start.14 = (bf16[16,4,832]{2,0,1:T(8,128)(2,1)}, bf16[16,4,832]{2,0,1:T(8,128)(2,1)S(1)}, u32[]{:S(2)}, u32[]{:S(2)}) collective-permute-start(bf16[16,4,832]{2,0,1:T(8,128)(2,1)} %bitcast.115), channel_id=1, source_target_pairs={{0,1},{1,0},{2,3},{3,2},{4,5},{5,4},{6,7},{7,6},{8,9},{9,8},{10,11... | collective-permute-start | bytes 319496 | tf_op jit(solution)/shard_map/ppermute | solution.py:38
  115.5 25.6 %collective-permute-start.15 = (bf16[2,16,832]{2,1,0:T(8,128)(2,1)S(1)}, bf16[2,16,832]{2,1,0:T(8,128)(2,1)S(1)}, u32[]{:S(2)}, u32[]{:S(2)}) collective-permute-start(bf16[2,16,832]{2,1,0:T(8,128)(2,1)S(1)} %get-tuple-element.35), channel_id=1, source_target_pairs={{0,2},{1,3},{2,4},{3,5},{4,6},{5,7},{6,0},{7,1},{8,10},{9,11},{10,... | collective-permute-start | bytes 159752 | tf_op jit(solution)/shard_map/ppermute | solution.py:42
  123.7 17.4 %collective-permute-start.16 = (bf16[2,16,832]{2,1,0:T(8,128)(2,1)S(1)}, bf16[2,16,832]{2,1,0:T(8,128)(2,1)S(1)}, u32[]{:S(2)}, u32[]{:S(2)}) collective-permute-start(bf16[2,16,832]{2,1,0:T(8,128)(2,1)S(1)} %get-tuple-element.34), channel_id=1, source_target_pairs={{0,4},{1,5},{2,6},{3,7},{4,0},{5,1},{6,2},{7,3},{8,12},{9,13},{10,... | collective-permute-start | bytes 159752 | tf_op jit(solution)/shard_map/ppermute | solution.py:42
  127.2 14.0 %collective-permute-start.17 = (bf16[2,16,832]{2,1,0:T(8,128)(2,1)S(1)}, bf16[2,16,832]{2,1,0:T(8,128)(2,1)S(1)}, u32[]{:S(2)}, u32[]{:S(2)}) collective-permute-start(bf16[2,16,832]{2,1,0:T(8,128)(2,1)S(1)} %get-tuple-element.33), channel_id=1, source_target_pairs={{0,6},{1,7},{2,0},{3,1},{4,2},{5,3},{6,4},{7,5},{8,14},{9,15},{10,... | collective-permute-start | bytes 159752 | tf_op jit(solution)/shard_map/ppermute | solution.py:42
  139.5 34.8 %collective-permute-start.32 = (bf16[3,160,1664]{2,1,0:T(8,128)(2,1)}, bf16[3,160,1664]{2,1,0:T(8,128)(2,1)}, u32[]{:S(2)}, u32[]{:S(2)}) collective-permute-start(bf16[3,160,1664]{2,1,0:T(8,128)(2,1)} %get-tuple-element.23), channel_id=1, source_target_pairs={{0,16},{8,24},{16,0},{24,8},{1,17},{9,25},{17,1},{25,9},{2,18},{10... | collective-permute-start | bytes 4792328 | tf_op jit(solution)/shard_map/ppermute | solution.py:158
  142.7 14.1 %copy-start.17 = (s32[1,1536]{1,0:T(1,128)S(1)}, s32[1,1536]{1,0:T(1,128)}, u32[]{:S(2)}) copy-start(s32[1,1536]{1,0:T(1,128)} %param.20) | copy-start | bytes 18436
  142.7 24.1 %copy-start.15 = (f32[1664]{0:T(1024)S(1)}, f32[1664]{0:T(1024)}, u32[]{:S(2)}) copy-start(f32[1664]{0:T(1024)} %param.21) | copy-start | bytes 19972
  143.5 6.3 %collective-permute-start.18 = (bf16[128,832]{1,0:T(8,128)(2,1)}, bf16[128,832]{1,0:T(8,128)(2,1)}, u32[]{:S(2)}, u32[]{:S(2)}) collective-permute-start(bf16[128,832]{1,0:T(8,128)(2,1)} %select_convert_fusion), channel_id=1, source_target_pairs={{0,1},{1,0},{2,3},{3,2},{4,5},{5,4},{6,7},{7,6},{8,9},{9,8},{10,11... | collective-permute-start | bytes 638984 | tf_op jit(solution)/shard_map/ppermute | solution.py:38
  144.1 25.0 %collective-permute-start.26 = (bf16[192,1664]{1,0:T(8,128)(2,1)}, bf16[192,1664]{1,0:T(8,128)(2,1)}, u32[]{:S(2)}, u32[]{:S(2)}) collective-permute-start(bf16[192,1664]{1,0:T(8,128)(2,1)} %bitcast.121), channel_id=1, source_target_pairs={{0,2},{1,3},{2,4},{3,5},{4,6},{5,7},{8,10},{9,11},{10,12},{11,13},... | collective-permute-start | bytes 1916936 | tf_op jit(solution)/shard_map/ppermute | solution.py:190
  152.7 6.4 %collective-permute-start.21 = (bf16[32,832]{1,0:T(8,128)(2,1)}, bf16[32,832]{1,0:T(8,128)(2,1)S(1)}, u32[]{:S(2)}, u32[]{:S(2)}) collective-permute-start(bf16[32,832]{1,0:T(8,128)(2,1)} %get-tuple-element.31), channel_id=1, source_target_pairs={{0,6},{1,7},{2,0},{3,1},{4,2},{5,3},{6,4},{7,5},{8,14},{9,15},{10,... | collective-permute-start | bytes 159752 | tf_op jit(solution)/shard_map/ppermute | solution.py:42
  152.7 7.0 %collective-permute-start.20 = (bf16[32,832]{1,0:T(8,128)(2,1)}, bf16[32,832]{1,0:T(8,128)(2,1)S(1)}, u32[]{:S(2)}, u32[]{:S(2)}) collective-permute-start(bf16[32,832]{1,0:T(8,128)(2,1)} %get-tuple-element.32), channel_id=1, source_target_pairs={{0,4},{1,5},{2,6},{3,7},{4,0},{5,1},{6,2},{7,3},{8,12},{9,13},{10,... | collective-permute-start | bytes 159752 | tf_op jit(solution)/shard_map/ppermute | solution.py:42
  153.1 7.3 %collective-permute-start.19 = (bf16[32,832]{1,0:T(8,128)(2,1)}, bf16[32,832]{1,0:T(8,128)(2,1)}, u32[]{:S(2)}, u32[]{:S(2)}) collective-permute-start(bf16[32,832]{1,0:T(8,128)(2,1)} %get-tuple-element.30), channel_id=1, source_target_pairs={{0,2},{1,3},{2,4},{3,5},{4,6},{5,7},{6,0},{7,1},{8,10},{9,11},{10,... | collective-permute-start | bytes 159752 | tf_op jit(solution)/shard_map/ppermute | solution.py:42
  162.6 8.9 %collective-permute-start.22 = (bf16[32,832]{1,0:T(8,128)(2,1)}, bf16[32,832]{1,0:T(8,128)(2,1)S(1)}, u32[]{:S(2)}, u32[]{:S(2)}) collective-permute-start(bf16[32,832]{1,0:T(8,128)(2,1)} %get-tuple-element.12), channel_id=1, source_target_pairs={{0,2},{1,3},{2,4},{3,5},{4,6},{5,7},{6,0},{7,1},{8,10},{9,11},{10,... | collective-permute-start | bytes 159752 | tf_op jit(solution)/shard_map/ppermute | solution.py:42
  167.7 17.5 %collective-permute-start.28 = (bf16[192,1664]{1,0:T(8,128)(2,1)}, bf16[192,1664]{1,0:T(8,128)(2,1)S(1)}, u32[]{:S(2)}, u32[]{:S(2)}) collective-permute-start(bf16[192,1664]{1,0:T(8,128)(2,1)} %bitcast.122), channel_id=1, source_target_pairs={{0,1},{1,0},{2,3},{3,2},{4,5},{5,4},{6,7},{7,6},{8,9},{9,8},{10,11... | collective-permute-start | bytes 1916936 | tf_op jit(solution)/shard_map/ppermute | solution.py:38
  169.1 37.8 %collective-permute-start.27 = (bf16[192,1664]{1,0:T(8,128)(2,1)}, bf16[192,1664]{1,0:T(8,128)(2,1)S(1)}, u32[]{:S(2)}, u32[]{:S(2)}) collective-permute-start(bf16[192,1664]{1,0:T(8,128)(2,1)} %collective-permute-done.26), channel_id=1, source_target_pairs={{0,1},{1,0},{2,3},{3,2},{4,5},{5,4},{6,7},{7,6},{8,9},{9,8},{10,11... | collective-permute-start | bytes 1916936 | tf_op jit(solution)/shard_map/ppermute | solution.py:38
  169.7 7.0 %collective-permute-start.23 = (bf16[32,832]{1,0:T(8,128)(2,1)}, bf16[32,832]{1,0:T(8,128)(2,1)S(1)}, u32[]{:S(2)}, u32[]{:S(2)}) collective-permute-start(bf16[32,832]{1,0:T(8,128)(2,1)} %get-tuple-element.12), channel_id=1, source_target_pairs={{0,4},{1,5},{2,6},{3,7},{4,0},{5,1},{6,2},{7,3},{8,12},{9,13},{10,... | collective-permute-start | bytes 159752 | tf_op jit(solution)/shard_map/ppermute | solution.py:42
  171.5 5.8 %collective-permute-start.24 = (bf16[32,832]{1,0:T(8,128)(2,1)}, bf16[32,832]{1,0:T(8,128)(2,1)S(1)}, u32[]{:S(2)}, u32[]{:S(2)}) collective-permute-start(bf16[32,832]{1,0:T(8,128)(2,1)} %get-tuple-element.12), channel_id=1, source_target_pairs={{0,6},{1,7},{2,0},{3,1},{4,2},{5,3},{6,4},{7,5},{8,14},{9,15},{10,... | collective-permute-start | bytes 159752 | tf_op jit(solution)/shard_map/ppermute | solution.py:42
  176.6 44.9 %copy-start.1 = (bf16[2,3,160,1664]{3,2,1,0:T(8,128)(2,1)}, bf16[2,3,160,1664]{3,2,1,0:T(8,128)(2,1)S(1)}, u32[]{:S(2)}) copy-start(bf16[2,3,160,1664]{3,2,1,0:T(8,128)(2,1)S(1)} %pad_maximum_fusion.ours) | copy-start | bytes 9584644
  176.6 44.9 %collective-permute-start.33 = (bf16[2,3,160,1664]{3,2,1,0:T(8,128)(2,1)S(1)}, bf16[2,3,160,1664]{3,2,1,0:T(8,128)(2,1)S(1)}, u32[]{:S(2)}, u32[]{:S(2)}) collective-permute-start(bf16[2,3,160,1664]{3,2,1,0:T(8,128)(2,1)S(1)} %pad_maximum_fusion.ours), channel_id=1, source_target_pairs={{0,8},{8,0},{16,24},{24,16},{1,9},{9,1},{17,25},{25,17},{2,10},{10... | collective-permute-start | bytes 9584648 | tf_op jit(solution)/shard_map/ppermute | solution.py:160
  178.3 20.4 %collective-permute-start.25 = (bf16[128,832]{1,0:T(8,128)(2,1)}, bf16[128,832]{1,0:T(8,128)(2,1)S(1)}, u32[]{:S(2)}, u32[]{:S(2)}) collective-permute-start(bf16[128,832]{1,0:T(8,128)(2,1)} %bitcast.31), channel_id=1, source_target_pairs={{0,1},{1,0},{2,3},{3,2},{4,5},{5,4},{6,7},{7,6},{8,9},{9,8},{10,11... | collective-permute-start | bytes 638984 | tf_op jit(solution)/shard_map/ppermute | solution.py:38
  185.3 14.9 %collective-permute-start.36 = (bf16[64,1664]{1,0:T(8,128)(2,1)S(1)}, bf16[64,1664]{1,0:T(8,128)(2,1)S(1)}, u32[]{:S(2)}, u32[]{:S(2)}) collective-permute-start(bf16[64,1664]{1,0:T(8,128)(2,1)S(1)} %copy-done.14), channel_id=1, source_target_pairs={{0,6},{1,7},{2,0},{3,1},{4,2},{5,3},{6,4},{7,5},{8,14},{9,15},{10,... | collective-permute-start | bytes 638984 | tf_op jit(solution)/shard_map/ppermute | solution.py:42
  186.8 13.5 %collective-permute-start.35 = (bf16[64,1664]{1,0:T(8,128)(2,1)S(1)}, bf16[64,1664]{1,0:T(8,128)(2,1)S(1)}, u32[]{:S(2)}, u32[]{:S(2)}) collective-permute-start(bf16[64,1664]{1,0:T(8,128)(2,1)S(1)} %copy-done.14), channel_id=1, source_target_pairs={{0,4},{1,5},{2,6},{3,7},{4,0},{5,1},{6,2},{7,3},{8,12},{9,13},{10,... | collective-permute-start | bytes 638984 | tf_op jit(solution)/shard_map/ppermute | solution.py:42
  198.7 7.6 %collective-permute-start.34 = (bf16[64,1664]{1,0:T(8,128)(2,1)S(1)}, bf16[64,1664]{1,0:T(8,128)(2,1)S(1)}, u32[]{:S(2)}, u32[]{:S(2)}) collective-permute-start(bf16[64,1664]{1,0:T(8,128)(2,1)S(1)} %copy-done.14), channel_id=1, source_target_pairs={{0,2},{1,3},{2,4},{3,5},{4,6},{5,7},{6,0},{7,1},{8,10},{9,11},{10,... | collective-permute-start | bytes 638984 | tf_op jit(solution)/shard_map/ppermute | solution.py:42
  200.2 31.7 %copy-start.2 = (bf16[128,1664]{1,0:T(8,128)(2,1)}, bf16[128,1664]{1,0:T(8,128)(2,1)S(1)}, u32[]{:S(2)}) copy-start(bf16[128,1664]{1,0:T(8,128)(2,1)S(1)} %maximum_select_fusion.merged) | copy-start | bytes 1277956
  206.4 10.5 %collective-permute-start.37 = (bf16[3,64,1664]{2,1,0:T(8,128)(2,1)S(1)}, bf16[3,64,1664]{2,1,0:T(8,128)(2,1)S(1)}, u32[]{:S(2)}, u32[]{:S(2)}) collective-permute-start(bf16[3,64,1664]{2,1,0:T(8,128)(2,1)S(1)} %get-tuple-element.29), channel_id=1, source_target_pairs={{0,16},{8,24},{16,0},{24,8},{1,17},{9,25},{17,1},{25,9},{2,18},{10... | collective-permute-start | bytes 1916936 | tf_op jit(solution)/shard_map/ppermute | solution.py:158
  217.0 14.9 %collective-permute-start.38 = (bf16[2,3,64,1664]{3,2,1,0:T(8,128)(2,1)S(1)}, bf16[2,3,64,1664]{3,2,1,0:T(8,128)(2,1)S(1)}, u32[]{:S(2)}, u32[]{:S(2)}) collective-permute-start(bf16[2,3,64,1664]{3,2,1,0:T(8,128)(2,1)S(1)} %pad_maximum_fusion.3.ours_out), channel_id=1, source_target_pairs={{0,8},{8,0},{16,24},{24,16},{1,9},{9,1},{17,25},{25,17},{2,10},{10... | collective-permute-start | bytes 3833864 | tf_op jit(solution)/shard_map/ppermute | solution.py:160
  232.0 23.9 %copy-start.18 = (s32[1,128]{1,0:T(1,128)S(1)}, s32[1,128]{1,0:T(1,128)}, u32[]{:S(2)}) copy-start(s32[1,128]{1,0:T(1,128)} %param.18) | copy-start | bytes 1540
  254.4 17.1 %collective-permute-start.39 = (bf16[192,1664]{1,0:T(8,128)(2,1)}, bf16[192,1664]{1,0:T(8,128)(2,1)}, u32[]{:S(2)}, u32[]{:S(2)}) collective-permute-start(bf16[192,1664]{1,0:T(8,128)(2,1)} %dynamic-slice_bitcast_fusion), channel_id=1, source_target_pairs={{0,1},{1,0},{2,3},{3,2},{4,5},{5,4},{6,7},{7,6},{8,9},{9,8},{10,11... | collective-permute-start | bytes 1916936 | tf_op jit(solution)/shard_map/ppermute | solution.py:38
  (12 other events, 69.7 us)

commit v3 on v0

v3 whole, which is shorter than its diff:
```python
import functools
import math

import jax
import jax.numpy as jnp
from jax import lax
from jax.experimental import pallas as pl
from jax.experimental.pallas import tpu as pltpu
from jax.sharding import PartitionSpec as P

HD = 104
IMG_ROWS = 64


EPSILON = 1e-06


def layer_norm(values, gains):
    average = jnp.mean(values, axis=-1, keepdims=True)
    centred = values - average
    variance = jnp.mean(centred * centred, axis=-1, keepdims=True)
    return centred * lax.rsqrt(variance + EPSILON) * gains


def rms_norm(values, gains):
    return values * lax.rsqrt(jnp.mean(values * values, axis=-1, keepdims=True) + EPSILON) * gains


def pair_steps(tp_size):
    return [(i, i ^ 1) for i in range(tp_size)]


def turn_steps(tp_size, turn):
    lines = tp_size // 2
    return [(a * 2 + b, ((a + turn) % lines) * 2 + b) for a in range(lines) for b in range(2)]


def swap_pair(values, tp_size):
    return lax.ppermute(values, "tp", pair_steps(tp_size))


def turned(values, tp_size, turn):
    return lax.ppermute(values, "tp", turn_steps(tp_size, turn))


NT = (((1,), (1,)), ((), ()))
TN = (((0,), (0,)), ((), ()))


def put_quarters(whole, ours, theirs, starts, offset):
    size = ours.shape[2]
    for index in range(4):
        quarter = ours[index // 2, 0] if index % 2 == 0 else theirs[index // 2, 0]
        start = pl.multiple_of(starts[offset + index], 16)
        whole[pl.ds(start, size), :] = quarter


def put_line(whole, own, sides, middle, starts, offset, line):
    last = pl.num_programs(0) - 1

    @pl.when(line == 0)
    def _():
        whole[...] = own[...]

    @pl.when((line > 0) & (line < last))
    def _():
        put_quarters(whole, *sides, starts, offset)

    @pl.when(line == last)
    def _():
        put_quarters(whole, *middle, starts, offset)


def text_kernel(starts, gain, own, ours, theirs, *refs):
    pieces, (rows, out, whole) = refs[:-3], refs[-3:]
    step = pl.program_id(0)

    @pl.when(step == 0)
    def _():
        count = pieces[0].shape[0]
        first_side = starts[9] == 0
        for index in range(0, len(pieces), 2):
            mine, other = pieces[index][...], pieces[index + 1][...]
            both = (jnp.where(first_side, mine, other), jnp.where(first_side, other, mine))
            for half, part in enumerate(both):
                normed = rms_norm(part.astype(jnp.float32), gain[...])
                rows[pl.ds((index + half) * count, count), :] = normed.astype(jnp.bfloat16)
        whole[...] = own[...]

    @pl.when(step > 0)
    def _():
        put_quarters(whole, ours, theirs, starts, 0)

    out[0] = lax.dot_general(
        whole[...], rows[...], NT, preferred_element_type=jnp.float32
    ).astype(jnp.bfloat16)


def text_last_kernel(starts, rows, ours, theirs, before, out, whole):
    put_quarters(whole, ours, theirs, starts, 0)
    out[0] = lax.dot_general(
        whole[...], rows[...], NT, preferred_element_type=jnp.float32
    ).astype(jnp.bfloat16)


def mask_kernel(blk, longest, starts, slots, key_docs, query_docs, spread, hits, bias):
    ahead = spread.shape[1] - blk
    position = starts[8] + lax.broadcasted_iota(jnp.int32, spread.shape, 1)
    match = jnp.where(slots[...] == position, 1.0, 0.0)
    spread[...] = match.astype(jnp.bfloat16)
    hits[...] = jnp.broadcast_to(jnp.max(match, axis=0, keepdims=True), hits.shape)
    reach = longest + 128
    for block in range(blk // 128):
        first = ahead - longest + block * 128
        key_place = first + lax.broadcasted_iota(jnp.int32, (reach, 128), 0)
        query_place = ahead + block * 128 + lax.broadcasted_iota(jnp.int32, (reach, 128), 1)
        allowed = (key_place <= query_place) & (
            key_docs[pl.ds(first, reach), :] == query_docs[:, pl.ds(block * 128, 128)]
        )
        bias[block] = jnp.where(allowed, 0.0, -1e30)


def image_rows_kernel(starts, ours, theirs, gain, merged, normed):
    first_side = starts[9] == 0
    mine, other = ours[...], theirs[...]
    merged[...] = jnp.concatenate(
        [jnp.where(first_side, mine, other), jnp.where(first_side, other, mine)], axis=1
    )
    normed[...] = rms_norm(merged[...].astype(jnp.float32), gain[...]).astype(jnp.bfloat16)


def late_kernel(
    blk, longest,
    starts, image_rows, spread, hits, bias, own, ours, theirs, ours_middle, theirs_middle, text,
    kept, given, whole, blended,
):
    step = pl.program_id(0)
    put_line(whole, own, (ours, theirs), (ours_middle, theirs_middle), starts, 0, step)
    depth = blended.shape[0] // pl.num_programs(0)
    line_rows = pl.ds(pl.multiple_of(step * depth, 16), depth)
    ahead = spread.shape[1] - blk
    reach = longest + 128
    factor = math.log2(math.e) / math.sqrt(HD)
    hit = hits[0:1, :] > 0.5
    heads = whole.shape[0] // (3 * HD)
    if heads * HD < depth:
        blended[line_rows, :] = jnp.zeros((depth, blk), jnp.float32)
    image_part = lax.dot_general(
        whole[...], image_rows[...], NT, preferred_element_type=jnp.float32
    ).astype(jnp.bfloat16)
    placed = jnp.dot(image_part, spread[...], preferred_element_type=jnp.float32)
    for head in range(heads):
        base = head * 3 * HD

        def picked(part, start):
            rows = pl.ds(base + part * HD, HD)
            image = placed[base + part * HD : base + (part + 1) * HD, start:]
            return jnp.where(hit[:, start:], image, text[0, rows, start:].astype(jnp.float32))

        queries = (picked(0, ahead) * factor).astype(jnp.bfloat16)
        keys = picked(1, 0).T.astype(jnp.bfloat16)
        values = picked(2, 0).astype(jnp.bfloat16)
        for block in range(blk // 128):
            first = ahead - longest + block * 128
            columns = pl.ds(block * 128, 128)
            scores = jnp.dot(
                keys[first : first + reach],
                queries[:, block * 128 : block * 128 + 128],
                preferred_element_type=jnp.float32,
            ) + bias[block]
            raised = jnp.exp2(scores - jnp.max(scores, axis=0, keepdims=True))
            mixed = jnp.dot(
                values[:, first : first + reach],
                raised.astype(jnp.bfloat16),
                preferred_element_type=jnp.float32,
            )
            share = 1.0 / jnp.sum(raised, axis=0, keepdims=True)
            blended[pl.ds(pl.multiple_of(step * depth + head * HD, 8), HD), columns] = mixed * share

    @pl.when(step == pl.num_programs(0) - 1)
    def _():
        attended = blended[...].T.astype(jnp.bfloat16)
        half = blk // 2
        low, high = attended[:half], attended[half:]
        first_side = starts[9] == 0
        kept[...] = jnp.where(first_side, low, high)
        given[...] = jnp.where(first_side, high, low)


def project_kernel(starts, rows, own, ours, theirs, out, whole):
    depth = own.shape[0]
    whole[:depth] = own[...]
    size = ours.shape[2]
    for line in range(ours.shape[1]):
        for index in range(4):
            quarter = (ours if index % 2 == 0 else theirs)[index // 2, line]
            start = pl.multiple_of((line + 1) * depth + starts[4 + index], 16)
            whole[pl.ds(start, size), :] = quarter
    total = jnp.dot(rows[...], whole[...], preferred_element_type=jnp.float32)
    out[...] = total.astype(jnp.bfloat16)


def out_kernel(starts, text, slots, merged, kept, got, out):
    count = text.shape[0]
    position = starts[10] + lax.broadcasted_iota(jnp.int32, (count, merged.shape[0]), 0)
    match = jnp.where(slots[...] == position, 1.0, 0.0)
    placed = jnp.dot(match.astype(jnp.bfloat16), merged[...], preferred_element_type=jnp.float32)
    hit = jnp.max(match, axis=1, keepdims=True) > 0.5
    embedded = jnp.where(hit, placed, text[...].astype(jnp.float32))
    total = kept[...].astype(jnp.float32) + got[...].astype(jnp.float32)
    out[...] = (embedded + total).astype(jnp.bfloat16)


SMEM = pl.BlockSpec(memory_space=pltpu.SMEM)


def kernel_call(body, name, results, *operands, scratch=(), grid=(), specs={}, out_specs=None, aliases={}):
    return pl.pallas_call(
        body,
        grid=grid,
        in_specs=[SMEM]
        + [
            specs.get(place, whole_block(value.shape))
            for place, value in enumerate(operands)
            if place
        ],
        out_specs=out_specs or [whole_block(shape) for shape, _ in results],
        out_shape=[jax.ShapeDtypeStruct(shape, dtype) for shape, dtype in results],
        scratch_shapes=list(scratch),
        input_output_aliases=aliases,
        compiler_params=pltpu.CompilerParams(vmem_limit_bytes=56 << 20),
        cost_estimate=pl.CostEstimate(flops=1, bytes_accessed=1, transcendentals=0),
        name=name,
    )(*operands)


def quarters_spec(values, line_of):
    shape = (2, 1) + values.shape[2:]
    return pl.BlockSpec(shape, lambda k: (0, line_of(k), 0, 0))


def project(starts, rows, own, ours, theirs):
    lines = ours.shape[1] + 1
    return kernel_call(
        project_kernel, "project", [((rows.shape[0], own.shape[1]), jnp.bfloat16)],
        starts, rows, own, ours, theirs,
        scratch=[pltpu.VMEM((lines * own.shape[0], own.shape[1]), jnp.bfloat16)],
    )


def mlp_kernel(mine, other, gain, w_in, w_back, out_mine, out_other, rows, total):
    step = pl.program_id(0)
    count = mine.shape[0]

    @pl.when(step == 0)
    def _():
        for place, part in ((0, mine), (count, other)):
            normed = layer_norm(part[...].astype(jnp.float32), gain[...])
            rows[pl.ds(place, count), :] = normed.astype(jnp.bfloat16)
        total[...] = jnp.zeros_like(total)

    wide = jnp.dot(rows[...], w_in[...], preferred_element_type=jnp.float32)
    hidden = 0.5 * wide * (1.0 + lax.erf(wide * math.sqrt(0.5)))
    total[...] += jnp.dot(
        hidden.astype(jnp.bfloat16), w_back[...], preferred_element_type=jnp.float32
    )

    @pl.when(step == pl.num_programs(0) - 1)
    def _():
        out_mine[...] = total[:count].astype(jnp.bfloat16)
        out_other[...] = total[count:].astype(jnp.bfloat16)


def whole_block(shape):
    return pl.BlockSpec(shape, lambda *_: (0,) * len(shape))


def mlp(mine, other, gain, w_in, w_back):
    count, width = mine.shape
    units = w_in.shape[1]
    step = 256
    return pl.pallas_call(
        mlp_kernel,
        grid=(units // step,),
        in_specs=[
            whole_block((count, width)),
            whole_block((count, width)),
            whole_block((1, width)),
            pl.BlockSpec((width, step), lambda i: (0, i)),
            pl.BlockSpec((step, width), lambda i: (i, 0)),
        ],
        out_specs=[whole_block((count, width))] * 2,
        out_shape=[jax.ShapeDtypeStruct((count, width), jnp.bfloat16)] * 2,
        scratch_shapes=[
            pltpu.VMEM((2 * count, width), jnp.bfloat16),
            pltpu.VMEM((2 * count, width), jnp.float32),
        ],
        compiler_params=pltpu.CompilerParams(vmem_limit_bytes=16 << 20),
        cost_estimate=pl.CostEstimate(flops=1, bytes_accessed=1, transcendentals=0),
        name="mlp_rows",
    )(mine, other, gain[None], w_in, w_back)


def spread_kernel(lines, place, rows, *refs):
    parts, (gain, kept, given) = refs[:-3], refs[-3:]
    wide = rows[...].astype(jnp.float32)
    for part in parts:
        wide = wide + part[...].astype(jnp.float32)
    normed = layer_norm(wide, gain[...]).astype(jnp.bfloat16)
    size = kept.shape[2]
    quads = kept.shape[1]
    to = lax.broadcasted_iota(jnp.int32, (4 * quads, 4 * quads), 0)
    by = lax.broadcasted_iota(jnp.int32, (4 * quads, 4 * quads), 1)
    moves = jnp.where(by == to % quads * 4 + to // quads, 1.0, 0.0).astype(jnp.bfloat16)
    sorted_rows = jnp.dot(moves, normed, preferred_element_type=jnp.float32).astype(jnp.bfloat16)
    first_side = place[0] == 0
    for target in range(lines):
        row, base = target // (lines // 4), target % (lines // 4) * 2 * size
        picked = sorted_rows[row * quads : (row + 1) * quads]
        low, high = picked[:, base : base + size], picked[:, base + size : base + 2 * size]
        turn = lax.rem(target + lines - place[1], lines)
        kept[turn] = jnp.where(first_side, low, high)
        given[turn] = jnp.where(first_side, high, low)


def spread_rows(place, rows, parts, gain, lines):
    count, width = rows.shape
    shape = (lines, count // 4, 2 * width // lines)
    return pl.pallas_call(
        functools.partial(spread_kernel, lines),
        in_specs=[pl.BlockSpec(memory_space=pltpu.SMEM)]
        + [whole_block((count, width))] * (1 + len(parts))
        + [whole_block((1, width))],
        out_specs=[whole_block(shape)] * 2,
        out_shape=[jax.ShapeDtypeStruct(shape, jnp.bfloat16)] * 2,
        compiler_params=pltpu.CompilerParams(vmem_limit_bytes=56 << 20),
        cost_estimate=pl.CostEstimate(flops=1, bytes_accessed=1, transcendentals=0),
        name="spread_rows",
    )(place, rows, *parts, gain[None])


def merge_kernel(place, *refs):
    blocks, (weights, kept, given, rows) = refs[:-4], refs[-4:]
    lines = len(blocks)
    quads = blocks[0].shape[0] // 2
    for index, block in enumerate(blocks):
        base = lax.rem(place[1] + lines - index, lines) * 2
        for half in (0, 1):
            start = (base + (place[0] if half == 0 else 1 - place[0])) * quads
            rows[pl.ds(pl.multiple_of(start, 16), quads), :] = block[half * quads : half * quads + quads]
    wide = jnp.dot(rows[...], weights[...], preferred_element_type=jnp.float32)
    half = kept.shape[1]
    low, high = wide[:, :half], wide[:, half:]
    first_side = place[0] == 0
    kept[...] = jnp.where(first_side, low, high)
    given[...] = jnp.where(first_side, high, low).astype(jnp.bfloat16)


def split_kernel(needed, place, kept, got, *outs):
    for index, out in enumerate(outs):
        for image in range(needed):
            rows = pl.ds(pl.multiple_of(place[2 + index * needed + image] * IMG_ROWS, 16), IMG_ROWS)
            both = kept[rows, :] + got[rows, :].astype(jnp.float32)
            out[image * IMG_ROWS : (image + 1) * IMG_ROWS] = both.astype(jnp.bfloat16)


def merge(place, blocks, weights):
    count, size = blocks[0].shape
    rows, half = count * len(blocks), weights.shape[1] // 2
    return pl.pallas_call(
        merge_kernel,
        in_specs=[pl.BlockSpec(memory_space=pltpu.SMEM)]
        + [whole_block((count, size))] * len(blocks)
        + [whole_block(weights.shape)],
        out_specs=[whole_block((rows, half))] * 2,
        out_shape=[
            jax.ShapeDtypeStruct((rows, half), jnp.float32),
            jax.ShapeDtypeStruct((rows, half), jnp.bfloat16),
        ],
        scratch_shapes=[pltpu.VMEM((rows, size), jnp.bfloat16)],
        compiler_params=pltpu.CompilerParams(vmem_limit_bytes=56 << 20),
        cost_estimate=pl.CostEstimate(flops=1, bytes_accessed=1, transcendentals=0),
        name="merge_rows",
    )(place, *blocks, weights)


def after(values, first):
    return lax.optimization_barrier((values, first))[0]


class Queue:
    def __init__(self):
        self.last = []

    def held(self, value):
        return after(value, self.last) if self.last else value

    def passed(self, value):
        self.last = [value]
        return value

    def wait(self, value):
        self.last = self.last + [value]
        return value


def quarter_size(rows):
    return -(-rows // 64) * 16


def quarter_start(rows, index):
    return jnp.minimum(index * quarter_size(rows), rows - quarter_size(rows))


def padded(weights):
    return jnp.pad(weights, ((0, -weights.shape[0] % 16), (0, 0)))


def own_quarter(weights):
    place = lax.axis_index("req") % 4
    size = quarter_size(weights.shape[0])
    return lax.dynamic_slice_in_dim(weights, quarter_start(weights.shape[0], place), size, 0)


def other_copy(values, flip):
    return lax.ppermute(values, "req", [(i, i ^ flip) for i in range(lax.axis_size("req"))])


def line_neighbours(values, tp_size):
    lines = tp_size // 2
    if lines != 4:
        return [turned(values, tp_size, k) for k in range(1, lines)]
    up = lax.ppermute(values, "tp", [(i, i + 2) for i in range(tp_size - 2)])
    down = lax.ppermute(values, "tp", [(i + 2, i) for i in range(tp_size - 2)])
    return [up, turned(values, tp_size, 2), down]


def line_ends(parts, tp_size, queue):
    if tp_size // 2 != 4:
        return parts
    line = lax.axis_index("tp") // 2
    ends = lax.ppermute(queue.held(parts[1]), "tp", [(2, 0), (3, 1), (4, 6), (5, 7)])
    return [jnp.where(line == 0, ends, parts[0]), parts[1], jnp.where(line == 3, ends, parts[2])]


def shards(
    patches, vis_gain, w_fc1, w_fc2, merge_gain, w_merge, slots, text, docs, dec_gain, w_qkv, w_out
):
    patch_rows = patches[0]
    slot_row = slots[0]
    text_rows = text[0]
    doc_row = docs[0]
    width = patch_rows.shape[1]
    seq_here = text_rows.shape[0]
    tp_size = lax.axis_size("tp")
    lines = tp_size // 2
    line = lax.axis_index("tp") // 2
    side = lax.axis_index("tp") % 2
    place_here = jnp.stack([side, line]).astype(jnp.int32)

    blk = 2 * seq_here
    longest = seq_here * tp_size // 4
    halo = -(-longest // blk)
    ahead = halo * blk
    window = ahead + blk
    qkv_own = padded(w_qkv.T)
    out_own = padded(w_out)
    columns, depth = qkv_own.shape[0], out_own.shape[0]
    place = lax.axis_index("req") % 4
    starts = jnp.stack(
        [quarter_start(columns, place ^ i) for i in (0, 1, 2, 3)]
        + [quarter_start(depth, place ^ i) for i in (0, 1, 2, 3)]
        + [line * blk - ahead, side, (2 * line + side) * seq_here]
    ).astype(jnp.int32)
    bf16 = jnp.bfloat16

    images = slot_row.shape[0] // IMG_ROWS
    span = seq_here * tp_size // images
    tables = []
    for target in range(lines):
        held = []
        for place_of in range(images):
            low = place_of * span if place_of < images - 1 else images * span - IMG_ROWS
            inside = low < (target + 1) * blk and (place_of + 1) * span > target * blk - ahead
            held.append((not inside, (place_of - images // 2) % images))
        tables.append(sorted(held))
    needed = max(sum(not outside for outside, _ in held) for held in tables)
    table = jnp.array([[image for _, image in held[:needed]] for held in tables], jnp.int32)
    turned_table = table[(line + jnp.arange(lines)) % lines]
    place_here = jnp.concatenate([place_here, turned_table.reshape(-1)])
    by_image = slot_row.reshape(images, IMG_ROWS)
    slot_row = jnp.concatenate(
        [lax.dynamic_index_in_dim(by_image, turned_table[0, i], 0, False) for i in range(needed)]
    )
    count = needed * IMG_ROWS
    doc_window = lax.dynamic_slice_in_dim(
        jnp.concatenate([jnp.full((ahead,), -1, jnp.int32), doc_row]), line * blk, window, 0
    )

    queue = Queue()
    rounds = [k for k in range(1, lines) if k != lines // 2]
    middle = lines // 2
    other, sums, part = {}, {}, {}

    def run_mlp(k, mine):
        own, given = mlp(queue.held(mine), other[k], vis_gain, w_fc1, w_fc2)
        queue.passed((own, given))
        part[k] = own
        return swap_pair(given, tp_size)

    def add_pair(k, got):
        pair = (queue.held(part[k]).astype(jnp.float32) + got.astype(jnp.float32)).astype(bf16)
        queue.passed(pair)
        return turned(pair, tp_size, lines - k)

    swapping = swap_pair(patch_rows, tp_size)
    moving = {k: turned(patch_rows, tp_size, k) for k in rounds + [middle]}
    other[0] = queue.wait(swapping)
    text_back = []
    for steps_back in range(1, halo + 1):
        steps = [(i, i + 2 * steps_back) for i in range(tp_size - 2 * steps_back)]
        text_back.append(lax.ppermute(queue.held(text_rows), "tp", steps))
    text_other = swap_pair(queue.held(text_rows), tp_size)
    back = {0: run_mlp(0, patch_rows)}
    mine, swapping = {}, {}
    for k in rounds + [middle]:
        mine[k] = queue.wait(moving[k])
        swapping[k] = swap_pair(queue.held(mine[k]), tp_size)
    qkv_quarter, out_quarter = own_quarter(qkv_own), own_quarter(out_own)
    qkv_moving = {}

    def move_weights(k):
        qkv_moving[k] = turned(queue.held(qkv_quarter), tp_size, k)

    move_weights(rounds[0])
    for index, k in enumerate(rounds):
        other[k] = queue.wait(swapping[k])
        if index == 1:
            text_other = queue.wait(text_other)
            text_back = queue.wait(text_back)
        back[k] = run_mlp(k, mine[k])
    for index, k in enumerate(rounds):
        queue.wait(qkv_moving[k])
        if index + 1 < len(rounds):
            move_weights(rounds[index + 1])
        if index == 0:
            other[middle] = queue.wait(swapping[middle])
            back[middle] = run_mlp(middle, mine[middle])
            for j in rounds:
                sums[j] = add_pair(j, queue.wait(back[j]))
    for k in rounds:
        queue.wait(sums[k])
    sides = queue.passed(jnp.stack([queue.held(qkv_moving[k]) for k in rounds]))
    sides_far = other_copy(sides, 2)
    sums[middle] = add_pair(middle, queue.wait(back[middle]))
    pieces = []
    for rows in text_back[::-1]:
        pieces += [rows, swap_pair(queue.held(rows), tp_size)]
    spread, hits, bias = queue.passed(kernel_call(
        functools.partial(mask_kernel, blk, longest), "masks",
        [
            ((count, window), bf16),
            ((8, window), jnp.float32),
            ((blk // 128, longest + 128, 128), jnp.float32),
        ],
        starts, queue.held(slot_row[:, None]), doc_window[:, None], doc_window[None, ahead:],
    ))
    sums[0] = part[0]
    sums = [queue.wait(back[0])] + [queue.wait(sums[k]) for k in range(lines)]
    move_weights(middle)
    kept, given = queue.passed(
        spread_rows(place_here, queue.held(patch_rows), sums, merge_gain, lines)
    )
    pieces = queue.wait(pieces) + [text_rows, text_other]
    got = swap_pair(queue.held(given), tp_size)
    sides_ours = queue.passed(jnp.stack([queue.held(sides), queue.wait(sides_far)]))
    sides_theirs = other_copy(sides_ours, 1)
    got = queue.wait(got)
    blocks = queue.passed([jnp.concatenate([queue.held(kept[k]), got[k]]) for k in range(lines)])
    blocks = [blocks[0]] + [turned(blocks[k], tp_size, k) for k in range(1, lines)]
    sides_theirs = queue.wait(sides_theirs)

    def after_own(k):
        return jnp.clip(k - 1, 0, lines - 3)

    text_normed, text_parts = queue.passed(kernel_call(
        text_kernel, "text_qkv", [((window, width), bf16), ((lines, columns, window), bf16)],
        starts, queue.held(dec_gain[None]), qkv_own, sides_ours, sides_theirs, *pieces,
        grid=(lines - 1,),
        specs={place: quarters_spec(sides_ours, after_own) for place in (3, 4)},
        out_specs=[
            whole_block((window, width)),
            pl.BlockSpec((1, columns, window), lambda k: (k, 0, 0)),
        ],
        scratch=[pltpu.VMEM((columns, width), bf16)],
    ))
    queue.wait(blocks)
    kept, given = queue.passed(merge(place_here, [queue.held(blocks[0])] + blocks[1:], w_merge))
    half = kept.shape[1]
    got = swap_pair(given, tp_size)
    middle_near = queue.wait(qkv_moving[middle])
    middle_far = other_copy(queue.held(middle_near), 2)
    share = queue.passed(kernel_call(
        functools.partial(split_kernel, needed), "image_shares", [((count, half), bf16)] * lines,
        place_here, queue.held(kept), queue.wait(got),
    ))
    moving = [turned(share[k], tp_size, k) for k in range(1, lines)]
    out_moving = [turned(queue.held(out_quarter), tp_size, k) for k in rounds + [middle]]
    middle_ours = queue.passed(jnp.stack([queue.held(middle_near), queue.wait(middle_far)])[:, None])
    middle_theirs = other_copy(middle_ours, 1)
    total = queue.held(share[0]).astype(jnp.float32)
    for block in queue.wait(moving):
        total = total + block.astype(jnp.float32)
    total = queue.passed(total.astype(bf16))
    far = swap_pair(total, tp_size)
    (text_parts,) = queue.passed(kernel_call(
        text_last_kernel, "text_last", [((lines, columns, window), bf16)],
        starts, queue.held(text_normed), middle_ours, queue.wait(middle_theirs), text_parts,
        grid=(1,),
        specs={4: pl.BlockSpec(memory_space=pl.ANY)},
        out_specs=[pl.BlockSpec((1, columns, window), lambda k: (lines - 1, 0, 0))],
        scratch=[pltpu.VMEM((columns, width), bf16)],
        aliases={4: 0},
    ))
    merged, image_rows = queue.passed(kernel_call(
        image_rows_kernel, "image_rows", [((count, width), bf16)] * 2,
        starts, queue.held(total), queue.wait(far), dec_gain[None],
    ))
    out_near = queue.passed(jnp.stack(queue.wait([queue.held(part) for part in out_moving])))
    out_far = other_copy(out_near, 2)
    kept, given = queue.passed(kernel_call(
        functools.partial(late_kernel, blk, longest), "late_attention",
        [((seq_here, lines * depth), bf16)] * 2,
        starts, queue.held(image_rows), spread, hits, bias,
        qkv_own, sides_ours, sides_theirs, middle_ours, middle_theirs, text_parts,
        grid=(lines,),
        specs={
            6: quarters_spec(sides_ours, after_own),
            7: quarters_spec(sides_ours, after_own),
            10: pl.BlockSpec((1, columns, window), lambda k: (k, 0, 0)),
        },
        scratch=[pltpu.VMEM((columns, width), bf16), pltpu.VMEM((lines * depth, blk), jnp.float32)],
    ))
    out_ours = queue.passed(jnp.stack([queue.held(out_near), queue.wait(out_far)]))
    out_theirs = other_copy(out_ours, 1)
    (given,) = queue.passed(project(starts, queue.held(given), out_own, out_ours, queue.wait(out_theirs)))
    got = swap_pair(given, tp_size)
    (kept,) = queue.passed(project(starts, queue.held(kept), out_own, out_ours, out_theirs))
    (decoded,) = kernel_call(
        out_kernel, "out_rows", [((seq_here, width), bf16)],
        starts, queue.held(text_rows), slot_row[None], merged, kept, queue.wait(got),
    )
    return decoded[None]


def solution(mesh):
    placed = (
        P("req", "tp", None),
        P(),
        P(None, "tp"),
        P("tp", None),
        P(),
        P("tp", None),
        P("req", None),
        P("req", "tp", None),
        P("req", None),
        P(),
        P(None, "tp"),
        P("tp", None),
    )
    return jax.shard_map(
        shards, mesh=mesh, in_specs=placed, out_specs=P("req", "tp", None), check_vma=False
    )
```

time: 500 us -> 233 us (0.47)
  waiting for transfers between devices: 350 us -> 82.9 us
  Pallas kernels: 0 us -> 74.1 us
  matrix products: 62.5 us -> 0 us
  starting transfers between devices: 0.35 us -> 50.1 us
  blocking collectives: 42.7 us -> 0 us
  other arithmetic: 17.2 us -> 3.53 us
  between operations: 13.3 us -> 0.62 us
  local copies, waits for them, and re-layouts: 11.8 us -> 20.8 us
    reduce_scatter x3 -> x0, waiting for transfers between devices: 218 us -> none  [the longest x1 99.5 us: shards(): lax.psum_scatter(jnp.dot(attended, w_out, preferred_element_type=jnp.floa...]
    all_gather x2 -> x0, waiting for transfers between devices: 132 us -> none  [the longest x1 83.8 us: shards(): lax.all_gather(dec_in, 'tp', axis=0, tiled=True)]
    ppermute x0 -> x39, waiting for transfers between devices: none -> 82.9 us  [the longest x18 42.8 us: turned(): return lax.ppermute(values, 'tp', turn_steps(tp_size, turn))]
    pallas_call x0 -> x15, Pallas kernels: none -> 74.1 us  [the longest x9 52.6 us: kernel_call(): pl.pallas_call(body, grid=grid, in_specs=[SMEM] + [specs.get(place, whole...]
    ppermute x0 -> x39, starting transfers between devices: none -> 50.1 us  [the longest x18 25.1 us: turned(): return lax.ppermute(values, 'tp', turn_steps(tp_size, turn))]
    dot_general x8 -> x0, matrix products: 40.5 us -> none  [the longest x3 12.2 us: one_block(): jnp.einsum('hqk,khe->qhe', weights, value_rows, preferred_element_type=jn...]
    all_gather x1 -> x0, blocking collectives: 31.3 us -> none  [shards(): merged = lax.all_gather(merged_share, 'tp', axis=0, tiled=True)]
    sub x3 -> x0, matrix products: 22 us -> none  [one_block(): raised = jnp.where(allowed[None], jnp.exp(scores - largest), 0.0)]
  transfers between devices with their start and end apart: 5 -> 39, of which waited for: 5 -> 16; matrix products, arithmetic and copies ran while one was open for 0% -> 5% of each run, Pallas kernels for 0% -> 29%
where the time goes in v3:
time: 233 us; the launch traced here: 232 us
  waiting for transfers between devices  82.9 us (36%)
  Pallas kernels  74.1 us (32%)
  starting transfers between devices  50.1 us (22%)
  local copies, waits for them, and re-layouts  20.8 us (9%)
  other arithmetic  3.53 us (2%)
    pallas_call x9, Pallas kernels, kernel_call(): pl.pallas_call(body, grid=grid, in_specs=[SMEM] + [specs.get(place, whole...  52.6 us
    ppermute x18, waiting for transfers between devices, turned(): return lax.ppermute(values, 'tp', turn_steps(tp_size, turn))  42.8 us
    ppermute x14, waiting for transfers between devices, swap_pair(): return lax.ppermute(values, 'tp', pair_steps(tp_size))  34.4 us
    ppermute x18, starting transfers between devices, turned(): return lax.ppermute(values, 'tp', turn_steps(tp_size, turn))  25.1 us
    ppermute x14, starting transfers between devices, swap_pair(): return lax.ppermute(values, 'tp', pair_steps(tp_size))  17 us
    pallas_call x4, Pallas kernels, mlp(): pl.pallas_call(mlp_kernel, grid=(units // step,), in_specs=[whole_block((...  15.2 us
    unnamed x69, local copies, waits for them, and re-layouts  12.1 us
    ppermute x6, waiting for transfers between devices, other_copy(): lax.ppermute(values, 'req', [(i, i ^ flip) for i in range(lax.axis_size('...  5.67 us
  transfers between devices with their start and end apart: 39, of which 16 were waited for; matrix products, arithmetic and copies ran while one was open for 5% of the time, Pallas kernels for 29%

profile of v3, /device:TPU:0, one launch (start us, length us, event | category | flops | bytes accessed | tf_op | source)
XLA Modules:
  0.0 231.9 jit_solution(1542305242466043613)
XLA Ops:
  0.0 2.9 %collective-permute-start.3 = (bf16[64,1664]{1,0:T(8,128)(2,1)}, bf16[64,1664]{1,0:T(8,128)(2,1)S(1)}, u32[]{:S(2)}, u32[]{:S(2)}) collective-permute-start(bf16[64,1664]{1,0:T(8,128)(2,1)} %bitcast.53), channel_id=1, source_target_pairs={{0,1},{1,0},{2,3},{3,2},{4,5},{5,4},{6,7},{7,6},{8,9},{9,8},{10,11... | collective-permute-start | bytes 638984 | tf_op jit(solution)/shard_map/ppermute | solution.py:39
  2.9 1.6 collective-permute-start.2
  4.5 2.2 collective-permute-start.1
  8.4 3.8 %collective-permute-start.7 = (bf16[192,1664]{1,0:T(8,128)(2,1)}, bf16[192,1664]{1,0:T(8,128)(2,1)S(1)}, u32[]{:S(2)}, u32[]{:S(2)}) collective-permute-start(bf16[192,1664]{1,0:T(8,128)(2,1)} %bitcast.63), channel_id=1, source_target_pairs={{0,2},{1,3},{2,4},{3,5},{4,6},{5,7},{8,10},{9,11},{10,12},{11,13},... | collective-permute-start | bytes 1916936 | tf_op jit(solution)/shard_map/ppermute | solution.py:522
  12.2 1.6 collective-permute-start.6
  15.6 2.0 copy-done
  17.6 2.0 copy-done.2
  20.5 3.8 %mlp_rows.4 = (bf16[64,1664]{1,0:T(8,128)(2,1)S(1)}, bf16[64,1664]{1,0:T(8,128)(2,1)S(1)}) custom-call(bf16[64,1664]{1,0:T(8,128)(2,1)S(1)} %bitcast.58, bf16[64,1664]{1,0:T(8,128)(2,1)S(1)} %collective-permute-done.3.other, f32[1,1664]{1,0:T(1,128)S(1)} %broadcast_in_dim.32.gain, bf16[1664,1024]{1,0:T(8,128)(2,1)S(1)} %copy-done, ...), custom_call_target="tpu_custom_call" | custom-call | flops 1 | bytes 1 | tf_op jit(solution)/shard_map/mlp_rows/pallas_call | solution.py:282
  26.5 1.5 collective-permute-start.5
  28.0 6.2 %collective-permute-done.4.other = bf16[64,1664]{1,0:T(8,128)(2,1)S(1)} collective-permute-done((bf16[64,1664]{1,0:T(8,128)(2,1)S(1)}, bf16[64,1664]{1,0:T(8,128)(2,1)S(1)}, u32[]{:S(2)}, u32[]{:S(2)}) %collective-permute-start.4) | collective-permute-done | bytes 213024 | tf_op jit(solution)/shard_map/ppermute | solution.py:39
  34.7 3.8 %mlp_rows.5 = (bf16[64,1664]{1,0:T(8,128)(2,1)S(1)}, bf16[64,1664]{1,0:T(8,128)(2,1)S(1)}) custom-call(bf16[64,1664]{1,0:T(8,128)(2,1)S(1)} %collective-permute-done.2.mine, bf16[64,1664]{1,0:T(8,128)(2,1)S(1)} %collective-permute-done.4.other, f32[1,1664]{1,0:T(1,128)S(1)} %broadcast_in_dim.32.gain, bf16[1664,1024]{1,0:T(8,128)(2,1)S(1)} %copy-done.1, ...), custom_call_target="tpu_custom_call" | custom-call | flops 1 | bytes 1 | tf_op jit(solution)/shard_map/mlp_rows/pallas_call | solution.py:282
  38.7 1.4 collective-permute-start.10
  40.1 3.8 %mlp_rows.6 = (bf16[64,1664]{1,0:T(8,128)(2,1)S(1)}, bf16[64,1664]{1,0:T(8,128)(2,1)S(1)}) custom-call(bf16[64,1664]{1,0:T(8,128)(2,1)S(1)} %collective-permute-done.1.mine, bf16[64,1664]{1,0:T(8,128)(2,1)S(1)} %collective-permute-done.5.other, f32[1,1664]{1,0:T(1,128)S(1)} %broadcast_in_dim.32.gain, bf16[1664,1024]{1,0:T(8,128)(2,1)S(1)} %copy-done.1, ...), custom_call_target="tpu_custom_call" | custom-call | flops 1 | bytes 1 | tf_op jit(solution)/shard_map/mlp_rows/pallas_call | solution.py:282
  44.6 3.8 %mlp_rows.7 = (bf16[64,1664]{1,0:T(8,128)(2,1)S(1)}, bf16[64,1664]{1,0:T(8,128)(2,1)S(1)}) custom-call(bf16[64,1664]{1,0:T(8,128)(2,1)S(1)} %collective-permute-done.mine, bf16[64,1664]{1,0:T(8,128)(2,1)S(1)} %collective-permute-done.9.other, f32[1,1664]{1,0:T(1,128)S(1)} %broadcast_in_dim.32.gain, bf16[1664,1024]{1,0:T(8,128)(2,1)S(1)} %copy-done.1, ...), custom_call_target="tpu_custom_call" | custom-call | flops 1 | bytes 1 | tf_op jit(solution)/shard_map/mlp_rows/pallas_call | solution.py:282
  48.5 3.4 %collective-permute-start.13 = (bf16[64,1664]{1,0:T(8,128)(2,1)S(1)}, bf16[64,1664]{1,0:T(8,128)(2,1)S(1)}, u32[]{:S(2)}, u32[]{:S(2)}) collective-permute-start(bf16[64,1664]{1,0:T(8,128)(2,1)S(1)} %add_convert_fusion.2), channel_id=1, source_target_pairs={{0,6},{1,7},{2,0},{3,1},{4,2},{5,3},{6,4},{7,5},{8,14},{9,15},{10,... | collective-permute-start | bytes 638984 | tf_op jit(solution)/shard_map/ppermute | solution.py:43
  51.9 4.8 %collective-permute-start.12 = (bf16[160,1664]{1,0:T(8,128)(2,1)S(1)}, bf16[160,1664]{1,0:T(8,128)(2,1)S(1)}, u32[]{:S(2)}, u32[]{:S(2)}) collective-permute-start(bf16[160,1664]{1,0:T(8,128)(2,1)S(1)} %dynamic-slice_bitcast_fusion), channel_id=1, source_target_pairs={{0,6},{1,7},{2,0},{3,1},{4,2},{5,3},{6,4},{7,5},{8,14},{9,15},{10,... | collective-permute-start | bytes 1597448 | tf_op jit(solution)/shard_map/ppermute | solution.py:43
  57.4 2.1 collective-permute-done.13.refs_2_
  59.5 17.0 %collective-permute-done.14.refs_4_ = bf16[64,1664]{1,0:T(8,128)(2,1)S(1)} collective-permute-done((bf16[64,1664]{1,0:T(8,128)(2,1)S(1)}, bf16[64,1664]{1,0:T(8,128)(2,1)S(1)}, u32[]{:S(2)}, u32[]{:S(2)}) %collective-permute-start.14) | collective-permute-done | bytes 213024 | tf_op jit(solution)/shard_map/ppermute | solution.py:43
  76.6 1.6 collective-permute-start.19
  84.0 1.5 collective-permute-start.16
  87.4 2.1 masks.1
  89.6 7.5 %collective-permute-done.16.refs_0_ = bf16[64,1664]{1,0:T(8,128)(2,1)} collective-permute-done((bf16[64,1664]{1,0:T(8,128)(2,1)S(1)}, bf16[64,1664]{1,0:T(8,128)(2,1)}, u32[]{:S(2)}, u32[]{:S(2)}) %collective-permute-start.16) | collective-permute-done | bytes 213024 | tf_op jit(solution)/shard_map/ppermute | solution.py:39
  97.1 2.7 %spread_rows.1 = (bf16[4,16,832]{2,1,0:T(8,128)(2,1)}, bf16[4,16,832]{2,1,0:T(8,128)(2,1)}) custom-call(s32[6]{0:T(128)} %pad_add_fusion.place, bf16[64,1664]{1,0:T(8,128)(2,1)} %bitcast.57, bf16[64,1664]{1,0:T(8,128)(2,1)} %collective-permute-done.16.refs_0_, bf16[64,1664]{1,0:T(8,128)(2,1)} %copy-done.5, bf16[64,1664]{1,0:T(8,128)(2,1)} %copy-done.18, ...), custom_call_target="tpu_custom_call" | custom-call | flops 1 | bytes 1 | tf_op jit(solution)/shard_map/spread_rows/pallas_call | solution.py:329
  103.3 3.0 %collective-permute-done.20 = bf16[4,16,832]{2,1,0:T(8,128)(2,1)S(1)} collective-permute-done((bf16[4,16,832]{2,1,0:T(8,128)(2,1)S(1)}, bf16[4,16,832]{2,1,0:T(8,128)(2,1)S(1)}, u32[]{:S(2)}, u32[]{:S(2)}) %collective-permute-start.20) | collective-permute-done | bytes 106528 | tf_op jit(solution)/shard_map/ppermute | solution.py:39
  106.3 2.1 collective-permute-start.24
  111.8 11.4 %text_qkv.1 = (bf16[768,1664]{1,0:T(8,128)(2,1)}, bf16[4,624,768]{2,1,0:T(8,128)(2,1)}) custom-call(s32[11]{0:T(128)} %stack.99.starts, f32[1,1664]{1,0:T(1,128)} %broadcast_in_dim.36.gain, bf16[624,1664]{1,0:T(8,128)(2,1)} %bitcast.59, bf16[2,2,160,1664]{3,2,1,0:T(8,128)(2,1)} %copy-done.7, bf16[2,2,160,1664]{3,2,1,0:T(8,128)(2,1)} %copy-done.10, ...), custom_call_target="tpu_custom_call" | custom-call | flops 1 | bytes 1 | tf_op jit(solution)/shard_map/text_qkv/pallas_call | solution.py:218
  123.3 9.0 %collective-permute-done.23.refs_2_ = bf16[32,832]{1,0:T(8,128)(2,1)S(1)} collective-permute-done((bf16[32,832]{1,0:T(8,128)(2,1)S(1)}, bf16[32,832]{1,0:T(8,128)(2,1)S(1)}, u32[]{:S(2)}, u32[]{:S(2)}) %collective-permute-start.23) | collective-permute-done | bytes 53280 | tf_op jit(solution)/shard_map/ppermute | solution.py:43
  132.9 3.5 %merge_rows.1 = (f32[128,832]{1,0:T(8,128)}, bf16[128,832]{1,0:T(8,128)(2,1)}) custom-call(s32[6]{0:T(128)} %pad_add_fusion.place, bf16[32,832]{1,0:T(8,128)(2,1)} %pad_maximum_fusion.4.refs_0_, bf16[32,832]{1,0:T(8,128)(2,1)} %copy-done.25, bf16[32,832]{1,0:T(8,128)(2,1)} %copy-done.24, bf16[32,832]{1,0:T(8,128)(2,1)} %copy-done.23, bf16[832,1664]{1,0:T(8,128)(2,1)} %refs_4_.1), custom_call_target="tpu_custom_call" | custom-call | flops 1 | bytes 1 | tf_op jit(solution)/shard_map/merge_rows/pallas_call | solution.py:370
  137.6 1.5 collective-permute-start.26
  139.1 5.9 %collective-permute-done.26.got = bf16[128,832]{1,0:T(8,128)(2,1)S(1)} collective-permute-done((bf16[128,832]{1,0:T(8,128)(2,1)}, bf16[128,832]{1,0:T(8,128)(2,1)S(1)}, u32[]{:S(2)}, u32[]{:S(2)}) %collective-permute-start.26) | collective-permute-done | bytes 213024 | tf_op jit(solution)/shard_map/ppermute | solution.py:39
  145.7 2.0 image_shares.1
  147.7 2.7 %collective-permute-done.27 = bf16[160,1664]{1,0:T(8,128)(2,1)S(1)} collective-permute-done((bf16[160,1664]{1,0:T(8,128)(2,1)S(1)}, bf16[160,1664]{1,0:T(8,128)(2,1)S(1)}, u32[]{:S(2)}, u32[]{:S(2)}) %collective-permute-start.27) | collective-permute-done | bytes 532512 | tf_op jit(solution)/shard_map/ppermute | solution.py:426
  150.7 1.9 collective-permute-start.29
  152.7 2.7 %collective-permute-start.30 = (bf16[64,832]{1,0:T(8,128)(2,1)S(1)}, bf16[64,832]{1,0:T(8,128)(2,1)S(1)}, u32[]{:S(2)}, u32[]{:S(2)}) collective-permute-start(bf16[64,832]{1,0:T(8,128)(2,1)S(1)} %copy-done.29), channel_id=1, source_target_pairs={{0,6},{1,7},{2,0},{3,1},{4,2},{5,3},{6,4},{7,5},{8,14},{9,15},{10,... | collective-permute-start | bytes 319496 | tf_op jit(solution)/shard_map/ppermute | solution.py:43
  156.4 2.2 collective-permute-done.28
  158.6 1.6 collective-permute-start.34
  160.2 2.4 %collective-permute-done.29 = bf16[64,832]{1,0:T(8,128)(2,1)S(1)} collective-permute-done((bf16[64,832]{1,0:T(8,128)(2,1)S(1)}, bf16[64,832]{1,0:T(8,128)(2,1)S(1)}, u32[]{:S(2)}, u32[]{:S(2)}) %collective-permute-start.29) | collective-permute-done | bytes 106528 | tf_op jit(solution)/shard_map/ppermute | solution.py:43
  163.4 1.6 collective-permute-start.32
  166.0 5.3 %text_last.1.text = bf16[4,624,768]{2,1,0:T(8,128)(2,1)} custom-call(s32[11]{0:T(128)} %stack.99.starts, bf16[768,1664]{1,0:T(8,128)(2,1)} %get-tuple-element.124.rows, bf16[2,1,160,1664]{3,2,1,0:T(8,128)(2,1)} %copy-done.9, bf16[2,1,160,1664]{3,2,1,0:T(8,128)(2,1)} %copy-done.12, ...), custom_call_target="tpu_custom_call", output_to_operand_aliasing={{}: (4, {})} | custom-call | flops 1 | bytes 1 | tf_op jit(solution)/shard_map/text_last/pallas_call | solution.py:218
  171.9 1.9 image_rows.1
  173.8 9.0 %collective-permute-done.35 = bf16[64,1664]{1,0:T(8,128)(2,1)S(1)} collective-permute-done((bf16[64,1664]{1,0:T(8,128)(2,1)S(1)}, bf16[64,1664]{1,0:T(8,128)(2,1)S(1)}, u32[]{:S(2)}, u32[]{:S(2)}) %collective-permute-start.35) | collective-permute-done | bytes 213024 | tf_op jit(solution)/shard_map/ppermute | solution.py:43
  184.2 19.3 %late_attention.1 = (bf16[192,832]{1,0:T(8,128)(2,1)}, bf16[192,832]{1,0:T(8,128)(2,1)}) custom-call(s32[11]{0:T(128)} %stack.99.starts, bf16[64,1664]{1,0:T(8,128)(2,1)} %get-tuple-element.132.image_rows, bf16[64,768]{1,0:T(8,128)(2,1)} %get-tuple-element.96.spread, f32[8,768]{1,0:T(8,128)} %get-tuple-element.97.hits, ...), custom_call_target="tpu_custom_call" | custom-call | flops 1 | bytes 1 | tf_op jit(solution)/shard_map/late_attention/pallas_call | solution.py:218
  203.7 3.0 %collective-permute-done.37.theirs = bf16[2,3,64,1664]{3,2,1,0:T(8,128)(2,1)S(1)} collective-permute-done((bf16[2,3,64,1664]{3,2,1,0:T(8,128)(2,1)S(1)}, bf16[2,3,64,1664]{3,2,1,0:T(8,128)(2,1)S(1)}, u32[]{:S(2)}, u32[]{:S(2)}) %collective-permute-start.37) | collective-permute-done | bytes 1277984 | tf_op jit(solution)/shard_map/ppermute | solution.py:426
  207.7 4.0 %project.2 = bf16[192,1664]{1,0:T(8,128)(2,1)} custom-call(s32[11]{0:T(128)} %stack.99.starts, bf16[192,832]{1,0:T(8,128)(2,1)} %get-tuple-element.136.rows, bf16[208,1664]{1,0:T(8,128)(2,1)} %own.3, bf16[2,3,64,1664]{3,2,1,0:T(8,128)(2,1)} %copy-done.8, bf16[2,3,64,1664]{3,2,1,0:T(8,128)(2,1)} %copy-done.11), custom_call_target="tpu_custom_call" | custom-call | flops 1 | bytes 1 | tf_op jit(solution)/shard_map/project/pallas_call | solution.py:218
  211.7 1.5 collective-permute-start.38
  213.7 3.9 %project.3.kept = bf16[192,1664]{1,0:T(8,128)(2,1)} custom-call(s32[11]{0:T(128)} %stack.99.starts, bf16[192,832]{1,0:T(8,128)(2,1)} %get-tuple-element.137.rows, bf16[208,1664]{1,0:T(8,128)(2,1)} %own.3, bf16[2,3,64,1664]{3,2,1,0:T(8,128)(2,1)} %copy-done.8, bf16[2,3,64,1664]{3,2,1,0:T(8,128)(2,1)} %copy-done.11), custom_call_target="tpu_custom_call" | custom-call | flops 1 | bytes 1 | tf_op jit(solution)/shard_map/project/pallas_call | solution.py:218
  217.6 10.7 %collective-permute-done.38.got = bf16[192,1664]{1,0:T(8,128)(2,1)S(1)} collective-permute-done((bf16[192,1664]{1,0:T(8,128)(2,1)}, bf16[192,1664]{1,0:T(8,128)(2,1)S(1)}, u32[]{:S(2)}, u32[]{:S(2)}) %collective-permute-start.38) | collective-permute-done | bytes 639008 | tf_op jit(solution)/shard_map/ppermute | solution.py:39
  229.2 2.8 %out_rows.1 = bf16[192,1664]{1,0:T(8,128)(2,1)} custom-call(s32[11]{0:T(128)} %stack.99.starts, bf16[192,1664]{1,0:T(8,128)(2,1)} %bitcast.66, s32[1,64]{1,0:T(1,128)} %constant_dynamic-slice_fusion.1.slots, bf16[64,1664]{1,0:T(8,128)(2,1)} %get-tuple-element.128.merged, bf16[192,1664]{1,0:T(8,128)(2,1)} %project.3.kept, bf16[192,1664]{1,0:T(8,128)(2,1)} %copy-done.13), custom_call_target="tpu_custom_call" | custom-call | flops 1 | bytes 1 | tf_op jit(solution)/shard_map/out_rows/pallas_call | solution.py:218
  (149 shorter events, 33.6 us)
Async XLA Ops:
  0.0 8.4 %collective-permute-start.3 = (bf16[64,1664]{1,0:T(8,128)(2,1)}, bf16[64,1664]{1,0:T(8,128)(2,1)S(1)}, u32[]{:S(2)}, u32[]{:S(2)}) collective-permute-start(bf16[64,1664]{1,0:T(8,128)(2,1)} %bitcast.53), channel_id=1, source_target_pairs={{0,1},{1,0},{2,3},{3,2},{4,5},{5,4},{6,7},{7,6},{8,9},{9,8},{10,11... | collective-permute-start | bytes 638984 | tf_op jit(solution)/shard_map/ppermute | solution.py:39
  2.9 21.4 %collective-permute-start.2 = (bf16[64,1664]{1,0:T(8,128)(2,1)}, bf16[64,1664]{1,0:T(8,128)(2,1)S(1)}, u32[]{:S(2)}, u32[]{:S(2)}) collective-permute-start(bf16[64,1664]{1,0:T(8,128)(2,1)} %bitcast.54), channel_id=1, source_target_pairs={{0,2},{1,3},{2,4},{3,5},{4,6},{5,7},{6,0},{7,1},{8,10},{9,11},{10,... | collective-permute-start | bytes 638984 | tf_op jit(solution)/shard_map/ppermute | solution.py:43
  4.5 19.8 %collective-permute-start.1 = (bf16[64,1664]{1,0:T(8,128)(2,1)}, bf16[64,1664]{1,0:T(8,128)(2,1)S(1)}, u32[]{:S(2)}, u32[]{:S(2)}) collective-permute-start(bf16[64,1664]{1,0:T(8,128)(2,1)} %bitcast.55), channel_id=1, source_target_pairs={{0,6},{1,7},{2,0},{3,1},{4,2},{5,3},{6,4},{7,5},{8,14},{9,15},{10,... | collective-permute-start | bytes 638984 | tf_op jit(solution)/shard_map/ppermute | solution.py:43
  6.8 18.7 %collective-permute-start = (bf16[64,1664]{1,0:T(8,128)(2,1)}, bf16[64,1664]{1,0:T(8,128)(2,1)S(1)}, u32[]{:S(2)}, u32[]{:S(2)}) collective-permute-start(bf16[64,1664]{1,0:T(8,128)(2,1)} %bitcast.56), channel_id=1, source_target_pairs={{0,4},{1,5},{2,6},{3,7},{4,0},{5,1},{6,2},{7,3},{8,12},{9,13},{10,... | collective-permute-start | bytes 638984 | tf_op jit(solution)/shard_map/ppermute | solution.py:43
  8.4 31.7 %collective-permute-start.7 = (bf16[192,1664]{1,0:T(8,128)(2,1)}, bf16[192,1664]{1,0:T(8,128)(2,1)S(1)}, u32[]{:S(2)}, u32[]{:S(2)}) collective-permute-start(bf16[192,1664]{1,0:T(8,128)(2,1)} %bitcast.63), channel_id=1, source_target_pairs={{0,2},{1,3},{2,4},{3,5},{4,6},{5,7},{8,10},{9,11},{10,12},{11,13},... | collective-permute-start | bytes 1916936 | tf_op jit(solution)/shard_map/ppermute | solution.py:522
  12.2 27.9 %collective-permute-start.6 = (bf16[192,1664]{1,0:T(8,128)(2,1)}, bf16[192,1664]{1,0:T(8,128)(2,1)S(1)}, u32[]{:S(2)}, u32[]{:S(2)}) collective-permute-start(bf16[192,1664]{1,0:T(8,128)(2,1)} %bitcast.64), channel_id=1, source_target_pairs={{0,1},{1,0},{2,3},{3,2},{4,5},{5,4},{6,7},{7,6},{8,9},{9,8},{10,11... | collective-permute-start | bytes 1916936 | tf_op jit(solution)/shard_map/ppermute | solution.py:39
  20.5 14.2 %copy-start.1 = (bf16[1664,1024]{1,0:T(8,128)(2,1)S(1)}, bf16[1664,1024]{1,0:T(8,128)(2,1)}, u32[]{:S(2)}) copy-start(bf16[1664,1024]{1,0:T(8,128)(2,1)} %w_in.7) | copy-start | bytes 10223620
  20.5 14.2 %copy-start.3 = (bf16[1024,1664]{1,0:T(8,128)(2,1)S(1)}, bf16[1024,1664]{1,0:T(8,128)(2,1)}, u32[]{:S(2)}) copy-start(bf16[1024,1664]{1,0:T(8,128)(2,1)} %w_back.7) | copy-start | bytes 10223620
  24.3 14.2 %copy-start.5 = (bf16[64,1664]{1,0:T(8,128)(2,1)}, bf16[64,1664]{1,0:T(8,128)(2,1)S(1)}, u32[]{:S(2)}) copy-start(bf16[64,1664]{1,0:T(8,128)(2,1)S(1)} %get-tuple-element.73.refs_1_) | copy-start | bytes 638980
  25.4 19.2 %collective-permute-start.8 = (bf16[160,1664]{1,0:T(8,128)(2,1)S(1)}, bf16[160,1664]{1,0:T(8,128)(2,1)S(1)}, u32[]{:S(2)}, u32[]{:S(2)}) collective-permute-start(bf16[160,1664]{1,0:T(8,128)(2,1)S(1)} %dynamic-slice_bitcast_fusion), channel_id=1, source_target_pairs={{0,2},{1,3},{2,4},{3,5},{4,6},{5,7},{6,0},{7,1},{8,10},{9,11},{10,... | collective-permute-start | bytes 1597448 | tf_op jit(solution)/shard_map/ppermute | solution.py:43
  25.9 8.2 %collective-permute-start.4 = (bf16[64,1664]{1,0:T(8,128)(2,1)S(1)}, bf16[64,1664]{1,0:T(8,128)(2,1)S(1)}, u32[]{:S(2)}, u32[]{:S(2)}) collective-permute-start(bf16[64,1664]{1,0:T(8,128)(2,1)S(1)} %collective-permute-done.2.mine), channel_id=1, source_target_pairs={{0,1},{1,0},{2,3},{3,2},{4,5},{5,4},{6,7},{7,6},{8,9},{9,8},{10,11... | collective-permute-start | bytes 638984 | tf_op jit(solution)/shard_map/ppermute | solution.py:39
  26.5 12.2 %collective-permute-start.5 = (bf16[64,1664]{1,0:T(8,128)(2,1)S(1)}, bf16[64,1664]{1,0:T(8,128)(2,1)S(1)}, u32[]{:S(2)}, u32[]{:S(2)}) collective-permute-start(bf16[64,1664]{1,0:T(8,128)(2,1)S(1)} %collective-permute-done.1.mine), channel_id=1, source_target_pairs={{0,1},{1,0},{2,3},{3,2},{4,5},{5,4},{6,7},{7,6},{8,9},{9,8},{10,11... | collective-permute-start | bytes 638984 | tf_op jit(solution)/shard_map/ppermute | solution.py:39
  34.1 10.5 %collective-permute-start.9 = (bf16[64,1664]{1,0:T(8,128)(2,1)S(1)}, bf16[64,1664]{1,0:T(8,128)(2,1)S(1)}, u32[]{:S(2)}, u32[]{:S(2)}) collective-permute-start(bf16[64,1664]{1,0:T(8,128)(2,1)S(1)} %collective-permute-done.mine), channel_id=1, source_target_pairs={{0,1},{1,0},{2,3},{3,2},{4,5},{5,4},{6,7},{7,6},{8,9},{9,8},{10,11... | collective-permute-start | bytes 638984 | tf_op jit(solution)/shard_map/ppermute | solution.py:39
  38.7 9.8 %collective-permute-start.10 = (bf16[64,1664]{1,0:T(8,128)(2,1)S(1)}, bf16[64,1664]{1,0:T(8,128)(2,1)S(1)}, u32[]{:S(2)}, u32[]{:S(2)}) collective-permute-start(bf16[64,1664]{1,0:T(8,128)(2,1)S(1)} %get-tuple-element.78), channel_id=1, source_target_pairs={{0,1},{1,0},{2,3},{3,2},{4,5},{5,4},{6,7},{7,6},{8,9},{9,8},{10,11... | collective-permute-start | bytes 638984 | tf_op jit(solution)/shard_map/ppermute | solution.py:39
  40.1 38.9 %copy-start.14 = (bf16[192,1664]{1,0:T(8,128)(2,1)}, bf16[192,1664]{1,0:T(8,128)(2,1)S(1)}, u32[]{:S(2)}) copy-start(bf16[192,1664]{1,0:T(8,128)(2,1)S(1)} %collective-permute-done.7.refs_0_) | copy-start | bytes 1916932
  43.9 12.8 %collective-permute-start.11 = (bf16[64,1664]{1,0:T(8,128)(2,1)S(1)}, bf16[64,1664]{1,0:T(8,128)(2,1)S(1)}, u32[]{:S(2)}, u32[]{:S(2)}) collective-permute-start(bf16[64,1664]{1,0:T(8,128)(2,1)S(1)} %get-tuple-element.83), channel_id=1, source_target_pairs={{0,1},{1,0},{2,3},{3,2},{4,5},{5,4},{6,7},{7,6},{8,9},{9,8},{10,11... | collective-permute-start | bytes 638984 | tf_op jit(solution)/shard_map/ppermute | solution.py:39
  48.5 11.0 %collective-permute-start.13 = (bf16[64,1664]{1,0:T(8,128)(2,1)S(1)}, bf16[64,1664]{1,0:T(8,128)(2,1)S(1)}, u32[]{:S(2)}, u32[]{:S(2)}) collective-permute-start(bf16[64,1664]{1,0:T(8,128)(2,1)S(1)} %add_convert_fusion.2), channel_id=1, source_target_pairs={{0,6},{1,7},{2,0},{3,1},{4,2},{5,3},{6,4},{7,5},{8,14},{9,15},{10,... | collective-permute-start | bytes 638984 | tf_op jit(solution)/shard_map/ppermute | solution.py:43
  51.9 24.6 %collective-permute-start.12 = (bf16[160,1664]{1,0:T(8,128)(2,1)S(1)}, bf16[160,1664]{1,0:T(8,128)(2,1)S(1)}, u32[]{:S(2)}, u32[]{:S(2)}) collective-permute-start(bf16[160,1664]{1,0:T(8,128)(2,1)S(1)} %dynamic-slice_bitcast_fusion), channel_id=1, source_target_pairs={{0,6},{1,7},{2,0},{3,1},{4,2},{5,3},{6,4},{7,5},{8,14},{9,15},{10,... | collective-permute-start | bytes 1597448 | tf_op jit(solution)/shard_map/ppermute | solution.py:43
  56.8 19.7 %collective-permute-start.14 = (bf16[64,1664]{1,0:T(8,128)(2,1)S(1)}, bf16[64,1664]{1,0:T(8,128)(2,1)S(1)}, u32[]{:S(2)}, u32[]{:S(2)}) collective-permute-start(bf16[64,1664]{1,0:T(8,128)(2,1)S(1)} %add_convert_fusion.1), channel_id=1, source_target_pairs={{0,2},{1,3},{2,4},{3,5},{4,6},{5,7},{6,0},{7,1},{8,10},{9,11},{10,... | collective-permute-start | bytes 638984 | tf_op jit(solution)/shard_map/ppermute | solution.py:43
  56.8 21.4 %collective-permute-start.15 = (bf16[64,1664]{1,0:T(8,128)(2,1)S(1)}, bf16[64,1664]{1,0:T(8,128)(2,1)S(1)}, u32[]{:S(2)}, u32[]{:S(2)}) collective-permute-start(bf16[64,1664]{1,0:T(8,128)(2,1)S(1)} %get-tuple-element.88), channel_id=1, source_target_pairs={{0,1},{1,0},{2,3},{3,2},{4,5},{5,4},{6,7},{7,6},{8,9},{9,8},{10,11... | collective-permute-start | bytes 638984 | tf_op jit(solution)/shard_map/ppermute | solution.py:39
  59.5 19.4 %copy-start.18 = (bf16[64,1664]{1,0:T(8,128)(2,1)}, bf16[64,1664]{1,0:T(8,128)(2,1)S(1)}, u32[]{:S(2)}) copy-start(bf16[64,1664]{1,0:T(8,128)(2,1)S(1)} %collective-permute-done.13.refs_2_) | copy-start | bytes 638980
  76.6 10.2 %copy-start.26 = (f32[1664]{0:T(1024)S(1)}, f32[1664]{0:T(1024)}, u32[]{:S(2)}) copy-start(f32[1664]{0:T(1024)} %param.17) | copy-start | bytes 19972
  76.6 23.2 %collective-permute-start.19 = (bf16[2,160,1664]{2,1,0:T(8,128)(2,1)S(1)}, bf16[2,160,1664]{2,1,0:T(8,128)(2,1)S(1)}, u32[]{:S(2)}, u32[]{:S(2)}) collective-permute-start(bf16[2,160,1664]{2,1,0:T(8,128)(2,1)S(1)} %pad_maximum_fusion.2), channel_id=1, source_target_pairs={{0,16},{8,24},{16,0},{24,8},{1,17},{9,25},{17,1},{25,9},{2,18},{10... | collective-permute-start | bytes 3194888 | tf_op jit(solution)/shard_map/ppermute | solution.py:426
  78.9 20.9 %collective-permute-start.18 = (bf16[192,1664]{1,0:T(8,128)(2,1)S(1)}, bf16[192,1664]{1,0:T(8,128)(2,1)}, u32[]{:S(2)}, u32[]{:S(2)}) collective-permute-start(bf16[192,1664]{1,0:T(8,128)(2,1)S(1)} %collective-permute-done.7.refs_0_), channel_id=1, source_target_pairs={{0,1},{1,0},{2,3},{3,2},{4,5},{5,4},{6,7},{7,6},{8,9},{9,8},{10,11... | collective-permute-start | bytes 1916936 | tf_op jit(solution)/shard_map/ppermute | solution.py:39
  84.0 13.1 %collective-permute-start.16 = (bf16[64,1664]{1,0:T(8,128)(2,1)S(1)}, bf16[64,1664]{1,0:T(8,128)(2,1)}, u32[]{:S(2)}, u32[]{:S(2)}) collective-permute-start(bf16[64,1664]{1,0:T(8,128)(2,1)S(1)} %get-tuple-element.74), channel_id=1, source_target_pairs={{0,1},{1,0},{2,3},{3,2},{4,5},{5,4},{6,7},{7,6},{8,9},{9,8},{10,11... | collective-permute-start | bytes 638984 | tf_op jit(solution)/shard_map/ppermute | solution.py:39
  85.5 11.6 %collective-permute-start.17 = (bf16[64,1664]{1,0:T(8,128)(2,1)}, bf16[64,1664]{1,0:T(8,128)(2,1)}, u32[]{:S(2)}, u32[]{:S(2)}) collective-permute-start(bf16[64,1664]{1,0:T(8,128)(2,1)} %add_convert_fusion), channel_id=1, source_target_pairs={{0,4},{1,5},{2,6},{3,7},{4,0},{5,1},{6,2},{7,3},{8,12},{9,13},{10,... | collective-permute-start | bytes 638984 | tf_op jit(solution)/shard_map/ppermute | solution.py:43
  100.0 10.5 %copy-start.7 = (bf16[2,2,160,1664]{3,2,1,0:T(8,128)(2,1)}, bf16[2,2,160,1664]{3,2,1,0:T(8,128)(2,1)S(1)}, u32[]{:S(2)}) copy-start(bf16[2,2,160,1664]{3,2,1,0:T(8,128)(2,1)S(1)} %pad_maximum_fusion.ours) | copy-start | bytes 6389764
  100.1 10.5 %collective-permute-start.21 = (bf16[2,2,160,1664]{3,2,1,0:T(8,128)(2,1)S(1)}, bf16[2,2,160,1664]{3,2,1,0:T(8,128)(2,1)S(1)}, u32[]{:S(2)}, u32[]{:S(2)}) collective-permute-start(bf16[2,2,160,1664]{3,2,1,0:T(8,128)(2,1)S(1)} %pad_maximum_fusion.ours), channel_id=1, source_target_pairs={{0,8},{8,0},{16,24},{24,16},{1,9},{9,1},{17,25},{25,17},{2,10},{10... | collective-permute-start | bytes 6389768 | tf_op jit(solution)/shard_map/ppermute | solution.py:426
  101.5 4.8 %collective-permute-start.20 = (bf16[4,16,832]{2,1,0:T(8,128)(2,1)S(1)}, bf16[4,16,832]{2,1,0:T(8,128)(2,1)S(1)}, u32[]{:S(2)}, u32[]{:S(2)}) collective-permute-start(bf16[4,16,832]{2,1,0:T(8,128)(2,1)S(1)} %copy-done.32), channel_id=1, source_target_pairs={{0,1},{1,0},{2,3},{3,2},{4,5},{5,4},{6,7},{7,6},{8,9},{9,8},{10,11... | collective-permute-start | bytes 319496 | tf_op jit(solution)/shard_map/ppermute | solution.py:39
  102.0 34.4 %collective-permute-start.25 = (bf16[160,1664]{1,0:T(8,128)(2,1)S(1)}, bf16[160,1664]{1,0:T(8,128)(2,1)S(1)}, u32[]{:S(2)}, u32[]{:S(2)}) collective-permute-start(bf16[160,1664]{1,0:T(8,128)(2,1)S(1)} %dynamic-slice_bitcast_fusion), channel_id=1, source_target_pairs={{0,4},{1,5},{2,6},{3,7},{4,0},{5,1},{6,2},{7,3},{8,12},{9,13},{10,... | collective-permute-start | bytes 1597448 | tf_op jit(solution)/shard_map/ppermute | solution.py:43
  106.3 16.9 %collective-permute-start.24 = (bf16[32,832]{1,0:T(8,128)(2,1)S(1)}, bf16[32,832]{1,0:T(8,128)(2,1)S(1)}, u32[]{:S(2)}, u32[]{:S(2)}) collective-permute-start(bf16[32,832]{1,0:T(8,128)(2,1)S(1)} %pad_maximum_fusion.7), channel_id=1, source_target_pairs={{0,6},{1,7},{2,0},{3,1},{4,2},{5,3},{6,4},{7,5},{8,14},{9,15},{10,... | collective-permute-start | bytes 159752 | tf_op jit(solution)/shard_map/ppermute | solution.py:43
  108.5 23.8 %collective-permute-start.23 = (bf16[32,832]{1,0:T(8,128)(2,1)S(1)}, bf16[32,832]{1,0:T(8,128)(2,1)S(1)}, u32[]{:S(2)}, u32[]{:S(2)}) collective-permute-start(bf16[32,832]{1,0:T(8,128)(2,1)S(1)} %pad_maximum_fusion.6), channel_id=1, source_target_pairs={{0,4},{1,5},{2,6},{3,7},{4,0},{5,1},{6,2},{7,3},{8,12},{9,13},{10,... | collective-permute-start | bytes 159752 | tf_op jit(solution)/shard_map/ppermute | solution.py:43
  108.6 23.7 %collective-permute-start.22 = (bf16[32,832]{1,0:T(8,128)(2,1)S(1)}, bf16[32,832]{1,0:T(8,128)(2,1)S(1)}, u32[]{:S(2)}, u32[]{:S(2)}) collective-permute-start(bf16[32,832]{1,0:T(8,128)(2,1)S(1)} %pad_maximum_fusion.5), channel_id=1, source_target_pairs={{0,2},{1,3},{2,4},{3,5},{4,6},{5,7},{6,0},{7,1},{8,10},{9,11},{10,... | collective-permute-start | bytes 159752 | tf_op jit(solution)/shard_map/ppermute | solution.py:43
  136.4 14.0 %collective-permute-start.27 = (bf16[160,1664]{1,0:T(8,128)(2,1)S(1)}, bf16[160,1664]{1,0:T(8,128)(2,1)S(1)}, u32[]{:S(2)}, u32[]{:S(2)}) collective-permute-start(bf16[160,1664]{1,0:T(8,128)(2,1)S(1)} %collective-permute-done.25), channel_id=1, source_target_pairs={{0,16},{8,24},{16,0},{24,8},{1,17},{9,25},{17,1},{25,9},{2,18},{10... | collective-permute-start | bytes 1597448 | tf_op jit(solution)/shard_map/ppermute | solution.py:426
  137.6 7.5 %collective-permute-start.26 = (bf16[128,832]{1,0:T(8,128)(2,1)}, bf16[128,832]{1,0:T(8,128)(2,1)S(1)}, u32[]{:S(2)}, u32[]{:S(2)}) collective-permute-start(bf16[128,832]{1,0:T(8,128)(2,1)} %get-tuple-element.114), channel_id=1, source_target_pairs={{0,1},{1,0},{2,3},{3,2},{4,5},{5,4},{6,7},{7,6},{8,9},{9,8},{10,11... | collective-permute-start | bytes 638984 | tf_op jit(solution)/shard_map/ppermute | solution.py:39
  150.4 12.9 %copy-start.22 = (bf16[64,832]{1,0:T(8,128)(2,1)S(1)}, bf16[64,832]{1,0:T(8,128)(2,1)}, u32[]{:S(2)}) copy-start(bf16[64,832]{1,0:T(8,128)(2,1)} %get-tuple-element.123) | copy-start | bytes 319492
  150.5 14.4 %copy-start.9 = (bf16[2,1,160,1664]{3,2,1,0:T(8,128)(2,1)}, bf16[2,1,160,1664]{3,2,1,0:T(8,128)(2,1)S(1)}, u32[]{:S(2)}) copy-start(bf16[2,1,160,1664]{3,2,1,0:T(8,128)(2,1)S(1)} %maximum_bitcast_fusion.ours.ours_middle) | copy-start | bytes 3194884
  150.5 14.4 %collective-permute-start.31 = (bf16[2,1,160,1664]{3,2,1,0:T(8,128)(2,1)S(1)}, bf16[2,1,160,1664]{3,2,1,0:T(8,128)(2,1)S(1)}, u32[]{:S(2)}, u32[]{:S(2)}) collective-permute-start(bf16[2,1,160,1664]{3,2,1,0:T(8,128)(2,1)S(1)} %maximum_bitcast_fusion.ours.ours_middle), channel_id=1, source_target_pairs={{0,8},{8,0},{16,24},{24,16},{1,9},{9,1},{17,25},{25,17},{2,10},{10... | collective-permute-start | bytes 3194888 | tf_op jit(solution)/shard_map/ppermute | solution.py:426
  150.6 7.9 %collective-permute-start.28 = (bf16[64,832]{1,0:T(8,128)(2,1)S(1)}, bf16[64,832]{1,0:T(8,128)(2,1)S(1)}, u32[]{:S(2)}, u32[]{:S(2)}) collective-permute-start(bf16[64,832]{1,0:T(8,128)(2,1)S(1)} %copy-done.31), channel_id=1, source_target_pairs={{0,2},{1,3},{2,4},{3,5},{4,6},{5,7},{6,0},{7,1},{8,10},{9,11},{10,... | collective-permute-start | bytes 319496 | tf_op jit(solution)/shard_map/ppermute | solution.py:43
  150.7 11.9 %collective-permute-start.29 = (bf16[64,832]{1,0:T(8,128)(2,1)S(1)}, bf16[64,832]{1,0:T(8,128)(2,1)S(1)}, u32[]{:S(2)}, u32[]{:S(2)}) collective-permute-start(bf16[64,832]{1,0:T(8,128)(2,1)S(1)} %copy-done.30), channel_id=1, source_target_pairs={{0,4},{1,5},{2,6},{3,7},{4,0},{5,1},{6,2},{7,3},{8,12},{9,13},{10,... | collective-permute-start | bytes 319496 | tf_op jit(solution)/shard_map/ppermute | solution.py:43
  152.7 10.7 %collective-permute-start.30 = (bf16[64,832]{1,0:T(8,128)(2,1)S(1)}, bf16[64,832]{1,0:T(8,128)(2,1)S(1)}, u32[]{:S(2)}, u32[]{:S(2)}) collective-permute-start(bf16[64,832]{1,0:T(8,128)(2,1)S(1)} %copy-done.29), channel_id=1, source_target_pairs={{0,6},{1,7},{2,0},{3,1},{4,2},{5,3},{6,4},{7,5},{8,14},{9,15},{10,... | collective-permute-start | bytes 319496 | tf_op jit(solution)/shard_map/ppermute | solution.py:43
  156.3 17.5 %collective-permute-start.33 = (bf16[64,1664]{1,0:T(8,128)(2,1)S(1)}, bf16[64,1664]{1,0:T(8,128)(2,1)S(1)}, u32[]{:S(2)}, u32[]{:S(2)}) collective-permute-start(bf16[64,1664]{1,0:T(8,128)(2,1)S(1)} %constant_dynamic-slice_fusion), channel_id=1, source_target_pairs={{0,2},{1,3},{2,4},{3,5},{4,6},{5,7},{6,0},{7,1},{8,10},{9,11},{10,... | collective-permute-start | bytes 638984 | tf_op jit(solution)/shard_map/ppermute | solution.py:43
  158.6 15.2 %collective-permute-start.34 = (bf16[64,1664]{1,0:T(8,128)(2,1)S(1)}, bf16[64,1664]{1,0:T(8,128)(2,1)S(1)}, u32[]{:S(2)}, u32[]{:S(2)}) collective-permute-start(bf16[64,1664]{1,0:T(8,128)(2,1)S(1)} %constant_dynamic-slice_fusion), channel_id=1, source_target_pairs={{0,6},{1,7},{2,0},{3,1},{4,2},{5,3},{6,4},{7,5},{8,14},{9,15},{10,... | collective-permute-start | bytes 638984 | tf_op jit(solution)/shard_map/ppermute | solution.py:43
  162.6 20.2 %collective-permute-start.35 = (bf16[64,1664]{1,0:T(8,128)(2,1)S(1)}, bf16[64,1664]{1,0:T(8,128)(2,1)S(1)}, u32[]{:S(2)}, u32[]{:S(2)}) collective-permute-start(bf16[64,1664]{1,0:T(8,128)(2,1)S(1)} %constant_dynamic-slice_fusion), channel_id=1, source_target_pairs={{0,4},{1,5},{2,6},{3,7},{4,0},{5,1},{6,2},{7,3},{8,12},{9,13},{10,... | collective-permute-start | bytes 638984 | tf_op jit(solution)/shard_map/ppermute | solution.py:43
  163.4 7.9 %collective-permute-start.32 = (bf16[64,832]{1,0:T(8,128)(2,1)S(1)}, bf16[64,832]{1,0:T(8,128)(2,1)S(1)}, u32[]{:S(2)}, u32[]{:S(2)}) collective-permute-start(bf16[64,832]{1,0:T(8,128)(2,1)S(1)} %add_convert_fusion.3.ours), channel_id=1, source_target_pairs={{0,1},{1,0},{2,3},{3,2},{4,5},{5,4},{6,7},{7,6},{8,9},{9,8},{10,11... | collective-permute-start | bytes 319496 | tf_op jit(solution)/shard_map/ppermute | solution.py:39
  182.9 20.6 %collective-permute-start.36 = (bf16[3,64,1664]{2,1,0:T(8,128)(2,1)S(1)}, bf16[3,64,1664]{2,1,0:T(8,128)(2,1)S(1)}, u32[]{:S(2)}, u32[]{:S(2)}) collective-permute-start(bf16[3,64,1664]{2,1,0:T(8,128)(2,1)S(1)} %pad_maximum_fusion.3), channel_id=1, source_target_pairs={{0,16},{8,24},{16,0},{24,8},{1,17},{9,25},{17,1},{25,9},{2,18},{10... | collective-permute-start | bytes 1916936 | tf_op jit(solution)/shard_map/ppermute | solution.py:426
  203.6 3.1 %collective-permute-start.37 = (bf16[2,3,64,1664]{3,2,1,0:T(8,128)(2,1)S(1)}, bf16[2,3,64,1664]{3,2,1,0:T(8,128)(2,1)S(1)}, u32[]{:S(2)}, u32[]{:S(2)}) collective-permute-start(bf16[2,3,64,1664]{3,2,1,0:T(8,128)(2,1)S(1)} %pad_maximum_fusion.1.ours), channel_id=1, source_target_pairs={{0,8},{8,0},{16,24},{24,16},{1,9},{9,1},{17,25},{25,17},{2,10},{10... | collective-permute-start | bytes 3833864 | tf_op jit(solution)/shard_map/ppermute | solution.py:426
  211.7 16.6 %collective-permute-start.38 = (bf16[192,1664]{1,0:T(8,128)(2,1)}, bf16[192,1664]{1,0:T(8,128)(2,1)S(1)}, u32[]{:S(2)}, u32[]{:S(2)}) collective-permute-start(bf16[192,1664]{1,0:T(8,128)(2,1)} %project.2), channel_id=1, source_target_pairs={{0,1},{1,0},{2,3},{3,2},{4,5},{5,4},{6,7},{7,6},{8,9},{9,8},{10,11... | collective-permute-start | bytes 1916936 | tf_op jit(solution)/shard_map/ppermute | solution.py:39
  (25 other events, 65.7 us)

commit v4 on v3

v4 whole, which is shorter than its diff:
```python
import functools
import math

import jax
import jax.numpy as jnp
from jax import lax
from jax.experimental import pallas as pl
from jax.experimental.pallas import tpu as pltpu
from jax.sharding import PartitionSpec as P

HD = 104
IMG_ROWS = 64
TABLE = 12


EPSILON = 1e-06


def layer_norm(values, gains):
    average = jnp.mean(values, axis=-1, keepdims=True)
    centred = values - average
    variance = jnp.mean(centred * centred, axis=-1, keepdims=True)
    return centred * lax.rsqrt(variance + EPSILON) * gains


def rms_norm(values, gains):
    return values * lax.rsqrt(jnp.mean(values * values, axis=-1, keepdims=True) + EPSILON) * gains


def pair_steps(tp_size):
    return [(i, i ^ 1) for i in range(tp_size)]


def turn_steps(tp_size, turn):
    lines = tp_size // 2
    return [(a * 2 + b, ((a + turn) % lines) * 2 + b) for a in range(lines) for b in range(2)]


def swap_pair(values, tp_size):
    return lax.ppermute(values, "tp", pair_steps(tp_size))


def turned(values, tp_size, turn):
    return lax.ppermute(values, "tp", turn_steps(tp_size, turn))


NT = (((1,), (1,)), ((), ()))
TN = (((0,), (0,)), ((), ()))


def put_quarters(whole, ours, theirs, starts, offset):
    size = ours.shape[2]
    for index in range(4):
        quarter = ours[index // 2, 0] if index % 2 == 0 else theirs[index // 2, 0]
        start = pl.multiple_of(starts[offset + index], 16)
        whole[pl.ds(start, size), :] = quarter


def text_kernel(starts, gain, own, *refs):
    pieces, (rows, out) = refs[:-2], refs[-2:]
    count = pieces[0].shape[0]
    first_side = starts[9] == 0
    for index in range(0, len(pieces), 2):
        mine, other = pieces[index][...], pieces[index + 1][...]
        both = (jnp.where(first_side, mine, other), jnp.where(first_side, other, mine))
        for half, part in enumerate(both):
            normed = rms_norm(part.astype(jnp.float32), gain[...].reshape(1, -1))
            rows[pl.ds((index + half) * count, count), :] = normed.astype(jnp.bfloat16)
    out[0] = lax.dot_general(
        own[...], rows[...], NT, preferred_element_type=jnp.float32
    ).astype(jnp.bfloat16)


def text_next_kernel(starts, rows, ours, theirs, before, out, whole):
    @pl.when(pl.program_id(0) == 0)
    def _():
        put_quarters(whole, ours, theirs, starts, 0)

    out[0] = lax.dot_general(
        whole[...], rows[...], NT, preferred_element_type=jnp.float32
    ).astype(jnp.bfloat16)


def mask_kernel(blk, longest, starts, slots, docs, spread, hits, bias, slots_here):
    count, window = spread.shape
    ahead = window - blk
    for index in range(count // IMG_ROWS):
        picked = slots[:, :IMG_ROWS]
        for image in range(1, slots.shape[1] // IMG_ROWS):
            rows = slots[:, image * IMG_ROWS : (image + 1) * IMG_ROWS]
            picked = jnp.where(starts[TABLE + index] == image, rows, picked)
        slots_here[:, index * IMG_ROWS : (index + 1) * IMG_ROWS] = jnp.broadcast_to(
            picked, (8, IMG_ROWS)
        )
    slot_columns = jnp.broadcast_to(slots_here[0:1, :].astype(jnp.float32), (128, count)).T
    position = starts[8] + lax.broadcasted_iota(jnp.int32, spread.shape, 1)
    match = jnp.where(slot_columns[:, 0:1] == position.astype(jnp.float32), 1.0, 0.0)
    spread[...] = match.astype(jnp.bfloat16)
    hits[...] = jnp.broadcast_to(jnp.max(match, axis=0, keepdims=True), hits.shape)
    line = starts[11]
    parts = []
    for back in range(ahead // blk, -1, -1):
        start = pl.multiple_of(jnp.maximum(line - back, 0) * blk, 128)
        part = docs[:, pl.ds(start, blk)].astype(jnp.float32)
        parts.append(jnp.where(line >= back, part, -1.0))
    doc_row = jnp.concatenate(parts, axis=1)
    doc_columns = jnp.broadcast_to(doc_row, (128, window)).T
    reach = longest + 128
    for block in range(blk // 128):
        first = ahead - longest + block * 128
        key_place = first + lax.broadcasted_iota(jnp.int32, (reach, 128), 0)
        query_place = ahead + block * 128 + lax.broadcasted_iota(jnp.int32, (reach, 128), 1)
        query_docs = doc_row[:, ahead + block * 128 : ahead + block * 128 + 128]
        allowed = (key_place <= query_place) & (doc_columns[first : first + reach] == query_docs)
        bias[block] = jnp.where(allowed, 0.0, -1e30)


def image_rows_kernel(starts, ours, theirs, gain, merged, normed):
    first_side = starts[9] == 0
    mine, other = ours[...], theirs[...]
    merged[...] = jnp.concatenate(
        [jnp.where(first_side, mine, other), jnp.where(first_side, other, mine)], axis=1
    )
    normed[...] = rms_norm(merged[...].astype(jnp.float32), gain[...].reshape(1, -1)).astype(jnp.bfloat16)


def late_kernel(blk, longest, lines, depth, starts, image_rows, spread, hits, bias, *refs):
    sources, near = refs[: 2 * lines], refs[2 * lines + 2 : 4 * lines + 2]
    kept, given = refs[2 * lines : 2 * lines + 2]
    whole, blended, arrived = refs[-3:]
    texts, text_near = sources[0], near[0]
    copies = [pltpu.make_async_copy(texts.at[0], text_near.at[0], arrived.at[0])]
    copies.append(pltpu.make_async_copy(sources[1], near[1], arrived.at[1]))
    for line in range(1, lines):
        for place in (2 * line, 2 * line + 1):
            copies.append(pltpu.make_async_copy(sources[place], near[place], arrived.at[place]))
        copies.append(
            pltpu.make_async_copy(texts.at[line], text_near.at[line], arrived.at[2 * lines + line])
        )
    for copy in copies:
        copy.start()
    ahead = spread.shape[1] - blk
    reach = longest + 128
    factor = math.log2(math.e) / math.sqrt(HD)
    hit = hits[0:1, :] > 0.5
    heads = near[1].shape[0] // (3 * HD)
    if heads * HD < depth:
        blended[...] = jnp.zeros_like(blended)
    for line in range(lines):
        for copy in copies[: 2] if line == 0 else copies[3 * line - 1 : 3 * line + 2]:
            copy.wait()
        if line:
            put_quarters(whole, near[2 * line], near[2 * line + 1], starts, 0)
        weights = whole if line else near[1]
        image_part = lax.dot_general(
            image_rows[...], weights[...], NT, preferred_element_type=jnp.float32
        ).astype(jnp.bfloat16)
        placed = lax.dot_general(
            image_part, spread[...], TN, preferred_element_type=jnp.float32
        )
        for head in range(heads):
            base = head * 3 * HD

            def picked(part, start):
                rows = pl.ds(base + part * HD, HD)
                image = placed[base + part * HD : base + (part + 1) * HD, start:]
                text = text_near[line, rows, start:].astype(jnp.float32)
                return jnp.where(hit[:, start:], image, text)

            queries = (picked(0, ahead) * factor).astype(jnp.bfloat16)
            keys = picked(1, 0).T.astype(jnp.bfloat16)
            values = picked(2, 0).astype(jnp.bfloat16)
            blocks = range(blk // 128)
            firsts = [ahead - longest + block * 128 for block in blocks]
            scores = [
                jnp.dot(
                    keys[first : first + reach],
                    queries[:, block * 128 : block * 128 + 128],
                    preferred_element_type=jnp.float32,
                ) + bias[block]
                for block, first in zip(blocks, firsts)
            ]
            raised = [jnp.exp2(part - jnp.max(part, axis=0, keepdims=True)) for part in scores]
            shares = [1.0 / jnp.sum(part, axis=0, keepdims=True) for part in raised]
            mixed = [
                jnp.dot(
                    values[:, first : first + reach],
                    part.astype(jnp.bfloat16),
                    preferred_element_type=jnp.float32,
                )
                for first, part in zip(firsts, raised)
            ]
            for block in blocks:
                columns = pl.ds(block * 128, 128)
                blended[pl.ds(line * depth + head * HD, HD), columns] = mixed[block] * shares[block]
    attended = blended[...].T.astype(jnp.bfloat16)
    low, high = attended[: blk // 2], attended[blk // 2 :]
    first_side = starts[9] == 0
    kept[...] = jnp.where(first_side, low, high)
    given[...] = jnp.where(first_side, high, low)


def project_kernel(starts, rows, own, ours, theirs, out, whole):
    depth = own.shape[0]
    whole[:depth] = own[...]
    size = ours.shape[2]
    for line in range(ours.shape[1]):
        for index in range(4):
            quarter = (ours if index % 2 == 0 else theirs)[index // 2, line]
            start = pl.multiple_of((line + 1) * depth + starts[4 + index], 16)
            whole[pl.ds(start, size), :] = quarter
    total = jnp.dot(rows[...], whole[...], preferred_element_type=jnp.float32)
    out[...] = total.astype(jnp.bfloat16)


def out_kernel(starts, text, slots, merged, kept, got, out):
    count = text.shape[0]
    position = starts[10] + lax.broadcasted_iota(jnp.int32, (count, merged.shape[0]), 0)
    match = jnp.where(slots[0:1, :] == position, 1.0, 0.0)
    placed = jnp.dot(match.astype(jnp.bfloat16), merged[...], preferred_element_type=jnp.float32)
    hit = jnp.max(match, axis=1, keepdims=True) > 0.5
    embedded = jnp.where(hit, placed, text[...].astype(jnp.float32))
    total = kept[...].astype(jnp.float32) + got[...].astype(jnp.float32)
    out[...] = (embedded + total).astype(jnp.bfloat16)


SMEM = pl.BlockSpec(memory_space=pltpu.SMEM)


def kernel_call(body, name, results, *operands, scratch=(), grid=(), specs={}, out_specs=None, aliases={}):
    return pl.pallas_call(
        body,
        grid=grid,
        in_specs=[SMEM]
        + [
            specs.get(place, whole_block(value.shape))
            for place, value in enumerate(operands)
            if place
        ],
        out_specs=out_specs or [whole_block(shape) for shape, _ in results],
        out_shape=[jax.ShapeDtypeStruct(shape, dtype) for shape, dtype in results],
        scratch_shapes=list(scratch),
        input_output_aliases=aliases,
        compiler_params=pltpu.CompilerParams(vmem_limit_bytes=56 << 20),
        cost_estimate=pl.CostEstimate(flops=1, bytes_accessed=1, transcendentals=0),
        name=name,
    )(*operands)


def quarters_spec(values, line_of):
    shape = (2, 1) + values.shape[2:]
    return pl.BlockSpec(shape, lambda k: (0, line_of(k), 0, 0))


def project(starts, rows, own, ours, theirs):
    lines = ours.shape[1] + 1
    return kernel_call(
        project_kernel, "project", [((rows.shape[0], own.shape[1]), jnp.bfloat16)],
        starts, rows, own, ours, theirs,
        scratch=[pltpu.VMEM((lines * own.shape[0], own.shape[1]), jnp.bfloat16)],
    )


def mlp_kernel(mine, other, gain, w_in, w_back, out_mine, out_other, rows, total):
    step = pl.program_id(0)
    count = mine.shape[0]

    @pl.when(step == 0)
    def _():
        for place, part in ((0, mine), (count, other)):
            normed = layer_norm(part[...].astype(jnp.float32), gain[...].reshape(1, -1))
            rows[pl.ds(place, count), :] = normed.astype(jnp.bfloat16)
        total[...] = jnp.zeros_like(total)

    wide = jnp.dot(rows[...], w_in[...], preferred_element_type=jnp.float32)
    hidden = 0.5 * wide * (1.0 + lax.erf(wide * math.sqrt(0.5)))
    total[...] += jnp.dot(
        hidden.astype(jnp.bfloat16), w_back[...], preferred_element_type=jnp.float32
    )

    @pl.when(step == pl.num_programs(0) - 1)
    def _():
        out_mine[...] = total[:count].astype(jnp.bfloat16)
        out_other[...] = total[count:].astype(jnp.bfloat16)


def whole_block(shape):
    return pl.BlockSpec(shape, lambda *_: (0,) * len(shape))


def mlp(mine, other, gain, w_in, w_back):
    count, width = mine.shape
    units = w_in.shape[1]
    step = 256
    return pl.pallas_call(
        mlp_kernel,
        grid=(units // step,),
        in_specs=[
            whole_block((count, width)),
            whole_block((count, width)),
            whole_block((width,)),
            pl.BlockSpec((width, step), lambda i: (0, i)),
            pl.BlockSpec((step, width), lambda i: (i, 0)),
        ],
        out_specs=[whole_block((count, width))] * 2,
        out_shape=[jax.ShapeDtypeStruct((count, width), jnp.bfloat16)] * 2,
        scratch_shapes=[
            pltpu.VMEM((2 * count, width), jnp.bfloat16),
            pltpu.VMEM((2 * count, width), jnp.float32),
        ],
        compiler_params=pltpu.CompilerParams(vmem_limit_bytes=16 << 20),
        cost_estimate=pl.CostEstimate(flops=1, bytes_accessed=1, transcendentals=0),
        name="mlp_rows",
    )(mine, other, gain, w_in, w_back)


def spread_kernel(lines, place, rows, *refs):
    parts, (gain, kept, given) = refs[:-3], refs[-3:]
    wide = rows[...].astype(jnp.float32)
    for part in parts:
        wide = wide + part[...].astype(jnp.float32)
    normed = layer_norm(wide, gain[...].reshape(1, -1)).astype(jnp.bfloat16)
    size = kept.shape[2]
    quads = kept.shape[1]
    to = lax.broadcasted_iota(jnp.int32, (4 * quads, 4 * quads), 0)
    by = lax.broadcasted_iota(jnp.int32, (4 * quads, 4 * quads), 1)
    moves = jnp.where(by == to % quads * 4 + to // quads, 1.0, 0.0).astype(jnp.bfloat16)
    sorted_rows = jnp.dot(moves, normed, preferred_element_type=jnp.float32).astype(jnp.bfloat16)
    first_side = place[9] == 0
    for target in range(lines):
        row, base = target // (lines // 4), target % (lines // 4) * 2 * size
        picked = sorted_rows[row * quads : (row + 1) * quads]
        low, high = picked[:, base : base + size], picked[:, base + size : base + 2 * size]
        turn = lax.rem(target + lines - place[11], lines)
        kept[turn] = jnp.where(first_side, low, high)
        given[turn] = jnp.where(first_side, high, low)


def spread_rows(place, rows, parts, gain, lines):
    count, width = rows.shape
    shape = (lines, count // 4, 2 * width // lines)
    return pl.pallas_call(
        functools.partial(spread_kernel, lines),
        in_specs=[pl.BlockSpec(memory_space=pltpu.SMEM)]
        + [whole_block((count, width))] * (1 + len(parts))
        + [whole_block((width,))],
        out_specs=[whole_block(shape)] * 2,
        out_shape=[jax.ShapeDtypeStruct(shape, jnp.bfloat16)] * 2,
        compiler_params=pltpu.CompilerParams(vmem_limit_bytes=56 << 20),
        cost_estimate=pl.CostEstimate(flops=1, bytes_accessed=1, transcendentals=0),
        name="spread_rows",
    )(place, rows, *parts, gain)


def merge_kernel(place, *refs):
    blocks, (weights, kept, given, rows) = refs[:-4], refs[-4:]
    lines = len(blocks)
    quads = blocks[0].shape[0] // 2
    for index, block in enumerate(blocks):
        base = lax.rem(place[11] + lines - index, lines) * 2
        for half in (0, 1):
            start = (base + (place[9] if half == 0 else 1 - place[9])) * quads
            rows[pl.ds(pl.multiple_of(start, 16), quads), :] = block[half * quads : half * quads + quads]
    wide = jnp.dot(rows[...], weights[...], preferred_element_type=jnp.float32)
    half = kept.shape[1]
    low, high = wide[:, :half], wide[:, half:]
    first_side = place[9] == 0
    kept[...] = jnp.where(first_side, low, high)
    given[...] = jnp.where(first_side, high, low).astype(jnp.bfloat16)


def split_kernel(needed, place, kept, got, *outs):
    for index, out in enumerate(outs):
        for image in range(needed):
            rows = pl.ds(pl.multiple_of(place[TABLE + index * needed + image] * IMG_ROWS, 16), IMG_ROWS)
            both = kept[rows, :] + got[rows, :].astype(jnp.float32)
            out[image * IMG_ROWS : (image + 1) * IMG_ROWS] = both.astype(jnp.bfloat16)


def merge(place, blocks, weights):
    count, size = blocks[0].shape
    rows, half = count * len(blocks), weights.shape[1] // 2
    return pl.pallas_call(
        merge_kernel,
        in_specs=[pl.BlockSpec(memory_space=pltpu.SMEM)]
        + [whole_block((count, size))] * len(blocks)
        + [whole_block(weights.shape)],
        out_specs=[whole_block((rows, half))] * 2,
        out_shape=[
            jax.ShapeDtypeStruct((rows, half), jnp.float32),
            jax.ShapeDtypeStruct((rows, half), jnp.bfloat16),
        ],
        scratch_shapes=[pltpu.VMEM((rows, size), jnp.bfloat16)],
        compiler_params=pltpu.CompilerParams(vmem_limit_bytes=16 << 20),
        cost_estimate=pl.CostEstimate(flops=1, bytes_accessed=1, transcendentals=0),
        name="merge_rows",
    )(place, *blocks, weights)


def after(values, first):
    return lax.optimization_barrier((values, first))[0]


class Queue:
    def __init__(self):
        self.last = []

    def held(self, value):
        return after(value, self.last) if self.last else value

    def passed(self, value):
        self.last = [value]
        return value

    def wait(self, value):
        self.last = self.last + [value]
        return value


def quarter_size(rows):
    return -(-rows // 64) * 16


def quarter_start(rows, index):
    return jnp.minimum(index * quarter_size(rows), rows - quarter_size(rows))


def padded(weights):
    return jnp.pad(weights, ((0, -weights.shape[0] % 16), (0, 0)))


def own_quarter(weights):
    place = lax.axis_index("req") % 4
    size = quarter_size(weights.shape[0])
    return lax.dynamic_slice_in_dim(weights, quarter_start(weights.shape[0], place), size, 0)


def other_copy(values, flip):
    return lax.ppermute(values, "req", [(i, i ^ flip) for i in range(lax.axis_size("req"))])


def line_neighbours(values, tp_size):
    lines = tp_size // 2
    if lines != 4:
        return [turned(values, tp_size, k) for k in range(1, lines)]
    up = lax.ppermute(values, "tp", [(i, i + 2) for i in range(tp_size - 2)])
    down = lax.ppermute(values, "tp", [(i + 2, i) for i in range(tp_size - 2)])
    return [up, turned(values, tp_size, 2), down]


def line_ends(parts, tp_size, queue):
    if tp_size // 2 != 4:
        return parts
    line = lax.axis_index("tp") // 2
    ends = lax.ppermute(queue.held(parts[1]), "tp", [(2, 0), (3, 1), (4, 6), (5, 7)])
    return [jnp.where(line == 0, ends, parts[0]), parts[1], jnp.where(line == 3, ends, parts[2])]


def shards(
    patches, vis_gain, w_fc1, w_fc2, merge_gain, w_merge, slots, text, docs, dec_gain, w_qkv, w_out
):
    patch_rows = patches[0]
    text_rows = text[0]
    width = patch_rows.shape[1]
    seq_here = text_rows.shape[0]
    tp_size = lax.axis_size("tp")
    lines = tp_size // 2
    line = lax.axis_index("tp") // 2
    side = lax.axis_index("tp") % 2

    blk = 2 * seq_here
    longest = seq_here * tp_size // 4
    halo = -(-longest // blk)
    ahead = halo * blk
    window = ahead + blk
    qkv_own = padded(w_qkv.T)
    out_own = padded(w_out)
    columns, depth = qkv_own.shape[0], out_own.shape[0]
    place = lax.axis_index("req") % 4
    starts = jnp.stack(
        [quarter_start(columns, place ^ i) for i in (0, 1, 2, 3)]
        + [quarter_start(depth, place ^ i) for i in (0, 1, 2, 3)]
        + [line * blk - ahead, side, (2 * line + side) * seq_here, line]
    ).astype(jnp.int32)
    bf16 = jnp.bfloat16

    images = slots.shape[1] // IMG_ROWS
    span = seq_here * tp_size // images
    tables = []
    for target in range(lines):
        held = []
        for place_of in range(images):
            low = place_of * span if place_of < images - 1 else images * span - IMG_ROWS
            inside = low < (target + 1) * blk and (place_of + 1) * span > target * blk - ahead
            held.append((not inside, (place_of - images // 2) % images))
        tables.append(sorted(held))
    needed = max(sum(not outside for outside, _ in held) for held in tables)
    table = jnp.array([[image for _, image in held[:needed]] for held in tables], jnp.int32)
    turned_table = table[(line + jnp.arange(lines)) % lines]
    starts = jnp.concatenate([starts, turned_table.reshape(-1)])
    count = needed * IMG_ROWS
    queue = Queue()
    rounds = [k for k in range(1, lines) if k != lines // 2]
    middle = lines // 2
    other, sums, part = {}, {}, {}

    def run_mlp(k, mine):
        own, given = mlp(queue.held(mine), other[k], vis_gain, w_fc1, w_fc2)
        queue.passed((own, given))
        part[k] = own
        return swap_pair(given, tp_size)

    def add_pair(k, got):
        pair = (queue.held(part[k]).astype(jnp.float32) + got.astype(jnp.float32)).astype(bf16)
        queue.passed(pair)
        return turned(pair, tp_size, lines - k)

    swapping = swap_pair(patch_rows, tp_size)
    moving = {k: turned(patch_rows, tp_size, k) for k in rounds + [middle]}
    text_other = swap_pair(text_rows, tp_size)
    other[0] = queue.wait(swapping)
    mine, swapping = {}, {}
    for k in rounds + [middle]:
        mine[k] = queue.wait(moving[k])
    text_other = queue.wait(text_other)
    for k in rounds + [middle]:
        swapping[k] = swap_pair(queue.held(mine[k]), tp_size)
    qkv_quarter, out_quarter = own_quarter(qkv_own), own_quarter(out_own)
    qkv_moving, qkv_ours, qkv_theirs = {}, {}, {}
    place_of = {0: 0, middle: lines - 1, **{k: i + 1 for i, k in enumerate(rounds)}}

    def move_weights(k, part=0, parts=1):
        size = qkv_quarter.shape[0] // parts
        piece = qkv_quarter[part * size : (part + 1) * size]
        qkv_moving.setdefault(k, []).append(turned(queue.held(piece), tp_size, k))

    def cross_weights(k):
        halves = queue.wait(qkv_moving[k])
        qkv_moving[k] = halves[0] if len(halves) == 1 else jnp.concatenate(queue.held(halves))
        qkv_theirs[k] = other_copy(queue.held(qkv_moving[k]), 2)

    def share_weights(k):
        both = jnp.stack([queue.held(qkv_moving[k]), queue.wait(qkv_theirs[k])])
        qkv_ours[k] = queue.passed(both[:, None])
        qkv_theirs[k] = other_copy(qkv_ours[k], 1)

    text_back = []
    for steps_back in range(1, halo + 1):
        steps = [(i, i + 2 * steps_back) for i in range(tp_size - 2 * steps_back)]
        text_back.append(lax.ppermute(queue.held(text_rows), "tp", steps))
    back = {0: run_mlp(0, patch_rows)}
    for index, k in enumerate(rounds):
        other[k] = queue.wait(swapping[k])
        if index == 1:
            text_back = queue.wait(text_back)
            move_weights(middle, 0, 2)
        back[k] = run_mlp(k, mine[k])
    other[middle] = queue.wait(swapping[middle])
    back[middle] = run_mlp(middle, mine[middle])
    queue.wait(qkv_moving[middle][0])
    for k in rounds:
        sums[k] = add_pair(k, queue.wait(back[k]))
    sums[middle] = add_pair(middle, queue.wait(back[middle]))
    move_weights(middle, 1, 2)
    pieces = []
    for rows in text_back[::-1]:
        pieces += [rows, swap_pair(queue.held(rows), tp_size)]
    spread, hits, bias, slots_here = queue.passed(kernel_call(
        functools.partial(mask_kernel, blk, longest), "masks",
        [
            ((count, window), bf16),
            ((8, window), jnp.float32),
            ((blk // 128, longest + 128, 128), jnp.float32),
            ((8, count), jnp.int32),
        ],
        starts, queue.held(slots), docs,
    ))
    sums[0] = part[0]
    sums = [queue.wait(back[0])] + [queue.wait(sums[k]) for k in range(lines)]
    cross_weights(middle)
    kept, given = queue.passed(
        spread_rows(starts, queue.held(patch_rows), sums, merge_gain, lines)
    )
    got = swap_pair(queue.held(given), tp_size)
    move_weights(rounds[0])
    pieces = queue.wait(pieces) + [text_rows, text_other]
    text_normed, text_parts = queue.passed(kernel_call(
        text_kernel, "text_first", [((window, width), bf16), ((lines, columns, window), bf16)],
        starts, queue.held(dec_gain), qkv_own, *pieces,
        grid=(1,),
        out_specs=[
            whole_block((window, width)),
            pl.BlockSpec((1, columns, window), lambda _: (0, 0, 0)),
        ],
    ))

    def run_text(text_parts, k):
        return queue.passed(kernel_call(
            text_next_kernel, "text_next", [((lines, columns, window), bf16)],
            starts, queue.held(text_normed), qkv_ours[k], queue.wait(qkv_theirs[k]), text_parts,
            grid=(window // 256,),
            specs={
                1: pl.BlockSpec((256, width), lambda i: (i, 0)),
                4: pl.BlockSpec(memory_space=pl.ANY),
            },
            out_specs=[pl.BlockSpec((1, columns, 256), lambda i: (place_of[k], 0, i))],
            scratch=[pltpu.VMEM((columns, width), bf16)],
            aliases={4: 0},
        ))[0]

    got = queue.wait(got)
    cross_weights(rounds[0])
    share_weights(middle)
    blocks = queue.passed([jnp.concatenate([queue.held(kept[k]), got[k]]) for k in range(lines)])
    blocks = [blocks[0]] + [turned(blocks[k], tp_size, k) for k in range(1, lines)]
    queue.wait(blocks)
    kept, given = queue.passed(merge(starts, [queue.held(blocks[0])] + blocks[1:], w_merge))
    half = kept.shape[1]
    got = swap_pair(given, tp_size)
    for k in rounds[1:]:
        move_weights(k)
    text_parts = run_text(text_parts, middle)
    got = queue.wait(got)
    for k in rounds[1:]:
        cross_weights(k)
    share_weights(rounds[0])
    share = queue.passed(kernel_call(
        functools.partial(split_kernel, needed), "image_shares", [((count, half), bf16)] * lines,
        starts, queue.held(kept), got,
    ))
    moving = [turned(share[k], tp_size, k) for k in range(1, lines)]
    text_parts = run_text(text_parts, rounds[0])
    total = queue.held(share[0]).astype(jnp.float32)
    for block in queue.wait(moving):
        total = total + block.astype(jnp.float32)
    total = queue.passed(total.astype(bf16))
    for k in rounds[1:]:
        share_weights(k)
    far = swap_pair(queue.held(total), tp_size)
    out_moving = [turned(queue.held(out_quarter), tp_size, k) for k in rounds + [middle]]
    for k in rounds[1:]:
        text_parts = run_text(text_parts, k)
    merged, image_rows = queue.passed(kernel_call(
        image_rows_kernel, "image_rows", [((count, width), bf16)] * 2,
        starts, queue.held(total), queue.wait(far), dec_gain,
    ))
    line_pieces = [x[k] for k in rounds + [middle] for x in (qkv_ours, qkv_theirs)]
    sources = [text_parts, qkv_own] + line_pieces
    out_near = queue.passed(jnp.stack(queue.wait([queue.held(part) for part in out_moving])))
    out_far = other_copy(out_near, 2)
    kept, given = queue.passed(kernel_call(
        functools.partial(late_kernel, blk, longest, lines, depth), "late_attention",
        [((seq_here, lines * depth), bf16)] * 2,
        starts, queue.held(image_rows), spread, hits, bias, *sources,
        specs={5 + i: pl.BlockSpec(memory_space=pl.ANY) for i in range(2 * lines)},
        scratch=[pltpu.VMEM(source.shape, bf16) for source in sources] + [
            pltpu.VMEM((columns, width), bf16),
            pltpu.VMEM((lines * depth, blk), jnp.float32),
            pltpu.SemaphoreType.DMA((3 * lines,)),
        ],
    ))
    out_ours = queue.passed(jnp.stack([queue.held(out_near), queue.wait(out_far)]))
    out_theirs = other_copy(out_ours, 1)
    (given,) = queue.passed(project(starts, queue.held(given), out_own, out_ours, queue.wait(out_theirs)))
    got = swap_pair(given, tp_size)
    (kept,) = queue.passed(project(starts, queue.held(kept), out_own, out_ours, out_theirs))
    (decoded,) = kernel_call(
        out_kernel, "out_rows", [((seq_here, width), bf16)],
        starts, queue.held(text_rows), slots_here, merged, kept, queue.wait(got),
    )
    return decoded[None]


def solution(mesh):
    placed = (
        P("req", "tp", None),
        P(),
        P(None, "tp"),
        P("tp", None),
        P(),
        P("tp", None),
        P("req", None),
        P("req", "tp", None),
        P("req", None),
        P(),
        P(None, "tp"),
        P("tp", None),
    )
    return jax.shard_map(
        shards, mesh=mesh, in_specs=placed, out_specs=P("req", "tp", None), check_vma=False
    )
```

time: 233 us -> 223 us (0.957)
  waiting for transfers between devices: 82.9 us -> 70.3 us
  starting transfers between devices: 50.1 us -> 60.8 us
  local copies, waits for them, and re-layouts: 20.8 us -> 16.3 us
  Pallas kernels: 74.1 us -> 70.8 us
    ppermute x18 -> x19, waiting for transfers between devices: 42.8 us -> 30.3 us  [turned(): return lax.ppermute(values, 'tp', turn_steps(tp_size, turn))]
    ppermute x18 -> x19, starting transfers between devices: 25.1 us -> 35.9 us  [turned(): return lax.ppermute(values, 'tp', turn_steps(tp_size, turn))]
    ppermute x14, waiting for transfers between devices: 34.4 us -> 30.4 us  [swap_pair(): return lax.ppermute(values, 'tp', pair_steps(tp_size))]
    ppermute x6 -> x8, waiting for transfers between devices: 5.67 us -> 9.62 us  [other_copy(): lax.ppermute(values, 'req', [(i, i ^ flip) for i in range(lax.axis_size('...]
    broadcast_in_dim x6 -> x0, local copies, waits for them, and re-layouts: 3.8 us -> none  [the longest x1 0.97 us: shards(): dec_gain[None]]
    ppermute x1, starting transfers between devices: 3.76 us -> 1.32 us  [shards(): text_back.append(lax.ppermute(queue.held(text_rows), 'tp', steps))]
    broadcast_in_dim x1 -> x3, other arithmetic: 0.11 us -> 2.44 us  [share_weights(): qkv_ours[k] = queue.passed(both[:, None])]
    ppermute x6 -> x8, starting transfers between devices: 4.26 us -> 5.34 us  [other_copy(): lax.ppermute(values, 'req', [(i, i ^ flip) for i in range(lax.axis_size('...]
  transfers between devices with their start and end apart: 39 -> 42, of which waited for: 16 -> 17; matrix products, arithmetic and copies ran while one was open for 5% -> 2% of each run, Pallas kernels for 29% -> 29%
where the time goes in v4:
time: 223 us; the launch traced here: 222 us
  Pallas kernels  70.8 us (32%)
  waiting for transfers between devices  70.3 us (32%)
  starting transfers between devices  60.8 us (27%)
  local copies, waits for them, and re-layouts  16.3 us (7%)
  other arithmetic  3.62 us (2%)
    pallas_call x11, Pallas kernels, kernel_call(): pl.pallas_call(body, grid=grid, in_specs=[SMEM] + [specs.get(place, whole...  51.6 us
    ppermute x19, starting transfers between devices, turned(): return lax.ppermute(values, 'tp', turn_steps(tp_size, turn))  35.9 us
    ppermute x14, waiting for transfers between devices, swap_pair(): return lax.ppermute(values, 'tp', pair_steps(tp_size))  30.4 us
    ppermute x19, waiting for transfers between devices, turned(): return lax.ppermute(values, 'tp', turn_steps(tp_size, turn))  30.3 us
    ppermute x14, starting transfers between devices, swap_pair(): return lax.ppermute(values, 'tp', pair_steps(tp_size))  18.2 us
    pallas_call x4, Pallas kernels, mlp(): pl.pallas_call(mlp_kernel, grid=(units // step,), in_specs=[whole_block((...  15.2 us
    unnamed x63, local copies, waits for them, and re-layouts  12.7 us
    ppermute x8, waiting for transfers between devices, other_copy(): lax.ppermute(values, 'req', [(i, i ^ flip) for i in range(lax.axis_size('...  9.62 us
  transfers between devices with their start and end apart: 42, of which 17 were waited for; matrix products, arithmetic and copies ran while one was open for 2% of the time, Pallas kernels for 29%

profile of v4, /device:TPU:0, one launch (start us, length us, event | category | flops | bytes accessed | tf_op | source)
XLA Modules:
  0.0 222.2 jit_solution(15797299779035746442)
XLA Ops:
  0.0 2.9 %collective-permute-start.4 = (bf16[192,1664]{1,0:T(8,128)(2,1)}, bf16[192,1664]{1,0:T(8,128)(2,1)S(1)}, u32[]{:S(2)}, u32[]{:S(2)}) collective-permute-start(bf16[192,1664]{1,0:T(8,128)(2,1)} %bitcast.74), channel_id=1, source_target_pairs={{0,1},{1,0},{2,3},{3,2},{4,5},{5,4},{6,7},{7,6},{8,9},{9,8},{10,11... | collective-permute-start | bytes 1916936 | tf_op jit(solution)/shard_map/ppermute | solution.py:40
  3.0 2.1 collective-permute-start.2
  5.1 2.0 collective-permute-start.1
  8.1 14.0 %collective-permute-done.3.other = bf16[64,1664]{1,0:T(8,128)(2,1)S(1)} collective-permute-done((bf16[64,1664]{1,0:T(8,128)(2,1)}, bf16[64,1664]{1,0:T(8,128)(2,1)S(1)}, u32[]{:S(2)}, u32[]{:S(2)}) %collective-permute-start.3) | collective-permute-done | bytes 213024 | tf_op jit(solution)/shard_map/ppermute | solution.py:40
  22.1 3.6 %collective-permute-done.mine = bf16[64,1664]{1,0:T(8,128)(2,1)S(1)} collective-permute-done((bf16[64,1664]{1,0:T(8,128)(2,1)}, bf16[64,1664]{1,0:T(8,128)(2,1)S(1)}, u32[]{:S(2)}, u32[]{:S(2)}) %collective-permute-start) | collective-permute-done | bytes 213024 | tf_op jit(solution)/shard_map/ppermute | solution.py:44
  28.2 1.6 collective-permute-start.5
  30.4 2.0 copy-done
  32.4 2.0 copy-done.2
  34.3 3.8 %mlp_rows.4 = (bf16[64,1664]{1,0:T(8,128)(2,1)S(1)}, bf16[64,1664]{1,0:T(8,128)(2,1)S(1)}) custom-call(bf16[64,1664]{1,0:T(8,128)(2,1)S(1)} %bitcast.66, bf16[64,1664]{1,0:T(8,128)(2,1)S(1)} %collective-permute-done.3.other, f32[1664]{0:T(1024)S(1)} %copy-done.8, bf16[1664,1024]{1,0:T(8,128)(2,1)S(1)} %copy-done, bf16[1024,1664]{1,0:T(8,128)(2,1)S(1)} %copy-done.2), custom_call_target="tpu_custom_call" | custom-call | flops 1 | bytes 1 | tf_op jit(solution)/shard_map/mlp_rows/pallas_call | solution.py:295
  38.8 3.8 %mlp_rows.5 = (bf16[64,1664]{1,0:T(8,128)(2,1)S(1)}, bf16[64,1664]{1,0:T(8,128)(2,1)S(1)}) custom-call(bf16[64,1664]{1,0:T(8,128)(2,1)S(1)} %collective-permute-done.2.mine, bf16[64,1664]{1,0:T(8,128)(2,1)S(1)} %collective-permute-done.5.other, f32[1664]{0:T(1024)S(1)} %copy-done.8, bf16[1664,1024]{1,0:T(8,128)(2,1)S(1)} %copy-done.1, ...), custom_call_target="tpu_custom_call" | custom-call | flops 1 | bytes 1 | tf_op jit(solution)/shard_map/mlp_rows/pallas_call | solution.py:295
  42.7 2.8 %collective-permute-start.9 = (bf16[80,1664]{1,0:T(8,128)(2,1)S(1)}, bf16[80,1664]{1,0:T(8,128)(2,1)S(1)}, u32[]{:S(2)}, u32[]{:S(2)}) collective-permute-start(bf16[80,1664]{1,0:T(8,128)(2,1)S(1)} %get-tuple-element.96), channel_id=1, source_target_pairs={{0,4},{1,5},{2,6},{3,7},{4,0},{5,1},{6,2},{7,3},{8,12},{9,13},{10,... | collective-permute-start | bytes 798728 | tf_op jit(solution)/shard_map/ppermute | solution.py:44
  47.5 3.8 %mlp_rows.6 = (bf16[64,1664]{1,0:T(8,128)(2,1)S(1)}, bf16[64,1664]{1,0:T(8,128)(2,1)S(1)}) custom-call(bf16[64,1664]{1,0:T(8,128)(2,1)S(1)} %collective-permute-done.1.mine, bf16[64,1664]{1,0:T(8,128)(2,1)S(1)} %collective-permute-done.6.other, f32[1664]{0:T(1024)S(1)} %copy-done.8, bf16[1664,1024]{1,0:T(8,128)(2,1)S(1)} %copy-done.1, ...), custom_call_target="tpu_custom_call" | custom-call | flops 1 | bytes 1 | tf_op jit(solution)/shard_map/mlp_rows/pallas_call | solution.py:295
  51.3 1.6 collective-permute-start.11
  53.6 3.8 %mlp_rows.7 = (bf16[64,1664]{1,0:T(8,128)(2,1)S(1)}, bf16[64,1664]{1,0:T(8,128)(2,1)S(1)}) custom-call(bf16[64,1664]{1,0:T(8,128)(2,1)S(1)} %collective-permute-done.mine, bf16[64,1664]{1,0:T(8,128)(2,1)S(1)} %collective-permute-done.8.other, f32[1664]{0:T(1024)S(1)} %copy-done.8, bf16[1664,1024]{1,0:T(8,128)(2,1)S(1)} %copy-done.1, ...), custom_call_target="tpu_custom_call" | custom-call | flops 1 | bytes 1 | tf_op jit(solution)/shard_map/mlp_rows/pallas_call | solution.py:295
  57.4 1.5 collective-permute-start.12
  59.0 2.2 %collective-permute-done.11 = bf16[64,1664]{1,0:T(8,128)(2,1)S(1)} collective-permute-done((bf16[64,1664]{1,0:T(8,128)(2,1)S(1)}, bf16[64,1664]{1,0:T(8,128)(2,1)S(1)}, u32[]{:S(2)}, u32[]{:S(2)}) %collective-permute-start.11) | collective-permute-done | bytes 213024 | tf_op jit(solution)/shard_map/ppermute | solution.py:40
  61.4 2.2 collective-permute-done.12
  64.3 2.1 collective-permute-start.17
  69.3 3.3 %collective-permute-start.14 = (bf16[64,1664]{1,0:T(8,128)(2,1)S(1)}, bf16[64,1664]{1,0:T(8,128)(2,1)S(1)}, u32[]{:S(2)}, u32[]{:S(2)}) collective-permute-start(bf16[64,1664]{1,0:T(8,128)(2,1)S(1)} %add_convert_fusion.2), channel_id=1, source_target_pairs={{0,6},{1,7},{2,0},{3,1},{4,2},{5,3},{6,4},{7,5},{8,14},{9,15},{10,... | collective-permute-start | bytes 638984 | tf_op jit(solution)/shard_map/ppermute | solution.py:44
  73.9 2.0 masks.1
  76.6 14.8 %collective-permute-done.15.refs_3_ = bf16[64,1664]{1,0:T(8,128)(2,1)S(1)} collective-permute-done((bf16[64,1664]{1,0:T(8,128)(2,1)}, bf16[64,1664]{1,0:T(8,128)(2,1)S(1)}, u32[]{:S(2)}, u32[]{:S(2)}) %collective-permute-start.15) | collective-permute-done | bytes 213024 | tf_op jit(solution)/shard_map/ppermute | solution.py:44
  92.2 2.7 %spread_rows.1 = (bf16[4,16,832]{2,1,0:T(8,128)(2,1)}, bf16[4,16,832]{2,1,0:T(8,128)(2,1)}) custom-call(s32[16]{0:T(128)} %concatenate.18.starts.place, bf16[64,1664]{1,0:T(8,128)(2,1)} %bitcast.65, bf16[64,1664]{1,0:T(8,128)(2,1)} %copy-done.23, bf16[64,1664]{1,0:T(8,128)(2,1)} %copy-done.7, bf16[64,1664]{1,0:T(8,128)(2,1)} %copy-done.26, ...), custom_call_target="tpu_custom_call" | custom-call | flops 1 | bytes 1 | tf_op jit(solution)/shard_map/spread_rows/pallas_call | solution.py:342
  94.9 4.3 %collective-permute-start.20 = (bf16[160,1664]{1,0:T(8,128)(2,1)S(1)}, bf16[160,1664]{1,0:T(8,128)(2,1)S(1)}, u32[]{:S(2)}, u32[]{:S(2)}) collective-permute-start(bf16[160,1664]{1,0:T(8,128)(2,1)S(1)} %dynamic-slice_bitcast_fusion), channel_id=1, source_target_pairs={{0,2},{1,3},{2,4},{3,5},{4,6},{5,7},{6,0},{7,1},{8,10},{9,11},{10,... | collective-permute-start | bytes 1597448 | tf_op jit(solution)/shard_map/ppermute | solution.py:44
  99.2 1.6 collective-permute-start.21
  103.2 5.7 %text_first.1 = (bf16[768,1664]{1,0:T(8,128)(2,1)}, bf16[4,624,768]{2,1,0:T(8,128)(2,1)}) custom-call(s32[16]{0:T(128)} %concatenate.18.starts.place, f32[1664]{0:T(1024)} %gain.10, bf16[624,1664]{1,0:T(8,128)(2,1)} %bitcast.67, bf16[192,1664]{1,0:T(8,128)(2,1)} %copy-done.19, bf16[192,1664]{1,0:T(8,128)(2,1)} %copy-done.20, bf16[192,1664]{1,0:T(8,128)(2,1)} %bitcast.76, ...), custom_call_target="tpu_custom_call" | custom-call | flops 1 | bytes 1 | tf_op jit(solution)/shard_map/text_first/pallas_call | solution.py:231
  110.2 2.3 %collective-permute-done.21 = bf16[160,1664]{1,0:T(8,128)(2,1)S(1)} collective-permute-done((bf16[160,1664]{1,0:T(8,128)(2,1)S(1)}, bf16[160,1664]{1,0:T(8,128)(2,1)S(1)}, u32[]{:S(2)}, u32[]{:S(2)}) %collective-permute-start.21) | collective-permute-done | bytes 532512 | tf_op jit(solution)/shard_map/ppermute | solution.py:439
  112.8 2.5 %collective-permute-start.22 = (bf16[32,832]{1,0:T(8,128)(2,1)S(1)}, bf16[32,832]{1,0:T(8,128)(2,1)S(1)}, u32[]{:S(2)}, u32[]{:S(2)}) collective-permute-start(bf16[32,832]{1,0:T(8,128)(2,1)S(1)} %pad_maximum_fusion.5), channel_id=1, source_target_pairs={{0,2},{1,3},{2,4},{3,5},{4,6},{5,7},{6,0},{7,1},{8,10},{9,11},{10,... | collective-permute-start | bytes 159752 | tf_op jit(solution)/shard_map/ppermute | solution.py:44
  115.4 2.7 %collective-permute-start.24 = (bf16[32,832]{1,0:T(8,128)(2,1)S(1)}, bf16[32,832]{1,0:T(8,128)(2,1)S(1)}, u32[]{:S(2)}, u32[]{:S(2)}) collective-permute-start(bf16[32,832]{1,0:T(8,128)(2,1)S(1)} %pad_maximum_fusion.7), channel_id=1, source_target_pairs={{0,6},{1,7},{2,0},{3,1},{4,2},{5,3},{6,4},{7,5},{8,14},{9,15},{10,... | collective-permute-start | bytes 159752 | tf_op jit(solution)/shard_map/ppermute | solution.py:44
  119.1 2.4 %collective-permute-done.23.refs_2_ = bf16[32,832]{1,0:T(8,128)(2,1)S(1)} collective-permute-done((bf16[32,832]{1,0:T(8,128)(2,1)S(1)}, bf16[32,832]{1,0:T(8,128)(2,1)S(1)}, u32[]{:S(2)}, u32[]{:S(2)}) %collective-permute-start.23) | collective-permute-done | bytes 53280 | tf_op jit(solution)/shard_map/ppermute | solution.py:44
  123.6 2.7 %collective-permute-start.27 = (bf16[160,1664]{1,0:T(8,128)(2,1)S(1)}, bf16[160,1664]{1,0:T(8,128)(2,1)S(1)}, u32[]{:S(2)}, u32[]{:S(2)}) collective-permute-start(bf16[160,1664]{1,0:T(8,128)(2,1)S(1)} %dynamic-slice_bitcast_fusion), channel_id=1, source_target_pairs={{0,6},{1,7},{2,0},{3,1},{4,2},{5,3},{6,4},{7,5},{8,14},{9,15},{10,... | collective-permute-start | bytes 1597448 | tf_op jit(solution)/shard_map/ppermute | solution.py:44
  126.3 1.5 collective-permute-start.28
  130.3 5.6 %text_next.3.before = bf16[4,624,768]{2,1,0:T(8,128)(2,1)} custom-call(s32[16]{0:T(128)} %concatenate.18.starts.place, bf16[768,1664]{1,0:T(8,128)(2,1)} %get-tuple-element.139.rows, bf16[2,1,160,1664]{3,2,1,0:T(8,128)(2,1)} %copy-done.12, bf16[2,1,160,1664]{3,2,1,0:T(8,128)(2,1)} %copy-done.14, ...), custom_call_target="tpu_custom_call", output_to_operand_aliasing={{}: (4, {})} | custom-call | flops 1 | bytes 1 | tf_op jit(solution)/shard_map/text_next/pallas_call | solution.py:231
  135.9 1.6 collective-permute-done.27
  141.7 1.9 image_shares.1
  144.0 2.3 %collective-permute-start.31 = (bf16[64,832]{1,0:T(8,128)(2,1)}, bf16[64,832]{1,0:T(8,128)(2,1)S(1)}, u32[]{:S(2)}, u32[]{:S(2)}) collective-permute-start(bf16[64,832]{1,0:T(8,128)(2,1)} %get-tuple-element.133), channel_id=1, source_target_pairs={{0,4},{1,5},{2,6},{3,7},{4,0},{5,1},{6,2},{7,3},{8,12},{9,13},{10,... | collective-permute-start | bytes 319496 | tf_op jit(solution)/shard_map/ppermute | solution.py:44
  146.3 1.8 collective-permute-start.32
  149.1 5.6 %text_next.4.before = bf16[4,624,768]{2,1,0:T(8,128)(2,1)} custom-call(s32[16]{0:T(128)} %concatenate.18.starts.place, bf16[768,1664]{1,0:T(8,128)(2,1)} %get-tuple-element.139.rows, bf16[2,1,160,1664]{3,2,1,0:T(8,128)(2,1)} %get-tuple-element.157.ours.refs_2_, bf16[2,1,160,1664]{3,2,1,0:T(8,128)(2,1)} %bitcast.69, ...), custom_call_target="tpu_custom_call", output_to_operand_aliasing={{}: (4, {})} | custom-call | flops 1 | bytes 1 | tf_op jit(solution)/shard_map/text_next/pallas_call | solution.py:231
  159.5 3.3 %collective-permute-start.37 = (bf16[64,1664]{1,0:T(8,128)(2,1)S(1)}, bf16[64,1664]{1,0:T(8,128)(2,1)S(1)}, u32[]{:S(2)}, u32[]{:S(2)}) collective-permute-start(bf16[64,1664]{1,0:T(8,128)(2,1)S(1)} %constant_dynamic-slice_fusion), channel_id=1, source_target_pairs={{0,6},{1,7},{2,0},{3,1},{4,2},{5,3},{6,4},{7,5},{8,14},{9,15},{10,... | collective-permute-start | bytes 638984 | tf_op jit(solution)/shard_map/ppermute | solution.py:44
  165.2 5.6 %text_next.5.refs_0_ = bf16[4,624,768]{2,1,0:T(8,128)(2,1)} custom-call(s32[16]{0:T(128)} %concatenate.18.starts.place, bf16[768,1664]{1,0:T(8,128)(2,1)} %get-tuple-element.139.rows, bf16[2,1,160,1664]{3,2,1,0:T(8,128)(2,1)} %get-tuple-element.155.ours.refs_4_, bf16[2,1,160,1664]{3,2,1,0:T(8,128)(2,1)} %bitcast.71, ...), custom_call_target="tpu_custom_call", output_to_operand_aliasing={{}: (4, {})} | custom-call | flops 1 | bytes 1 | tf_op jit(solution)/shard_map/text_next/pallas_call | solution.py:231
  171.4 1.9 image_rows.1
  173.3 4.3 %collective-permute-done.36 = bf16[64,1664]{1,0:T(8,128)(2,1)S(1)} collective-permute-done((bf16[64,1664]{1,0:T(8,128)(2,1)S(1)}, bf16[64,1664]{1,0:T(8,128)(2,1)S(1)}, u32[]{:S(2)}, u32[]{:S(2)}) %collective-permute-start.36) | collective-permute-done | bytes 213024 | tf_op jit(solution)/shard_map/ppermute | solution.py:44
  178.3 12.5 %late_attention.1 = (bf16[192,832]{1,0:T(8,128)(2,1)}, bf16[192,832]{1,0:T(8,128)(2,1)}) custom-call(s32[16]{0:T(128)} %concatenate.18.starts.place, bf16[64,1664]{1,0:T(8,128)(2,1)} %get-tuple-element.148.image_rows, bf16[64,768]{1,0:T(8,128)(2,1)} %get-tuple-element.101.spread, f32[8,768]{1,0:T(8,128)} %get-tuple-element.102.hits, ...), custom_call_target="tpu_custom_call" | custom-call | flops 1 | bytes 1 | tf_op jit(solution)/shard_map/late_attention/pallas_call | solution.py:231
  190.8 2.9 %collective-permute-done.39 = bf16[3,64,1664]{2,1,0:T(8,128)(2,1)S(1)} collective-permute-done((bf16[3,64,1664]{2,1,0:T(8,128)(2,1)S(1)}, bf16[3,64,1664]{2,1,0:T(8,128)(2,1)S(1)}, u32[]{:S(2)}, u32[]{:S(2)}) %collective-permute-start.39) | collective-permute-done | bytes 639008 | tf_op jit(solution)/shard_map/ppermute | solution.py:439
  194.0 3.0 %collective-permute-done.40.theirs = bf16[2,3,64,1664]{3,2,1,0:T(8,128)(2,1)S(1)} collective-permute-done((bf16[2,3,64,1664]{3,2,1,0:T(8,128)(2,1)S(1)}, bf16[2,3,64,1664]{3,2,1,0:T(8,128)(2,1)S(1)}, u32[]{:S(2)}, u32[]{:S(2)}) %collective-permute-start.40) | collective-permute-done | bytes 1277984 | tf_op jit(solution)/shard_map/ppermute | solution.py:439
  198.0 4.0 %project.2 = bf16[192,1664]{1,0:T(8,128)(2,1)} custom-call(s32[16]{0:T(128)} %concatenate.18.starts.place, bf16[192,832]{1,0:T(8,128)(2,1)} %get-tuple-element.152.rows, bf16[208,1664]{1,0:T(8,128)(2,1)} %own.3, bf16[2,3,64,1664]{3,2,1,0:T(8,128)(2,1)} %copy-done.11, bf16[2,3,64,1664]{3,2,1,0:T(8,128)(2,1)} %copy-done.13), custom_call_target="tpu_custom_call" | custom-call | flops 1 | bytes 1 | tf_op jit(solution)/shard_map/project/pallas_call | solution.py:231
  203.4 4.0 %project.3.kept = bf16[192,1664]{1,0:T(8,128)(2,1)} custom-call(s32[16]{0:T(128)} %concatenate.18.starts.place, bf16[192,832]{1,0:T(8,128)(2,1)} %get-tuple-element.153.rows, bf16[208,1664]{1,0:T(8,128)(2,1)} %own.3, bf16[2,3,64,1664]{3,2,1,0:T(8,128)(2,1)} %copy-done.11, bf16[2,3,64,1664]{3,2,1,0:T(8,128)(2,1)} %copy-done.13), custom_call_target="tpu_custom_call" | custom-call | flops 1 | bytes 1 | tf_op jit(solution)/shard_map/project/pallas_call | solution.py:231
  207.4 11.2 %collective-permute-done.41.got = bf16[192,1664]{1,0:T(8,128)(2,1)S(1)} collective-permute-done((bf16[192,1664]{1,0:T(8,128)(2,1)}, bf16[192,1664]{1,0:T(8,128)(2,1)S(1)}, u32[]{:S(2)}, u32[]{:S(2)}) %collective-permute-start.41) | collective-permute-done | bytes 639008 | tf_op jit(solution)/shard_map/ppermute | solution.py:40
  219.4 2.8 %out_rows.1 = bf16[192,1664]{1,0:T(8,128)(2,1)} custom-call(s32[16]{0:T(128)} %concatenate.18.starts.place, bf16[192,1664]{1,0:T(8,128)(2,1)} %bitcast.77, s32[8,64]{1,0:T(8,128)} %get-tuple-element.104.slots, bf16[64,1664]{1,0:T(8,128)(2,1)} %get-tuple-element.144.merged, bf16[192,1664]{1,0:T(8,128)(2,1)} %project.3.kept, bf16[192,1664]{1,0:T(8,128)(2,1)} %copy-done.17), custom_call_target="tpu_custom_call" | custom-call | flops 1 | bytes 1 | tf_op jit(solution)/shard_map/out_rows/pallas_call | solution.py:231
  (139 shorter events, 41.2 us)
Async XLA Ops:
  0.0 25.7 %collective-permute-start.4 = (bf16[192,1664]{1,0:T(8,128)(2,1)}, bf16[192,1664]{1,0:T(8,128)(2,1)S(1)}, u32[]{:S(2)}, u32[]{:S(2)}) collective-permute-start(bf16[192,1664]{1,0:T(8,128)(2,1)} %bitcast.74), channel_id=1, source_target_pairs={{0,1},{1,0},{2,3},{3,2},{4,5},{5,4},{6,7},{7,6},{8,9},{9,8},{10,11... | collective-permute-start | bytes 1916936 | tf_op jit(solution)/shard_map/ppermute | solution.py:40
  2.9 19.2 %collective-permute-start.3 = (bf16[64,1664]{1,0:T(8,128)(2,1)}, bf16[64,1664]{1,0:T(8,128)(2,1)S(1)}, u32[]{:S(2)}, u32[]{:S(2)}) collective-permute-start(bf16[64,1664]{1,0:T(8,128)(2,1)} %bitcast.61), channel_id=1, source_target_pairs={{0,1},{1,0},{2,3},{3,2},{4,5},{5,4},{6,7},{7,6},{8,9},{9,8},{10,11... | collective-permute-start | bytes 638984 | tf_op jit(solution)/shard_map/ppermute | solution.py:40
  3.0 19.1 %collective-permute-start.2 = (bf16[64,1664]{1,0:T(8,128)(2,1)}, bf16[64,1664]{1,0:T(8,128)(2,1)S(1)}, u32[]{:S(2)}, u32[]{:S(2)}) collective-permute-start(bf16[64,1664]{1,0:T(8,128)(2,1)} %bitcast.62), channel_id=1, source_target_pairs={{0,2},{1,3},{2,4},{3,5},{4,6},{5,7},{6,0},{7,1},{8,10},{9,11},{10,... | collective-permute-start | bytes 638984 | tf_op jit(solution)/shard_map/ppermute | solution.py:44
  5.1 17.0 %collective-permute-start.1 = (bf16[64,1664]{1,0:T(8,128)(2,1)}, bf16[64,1664]{1,0:T(8,128)(2,1)S(1)}, u32[]{:S(2)}, u32[]{:S(2)}) collective-permute-start(bf16[64,1664]{1,0:T(8,128)(2,1)} %bitcast.63), channel_id=1, source_target_pairs={{0,6},{1,7},{2,0},{3,1},{4,2},{5,3},{6,4},{7,5},{8,14},{9,15},{10,... | collective-permute-start | bytes 638984 | tf_op jit(solution)/shard_map/ppermute | solution.py:44
  7.1 18.6 %collective-permute-start = (bf16[64,1664]{1,0:T(8,128)(2,1)}, bf16[64,1664]{1,0:T(8,128)(2,1)S(1)}, u32[]{:S(2)}, u32[]{:S(2)}) collective-permute-start(bf16[64,1664]{1,0:T(8,128)(2,1)} %bitcast.64), channel_id=1, source_target_pairs={{0,4},{1,5},{2,6},{3,7},{4,0},{5,1},{6,2},{7,3},{8,12},{9,13},{10,... | collective-permute-start | bytes 638984 | tf_op jit(solution)/shard_map/ppermute | solution.py:44
  8.1 22.3 %copy-start.5 = (bf16[1,64,1664]{2,1,0:T(8,128)(2,1)S(1)}, bf16[1,64,1664]{2,1,0:T(8,128)(2,1)}, u32[]{:S(2)}) copy-start(bf16[1,64,1664]{2,1,0:T(8,128)(2,1)} %param.13) | copy-start | bytes 638980
  8.1 22.3 %copy-start.8 = (f32[1664]{0:T(1024)S(1)}, f32[1664]{0:T(1024)}, u32[]{:S(2)}) copy-start(f32[1664]{0:T(1024)} %gain.8) | copy-start | bytes 19972
  25.7 17.0 %collective-permute-start.7 = (bf16[192,1664]{1,0:T(8,128)(2,1)}, bf16[192,1664]{1,0:T(8,128)(2,1)S(1)}, u32[]{:S(2)}, u32[]{:S(2)}) collective-permute-start(bf16[192,1664]{1,0:T(8,128)(2,1)} %bitcast.75), channel_id=1, source_target_pairs={{0,2},{1,3},{2,4},{3,5},{4,6},{5,7},{8,10},{9,11},{10,12},{11,13},... | collective-permute-start | bytes 1916936 | tf_op jit(solution)/shard_map/ppermute | solution.py:550
  28.2 10.6 %collective-permute-start.5 = (bf16[64,1664]{1,0:T(8,128)(2,1)S(1)}, bf16[64,1664]{1,0:T(8,128)(2,1)S(1)}, u32[]{:S(2)}, u32[]{:S(2)}) collective-permute-start(bf16[64,1664]{1,0:T(8,128)(2,1)S(1)} %collective-permute-done.2.mine), channel_id=1, source_target_pairs={{0,1},{1,0},{2,3},{3,2},{4,5},{5,4},{6,7},{7,6},{8,9},{9,8},{10,11... | collective-permute-start | bytes 638984 | tf_op jit(solution)/shard_map/ppermute | solution.py:40
  29.8 12.9 %collective-permute-start.6 = (bf16[64,1664]{1,0:T(8,128)(2,1)S(1)}, bf16[64,1664]{1,0:T(8,128)(2,1)S(1)}, u32[]{:S(2)}, u32[]{:S(2)}) collective-permute-start(bf16[64,1664]{1,0:T(8,128)(2,1)S(1)} %collective-permute-done.1.mine), channel_id=1, source_target_pairs={{0,1},{1,0},{2,3},{3,2},{4,5},{5,4},{6,7},{7,6},{8,9},{9,8},{10,11... | collective-permute-start | bytes 638984 | tf_op jit(solution)/shard_map/ppermute | solution.py:40
  42.7 33.3 %copy-start.19 = (bf16[192,1664]{1,0:T(8,128)(2,1)}, bf16[192,1664]{1,0:T(8,128)(2,1)S(1)}, u32[]{:S(2)}) copy-start(bf16[192,1664]{1,0:T(8,128)(2,1)S(1)} %collective-permute-done.7.refs_0_) | copy-start | bytes 1916932
  42.7 16.3 %collective-permute-start.9 = (bf16[80,1664]{1,0:T(8,128)(2,1)S(1)}, bf16[80,1664]{1,0:T(8,128)(2,1)S(1)}, u32[]{:S(2)}, u32[]{:S(2)}) collective-permute-start(bf16[80,1664]{1,0:T(8,128)(2,1)S(1)} %get-tuple-element.96), channel_id=1, source_target_pairs={{0,4},{1,5},{2,6},{3,7},{4,0},{5,1},{6,2},{7,3},{8,12},{9,13},{10,... | collective-permute-start | bytes 798728 | tf_op jit(solution)/shard_map/ppermute | solution.py:44
  45.5 8.1 %collective-permute-start.8 = (bf16[64,1664]{1,0:T(8,128)(2,1)S(1)}, bf16[64,1664]{1,0:T(8,128)(2,1)S(1)}, u32[]{:S(2)}, u32[]{:S(2)}) collective-permute-start(bf16[64,1664]{1,0:T(8,128)(2,1)S(1)} %collective-permute-done.mine), channel_id=1, source_target_pairs={{0,1},{1,0},{2,3},{3,2},{4,5},{5,4},{6,7},{7,6},{8,9},{9,8},{10,11... | collective-permute-start | bytes 638984 | tf_op jit(solution)/shard_map/ppermute | solution.py:40
  47.0 12.0 %collective-permute-start.10 = (bf16[64,1664]{1,0:T(8,128)(2,1)S(1)}, bf16[64,1664]{1,0:T(8,128)(2,1)S(1)}, u32[]{:S(2)}, u32[]{:S(2)}) collective-permute-start(bf16[64,1664]{1,0:T(8,128)(2,1)S(1)} %get-tuple-element.86), channel_id=1, source_target_pairs={{0,1},{1,0},{2,3},{3,2},{4,5},{5,4},{6,7},{7,6},{8,9},{9,8},{10,11... | collective-permute-start | bytes 638984 | tf_op jit(solution)/shard_map/ppermute | solution.py:40
  51.3 10.0 %collective-permute-start.11 = (bf16[64,1664]{1,0:T(8,128)(2,1)S(1)}, bf16[64,1664]{1,0:T(8,128)(2,1)S(1)}, u32[]{:S(2)}, u32[]{:S(2)}) collective-permute-start(bf16[64,1664]{1,0:T(8,128)(2,1)S(1)} %get-tuple-element.91), channel_id=1, source_target_pairs={{0,1},{1,0},{2,3},{3,2},{4,5},{5,4},{6,7},{7,6},{8,9},{9,8},{10,11... | collective-permute-start | bytes 638984 | tf_op jit(solution)/shard_map/ppermute | solution.py:40
  57.4 15.2 %copy-start.10 = (s32[4]{0:T(128)S(1)}, s32[4]{0:T(128)}, u32[]{:S(2)}) copy-start(s32[4]{0:T(128)} %constant.84) | copy-start | bytes 52
  57.4 6.2 %collective-permute-start.12 = (bf16[64,1664]{1,0:T(8,128)(2,1)S(1)}, bf16[64,1664]{1,0:T(8,128)(2,1)S(1)}, u32[]{:S(2)}, u32[]{:S(2)}) collective-permute-start(bf16[64,1664]{1,0:T(8,128)(2,1)S(1)} %get-tuple-element.95), channel_id=1, source_target_pairs={{0,1},{1,0},{2,3},{3,2},{4,5},{5,4},{6,7},{7,6},{8,9},{9,8},{10,11... | collective-permute-start | bytes 638984 | tf_op jit(solution)/shard_map/ppermute | solution.py:40
  64.3 27.0 %collective-permute-start.17 = (bf16[80,1664]{1,0:T(8,128)(2,1)S(1)}, bf16[80,1664]{1,0:T(8,128)(2,1)S(1)}, u32[]{:S(2)}, u32[]{:S(2)}) collective-permute-start(bf16[80,1664]{1,0:T(8,128)(2,1)S(1)} %get-tuple-element.105), channel_id=1, source_target_pairs={{0,4},{1,5},{2,6},{3,7},{4,0},{5,1},{6,2},{7,3},{8,12},{9,13},{10,... | collective-permute-start | bytes 798728 | tf_op jit(solution)/shard_map/ppermute | solution.py:44
  66.4 9.5 %collective-permute-start.13 = (bf16[64,1664]{1,0:T(8,128)(2,1)S(1)}, bf16[64,1664]{1,0:T(8,128)(2,1)S(1)}, u32[]{:S(2)}, u32[]{:S(2)}) collective-permute-start(bf16[64,1664]{1,0:T(8,128)(2,1)S(1)} %get-tuple-element.82), channel_id=1, source_target_pairs={{0,1},{1,0},{2,3},{3,2},{4,5},{5,4},{6,7},{7,6},{8,9},{9,8},{10,11... | collective-permute-start | bytes 638984 | tf_op jit(solution)/shard_map/ppermute | solution.py:40
  67.9 23.4 %collective-permute-start.15 = (bf16[64,1664]{1,0:T(8,128)(2,1)}, bf16[64,1664]{1,0:T(8,128)(2,1)S(1)}, u32[]{:S(2)}, u32[]{:S(2)}) collective-permute-start(bf16[64,1664]{1,0:T(8,128)(2,1)} %add_convert_fusion), channel_id=1, source_target_pairs={{0,4},{1,5},{2,6},{3,7},{4,0},{5,1},{6,2},{7,3},{8,12},{9,13},{10,... | collective-permute-start | bytes 638984 | tf_op jit(solution)/shard_map/ppermute | solution.py:44
  68.7 22.6 %collective-permute-start.16 = (bf16[64,1664]{1,0:T(8,128)(2,1)S(1)}, bf16[64,1664]{1,0:T(8,128)(2,1)S(1)}, u32[]{:S(2)}, u32[]{:S(2)}) collective-permute-start(bf16[64,1664]{1,0:T(8,128)(2,1)S(1)} %add_convert_fusion.1), channel_id=1, source_target_pairs={{0,2},{1,3},{2,4},{3,5},{4,6},{5,7},{6,0},{7,1},{8,10},{9,11},{10,... | collective-permute-start | bytes 638984 | tf_op jit(solution)/shard_map/ppermute | solution.py:44
  69.3 22.1 %collective-permute-start.14 = (bf16[64,1664]{1,0:T(8,128)(2,1)S(1)}, bf16[64,1664]{1,0:T(8,128)(2,1)S(1)}, u32[]{:S(2)}, u32[]{:S(2)}) collective-permute-start(bf16[64,1664]{1,0:T(8,128)(2,1)S(1)} %add_convert_fusion.2), channel_id=1, source_target_pairs={{0,6},{1,7},{2,0},{3,1},{4,2},{5,3},{6,4},{7,5},{8,14},{9,15},{10,... | collective-permute-start | bytes 638984 | tf_op jit(solution)/shard_map/ppermute | solution.py:44
  76.0 15.4 %copy-start.23 = (bf16[64,1664]{1,0:T(8,128)(2,1)}, bf16[64,1664]{1,0:T(8,128)(2,1)S(1)}, u32[]{:S(2)}) copy-start(bf16[64,1664]{1,0:T(8,128)(2,1)S(1)} %collective-permute-done.13.refs_0_) | copy-start | bytes 638980
  76.0 26.4 %collective-permute-start.18 = (bf16[192,1664]{1,0:T(8,128)(2,1)S(1)}, bf16[192,1664]{1,0:T(8,128)(2,1)S(1)}, u32[]{:S(2)}, u32[]{:S(2)}) collective-permute-start(bf16[192,1664]{1,0:T(8,128)(2,1)S(1)} %collective-permute-done.7.refs_0_), channel_id=1, source_target_pairs={{0,1},{1,0},{2,3},{3,2},{4,5},{5,4},{6,7},{7,6},{8,9},{9,8},{10,11... | collective-permute-start | bytes 1916936 | tf_op jit(solution)/shard_map/ppermute | solution.py:40
  94.9 15.3 %collective-permute-start.20 = (bf16[160,1664]{1,0:T(8,128)(2,1)S(1)}, bf16[160,1664]{1,0:T(8,128)(2,1)S(1)}, u32[]{:S(2)}, u32[]{:S(2)}) collective-permute-start(bf16[160,1664]{1,0:T(8,128)(2,1)S(1)} %dynamic-slice_bitcast_fusion), channel_id=1, source_target_pairs={{0,2},{1,3},{2,4},{3,5},{4,6},{5,7},{6,0},{7,1},{8,10},{9,11},{10,... | collective-permute-start | bytes 1597448 | tf_op jit(solution)/shard_map/ppermute | solution.py:44
  99.2 13.3 %collective-permute-start.21 = (bf16[160,1664]{1,0:T(8,128)(2,1)S(1)}, bf16[160,1664]{1,0:T(8,128)(2,1)S(1)}, u32[]{:S(2)}, u32[]{:S(2)}) collective-permute-start(bf16[160,1664]{1,0:T(8,128)(2,1)S(1)} %constant_dynamic-update-slice_fusion), channel_id=1, source_target_pairs={{0,16},{8,24},{16,0},{24,8},{1,17},{9,25},{17,1},{25,9},{2,18},{10... | collective-permute-start | bytes 1597448 | tf_op jit(solution)/shard_map/ppermute | solution.py:439
  100.8 8.1 %collective-permute-start.19 = (bf16[4,16,832]{2,1,0:T(8,128)(2,1)S(1)}, bf16[4,16,832]{2,1,0:T(8,128)(2,1)S(1)}, u32[]{:S(2)}, u32[]{:S(2)}) collective-permute-start(bf16[4,16,832]{2,1,0:T(8,128)(2,1)S(1)} %copy-done.30), channel_id=1, source_target_pairs={{0,1},{1,0},{2,3},{3,2},{4,5},{5,4},{6,7},{7,6},{8,9},{9,8},{10,11... | collective-permute-start | bytes 319496 | tf_op jit(solution)/shard_map/ppermute | solution.py:40
  112.6 10.1 %copy-start.12 = (bf16[2,1,160,1664]{3,2,1,0:T(8,128)(2,1)}, bf16[2,1,160,1664]{3,2,1,0:T(8,128)(2,1)S(1)}, u32[]{:S(2)}) copy-start(bf16[2,1,160,1664]{3,2,1,0:T(8,128)(2,1)S(1)} %maximum_bitcast_fusion.ours.refs_6_) | copy-start | bytes 3194884
  112.6 16.6 %collective-permute-start.25 = (bf16[2,1,160,1664]{3,2,1,0:T(8,128)(2,1)S(1)}, bf16[2,1,160,1664]{3,2,1,0:T(8,128)(2,1)S(1)}, u32[]{:S(2)}, u32[]{:S(2)}) collective-permute-start(bf16[2,1,160,1664]{3,2,1,0:T(8,128)(2,1)S(1)} %maximum_bitcast_fusion.ours.refs_6_), channel_id=1, source_target_pairs={{0,8},{8,0},{16,24},{24,16},{1,9},{9,1},{17,25},{25,17},{2,10},{10... | collective-permute-start | bytes 3194888 | tf_op jit(solution)/shard_map/ppermute | solution.py:439
  112.8 6.3 %collective-permute-start.22 = (bf16[32,832]{1,0:T(8,128)(2,1)S(1)}, bf16[32,832]{1,0:T(8,128)(2,1)S(1)}, u32[]{:S(2)}, u32[]{:S(2)}) collective-permute-start(bf16[32,832]{1,0:T(8,128)(2,1)S(1)} %pad_maximum_fusion.5), channel_id=1, source_target_pairs={{0,2},{1,3},{2,4},{3,5},{4,6},{5,7},{6,0},{7,1},{8,10},{9,11},{10,... | collective-permute-start | bytes 159752 | tf_op jit(solution)/shard_map/ppermute | solution.py:44
  115.3 6.1 %collective-permute-start.23 = (bf16[32,832]{1,0:T(8,128)(2,1)S(1)}, bf16[32,832]{1,0:T(8,128)(2,1)S(1)}, u32[]{:S(2)}, u32[]{:S(2)}) collective-permute-start(bf16[32,832]{1,0:T(8,128)(2,1)S(1)} %pad_maximum_fusion.6), channel_id=1, source_target_pairs={{0,4},{1,5},{2,6},{3,7},{4,0},{5,1},{6,2},{7,3},{8,12},{9,13},{10,... | collective-permute-start | bytes 159752 | tf_op jit(solution)/shard_map/ppermute | solution.py:44
  115.4 6.1 %collective-permute-start.24 = (bf16[32,832]{1,0:T(8,128)(2,1)S(1)}, bf16[32,832]{1,0:T(8,128)(2,1)S(1)}, u32[]{:S(2)}, u32[]{:S(2)}) collective-permute-start(bf16[32,832]{1,0:T(8,128)(2,1)S(1)} %pad_maximum_fusion.7), channel_id=1, source_target_pairs={{0,6},{1,7},{2,0},{3,1},{4,2},{5,3},{6,4},{7,5},{8,14},{9,15},{10,... | collective-permute-start | bytes 159752 | tf_op jit(solution)/shard_map/ppermute | solution.py:44
  123.6 14.0 %collective-permute-start.27 = (bf16[160,1664]{1,0:T(8,128)(2,1)S(1)}, bf16[160,1664]{1,0:T(8,128)(2,1)S(1)}, u32[]{:S(2)}, u32[]{:S(2)}) collective-permute-start(bf16[160,1664]{1,0:T(8,128)(2,1)S(1)} %dynamic-slice_bitcast_fusion), channel_id=1, source_target_pairs={{0,6},{1,7},{2,0},{3,1},{4,2},{5,3},{6,4},{7,5},{8,14},{9,15},{10,... | collective-permute-start | bytes 1597448 | tf_op jit(solution)/shard_map/ppermute | solution.py:44
  126.3 12.7 %collective-permute-start.28 = (bf16[160,1664]{1,0:T(8,128)(2,1)S(1)}, bf16[160,1664]{1,0:T(8,128)(2,1)S(1)}, u32[]{:S(2)}, u32[]{:S(2)}) collective-permute-start(bf16[160,1664]{1,0:T(8,128)(2,1)S(1)} %collective-permute-done.20), channel_id=1, source_target_pairs={{0,16},{8,24},{16,0},{24,8},{1,17},{9,25},{17,1},{25,9},{2,18},{10... | collective-permute-start | bytes 1597448 | tf_op jit(solution)/shard_map/ppermute | solution.py:439
  127.8 8.1 %collective-permute-start.26 = (bf16[128,832]{1,0:T(8,128)(2,1)S(1)}, bf16[128,832]{1,0:T(8,128)(2,1)S(1)}, u32[]{:S(2)}, u32[]{:S(2)}) collective-permute-start(bf16[128,832]{1,0:T(8,128)(2,1)S(1)} %get-tuple-element.125), channel_id=1, source_target_pairs={{0,1},{1,0},{2,3},{3,2},{4,5},{5,4},{6,7},{7,6},{8,9},{9,8},{10,11... | collective-permute-start | bytes 638984 | tf_op jit(solution)/shard_map/ppermute | solution.py:40
  140.2 7.9 %collective-permute-start.29 = (bf16[2,1,160,1664]{3,2,0,1:T(8,128)(2,1)S(1)}, bf16[2,1,160,1664]{3,2,0,1:T(8,128)(2,1)S(1)}, u32[]{:S(2)}, u32[]{:S(2)}) collective-permute-start(bf16[2,1,160,1664]{3,2,0,1:T(8,128)(2,1)S(1)} %get-tuple-element.158), channel_id=1, source_target_pairs={{0,8},{8,0},{16,24},{24,16},{1,9},{9,1},{17,25},{25,17},{2,10},{10... | collective-permute-start | bytes 3194888 | tf_op jit(solution)/shard_map/ppermute | solution.py:439
  140.2 15.9 %collective-permute-start.33 = (bf16[160,1664]{1,0:T(8,128)(2,1)S(1)}, bf16[160,1664]{1,0:T(8,128)(2,1)S(1)}, u32[]{:S(2)}, u32[]{:S(2)}) collective-permute-start(bf16[160,1664]{1,0:T(8,128)(2,1)S(1)} %collective-permute-done.27), channel_id=1, source_target_pairs={{0,16},{8,24},{16,0},{24,8},{1,17},{9,25},{17,1},{25,9},{2,18},{10... | collective-permute-start | bytes 1597448 | tf_op jit(solution)/shard_map/ppermute | solution.py:439
  143.7 11.0 %collective-permute-start.30 = (bf16[64,832]{1,0:T(8,128)(2,1)}, bf16[64,832]{1,0:T(8,128)(2,1)S(1)}, u32[]{:S(2)}, u32[]{:S(2)}) collective-permute-start(bf16[64,832]{1,0:T(8,128)(2,1)} %get-tuple-element.132), channel_id=1, source_target_pairs={{0,2},{1,3},{2,4},{3,5},{4,6},{5,7},{6,0},{7,1},{8,10},{9,11},{10,... | collective-permute-start | bytes 319496 | tf_op jit(solution)/shard_map/ppermute | solution.py:44
  144.0 12.0 %collective-permute-start.31 = (bf16[64,832]{1,0:T(8,128)(2,1)}, bf16[64,832]{1,0:T(8,128)(2,1)S(1)}, u32[]{:S(2)}, u32[]{:S(2)}) collective-permute-start(bf16[64,832]{1,0:T(8,128)(2,1)} %get-tuple-element.133), channel_id=1, source_target_pairs={{0,4},{1,5},{2,6},{3,7},{4,0},{5,1},{6,2},{7,3},{8,12},{9,13},{10,... | collective-permute-start | bytes 319496 | tf_op jit(solution)/shard_map/ppermute | solution.py:44
  146.3 9.7 %collective-permute-start.32 = (bf16[64,832]{1,0:T(8,128)(2,1)}, bf16[64,832]{1,0:T(8,128)(2,1)S(1)}, u32[]{:S(2)}, u32[]{:S(2)}) collective-permute-start(bf16[64,832]{1,0:T(8,128)(2,1)} %get-tuple-element.134), channel_id=1, source_target_pairs={{0,6},{1,7},{2,0},{3,1},{4,2},{5,3},{6,4},{7,5},{8,14},{9,15},{10,... | collective-permute-start | bytes 319496 | tf_op jit(solution)/shard_map/ppermute | solution.py:44
  157.2 7.0 %collective-permute-start.34 = (bf16[2,1,160,1664]{3,2,0,1:T(8,128)(2,1)S(1)}, bf16[2,1,160,1664]{3,2,0,1:T(8,128)(2,1)S(1)}, u32[]{:S(2)}, u32[]{:S(2)}) collective-permute-start(bf16[2,1,160,1664]{3,2,0,1:T(8,128)(2,1)S(1)} %get-tuple-element.156), channel_id=1, source_target_pairs={{0,8},{8,0},{16,24},{24,16},{1,9},{9,1},{17,25},{25,17},{2,10},{10... | collective-permute-start | bytes 3194888 | tf_op jit(solution)/shard_map/ppermute | solution.py:439
  158.2 15.1 %collective-permute-start.38 = (bf16[64,1664]{1,0:T(8,128)(2,1)S(1)}, bf16[64,1664]{1,0:T(8,128)(2,1)S(1)}, u32[]{:S(2)}, u32[]{:S(2)}) collective-permute-start(bf16[64,1664]{1,0:T(8,128)(2,1)S(1)} %constant_dynamic-slice_fusion), channel_id=1, source_target_pairs={{0,4},{1,5},{2,6},{3,7},{4,0},{5,1},{6,2},{7,3},{8,12},{9,13},{10,... | collective-permute-start | bytes 638984 | tf_op jit(solution)/shard_map/ppermute | solution.py:44
  159.5 13.9 %collective-permute-start.37 = (bf16[64,1664]{1,0:T(8,128)(2,1)S(1)}, bf16[64,1664]{1,0:T(8,128)(2,1)S(1)}, u32[]{:S(2)}, u32[]{:S(2)}) collective-permute-start(bf16[64,1664]{1,0:T(8,128)(2,1)S(1)} %constant_dynamic-slice_fusion), channel_id=1, source_target_pairs={{0,6},{1,7},{2,0},{3,1},{4,2},{5,3},{6,4},{7,5},{8,14},{9,15},{10,... | collective-permute-start | bytes 638984 | tf_op jit(solution)/shard_map/ppermute | solution.py:44
  162.7 14.9 %collective-permute-start.36 = (bf16[64,1664]{1,0:T(8,128)(2,1)S(1)}, bf16[64,1664]{1,0:T(8,128)(2,1)S(1)}, u32[]{:S(2)}, u32[]{:S(2)}) collective-permute-start(bf16[64,1664]{1,0:T(8,128)(2,1)S(1)} %constant_dynamic-slice_fusion), channel_id=1, source_target_pairs={{0,2},{1,3},{2,4},{3,5},{4,6},{5,7},{6,0},{7,1},{8,10},{9,11},{10,... | collective-permute-start | bytes 638984 | tf_op jit(solution)/shard_map/ppermute | solution.py:44
  162.7 8.0 %collective-permute-start.35 = (bf16[64,832]{1,0:T(8,128)(2,1)S(1)}, bf16[64,832]{1,0:T(8,128)(2,1)S(1)}, u32[]{:S(2)}, u32[]{:S(2)}) collective-permute-start(bf16[64,832]{1,0:T(8,128)(2,1)S(1)} %add_convert_fusion.3.ours), channel_id=1, source_target_pairs={{0,1},{1,0},{2,3},{3,2},{4,5},{5,4},{6,7},{7,6},{8,9},{9,8},{10,11... | collective-permute-start | bytes 319496 | tf_op jit(solution)/shard_map/ppermute | solution.py:40
  177.7 16.0 %collective-permute-start.39 = (bf16[3,64,1664]{2,1,0:T(8,128)(2,1)S(1)}, bf16[3,64,1664]{2,1,0:T(8,128)(2,1)S(1)}, u32[]{:S(2)}, u32[]{:S(2)}) collective-permute-start(bf16[3,64,1664]{2,1,0:T(8,128)(2,1)S(1)} %pad_maximum_fusion.3), channel_id=1, source_target_pairs={{0,16},{8,24},{16,0},{24,8},{1,17},{9,25},{17,1},{25,9},{2,18},{10... | collective-permute-start | bytes 1916936 | tf_op jit(solution)/shard_map/ppermute | solution.py:439
  193.9 3.1 %collective-permute-start.40 = (bf16[2,3,64,1664]{3,2,1,0:T(8,128)(2,1)S(1)}, bf16[2,3,64,1664]{3,2,1,0:T(8,128)(2,1)S(1)}, u32[]{:S(2)}, u32[]{:S(2)}) collective-permute-start(bf16[2,3,64,1664]{3,2,1,0:T(8,128)(2,1)S(1)} %pad_maximum_fusion.ours), channel_id=1, source_target_pairs={{0,8},{8,0},{16,24},{24,16},{1,9},{9,1},{17,25},{25,17},{2,10},{10... | collective-permute-start | bytes 3833864 | tf_op jit(solution)/shard_map/ppermute | solution.py:439
  201.9 16.6 %collective-permute-start.41 = (bf16[192,1664]{1,0:T(8,128)(2,1)}, bf16[192,1664]{1,0:T(8,128)(2,1)S(1)}, u32[]{:S(2)}, u32[]{:S(2)}) collective-permute-start(bf16[192,1664]{1,0:T(8,128)(2,1)} %project.2), channel_id=1, source_target_pairs={{0,1},{1,0},{2,3},{3,2},{4,5},{5,4},{6,7},{7,6},{8,9},{9,8},{10,11... | collective-permute-start | bytes 1916936 | tf_op jit(solution)/shard_map/ppermute | solution.py:40
  (25 other events, 80.0 us)

commit v5 on v4

--- a/solution.py
+++ b/solution.py
@@ -213,15 +213,14 @@
     out[...] = total.astype(jnp.bfloat16)
 
 
-def out_kernel(starts, text, slots, merged, kept, got, out):
+def out_kernel(starts, text, slots, merged, kept, out):
     count = text.shape[0]
     position = starts[10] + lax.broadcasted_iota(jnp.int32, (count, merged.shape[0]), 0)
     match = jnp.where(slots[0:1, :] == position, 1.0, 0.0)
     placed = jnp.dot(match.astype(jnp.bfloat16), merged[...], preferred_element_type=jnp.float32)
     hit = jnp.max(match, axis=1, keepdims=True) > 0.5
     embedded = jnp.where(hit, placed, text[...].astype(jnp.float32))
-    total = kept[...].astype(jnp.float32) + got[...].astype(jnp.float32)
-    out[...] = (embedded + total).astype(jnp.bfloat16)
+    out[...] = embedded + kept[...].astype(jnp.float32)
 
 
 SMEM = pl.BlockSpec(memory_space=pltpu.SMEM)
@@ -518,6 +517,7 @@
     swapping = swap_pair(patch_rows, tp_size)
     moving = {k: turned(patch_rows, tp_size, k) for k in rounds + [middle]}
     text_other = swap_pair(text_rows, tp_size)
+    qkv_quarter, out_quarter = queue.passed((own_quarter(qkv_own), own_quarter(out_own)))
     other[0] = queue.wait(swapping)
     mine, swapping = {}, {}
     for k in rounds + [middle]:
@@ -525,7 +525,6 @@
     text_other = queue.wait(text_other)
     for k in rounds + [middle]:
         swapping[k] = swap_pair(queue.held(mine[k]), tp_size)
-    qkv_quarter, out_quarter = own_quarter(qkv_own), own_quarter(out_own)
     qkv_moving, qkv_ours, qkv_theirs = {}, {}, {}
     place_of = {0: 0, middle: lines - 1, **{k: i + 1 for i, k in enumerate(rounds)}}
 
@@ -621,14 +620,14 @@
         move_weights(k)
     text_parts = run_text(text_parts, middle)
     got = queue.wait(got)
-    for k in rounds[1:]:
-        cross_weights(k)
-    share_weights(rounds[0])
     share = queue.passed(kernel_call(
         functools.partial(split_kernel, needed), "image_shares", [((count, half), bf16)] * lines,
         starts, queue.held(kept), got,
     ))
     moving = [turned(share[k], tp_size, k) for k in range(1, lines)]
+    for k in rounds[1:]:
+        cross_weights(k)
+    share_weights(rounds[0])
     text_parts = run_text(text_parts, rounds[0])
     total = queue.held(share[0]).astype(jnp.float32)
     for block in queue.wait(moving):
@@ -664,10 +663,11 @@
     (given,) = queue.passed(project(starts, queue.held(given), out_own, out_ours, queue.wait(out_theirs)))
     got = swap_pair(given, tp_size)
     (kept,) = queue.passed(project(starts, queue.held(kept), out_own, out_ours, out_theirs))
-    (decoded,) = kernel_call(
-        out_kernel, "out_rows", [((seq_here, width), bf16)],
-        starts, queue.held(text_rows), slots_here, merged, kept, queue.wait(got),
-    )
+    (own_rows,) = queue.passed(kernel_call(
+        out_kernel, "out_rows", [((seq_here, width), jnp.float32)],
+        starts, queue.held(text_rows), slots_here, merged, kept,
+    ))
+    decoded = (queue.held(own_rows) + queue.wait(got).astype(jnp.float32)).astype(bf16)
     return decoded[None]
 
 

time: 223 us -> 220 us (0.987)
  waiting for transfers between devices: 70.3 us -> 62.4 us
  other arithmetic: 3.62 us -> 5.87 us
    ppermute x14, waiting for transfers between devices: 30.4 us -> 25.1 us  [swap_pair(): return lax.ppermute(values, 'tp', pair_steps(tp_size))]
    broadcast_in_dim x0 -> x1, other arithmetic: none -> 2.27 us  [shards(): return decoded[None]]
    unnamed x63 -> x67, local copies, waits for them, and re-layouts: 12.7 us -> 12.5 us
  transfers between devices with their start and end apart: 42 -> 42, of which waited for: 17 -> 17; matrix products, arithmetic and copies ran while one was open for 2% -> 3% of each run, Pallas kernels for 29% -> 31%
where the time goes in v5:
time: 220 us; the launch traced here: 218 us
  Pallas kernels  70.7 us (32%)
  waiting for transfers between devices  62.4 us (28%)
  starting transfers between devices  60.3 us (27%)
  local copies, waits for them, and re-layouts  18.4 us (8%)
  other arithmetic  5.87 us (3%)
    pallas_call x11, Pallas kernels, kernel_call(): pl.pallas_call(body, grid=grid, in_specs=[SMEM] + [specs.get(place, whole...  51.6 us
    ppermute x19, starting transfers between devices, turned(): return lax.ppermute(values, 'tp', turn_steps(tp_size, turn))  34.9 us
    ppermute x19, waiting for transfers between devices, turned(): return lax.ppermute(values, 'tp', turn_steps(tp_size, turn))  28.3 us
    ppermute x14, waiting for transfers between devices, swap_pair(): return lax.ppermute(values, 'tp', pair_steps(tp_size))  25.1 us
    ppermute x14, starting transfers between devices, swap_pair(): return lax.ppermute(values, 'tp', pair_steps(tp_size))  18.2 us
    pallas_call x4, Pallas kernels, mlp(): pl.pallas_call(mlp_kernel, grid=(units // step,), in_specs=[whole_block((...  15.1 us
    unnamed x67, local copies, waits for them, and re-layouts  12.5 us
    ppermute x8, waiting for transfers between devices, other_copy(): lax.ppermute(values, 'req', [(i, i ^ flip) for i in range(lax.axis_size('...  9 us
  transfers between devices with their start and end apart: 42, of which 17 were waited for; matrix products, arithmetic and copies ran while one was open for 3% of the time, Pallas kernels for 31%

profile of v5, /device:TPU:0, one launch (start us, length us, event | category | flops | bytes accessed | tf_op | source)
XLA Modules:
  0.0 218.1 jit_solution(13982708404060935094)
XLA Ops:
  0.0 2.9 %collective-permute-start.4 = (bf16[192,1664]{1,0:T(8,128)(2,1)}, bf16[192,1664]{1,0:T(8,128)(2,1)S(1)}, u32[]{:S(2)}, u32[]{:S(2)}) collective-permute-start(bf16[192,1664]{1,0:T(8,128)(2,1)} %bitcast.75), channel_id=1, source_target_pairs={{0,1},{1,0},{2,3},{3,2},{4,5},{5,4},{6,7},{7,6},{8,9},{9,8},{10,11... | collective-permute-start | bytes 1916936 | tf_op jit(solution)/shard_map/ppermute | solution.py:40
  3.0 2.0 collective-permute-start.2
  5.1 2.0 collective-permute-start.1
  9.3 1.7 constant_dynamic-slice_fusion
  11.0 11.1 %collective-permute-done.3.other = bf16[64,1664]{1,0:T(8,128)(2,1)S(1)} collective-permute-done((bf16[64,1664]{1,0:T(8,128)(2,1)}, bf16[64,1664]{1,0:T(8,128)(2,1)S(1)}, u32[]{:S(2)}, u32[]{:S(2)}) %collective-permute-start.3) | collective-permute-done | bytes 213024 | tf_op jit(solution)/shard_map/ppermute | solution.py:40
  22.2 3.5 %collective-permute-done.mine = bf16[64,1664]{1,0:T(8,128)(2,1)S(1)} collective-permute-done((bf16[64,1664]{1,0:T(8,128)(2,1)}, bf16[64,1664]{1,0:T(8,128)(2,1)S(1)}, u32[]{:S(2)}, u32[]{:S(2)}) %collective-permute-start) | collective-permute-done | bytes 213024 | tf_op jit(solution)/shard_map/ppermute | solution.py:44
  27.1 1.6 collective-permute-start.5
  29.9 2.0 copy-done
  31.9 2.0 copy-done.2
  33.8 3.8 %mlp_rows.4 = (bf16[64,1664]{1,0:T(8,128)(2,1)S(1)}, bf16[64,1664]{1,0:T(8,128)(2,1)S(1)}) custom-call(bf16[64,1664]{1,0:T(8,128)(2,1)S(1)} %bitcast.67, bf16[64,1664]{1,0:T(8,128)(2,1)S(1)} %collective-permute-done.3.other, f32[1664]{0:T(1024)S(1)} %copy-done.8, bf16[1664,1024]{1,0:T(8,128)(2,1)S(1)} %copy-done, bf16[1024,1664]{1,0:T(8,128)(2,1)S(1)} %copy-done.2), custom_call_target="tpu_custom_call" | custom-call | flops 1 | bytes 1 | tf_op jit(solution)/shard_map/mlp_rows/pallas_call | solution.py:294
  38.3 3.8 %mlp_rows.5 = (bf16[64,1664]{1,0:T(8,128)(2,1)S(1)}, bf16[64,1664]{1,0:T(8,128)(2,1)S(1)}) custom-call(bf16[64,1664]{1,0:T(8,128)(2,1)S(1)} %collective-permute-done.2.mine, bf16[64,1664]{1,0:T(8,128)(2,1)S(1)} %collective-permute-done.5.other, f32[1664]{0:T(1024)S(1)} %copy-done.8, bf16[1664,1024]{1,0:T(8,128)(2,1)S(1)} %copy-done.1, ...), custom_call_target="tpu_custom_call" | custom-call | flops 1 | bytes 1 | tf_op jit(solution)/shard_map/mlp_rows/pallas_call | solution.py:294
  42.2 2.8 %collective-permute-start.9 = (bf16[80,1664]{1,0:T(8,128)(2,1)S(1)}, bf16[80,1664]{1,0:T(8,128)(2,1)S(1)}, u32[]{:S(2)}, u32[]{:S(2)}) collective-permute-start(bf16[80,1664]{1,0:T(8,128)(2,1)S(1)} %get-tuple-element.96), channel_id=1, source_target_pairs={{0,4},{1,5},{2,6},{3,7},{4,0},{5,1},{6,2},{7,3},{8,12},{9,13},{10,... | collective-permute-start | bytes 798728 | tf_op jit(solution)/shard_map/ppermute | solution.py:44
  47.0 3.8 %mlp_rows.6 = (bf16[64,1664]{1,0:T(8,128)(2,1)S(1)}, bf16[64,1664]{1,0:T(8,128)(2,1)S(1)}) custom-call(bf16[64,1664]{1,0:T(8,128)(2,1)S(1)} %collective-permute-done.1.mine, bf16[64,1664]{1,0:T(8,128)(2,1)S(1)} %collective-permute-done.6.other, f32[1664]{0:T(1024)S(1)} %copy-done.8, bf16[1664,1024]{1,0:T(8,128)(2,1)S(1)} %copy-done.1, ...), custom_call_target="tpu_custom_call" | custom-call | flops 1 | bytes 1 | tf_op jit(solution)/shard_map/mlp_rows/pallas_call | solution.py:294
  50.8 1.6 collective-permute-start.11
  53.2 3.8 %mlp_rows.7 = (bf16[64,1664]{1,0:T(8,128)(2,1)S(1)}, bf16[64,1664]{1,0:T(8,128)(2,1)S(1)}) custom-call(bf16[64,1664]{1,0:T(8,128)(2,1)S(1)} %collective-permute-done.mine, bf16[64,1664]{1,0:T(8,128)(2,1)S(1)} %collective-permute-done.8.other, f32[1664]{0:T(1024)S(1)} %copy-done.8, bf16[1664,1024]{1,0:T(8,128)(2,1)S(1)} %copy-done.1, ...), custom_call_target="tpu_custom_call" | custom-call | flops 1 | bytes 1 | tf_op jit(solution)/shard_map/mlp_rows/pallas_call | solution.py:294
  57.0 1.6 collective-permute-start.12
  58.6 2.4 %collective-permute-done.11 = bf16[64,1664]{1,0:T(8,128)(2,1)S(1)} collective-permute-done((bf16[64,1664]{1,0:T(8,128)(2,1)S(1)}, bf16[64,1664]{1,0:T(8,128)(2,1)S(1)}, u32[]{:S(2)}, u32[]{:S(2)}) %collective-permute-start.11) | collective-permute-done | bytes 213024 | tf_op jit(solution)/shard_map/ppermute | solution.py:40
  61.1 2.2 %collective-permute-done.12 = bf16[64,1664]{1,0:T(8,128)(2,1)S(1)} collective-permute-done((bf16[64,1664]{1,0:T(8,128)(2,1)S(1)}, bf16[64,1664]{1,0:T(8,128)(2,1)S(1)}, u32[]{:S(2)}, u32[]{:S(2)}) %collective-permute-start.12) | collective-permute-done | bytes 213024 | tf_op jit(solution)/shard_map/ppermute | solution.py:40
  64.0 1.9 collective-permute-start.17
  69.1 3.2 %collective-permute-start.14 = (bf16[64,1664]{1,0:T(8,128)(2,1)S(1)}, bf16[64,1664]{1,0:T(8,128)(2,1)S(1)}, u32[]{:S(2)}, u32[]{:S(2)}) collective-permute-start(bf16[64,1664]{1,0:T(8,128)(2,1)S(1)} %add_convert_fusion.3), channel_id=1, source_target_pairs={{0,6},{1,7},{2,0},{3,1},{4,2},{5,3},{6,4},{7,5},{8,14},{9,15},{10,... | collective-permute-start | bytes 638984 | tf_op jit(solution)/shard_map/ppermute | solution.py:44
  73.6 2.0 masks.1
  76.3 15.1 %collective-permute-done.15.refs_3_ = bf16[64,1664]{1,0:T(8,128)(2,1)S(1)} collective-permute-done((bf16[64,1664]{1,0:T(8,128)(2,1)}, bf16[64,1664]{1,0:T(8,128)(2,1)S(1)}, u32[]{:S(2)}, u32[]{:S(2)}) %collective-permute-start.15) | collective-permute-done | bytes 213024 | tf_op jit(solution)/shard_map/ppermute | solution.py:44
  92.2 2.7 %spread_rows.1 = (bf16[4,16,832]{2,1,0:T(8,128)(2,1)}, bf16[4,16,832]{2,1,0:T(8,128)(2,1)}) custom-call(s32[16]{0:T(128)} %concatenate.18.starts.place, bf16[64,1664]{1,0:T(8,128)(2,1)} %bitcast.66, bf16[64,1664]{1,0:T(8,128)(2,1)} %copy-done.23, bf16[64,1664]{1,0:T(8,128)(2,1)} %copy-done.7, bf16[64,1664]{1,0:T(8,128)(2,1)} %copy-done.26, ...), custom_call_target="tpu_custom_call" | custom-call | flops 1 | bytes 1 | tf_op jit(solution)/shard_map/spread_rows/pallas_call | solution.py:341
  94.9 4.2 %collective-permute-start.20 = (bf16[160,1664]{1,0:T(8,128)(2,1)S(1)}, bf16[160,1664]{1,0:T(8,128)(2,1)S(1)}, u32[]{:S(2)}, u32[]{:S(2)}) collective-permute-start(bf16[160,1664]{1,0:T(8,128)(2,1)S(1)} %dynamic-slice_bitcast_fusion), channel_id=1, source_target_pairs={{0,2},{1,3},{2,4},{3,5},{4,6},{5,7},{6,0},{7,1},{8,10},{9,11},{10,... | collective-permute-start | bytes 1597448 | tf_op jit(solution)/shard_map/ppermute | solution.py:44
  99.2 1.6 collective-permute-start.21
  103.9 5.7 %text_first.1 = (bf16[768,1664]{1,0:T(8,128)(2,1)}, bf16[4,624,768]{2,1,0:T(8,128)(2,1)}) custom-call(s32[16]{0:T(128)} %concatenate.18.starts.place, f32[1664]{0:T(1024)} %gain.10, bf16[624,1664]{1,0:T(8,128)(2,1)} %bitcast.68, bf16[192,1664]{1,0:T(8,128)(2,1)} %copy-done.19, bf16[192,1664]{1,0:T(8,128)(2,1)} %copy-done.20, bf16[192,1664]{1,0:T(8,128)(2,1)} %bitcast.76, ...), custom_call_target="tpu_custom_call" | custom-call | flops 1 | bytes 1 | tf_op jit(solution)/shard_map/text_first/pallas_call | solution.py:230
  110.6 2.3 %collective-permute-done.21 = bf16[160,1664]{1,0:T(8,128)(2,1)S(1)} collective-permute-done((bf16[160,1664]{1,0:T(8,128)(2,1)S(1)}, bf16[160,1664]{1,0:T(8,128)(2,1)S(1)}, u32[]{:S(2)}, u32[]{:S(2)}) %collective-permute-start.21) | collective-permute-done | bytes 532512 | tf_op jit(solution)/shard_map/ppermute | solution.py:438
  113.2 2.5 %collective-permute-start.22 = (bf16[32,832]{1,0:T(8,128)(2,1)S(1)}, bf16[32,832]{1,0:T(8,128)(2,1)S(1)}, u32[]{:S(2)}, u32[]{:S(2)}) collective-permute-start(bf16[32,832]{1,0:T(8,128)(2,1)S(1)} %pad_maximum_fusion.5), channel_id=1, source_target_pairs={{0,2},{1,3},{2,4},{3,5},{4,6},{5,7},{6,0},{7,1},{8,10},{9,11},{10,... | collective-permute-start | bytes 159752 | tf_op jit(solution)/shard_map/ppermute | solution.py:44
  115.8 2.7 %collective-permute-start.24 = (bf16[32,832]{1,0:T(8,128)(2,1)S(1)}, bf16[32,832]{1,0:T(8,128)(2,1)S(1)}, u32[]{:S(2)}, u32[]{:S(2)}) collective-permute-start(bf16[32,832]{1,0:T(8,128)(2,1)S(1)} %pad_maximum_fusion.7), channel_id=1, source_target_pairs={{0,6},{1,7},{2,0},{3,1},{4,2},{5,3},{6,4},{7,5},{8,14},{9,15},{10,... | collective-permute-start | bytes 159752 | tf_op jit(solution)/shard_map/ppermute | solution.py:44
  119.5 2.3 %collective-permute-done.23.refs_2_ = bf16[32,832]{1,0:T(8,128)(2,1)S(1)} collective-permute-done((bf16[32,832]{1,0:T(8,128)(2,1)S(1)}, bf16[32,832]{1,0:T(8,128)(2,1)S(1)}, u32[]{:S(2)}, u32[]{:S(2)}) %collective-permute-start.23) | collective-permute-done | bytes 53280 | tf_op jit(solution)/shard_map/ppermute | solution.py:44
  124.0 2.7 %collective-permute-start.27 = (bf16[160,1664]{1,0:T(8,128)(2,1)S(1)}, bf16[160,1664]{1,0:T(8,128)(2,1)S(1)}, u32[]{:S(2)}, u32[]{:S(2)}) collective-permute-start(bf16[160,1664]{1,0:T(8,128)(2,1)S(1)} %dynamic-slice_bitcast_fusion), channel_id=1, source_target_pairs={{0,6},{1,7},{2,0},{3,1},{4,2},{5,3},{6,4},{7,5},{8,14},{9,15},{10,... | collective-permute-start | bytes 1597448 | tf_op jit(solution)/shard_map/ppermute | solution.py:44
  130.7 5.6 %text_next.3.before = bf16[4,624,768]{2,1,0:T(8,128)(2,1)} custom-call(s32[16]{0:T(128)} %concatenate.18.starts.place, bf16[768,1664]{1,0:T(8,128)(2,1)} %get-tuple-element.139.rows, bf16[2,1,160,1664]{3,2,1,0:T(8,128)(2,1)} %copy-done.12, bf16[2,1,160,1664]{3,2,1,0:T(8,128)(2,1)} %copy-done.14, ...), custom_call_target="tpu_custom_call", output_to_operand_aliasing={{}: (4, {})} | custom-call | flops 1 | bytes 1 | tf_op jit(solution)/shard_map/text_next/pallas_call | solution.py:230
  137.1 1.9 image_shares.1
  142.4 2.3 %collective-permute-start.31 = (bf16[64,832]{1,0:T(8,128)(2,1)S(1)}, bf16[64,832]{1,0:T(8,128)(2,1)S(1)}, u32[]{:S(2)}, u32[]{:S(2)}) collective-permute-start(bf16[64,832]{1,0:T(8,128)(2,1)S(1)} %copy-done.31), channel_id=1, source_target_pairs={{0,4},{1,5},{2,6},{3,7},{4,0},{5,1},{6,2},{7,3},{8,12},{9,13},{10,... | collective-permute-start | bytes 319496 | tf_op jit(solution)/shard_map/ppermute | solution.py:44
  144.7 1.8 collective-permute-start.32
  147.5 5.7 %text_next.4.before = bf16[4,624,768]{2,1,0:T(8,128)(2,1)} custom-call(s32[16]{0:T(128)} %concatenate.18.starts.place, bf16[768,1664]{1,0:T(8,128)(2,1)} %get-tuple-element.139.rows, bf16[2,1,160,1664]{3,2,1,0:T(8,128)(2,1)} %get-tuple-element.157.ours.refs_2_, bf16[2,1,160,1664]{3,2,1,0:T(8,128)(2,1)} %bitcast.70, ...), custom_call_target="tpu_custom_call", output_to_operand_aliasing={{}: (4, {})} | custom-call | flops 1 | bytes 1 | tf_op jit(solution)/shard_map/text_next/pallas_call | solution.py:230
  157.8 2.2 collective-permute-start.37
  162.4 5.6 %text_next.5.refs_0_ = bf16[4,624,768]{2,1,0:T(8,128)(2,1)} custom-call(s32[16]{0:T(128)} %concatenate.18.starts.place, bf16[768,1664]{1,0:T(8,128)(2,1)} %get-tuple-element.139.rows, bf16[2,1,160,1664]{3,2,1,0:T(8,128)(2,1)} %get-tuple-element.155.ours.refs_4_, bf16[2,1,160,1664]{3,2,1,0:T(8,128)(2,1)} %bitcast.72, ...), custom_call_target="tpu_custom_call", output_to_operand_aliasing={{}: (4, {})} | custom-call | flops 1 | bytes 1 | tf_op jit(solution)/shard_map/text_next/pallas_call | solution.py:230
  168.6 1.9 image_rows.1
  170.5 4.3 %collective-permute-done.36 = bf16[64,1664]{1,0:T(8,128)(2,1)S(1)} collective-permute-done((bf16[64,1664]{1,0:T(8,128)(2,1)S(1)}, bf16[64,1664]{1,0:T(8,128)(2,1)S(1)}, u32[]{:S(2)}, u32[]{:S(2)}) %collective-permute-start.36) | collective-permute-done | bytes 213024 | tf_op jit(solution)/shard_map/ppermute | solution.py:44
  175.9 12.5 %late_attention.1 = (bf16[192,832]{1,0:T(8,128)(2,1)}, bf16[192,832]{1,0:T(8,128)(2,1)}) custom-call(s32[16]{0:T(128)} %concatenate.18.starts.place, bf16[64,1664]{1,0:T(8,128)(2,1)} %get-tuple-element.148.image_rows, bf16[64,768]{1,0:T(8,128)(2,1)} %get-tuple-element.101.spread, f32[8,768]{1,0:T(8,128)} %get-tuple-element.102.hits, ...), custom_call_target="tpu_custom_call" | custom-call | flops 1 | bytes 1 | tf_op jit(solution)/shard_map/late_attention/pallas_call | solution.py:230
  188.4 2.5 %collective-permute-done.39 = bf16[3,64,1664]{2,1,0:T(8,128)(2,1)S(1)} collective-permute-done((bf16[3,64,1664]{2,1,0:T(8,128)(2,1)S(1)}, bf16[3,64,1664]{2,1,0:T(8,128)(2,1)S(1)}, u32[]{:S(2)}, u32[]{:S(2)}) %collective-permute-start.39) | collective-permute-done | bytes 639008 | tf_op jit(solution)/shard_map/ppermute | solution.py:438
  191.2 3.0 %collective-permute-done.40.theirs = bf16[2,3,64,1664]{3,2,1,0:T(8,128)(2,1)S(1)} collective-permute-done((bf16[2,3,64,1664]{3,2,1,0:T(8,128)(2,1)S(1)}, bf16[2,3,64,1664]{3,2,1,0:T(8,128)(2,1)S(1)}, u32[]{:S(2)}, u32[]{:S(2)}) %collective-permute-start.40) | collective-permute-done | bytes 1277984 | tf_op jit(solution)/shard_map/ppermute | solution.py:438
  195.2 3.9 %project.2 = bf16[192,1664]{1,0:T(8,128)(2,1)} custom-call(s32[16]{0:T(128)} %concatenate.18.starts.place, bf16[192,832]{1,0:T(8,128)(2,1)} %get-tuple-element.152.rows, bf16[208,1664]{1,0:T(8,128)(2,1)} %own.3, bf16[2,3,64,1664]{3,2,1,0:T(8,128)(2,1)} %copy-done.11, bf16[2,3,64,1664]{3,2,1,0:T(8,128)(2,1)} %copy-done.13), custom_call_target="tpu_custom_call" | custom-call | flops 1 | bytes 1 | tf_op jit(solution)/shard_map/project/pallas_call | solution.py:230
  200.6 4.0 %project.3.kept = bf16[192,1664]{1,0:T(8,128)(2,1)} custom-call(s32[16]{0:T(128)} %concatenate.18.starts.place, bf16[192,832]{1,0:T(8,128)(2,1)} %get-tuple-element.153.rows, bf16[208,1664]{1,0:T(8,128)(2,1)} %own.3, bf16[2,3,64,1664]{3,2,1,0:T(8,128)(2,1)} %copy-done.11, bf16[2,3,64,1664]{3,2,1,0:T(8,128)(2,1)} %copy-done.13), custom_call_target="tpu_custom_call" | custom-call | flops 1 | bytes 1 | tf_op jit(solution)/shard_map/project/pallas_call | solution.py:230
  204.6 2.7 %out_rows.1 = f32[192,1664]{1,0:T(8,128)} custom-call(s32[16]{0:T(128)} %concatenate.18.starts.place, bf16[192,1664]{1,0:T(8,128)(2,1)} %bitcast.77, s32[8,64]{1,0:T(8,128)} %get-tuple-element.104.slots, bf16[64,1664]{1,0:T(8,128)(2,1)} %get-tuple-element.144.merged, bf16[192,1664]{1,0:T(8,128)(2,1)} %project.3.kept), custom_call_target="tpu_custom_call" | custom-call | flops 1 | bytes 1 | tf_op jit(solution)/shard_map/out_rows/pallas_call | solution.py:230
  207.3 8.5 %collective-permute-done.41 = bf16[192,1664]{1,0:T(8,128)(2,1)S(1)} collective-permute-done((bf16[192,1664]{1,0:T(8,128)(2,1)}, bf16[192,1664]{1,0:T(8,128)(2,1)S(1)}, u32[]{:S(2)}, u32[]{:S(2)}) %collective-permute-start.41) | collective-permute-done | bytes 639008 | tf_op jit(solution)/shard_map/ppermute | solution.py:40
  215.8 2.3 %fusion.4 = bf16[1,192,1664]{2,1,0:T(8,128)(2,1)} fusion(f32[192,1664]{1,0:T(8,128)} %out_rows.1, bf16[192,1664]{1,0:T(8,128)(2,1)S(1)} %collective-permute-done.41), kind=kLoop, calls=%fused_computation.10 | loop fusion | flops 958464 | bytes 2555904 | tf_op jit(solution)/shard_map/broadcast_in_dim | solution.py:671
  (144 shorter events, 43.5 us)
Async XLA Ops:
  0.0 25.7 %copy-start.17 = (bf16[1,192,1664]{2,1,0:T(8,128)(2,1)S(1)}, bf16[1,192,1664]{2,1,0:T(8,128)(2,1)}, u32[]{:S(2)}) copy-start(bf16[1,192,1664]{2,1,0:T(8,128)(2,1)} %param.20) | copy-start | bytes 1916932
  0.0 25.7 %collective-permute-start.4 = (bf16[192,1664]{1,0:T(8,128)(2,1)}, bf16[192,1664]{1,0:T(8,128)(2,1)S(1)}, u32[]{:S(2)}, u32[]{:S(2)}) collective-permute-start(bf16[192,1664]{1,0:T(8,128)(2,1)} %bitcast.75), channel_id=1, source_target_pairs={{0,1},{1,0},{2,3},{3,2},{4,5},{5,4},{6,7},{7,6},{8,9},{9,8},{10,11... | collective-permute-start | bytes 1916936 | tf_op jit(solution)/shard_map/ppermute | solution.py:40
  2.9 19.2 %collective-permute-start.3 = (bf16[64,1664]{1,0:T(8,128)(2,1)}, bf16[64,1664]{1,0:T(8,128)(2,1)S(1)}, u32[]{:S(2)}, u32[]{:S(2)}) collective-permute-start(bf16[64,1664]{1,0:T(8,128)(2,1)} %bitcast.62), channel_id=1, source_target_pairs={{0,1},{1,0},{2,3},{3,2},{4,5},{5,4},{6,7},{7,6},{8,9},{9,8},{10,11... | collective-permute-start | bytes 638984 | tf_op jit(solution)/shard_map/ppermute | solution.py:40
  3.0 19.2 %collective-permute-start.2 = (bf16[64,1664]{1,0:T(8,128)(2,1)}, bf16[64,1664]{1,0:T(8,128)(2,1)S(1)}, u32[]{:S(2)}, u32[]{:S(2)}) collective-permute-start(bf16[64,1664]{1,0:T(8,128)(2,1)} %bitcast.63), channel_id=1, source_target_pairs={{0,2},{1,3},{2,4},{3,5},{4,6},{5,7},{6,0},{7,1},{8,10},{9,11},{10,... | collective-permute-start | bytes 638984 | tf_op jit(solution)/shard_map/ppermute | solution.py:44
  5.1 17.1 %collective-permute-start.1 = (bf16[64,1664]{1,0:T(8,128)(2,1)}, bf16[64,1664]{1,0:T(8,128)(2,1)S(1)}, u32[]{:S(2)}, u32[]{:S(2)}) collective-permute-start(bf16[64,1664]{1,0:T(8,128)(2,1)} %bitcast.64), channel_id=1, source_target_pairs={{0,6},{1,7},{2,0},{3,1},{4,2},{5,3},{6,4},{7,5},{8,14},{9,15},{10,... | collective-permute-start | bytes 638984 | tf_op jit(solution)/shard_map/ppermute | solution.py:44
  7.1 18.6 %collective-permute-start = (bf16[64,1664]{1,0:T(8,128)(2,1)}, bf16[64,1664]{1,0:T(8,128)(2,1)S(1)}, u32[]{:S(2)}, u32[]{:S(2)}) collective-permute-start(bf16[64,1664]{1,0:T(8,128)(2,1)} %bitcast.65), channel_id=1, source_target_pairs={{0,4},{1,5},{2,6},{3,7},{4,0},{5,1},{6,2},{7,3},{8,12},{9,13},{10,... | collective-permute-start | bytes 638984 | tf_op jit(solution)/shard_map/ppermute | solution.py:44
  8.1 21.8 %copy-start.5 = (bf16[1,64,1664]{2,1,0:T(8,128)(2,1)S(1)}, bf16[1,64,1664]{2,1,0:T(8,128)(2,1)}, u32[]{:S(2)}) copy-start(bf16[1,64,1664]{2,1,0:T(8,128)(2,1)} %param.13) | copy-start | bytes 638980
  8.1 21.8 %copy-start.8 = (f32[1664]{0:T(1024)S(1)}, f32[1664]{0:T(1024)}, u32[]{:S(2)}) copy-start(f32[1664]{0:T(1024)} %gain.8) | copy-start | bytes 19972
  25.7 16.4 %collective-permute-start.7 = (bf16[192,1664]{1,0:T(8,128)(2,1)S(1)}, bf16[192,1664]{1,0:T(8,128)(2,1)S(1)}, u32[]{:S(2)}, u32[]{:S(2)}) collective-permute-start(bf16[192,1664]{1,0:T(8,128)(2,1)S(1)} %bitcast.78), channel_id=1, source_target_pairs={{0,2},{1,3},{2,4},{3,5},{4,6},{5,7},{8,10},{9,11},{10,12},{11,13},... | collective-permute-start | bytes 1916936 | tf_op jit(solution)/shard_map/ppermute | solution.py:549
  27.1 11.3 %collective-permute-start.5 = (bf16[64,1664]{1,0:T(8,128)(2,1)S(1)}, bf16[64,1664]{1,0:T(8,128)(2,1)S(1)}, u32[]{:S(2)}, u32[]{:S(2)}) collective-permute-start(bf16[64,1664]{1,0:T(8,128)(2,1)S(1)} %collective-permute-done.2.mine), channel_id=1, source_target_pairs={{0,1},{1,0},{2,3},{3,2},{4,5},{5,4},{6,7},{7,6},{8,9},{9,8},{10,11... | collective-permute-start | bytes 638984 | tf_op jit(solution)/shard_map/ppermute | solution.py:40
  28.6 13.5 %collective-permute-start.6 = (bf16[64,1664]{1,0:T(8,128)(2,1)S(1)}, bf16[64,1664]{1,0:T(8,128)(2,1)S(1)}, u32[]{:S(2)}, u32[]{:S(2)}) collective-permute-start(bf16[64,1664]{1,0:T(8,128)(2,1)S(1)} %collective-permute-done.1.mine), channel_id=1, source_target_pairs={{0,1},{1,0},{2,3},{3,2},{4,5},{5,4},{6,7},{7,6},{8,9},{9,8},{10,11... | collective-permute-start | bytes 638984 | tf_op jit(solution)/shard_map/ppermute | solution.py:40
  42.2 33.5 %copy-start.19 = (bf16[192,1664]{1,0:T(8,128)(2,1)}, bf16[192,1664]{1,0:T(8,128)(2,1)S(1)}, u32[]{:S(2)}) copy-start(bf16[192,1664]{1,0:T(8,128)(2,1)S(1)} %collective-permute-done.7.refs_0_) | copy-start | bytes 1916932
  42.2 16.4 %collective-permute-start.9 = (bf16[80,1664]{1,0:T(8,128)(2,1)S(1)}, bf16[80,1664]{1,0:T(8,128)(2,1)S(1)}, u32[]{:S(2)}, u32[]{:S(2)}) collective-permute-start(bf16[80,1664]{1,0:T(8,128)(2,1)S(1)} %get-tuple-element.96), channel_id=1, source_target_pairs={{0,4},{1,5},{2,6},{3,7},{4,0},{5,1},{6,2},{7,3},{8,12},{9,13},{10,... | collective-permute-start | bytes 798728 | tf_op jit(solution)/shard_map/ppermute | solution.py:44
  45.0 8.2 %collective-permute-start.8 = (bf16[64,1664]{1,0:T(8,128)(2,1)S(1)}, bf16[64,1664]{1,0:T(8,128)(2,1)S(1)}, u32[]{:S(2)}, u32[]{:S(2)}) collective-permute-start(bf16[64,1664]{1,0:T(8,128)(2,1)S(1)} %collective-permute-done.mine), channel_id=1, source_target_pairs={{0,1},{1,0},{2,3},{3,2},{4,5},{5,4},{6,7},{7,6},{8,9},{9,8},{10,11... | collective-permute-start | bytes 638984 | tf_op jit(solution)/shard_map/ppermute | solution.py:40
  46.5 12.1 %collective-permute-start.10 = (bf16[64,1664]{1,0:T(8,128)(2,1)S(1)}, bf16[64,1664]{1,0:T(8,128)(2,1)S(1)}, u32[]{:S(2)}, u32[]{:S(2)}) collective-permute-start(bf16[64,1664]{1,0:T(8,128)(2,1)S(1)} %get-tuple-element.86), channel_id=1, source_target_pairs={{0,1},{1,0},{2,3},{3,2},{4,5},{5,4},{6,7},{7,6},{8,9},{9,8},{10,11... | collective-permute-start | bytes 638984 | tf_op jit(solution)/shard_map/ppermute | solution.py:40
  50.8 10.2 %collective-permute-start.11 = (bf16[64,1664]{1,0:T(8,128)(2,1)S(1)}, bf16[64,1664]{1,0:T(8,128)(2,1)S(1)}, u32[]{:S(2)}, u32[]{:S(2)}) collective-permute-start(bf16[64,1664]{1,0:T(8,128)(2,1)S(1)} %get-tuple-element.91), channel_id=1, source_target_pairs={{0,1},{1,0},{2,3},{3,2},{4,5},{5,4},{6,7},{7,6},{8,9},{9,8},{10,11... | collective-permute-start | bytes 638984 | tf_op jit(solution)/shard_map/ppermute | solution.py:40
  57.0 15.3 %copy-start.10 = (s32[4]{0:T(128)S(1)}, s32[4]{0:T(128)}, u32[]{:S(2)}) copy-start(s32[4]{0:T(128)} %constant.84) | copy-start | bytes 52
  57.0 6.3 %collective-permute-start.12 = (bf16[64,1664]{1,0:T(8,128)(2,1)S(1)}, bf16[64,1664]{1,0:T(8,128)(2,1)S(1)}, u32[]{:S(2)}, u32[]{:S(2)}) collective-permute-start(bf16[64,1664]{1,0:T(8,128)(2,1)S(1)} %get-tuple-element.95), channel_id=1, source_target_pairs={{0,1},{1,0},{2,3},{3,2},{4,5},{5,4},{6,7},{7,6},{8,9},{9,8},{10,11... | collective-permute-start | bytes 638984 | tf_op jit(solution)/shard_map/ppermute | solution.py:40
  64.0 27.3 %collective-permute-start.17 = (bf16[80,1664]{1,0:T(8,128)(2,1)}, bf16[80,1664]{1,0:T(8,128)(2,1)S(1)}, u32[]{:S(2)}, u32[]{:S(2)}) collective-permute-start(bf16[80,1664]{1,0:T(8,128)(2,1)} %get-tuple-element.105), channel_id=1, source_target_pairs={{0,4},{1,5},{2,6},{3,7},{4,0},{5,1},{6,2},{7,3},{8,12},{9,13},{10,... | collective-permute-start | bytes 798728 | tf_op jit(solution)/shard_map/ppermute | solution.py:44
  65.9 9.7 %collective-permute-start.13 = (bf16[64,1664]{1,0:T(8,128)(2,1)S(1)}, bf16[64,1664]{1,0:T(8,128)(2,1)S(1)}, u32[]{:S(2)}, u32[]{:S(2)}) collective-permute-start(bf16[64,1664]{1,0:T(8,128)(2,1)S(1)} %get-tuple-element.82), channel_id=1, source_target_pairs={{0,1},{1,0},{2,3},{3,2},{4,5},{5,4},{6,7},{7,6},{8,9},{9,8},{10,11... | collective-permute-start | bytes 638984 | tf_op jit(solution)/shard_map/ppermute | solution.py:40
  67.4 23.9 %collective-permute-start.15 = (bf16[64,1664]{1,0:T(8,128)(2,1)}, bf16[64,1664]{1,0:T(8,128)(2,1)S(1)}, u32[]{:S(2)}, u32[]{:S(2)}) collective-permute-start(bf16[64,1664]{1,0:T(8,128)(2,1)} %add_convert_fusion.1), channel_id=1, source_target_pairs={{0,4},{1,5},{2,6},{3,7},{4,0},{5,1},{6,2},{7,3},{8,12},{9,13},{10,... | collective-permute-start | bytes 638984 | tf_op jit(solution)/shard_map/ppermute | solution.py:44
  68.4 22.9 %collective-permute-start.16 = (bf16[64,1664]{1,0:T(8,128)(2,1)S(1)}, bf16[64,1664]{1,0:T(8,128)(2,1)S(1)}, u32[]{:S(2)}, u32[]{:S(2)}) collective-permute-start(bf16[64,1664]{1,0:T(8,128)(2,1)S(1)} %add_convert_fusion.2), channel_id=1, source_target_pairs={{0,2},{1,3},{2,4},{3,5},{4,6},{5,7},{6,0},{7,1},{8,10},{9,11},{10,... | collective-permute-start | bytes 638984 | tf_op jit(solution)/shard_map/ppermute | solution.py:44
  69.1 22.3 %collective-permute-start.14 = (bf16[64,1664]{1,0:T(8,128)(2,1)S(1)}, bf16[64,1664]{1,0:T(8,128)(2,1)S(1)}, u32[]{:S(2)}, u32[]{:S(2)}) collective-permute-start(bf16[64,1664]{1,0:T(8,128)(2,1)S(1)} %add_convert_fusion.3), channel_id=1, source_target_pairs={{0,6},{1,7},{2,0},{3,1},{4,2},{5,3},{6,4},{7,5},{8,14},{9,15},{10,... | collective-permute-start | bytes 638984 | tf_op jit(solution)/shard_map/ppermute | solution.py:44
  75.7 15.7 %copy-start.23 = (bf16[64,1664]{1,0:T(8,128)(2,1)}, bf16[64,1664]{1,0:T(8,128)(2,1)S(1)}, u32[]{:S(2)}) copy-start(bf16[64,1664]{1,0:T(8,128)(2,1)S(1)} %collective-permute-done.13.refs_0_) | copy-start | bytes 638980
  75.7 27.4 %collective-permute-start.18 = (bf16[192,1664]{1,0:T(8,128)(2,1)S(1)}, bf16[192,1664]{1,0:T(8,128)(2,1)S(1)}, u32[]{:S(2)}, u32[]{:S(2)}) collective-permute-start(bf16[192,1664]{1,0:T(8,128)(2,1)S(1)} %collective-permute-done.7.refs_0_), channel_id=1, source_target_pairs={{0,1},{1,0},{2,3},{3,2},{4,5},{5,4},{6,7},{7,6},{8,9},{9,8},{10,11... | collective-permute-start | bytes 1916936 | tf_op jit(solution)/shard_map/ppermute | solution.py:40
  94.9 15.7 %collective-permute-start.20 = (bf16[160,1664]{1,0:T(8,128)(2,1)S(1)}, bf16[160,1664]{1,0:T(8,128)(2,1)S(1)}, u32[]{:S(2)}, u32[]{:S(2)}) collective-permute-start(bf16[160,1664]{1,0:T(8,128)(2,1)S(1)} %dynamic-slice_bitcast_fusion), channel_id=1, source_target_pairs={{0,2},{1,3},{2,4},{3,5},{4,6},{5,7},{6,0},{7,1},{8,10},{9,11},{10,... | collective-permute-start | bytes 1597448 | tf_op jit(solution)/shard_map/ppermute | solution.py:44
  99.2 13.8 %collective-permute-start.21 = (bf16[160,1664]{1,0:T(8,128)(2,1)S(1)}, bf16[160,1664]{1,0:T(8,128)(2,1)S(1)}, u32[]{:S(2)}, u32[]{:S(2)}) collective-permute-start(bf16[160,1664]{1,0:T(8,128)(2,1)S(1)} %constant_dynamic-update-slice_fusion), channel_id=1, source_target_pairs={{0,16},{8,24},{16,0},{24,8},{1,17},{9,25},{17,1},{25,9},{2,18},{10... | collective-permute-start | bytes 1597448 | tf_op jit(solution)/shard_map/ppermute | solution.py:438
  100.7 8.9 %collective-permute-start.19 = (bf16[4,16,832]{2,1,0:T(8,128)(2,1)}, bf16[4,16,832]{2,1,0:T(8,128)(2,1)S(1)}, u32[]{:S(2)}, u32[]{:S(2)}) collective-permute-start(bf16[4,16,832]{2,1,0:T(8,128)(2,1)} %get-tuple-element.115), channel_id=1, source_target_pairs={{0,1},{1,0},{2,3},{3,2},{4,5},{5,4},{6,7},{7,6},{8,9},{9,8},{10,11... | collective-permute-start | bytes 319496 | tf_op jit(solution)/shard_map/ppermute | solution.py:40
  113.1 16.6 %collective-permute-start.25 = (bf16[2,1,160,1664]{3,2,1,0:T(8,128)(2,1)S(1)}, bf16[2,1,160,1664]{3,2,1,0:T(8,128)(2,1)S(1)}, u32[]{:S(2)}, u32[]{:S(2)}) collective-permute-start(bf16[2,1,160,1664]{3,2,1,0:T(8,128)(2,1)S(1)} %maximum_bitcast_fusion.ours.refs_6_), channel_id=1, source_target_pairs={{0,8},{8,0},{16,24},{24,16},{1,9},{9,1},{17,25},{25,17},{2,10},{10... | collective-permute-start | bytes 3194888 | tf_op jit(solution)/shard_map/ppermute | solution.py:438
  113.2 6.3 %collective-permute-start.22 = (bf16[32,832]{1,0:T(8,128)(2,1)S(1)}, bf16[32,832]{1,0:T(8,128)(2,1)S(1)}, u32[]{:S(2)}, u32[]{:S(2)}) collective-permute-start(bf16[32,832]{1,0:T(8,128)(2,1)S(1)} %pad_maximum_fusion.5), channel_id=1, source_target_pairs={{0,2},{1,3},{2,4},{3,5},{4,6},{5,7},{6,0},{7,1},{8,10},{9,11},{10,... | collective-permute-start | bytes 159752 | tf_op jit(solution)/shard_map/ppermute | solution.py:44
  115.7 6.1 %collective-permute-start.23 = (bf16[32,832]{1,0:T(8,128)(2,1)S(1)}, bf16[32,832]{1,0:T(8,128)(2,1)S(1)}, u32[]{:S(2)}, u32[]{:S(2)}) collective-permute-start(bf16[32,832]{1,0:T(8,128)(2,1)S(1)} %pad_maximum_fusion.6), channel_id=1, source_target_pairs={{0,4},{1,5},{2,6},{3,7},{4,0},{5,1},{6,2},{7,3},{8,12},{9,13},{10,... | collective-permute-start | bytes 159752 | tf_op jit(solution)/shard_map/ppermute | solution.py:44
  115.8 6.1 %collective-permute-start.24 = (bf16[32,832]{1,0:T(8,128)(2,1)S(1)}, bf16[32,832]{1,0:T(8,128)(2,1)S(1)}, u32[]{:S(2)}, u32[]{:S(2)}) collective-permute-start(bf16[32,832]{1,0:T(8,128)(2,1)S(1)} %pad_maximum_fusion.7), channel_id=1, source_target_pairs={{0,6},{1,7},{2,0},{3,1},{4,2},{5,3},{6,4},{7,5},{8,14},{9,15},{10,... | collective-permute-start | bytes 159752 | tf_op jit(solution)/shard_map/ppermute | solution.py:44
  124.0 15.0 %collective-permute-start.27 = (bf16[160,1664]{1,0:T(8,128)(2,1)S(1)}, bf16[160,1664]{1,0:T(8,128)(2,1)S(1)}, u32[]{:S(2)}, u32[]{:S(2)}) collective-permute-start(bf16[160,1664]{1,0:T(8,128)(2,1)S(1)} %dynamic-slice_bitcast_fusion), channel_id=1, source_target_pairs={{0,6},{1,7},{2,0},{3,1},{4,2},{5,3},{6,4},{7,5},{8,14},{9,15},{10,... | collective-permute-start | bytes 1597448 | tf_op jit(solution)/shard_map/ppermute | solution.py:44
  126.7 12.7 %collective-permute-start.28 = (bf16[160,1664]{1,0:T(8,128)(2,1)S(1)}, bf16[160,1664]{1,0:T(8,128)(2,1)S(1)}, u32[]{:S(2)}, u32[]{:S(2)}) collective-permute-start(bf16[160,1664]{1,0:T(8,128)(2,1)S(1)} %collective-permute-done.20), channel_id=1, source_target_pairs={{0,16},{8,24},{16,0},{24,8},{1,17},{9,25},{17,1},{25,9},{2,18},{10... | collective-permute-start | bytes 1597448 | tf_op jit(solution)/shard_map/ppermute | solution.py:438
  128.2 8.2 %collective-permute-start.26 = (bf16[128,832]{1,0:T(8,128)(2,1)S(1)}, bf16[128,832]{1,0:T(8,128)(2,1)S(1)}, u32[]{:S(2)}, u32[]{:S(2)}) collective-permute-start(bf16[128,832]{1,0:T(8,128)(2,1)S(1)} %get-tuple-element.125), channel_id=1, source_target_pairs={{0,1},{1,0},{2,3},{3,2},{4,5},{5,4},{6,7},{7,6},{8,9},{9,8},{10,11... | collective-permute-start | bytes 638984 | tf_op jit(solution)/shard_map/ppermute | solution.py:40
  140.6 6.0 %collective-permute-start.29 = (bf16[2,1,160,1664]{3,2,0,1:T(8,128)(2,1)S(1)}, bf16[2,1,160,1664]{3,2,0,1:T(8,128)(2,1)S(1)}, u32[]{:S(2)}, u32[]{:S(2)}) collective-permute-start(bf16[2,1,160,1664]{3,2,0,1:T(8,128)(2,1)S(1)} %get-tuple-element.158), channel_id=1, source_target_pairs={{0,8},{8,0},{16,24},{24,16},{1,9},{9,1},{17,25},{25,17},{2,10},{10... | collective-permute-start | bytes 3194888 | tf_op jit(solution)/shard_map/ppermute | solution.py:438
  140.6 14.5 %collective-permute-start.33 = (bf16[160,1664]{1,0:T(8,128)(2,1)S(1)}, bf16[160,1664]{1,0:T(8,128)(2,1)S(1)}, u32[]{:S(2)}, u32[]{:S(2)}) collective-permute-start(bf16[160,1664]{1,0:T(8,128)(2,1)S(1)} %collective-permute-done.27), channel_id=1, source_target_pairs={{0,16},{8,24},{16,0},{24,8},{1,17},{9,25},{17,1},{25,9},{2,18},{10... | collective-permute-start | bytes 1597448 | tf_op jit(solution)/shard_map/ppermute | solution.py:438
  142.1 11.1 %collective-permute-start.30 = (bf16[64,832]{1,0:T(8,128)(2,1)S(1)}, bf16[64,832]{1,0:T(8,128)(2,1)S(1)}, u32[]{:S(2)}, u32[]{:S(2)}) collective-permute-start(bf16[64,832]{1,0:T(8,128)(2,1)S(1)} %copy-done.32), channel_id=1, source_target_pairs={{0,2},{1,3},{2,4},{3,5},{4,6},{5,7},{6,0},{7,1},{8,10},{9,11},{10,... | collective-permute-start | bytes 319496 | tf_op jit(solution)/shard_map/ppermute | solution.py:44
  142.4 11.8 %collective-permute-start.31 = (bf16[64,832]{1,0:T(8,128)(2,1)S(1)}, bf16[64,832]{1,0:T(8,128)(2,1)S(1)}, u32[]{:S(2)}, u32[]{:S(2)}) collective-permute-start(bf16[64,832]{1,0:T(8,128)(2,1)S(1)} %copy-done.31), channel_id=1, source_target_pairs={{0,4},{1,5},{2,6},{3,7},{4,0},{5,1},{6,2},{7,3},{8,12},{9,13},{10,... | collective-permute-start | bytes 319496 | tf_op jit(solution)/shard_map/ppermute | solution.py:44
  144.7 9.4 %collective-permute-start.32 = (bf16[64,832]{1,0:T(8,128)(2,1)S(1)}, bf16[64,832]{1,0:T(8,128)(2,1)S(1)}, u32[]{:S(2)}, u32[]{:S(2)}) collective-permute-start(bf16[64,832]{1,0:T(8,128)(2,1)S(1)} %copy-done.30), channel_id=1, source_target_pairs={{0,6},{1,7},{2,0},{3,1},{4,2},{5,3},{6,4},{7,5},{8,14},{9,15},{10,... | collective-permute-start | bytes 319496 | tf_op jit(solution)/shard_map/ppermute | solution.py:44
  156.3 5.2 %collective-permute-start.34 = (bf16[2,1,160,1664]{3,2,0,1:T(8,128)(2,1)S(1)}, bf16[2,1,160,1664]{3,2,0,1:T(8,128)(2,1)S(1)}, u32[]{:S(2)}, u32[]{:S(2)}) collective-permute-start(bf16[2,1,160,1664]{3,2,0,1:T(8,128)(2,1)S(1)} %get-tuple-element.156), channel_id=1, source_target_pairs={{0,8},{8,0},{16,24},{24,16},{1,9},{9,1},{17,25},{25,17},{2,10},{10... | collective-permute-start | bytes 3194888 | tf_op jit(solution)/shard_map/ppermute | solution.py:438
  156.3 14.2 %collective-permute-start.38 = (bf16[64,1664]{1,0:T(8,128)(2,1)S(1)}, bf16[64,1664]{1,0:T(8,128)(2,1)S(1)}, u32[]{:S(2)}, u32[]{:S(2)}) collective-permute-start(bf16[64,1664]{1,0:T(8,128)(2,1)S(1)} %copy-done.27), channel_id=1, source_target_pairs={{0,4},{1,5},{2,6},{3,7},{4,0},{5,1},{6,2},{7,3},{8,12},{9,13},{10,... | collective-permute-start | bytes 638984 | tf_op jit(solution)/shard_map/ppermute | solution.py:44
  157.8 12.7 %collective-permute-start.37 = (bf16[64,1664]{1,0:T(8,128)(2,1)S(1)}, bf16[64,1664]{1,0:T(8,128)(2,1)S(1)}, u32[]{:S(2)}, u32[]{:S(2)}) collective-permute-start(bf16[64,1664]{1,0:T(8,128)(2,1)S(1)} %copy-done.27), channel_id=1, source_target_pairs={{0,6},{1,7},{2,0},{3,1},{4,2},{5,3},{6,4},{7,5},{8,14},{9,15},{10,... | collective-permute-start | bytes 638984 | tf_op jit(solution)/shard_map/ppermute | solution.py:44
  159.9 14.9 %collective-permute-start.36 = (bf16[64,1664]{1,0:T(8,128)(2,1)S(1)}, bf16[64,1664]{1,0:T(8,128)(2,1)S(1)}, u32[]{:S(2)}, u32[]{:S(2)}) collective-permute-start(bf16[64,1664]{1,0:T(8,128)(2,1)S(1)} %copy-done.27), channel_id=1, source_target_pairs={{0,2},{1,3},{2,4},{3,5},{4,6},{5,7},{6,0},{7,1},{8,10},{9,11},{10,... | collective-permute-start | bytes 638984 | tf_op jit(solution)/shard_map/ppermute | solution.py:44
  159.9 8.0 %collective-permute-start.35 = (bf16[64,832]{1,0:T(8,128)(2,1)S(1)}, bf16[64,832]{1,0:T(8,128)(2,1)S(1)}, u32[]{:S(2)}, u32[]{:S(2)}) collective-permute-start(bf16[64,832]{1,0:T(8,128)(2,1)S(1)} %add_convert_fusion.4.ours), channel_id=1, source_target_pairs={{0,1},{1,0},{2,3},{3,2},{4,5},{5,4},{6,7},{7,6},{8,9},{9,8},{10,11... | collective-permute-start | bytes 319496 | tf_op jit(solution)/shard_map/ppermute | solution.py:40
  174.9 16.0 %collective-permute-start.39 = (bf16[3,64,1664]{2,1,0:T(8,128)(2,1)S(1)}, bf16[3,64,1664]{2,1,0:T(8,128)(2,1)S(1)}, u32[]{:S(2)}, u32[]{:S(2)}) collective-permute-start(bf16[3,64,1664]{2,1,0:T(8,128)(2,1)S(1)} %pad_maximum_fusion.3), channel_id=1, source_target_pairs={{0,16},{8,24},{16,0},{24,8},{1,17},{9,25},{17,1},{25,9},{2,18},{10... | collective-permute-start | bytes 1916936 | tf_op jit(solution)/shard_map/ppermute | solution.py:438
  191.1 3.1 %collective-permute-start.40 = (bf16[2,3,64,1664]{3,2,1,0:T(8,128)(2,1)S(1)}, bf16[2,3,64,1664]{3,2,1,0:T(8,128)(2,1)S(1)}, u32[]{:S(2)}, u32[]{:S(2)}) collective-permute-start(bf16[2,3,64,1664]{3,2,1,0:T(8,128)(2,1)S(1)} %pad_maximum_fusion.ours), channel_id=1, source_target_pairs={{0,8},{8,0},{16,24},{24,16},{1,9},{9,1},{17,25},{25,17},{2,10},{10... | collective-permute-start | bytes 3833864 | tf_op jit(solution)/shard_map/ppermute | solution.py:438
  199.2 16.6 %collective-permute-start.41 = (bf16[192,1664]{1,0:T(8,128)(2,1)}, bf16[192,1664]{1,0:T(8,128)(2,1)S(1)}, u32[]{:S(2)}, u32[]{:S(2)}) collective-permute-start(bf16[192,1664]{1,0:T(8,128)(2,1)} %project.2), channel_id=1, source_target_pairs={{0,1},{1,0},{2,3},{3,2},{4,5},{5,4},{6,7},{7,6},{8,9},{9,8},{10,11... | collective-permute-start | bytes 1916936 | tf_op jit(solution)/shard_map/ppermute | solution.py:40
  (27 other events, 90.5 us)

commit v6 on v5

--- a/solution.py
+++ b/solution.py
@@ -200,15 +200,15 @@
     given[...] = jnp.where(first_side, high, low)
 
 
-def project_kernel(starts, rows, own, ours, theirs, out, whole):
+def project_kernel(starts, rows, own, *refs):
+    quarters, (out, whole) = refs[:4], refs[4:]
     depth = own.shape[0]
     whole[:depth] = own[...]
-    size = ours.shape[2]
-    for line in range(ours.shape[1]):
+    size = quarters[0].shape[1]
+    for line in range(quarters[0].shape[0]):
         for index in range(4):
-            quarter = (ours if index % 2 == 0 else theirs)[index // 2, line]
             start = pl.multiple_of((line + 1) * depth + starts[4 + index], 16)
-            whole[pl.ds(start, size), :] = quarter
+            whole[pl.ds(start, size), :] = quarters[index][line]
     total = jnp.dot(rows[...], whole[...], preferred_element_type=jnp.float32)
     out[...] = total.astype(jnp.bfloat16)
 
@@ -226,7 +226,7 @@
 SMEM = pl.BlockSpec(memory_space=pltpu.SMEM)
 
 
-def kernel_call(body, name, results, *operands, scratch=(), grid=(), specs={}, out_specs=None, aliases={}):
+def kernel_call(body, name, results, *operands, scratch=(), grid=(), specs={}, out_specs=None, aliases={}, room=56):
     return pl.pallas_call(
         body,
         grid=grid,
@@ -240,7 +240,7 @@
         out_shape=[jax.ShapeDtypeStruct(shape, dtype) for shape, dtype in results],
         scratch_shapes=list(scratch),
         input_output_aliases=aliases,
-        compiler_params=pltpu.CompilerParams(vmem_limit_bytes=56 << 20),
+        compiler_params=pltpu.CompilerParams(vmem_limit_bytes=room << 20),
         cost_estimate=pl.CostEstimate(flops=1, bytes_accessed=1, transcendentals=0),
         name=name,
     )(*operands)
@@ -251,11 +251,11 @@
     return pl.BlockSpec(shape, lambda k: (0, line_of(k), 0, 0))
 
 
-def project(starts, rows, own, ours, theirs):
-    lines = ours.shape[1] + 1
+def project(starts, rows, own, quarters):
+    lines = quarters[0].shape[0] + 1
     return kernel_call(
         project_kernel, "project", [((rows.shape[0], own.shape[1]), jnp.bfloat16)],
-        starts, rows, own, ours, theirs,
+        starts, rows, own, *quarters,
         scratch=[pltpu.VMEM((lines * own.shape[0], own.shape[1]), jnp.bfloat16)],
     )
 
@@ -559,7 +559,10 @@
     queue.wait(qkv_moving[middle][0])
     for k in rounds:
         sums[k] = add_pair(k, queue.wait(back[k]))
-    sums[middle] = add_pair(middle, queue.wait(back[middle]))
+    got = queue.wait(back[middle])
+    for k in rounds:
+        queue.wait(sums[k])
+    sums[middle] = add_pair(middle, got)
     move_weights(middle, 1, 2)
     pieces = []
     for rows in text_back[::-1]:
@@ -647,6 +650,7 @@
     sources = [text_parts, qkv_own] + line_pieces
     out_near = queue.passed(jnp.stack(queue.wait([queue.held(part) for part in out_moving])))
     out_far = other_copy(out_near, 2)
+    out_beside = other_copy(out_near, 1)
     kept, given = queue.passed(kernel_call(
         functools.partial(late_kernel, blk, longest, lines, depth), "late_attention",
         [((seq_here, lines * depth), bf16)] * 2,
@@ -657,12 +661,14 @@
             pltpu.VMEM((lines * depth, blk), jnp.float32),
             pltpu.SemaphoreType.DMA((3 * lines,)),
         ],
+        room=32,
     ))
-    out_ours = queue.passed(jnp.stack([queue.held(out_near), queue.wait(out_far)]))
-    out_theirs = other_copy(out_ours, 1)
-    (given,) = queue.passed(project(starts, queue.held(given), out_own, out_ours, queue.wait(out_theirs)))
+    out_far = queue.wait(out_far)
+    out_across = other_copy(queue.held(out_far), 1)
+    quarters = [out_near, queue.wait(out_beside), out_far, queue.wait(out_across)]
+    (given,) = queue.passed(project(starts, queue.held(given), out_own, quarters))
     got = swap_pair(given, tp_size)
-    (kept,) = queue.passed(project(starts, queue.held(kept), out_own, out_ours, out_theirs))
+    (kept,) = queue.passed(project(starts, queue.held(kept), out_own, quarters))
     (own_rows,) = queue.passed(kernel_call(
         out_kernel, "out_rows", [((seq_here, width), jnp.float32)],
         starts, queue.held(text_rows), slots_here, merged, kept,

time: 220 us -> 218 us (level)
  starting transfers between devices: 60.3 us -> 55.4 us
  local copies, waits for them, and re-layouts: 18.4 us -> 21.8 us
    ppermute x8 -> x9, waiting for transfers between devices: 9 us -> 2.35 us  [other_copy(): lax.ppermute(values, 'req', [(i, i ^ flip) for i in range(lax.axis_size('...]
    ppermute x19, waiting for transfers between devices: 28.3 us -> 34.1 us  [turned(): return lax.ppermute(values, 'tp', turn_steps(tp_size, turn))]
    unnamed x67 -> x101, local copies, waits for them, and re-layouts: 12.5 us -> 17.6 us
    ppermute x19, starting transfers between devices: 34.9 us -> 30.1 us  [turned(): return lax.ppermute(values, 'tp', turn_steps(tp_size, turn))]
    ppermute x8 -> x9, starting transfers between devices: 5.77 us -> 5.76 us  [other_copy(): lax.ppermute(values, 'req', [(i, i ^ flip) for i in range(lax.axis_size('...]
  transfers between devices with their start and end apart: 42 -> 43, of which waited for: 17 -> 17; matrix products, arithmetic and copies ran while one was open for 3% -> 2% of each run, Pallas kernels for 31% -> 31%
where the time goes in v6:
time: 218 us; the launch traced here: 216 us
  Pallas kernels  69.9 us (32%)
  waiting for transfers between devices  61.6 us (28%)
  starting transfers between devices  55.4 us (25%)
  local copies, waits for them, and re-layouts  21.8 us (10%)
  other arithmetic  6.75 us (3%)
    pallas_call x11, Pallas kernels, kernel_call(): pl.pallas_call(body, grid=grid, in_specs=[SMEM] + [specs.get(place, whole...  50.7 us
    ppermute x19, waiting for transfers between devices, turned(): return lax.ppermute(values, 'tp', turn_steps(tp_size, turn))  34.1 us
    ppermute x19, starting transfers between devices, turned(): return lax.ppermute(values, 'tp', turn_steps(tp_size, turn))  30.1 us
    ppermute x14, waiting for transfers between devices, swap_pair(): return lax.ppermute(values, 'tp', pair_steps(tp_size))  25.1 us
    ppermute x14, starting transfers between devices, swap_pair(): return lax.ppermute(values, 'tp', pair_steps(tp_size))  18.2 us
    unnamed x101, local copies, waits for them, and re-layouts  17.6 us
    pallas_call x4, Pallas kernels, mlp(): pl.pallas_call(mlp_kernel, grid=(units // step,), in_specs=[whole_block((...  15.2 us
    ppermute x9, starting transfers between devices, other_copy(): lax.ppermute(values, 'req', [(i, i ^ flip) for i in range(lax.axis_size('...  5.76 us
  transfers between devices with their start and end apart: 43, of which 17 were waited for; matrix products, arithmetic and copies ran while one was open for 2% of the time, Pallas kernels for 31%

profile of v6, /device:TPU:0, one launch (start us, length us, event | category | flops | bytes accessed | tf_op | source)
XLA Modules:
  0.0 216.0 jit_solution(8220881928094014677)
XLA Ops:
  0.0 2.9 %collective-permute-start.4 = (bf16[192,1664]{1,0:T(8,128)(2,1)}, bf16[192,1664]{1,0:T(8,128)(2,1)S(1)}, u32[]{:S(2)}, u32[]{:S(2)}) collective-permute-start(bf16[192,1664]{1,0:T(8,128)(2,1)} %bitcast.72), channel_id=1, source_target_pairs={{0,1},{1,0},{2,3},{3,2},{4,5},{5,4},{6,7},{7,6},{8,9},{9,8},{10,11... | collective-permute-start | bytes 1916936 | tf_op jit(solution)/shard_map/ppermute | solution.py:40
  3.0 2.0 collective-permute-start.2
  5.1 2.0 collective-permute-start.1
  9.3 1.7 constant_dynamic-slice_fusion
  11.0 11.2 %collective-permute-done.3.other = bf16[64,1664]{1,0:T(8,128)(2,1)S(1)} collective-permute-done((bf16[64,1664]{1,0:T(8,128)(2,1)}, bf16[64,1664]{1,0:T(8,128)(2,1)S(1)}, u32[]{:S(2)}, u32[]{:S(2)}) %collective-permute-start.3) | collective-permute-done | bytes 213024 | tf_op jit(solution)/shard_map/ppermute | solution.py:40
  22.2 3.5 %collective-permute-done.mine = bf16[64,1664]{1,0:T(8,128)(2,1)S(1)} collective-permute-done((bf16[64,1664]{1,0:T(8,128)(2,1)}, bf16[64,1664]{1,0:T(8,128)(2,1)S(1)}, u32[]{:S(2)}, u32[]{:S(2)}) %collective-permute-start) | collective-permute-done | bytes 213024 | tf_op jit(solution)/shard_map/ppermute | solution.py:44
  27.1 1.6 collective-permute-start.5
  29.2 2.0 copy-done.1
  31.2 2.0 copy-done.3
  33.1 3.8 %mlp_rows.4 = (bf16[64,1664]{1,0:T(8,128)(2,1)S(1)}, bf16[64,1664]{1,0:T(8,128)(2,1)S(1)}) custom-call(bf16[64,1664]{1,0:T(8,128)(2,1)S(1)} %bitcast.71, bf16[64,1664]{1,0:T(8,128)(2,1)S(1)} %collective-permute-done.3.other, f32[1664]{0:T(1024)S(1)} %copy-done.24, bf16[1664,1024]{1,0:T(8,128)(2,1)S(1)} %copy-done.1, bf16[1024,1664]{1,0:T(8,128)(2,1)S(1)} %copy-done.3), custom_call_target="tpu_custom_call" | custom-call | flops 1 | bytes 1 | tf_op jit(solution)/shard_map/mlp_rows/pallas_call | solution.py:294
  37.7 3.8 %mlp_rows.5 = (bf16[64,1664]{1,0:T(8,128)(2,1)S(1)}, bf16[64,1664]{1,0:T(8,128)(2,1)S(1)}) custom-call(bf16[64,1664]{1,0:T(8,128)(2,1)S(1)} %collective-permute-done.2.mine, bf16[64,1664]{1,0:T(8,128)(2,1)S(1)} %collective-permute-done.5.other, f32[1664]{0:T(1024)S(1)} %copy-done.24, bf16[1664,1024]{1,0:T(8,128)(2,1)S(1)} %copy-done.2, ...), custom_call_target="tpu_custom_call" | custom-call | flops 1 | bytes 1 | tf_op jit(solution)/shard_map/mlp_rows/pallas_call | solution.py:294
  41.5 2.8 %collective-permute-start.9 = (bf16[80,1664]{1,0:T(8,128)(2,1)S(1)}, bf16[80,1664]{1,0:T(8,128)(2,1)S(1)}, u32[]{:S(2)}, u32[]{:S(2)}) collective-permute-start(bf16[80,1664]{1,0:T(8,128)(2,1)S(1)} %get-tuple-element.96), channel_id=1, source_target_pairs={{0,4},{1,5},{2,6},{3,7},{4,0},{5,1},{6,2},{7,3},{8,12},{9,13},{10,... | collective-permute-start | bytes 798728 | tf_op jit(solution)/shard_map/ppermute | solution.py:44
  46.3 3.8 %mlp_rows.6 = (bf16[64,1664]{1,0:T(8,128)(2,1)S(1)}, bf16[64,1664]{1,0:T(8,128)(2,1)S(1)}) custom-call(bf16[64,1664]{1,0:T(8,128)(2,1)S(1)} %collective-permute-done.1.mine, bf16[64,1664]{1,0:T(8,128)(2,1)S(1)} %collective-permute-done.6.other, f32[1664]{0:T(1024)S(1)} %copy-done.24, bf16[1664,1024]{1,0:T(8,128)(2,1)S(1)} %copy-done.2, ...), custom_call_target="tpu_custom_call" | custom-call | flops 1 | bytes 1 | tf_op jit(solution)/shard_map/mlp_rows/pallas_call | solution.py:294
  50.2 1.6 collective-permute-start.11
  52.5 3.8 %mlp_rows.7 = (bf16[64,1664]{1,0:T(8,128)(2,1)S(1)}, bf16[64,1664]{1,0:T(8,128)(2,1)S(1)}) custom-call(bf16[64,1664]{1,0:T(8,128)(2,1)S(1)} %collective-permute-done.mine, bf16[64,1664]{1,0:T(8,128)(2,1)S(1)} %collective-permute-done.8.other, f32[1664]{0:T(1024)S(1)} %copy-done.24, bf16[1664,1024]{1,0:T(8,128)(2,1)S(1)} %copy-done.2, ...), custom_call_target="tpu_custom_call" | custom-call | flops 1 | bytes 1 | tf_op jit(solution)/shard_map/mlp_rows/pallas_call | solution.py:294
  56.3 1.5 collective-permute-start.12
  57.9 3.1 %collective-permute-done.11 = bf16[64,1664]{1,0:T(8,128)(2,1)S(1)} collective-permute-done((bf16[64,1664]{1,0:T(8,128)(2,1)S(1)}, bf16[64,1664]{1,0:T(8,128)(2,1)S(1)}, u32[]{:S(2)}, u32[]{:S(2)}) %collective-permute-start.11) | collective-permute-done | bytes 213024 | tf_op jit(solution)/shard_map/ppermute | solution.py:40
  61.8 3.2 %collective-permute-start.13 = (bf16[64,1664]{1,0:T(8,128)(2,1)S(1)}, bf16[64,1664]{1,0:T(8,128)(2,1)S(1)}, u32[]{:S(2)}, u32[]{:S(2)}) collective-permute-start(bf16[64,1664]{1,0:T(8,128)(2,1)S(1)} %add_convert_fusion.3), channel_id=1, source_target_pairs={{0,6},{1,7},{2,0},{3,1},{4,2},{5,3},{6,4},{7,5},{8,14},{9,15},{10,... | collective-permute-start | bytes 638984 | tf_op jit(solution)/shard_map/ppermute | solution.py:44
  65.0 4.0 %collective-permute-done.14.refs_4_ = bf16[64,1664]{1,0:T(8,128)(2,1)S(1)} collective-permute-done((bf16[64,1664]{1,0:T(8,128)(2,1)S(1)}, bf16[64,1664]{1,0:T(8,128)(2,1)S(1)}, u32[]{:S(2)}, u32[]{:S(2)}) %collective-permute-start.14) | collective-permute-done | bytes 213024 | tf_op jit(solution)/shard_map/ppermute | solution.py:44
  68.9 1.5 collective-permute-done.13.refs_2_
  70.5 3.3 %collective-permute-start.17 = (bf16[80,1664]{1,0:T(8,128)(2,1)S(1)}, bf16[80,1664]{1,0:T(8,128)(2,1)S(1)}, u32[]{:S(2)}, u32[]{:S(2)}) collective-permute-start(bf16[80,1664]{1,0:T(8,128)(2,1)S(1)} %get-tuple-element.105), channel_id=1, source_target_pairs={{0,4},{1,5},{2,6},{3,7},{4,0},{5,1},{6,2},{7,3},{8,12},{9,13},{10,... | collective-permute-start | bytes 798728 | tf_op jit(solution)/shard_map/ppermute | solution.py:44
  77.2 2.0 masks.1
  80.6 10.0 %collective-permute-done.16.refs_3_ = bf16[64,1664]{1,0:T(8,128)(2,1)S(1)} collective-permute-done((bf16[64,1664]{1,0:T(8,128)(2,1)S(1)}, bf16[64,1664]{1,0:T(8,128)(2,1)S(1)}, u32[]{:S(2)}, u32[]{:S(2)}) %collective-permute-start.16) | collective-permute-done | bytes 213024 | tf_op jit(solution)/shard_map/ppermute | solution.py:44
  91.3 2.7 %spread_rows.1 = (bf16[4,16,832]{2,1,0:T(8,128)(2,1)}, bf16[4,16,832]{2,1,0:T(8,128)(2,1)}) custom-call(s32[16]{0:T(128)} %concatenate.18.starts.place, bf16[64,1664]{1,0:T(8,128)(2,1)} %bitcast.70, bf16[64,1664]{1,0:T(8,128)(2,1)} %copy-done.42, bf16[64,1664]{1,0:T(8,128)(2,1)} %copy-done.22, bf16[64,1664]{1,0:T(8,128)(2,1)} %copy-done.41, ...), custom_call_target="tpu_custom_call" | custom-call | flops 1 | bytes 1 | tf_op jit(solution)/shard_map/spread_rows/pallas_call | solution.py:341
  94.1 1.6 collective-permute-start.21
  98.1 5.7 %text_first.1 = (bf16[768,1664]{1,0:T(8,128)(2,1)}, bf16[4,624,768]{2,1,0:T(8,128)(2,1)}) custom-call(s32[16]{0:T(128)} %concatenate.18.starts.place, f32[1664]{0:T(1024)} %gain.10, bf16[624,1664]{1,0:T(8,128)(2,1)} %bitcast.60, bf16[192,1664]{1,0:T(8,128)(2,1)} %copy-done.36, bf16[192,1664]{1,0:T(8,128)(2,1)} %copy-done.38, bf16[192,1664]{1,0:T(8,128)(2,1)} %bitcast.73, ...), custom_call_target="tpu_custom_call" | custom-call | flops 1 | bytes 1 | tf_op jit(solution)/shard_map/text_first/pallas_call | solution.py:230
  103.8 5.0 %collective-permute-done.20 = bf16[160,1664]{1,0:T(8,128)(2,1)S(1)} collective-permute-done((bf16[160,1664]{1,0:T(8,128)(2,1)S(1)}, bf16[160,1664]{1,0:T(8,128)(2,1)S(1)}, u32[]{:S(2)}, u32[]{:S(2)}) %collective-permute-start.20) | collective-permute-done | bytes 532512 | tf_op jit(solution)/shard_map/ppermute | solution.py:44
  109.2 2.4 %collective-permute-start.23 = (bf16[32,832]{1,0:T(8,128)(2,1)S(1)}, bf16[32,832]{1,0:T(8,128)(2,1)S(1)}, u32[]{:S(2)}, u32[]{:S(2)}) collective-permute-start(bf16[32,832]{1,0:T(8,128)(2,1)S(1)} %pad_maximum_fusion.5), channel_id=1, source_target_pairs={{0,4},{1,5},{2,6},{3,7},{4,0},{5,1},{6,2},{7,3},{8,12},{9,13},{10,... | collective-permute-start | bytes 159752 | tf_op jit(solution)/shard_map/ppermute | solution.py:44
  113.1 2.6 %collective-permute-done.22.refs_1_ = bf16[32,832]{1,0:T(8,128)(2,1)S(1)} collective-permute-done((bf16[32,832]{1,0:T(8,128)(2,1)S(1)}, bf16[32,832]{1,0:T(8,128)(2,1)S(1)}, u32[]{:S(2)}, u32[]{:S(2)}) %collective-permute-start.22) | collective-permute-done | bytes 53280 | tf_op jit(solution)/shard_map/ppermute | solution.py:44
  119.3 2.7 %collective-permute-start.27 = (bf16[160,1664]{1,0:T(8,128)(2,1)S(1)}, bf16[160,1664]{1,0:T(8,128)(2,1)S(1)}, u32[]{:S(2)}, u32[]{:S(2)}) collective-permute-start(bf16[160,1664]{1,0:T(8,128)(2,1)S(1)} %dynamic-slice_bitcast_fusion), channel_id=1, source_target_pairs={{0,6},{1,7},{2,0},{3,1},{4,2},{5,3},{6,4},{7,5},{8,14},{9,15},{10,... | collective-permute-start | bytes 1597448 | tf_op jit(solution)/shard_map/ppermute | solution.py:44
  122.0 1.5 collective-permute-start.28
  126.0 5.7 %text_next.3.before = bf16[4,624,768]{2,1,0:T(8,128)(2,1)} custom-call(s32[16]{0:T(128)} %concatenate.18.starts.place, bf16[768,1664]{1,0:T(8,128)(2,1)} %get-tuple-element.139.rows, bf16[2,1,160,1664]{3,2,1,0:T(8,128)(2,1)} %copy-done.6, bf16[2,1,160,1664]{3,2,1,0:T(8,128)(2,1)} %copy-done.10, ...), custom_call_target="tpu_custom_call", output_to_operand_aliasing={{}: (4, {})} | custom-call | flops 1 | bytes 1 | tf_op jit(solution)/shard_map/text_next/pallas_call | solution.py:230
  132.3 1.9 image_shares.1
  136.8 1.5 collective-permute-start.33
  138.4 2.6 %collective-permute-start.31 = (bf16[64,832]{1,0:T(8,128)(2,1)S(1)}, bf16[64,832]{1,0:T(8,128)(2,1)S(1)}, u32[]{:S(2)}, u32[]{:S(2)}) collective-permute-start(bf16[64,832]{1,0:T(8,128)(2,1)S(1)} %copy-done.47), channel_id=1, source_target_pairs={{0,4},{1,5},{2,6},{3,7},{4,0},{5,1},{6,2},{7,3},{8,12},{9,13},{10,... | collective-permute-start | bytes 319496 | tf_op jit(solution)/shard_map/ppermute | solution.py:44
  143.2 5.7 %text_next.4.before = bf16[4,624,768]{2,1,0:T(8,128)(2,1)} custom-call(s32[16]{0:T(128)} %concatenate.18.starts.place, bf16[768,1664]{1,0:T(8,128)(2,1)} %get-tuple-element.139.rows, bf16[2,1,160,1664]{3,2,1,0:T(8,128)(2,1)} %get-tuple-element.157.ours.refs_2_, bf16[2,1,160,1664]{3,2,1,0:T(8,128)(2,1)} %bitcast.62, ...), custom_call_target="tpu_custom_call", output_to_operand_aliasing={{}: (4, {})} | custom-call | flops 1 | bytes 1 | tf_op jit(solution)/shard_map/text_next/pallas_call | solution.py:230
  153.4 3.4 %collective-permute-start.37 = (bf16[64,1664]{1,0:T(8,128)(2,1)}, bf16[64,1664]{1,0:T(8,128)(2,1)}, u32[]{:S(2)}, u32[]{:S(2)}) collective-permute-start(bf16[64,1664]{1,0:T(8,128)(2,1)} %constant_dynamic-slice_fusion), channel_id=1, source_target_pairs={{0,6},{1,7},{2,0},{3,1},{4,2},{5,3},{6,4},{7,5},{8,14},{9,15},{10,... | collective-permute-start | bytes 638984 | tf_op jit(solution)/shard_map/ppermute | solution.py:44
  159.4 6.0 %text_next.5.refs_0_ = bf16[4,624,768]{2,1,0:T(8,128)(2,1)} custom-call(s32[16]{0:T(128)} %concatenate.18.starts.place, bf16[768,1664]{1,0:T(8,128)(2,1)} %get-tuple-element.139.rows, bf16[2,1,160,1664]{3,2,1,0:T(8,128)(2,1)} %get-tuple-element.155.ours.refs_4_, bf16[2,1,160,1664]{3,2,1,0:T(8,128)(2,1)} %bitcast.64, ...), custom_call_target="tpu_custom_call", output_to_operand_aliasing={{}: (4, {})} | custom-call | flops 1 | bytes 1 | tf_op jit(solution)/shard_map/text_next/pallas_call | solution.py:230
  165.4 2.0 image_rows.1
  167.4 4.6 %collective-permute-done.36 = bf16[64,1664]{1,0:T(8,128)(2,1)} collective-permute-done((bf16[64,1664]{1,0:T(8,128)(2,1)}, bf16[64,1664]{1,0:T(8,128)(2,1)}, u32[]{:S(2)}, u32[]{:S(2)}) %collective-permute-start.36) | collective-permute-done | bytes 213024 | tf_op jit(solution)/shard_map/ppermute | solution.py:44
  173.9 2.1 copy-done
  177.2 11.2 %late_attention.1 = (bf16[192,832]{1,0:T(8,128)(2,1)S(1)}, bf16[192,832]{1,0:T(8,128)(2,1)S(1)}) custom-call(s32[16]{0:T(128)S(1)} %copy-done.26, bf16[64,1664]{1,0:T(8,128)(2,1)S(1)} %copy-done.23, bf16[64,768]{1,0:T(8,128)(2,1)S(1)} %copy-done.27, f32[8,768]{1,0:T(8,128)S(1)} %copy-done.28, f32[3,512,128]{2,1,0:T(8,128)S(1)} %copy-done.18, ...), custom_call_target="tpu_custom_call" | custom-call | flops 1 | bytes 1 | tf_op jit(solution)/shard_map/late_attention/pallas_call | solution.py:230
  192.9 3.9 %project.2 = bf16[192,1664]{1,0:T(8,128)(2,1)} custom-call(s32[16]{0:T(128)} %concatenate.18.starts.place, bf16[192,832]{1,0:T(8,128)(2,1)} %copy-done.21, bf16[208,1664]{1,0:T(8,128)(2,1)} %own.3, bf16[3,64,1664]{2,1,0:T(8,128)(2,1)} %copy-done.30, bf16[3,64,1664]{2,1,0:T(8,128)(2,1)} %copy-done.32, bf16[3,64,1664]{2,1,0:T(8,128)(2,1)} %copy-done.31, ...), custom_call_target="tpu_custom_call" | custom-call | flops 1 | bytes 1 | tf_op jit(solution)/shard_map/project/pallas_call | solution.py:230
  196.8 1.5 collective-permute-start.42
  198.3 3.9 %project.3.kept = bf16[192,1664]{1,0:T(8,128)(2,1)} custom-call(s32[16]{0:T(128)} %concatenate.18.starts.place, bf16[192,832]{1,0:T(8,128)(2,1)} %copy-done.20, bf16[208,1664]{1,0:T(8,128)(2,1)} %own.3, bf16[3,64,1664]{2,1,0:T(8,128)(2,1)} %copy-done.30, bf16[3,64,1664]{2,1,0:T(8,128)(2,1)} %copy-done.32, bf16[3,64,1664]{2,1,0:T(8,128)(2,1)} %copy-done.31, ...), custom_call_target="tpu_custom_call" | custom-call | flops 1 | bytes 1 | tf_op jit(solution)/shard_map/project/pallas_call | solution.py:230
  202.2 2.7 %out_rows.1 = f32[192,1664]{1,0:T(8,128)} custom-call(s32[16]{0:T(128)} %concatenate.18.starts.place, bf16[192,1664]{1,0:T(8,128)(2,1)} %bitcast.74, s32[8,64]{1,0:T(8,128)} %get-tuple-element.104.slots, bf16[64,1664]{1,0:T(8,128)(2,1)} %get-tuple-element.144.merged, bf16[192,1664]{1,0:T(8,128)(2,1)} %project.3.kept), custom_call_target="tpu_custom_call" | custom-call | flops 1 | bytes 1 | tf_op jit(solution)/shard_map/out_rows/pallas_call | solution.py:230
  205.0 8.8 %collective-permute-done.42 = bf16[192,1664]{1,0:T(8,128)(2,1)S(1)} collective-permute-done((bf16[192,1664]{1,0:T(8,128)(2,1)}, bf16[192,1664]{1,0:T(8,128)(2,1)S(1)}, u32[]{:S(2)}, u32[]{:S(2)}) %collective-permute-start.42) | collective-permute-done | bytes 639008 | tf_op jit(solution)/shard_map/ppermute | solution.py:40
  213.7 2.2 %fusion.4 = bf16[1,192,1664]{2,1,0:T(8,128)(2,1)} fusion(f32[192,1664]{1,0:T(8,128)} %out_rows.1, bf16[192,1664]{1,0:T(8,128)(2,1)S(1)} %collective-permute-done.42), kind=kLoop, calls=%fused_computation.9 | loop fusion | flops 958464 | bytes 2555904 | tf_op jit(solution)/shard_map/broadcast_in_dim | solution.py:677
  (179 shorter events, 44.4 us)
Async XLA Ops:
  0.0 25.7 %copy-start.34 = (bf16[1,192,1664]{2,1,0:T(8,128)(2,1)S(1)}, bf16[1,192,1664]{2,1,0:T(8,128)(2,1)}, u32[]{:S(2)}) copy-start(bf16[1,192,1664]{2,1,0:T(8,128)(2,1)} %param.20) | copy-start | bytes 1916932
  0.0 25.7 %collective-permute-start.4 = (bf16[192,1664]{1,0:T(8,128)(2,1)}, bf16[192,1664]{1,0:T(8,128)(2,1)S(1)}, u32[]{:S(2)}, u32[]{:S(2)}) collective-permute-start(bf16[192,1664]{1,0:T(8,128)(2,1)} %bitcast.72), channel_id=1, source_target_pairs={{0,1},{1,0},{2,3},{3,2},{4,5},{5,4},{6,7},{7,6},{8,9},{9,8},{10,11... | collective-permute-start | bytes 1916936 | tf_op jit(solution)/shard_map/ppermute | solution.py:40
  2.9 19.2 %collective-permute-start.3 = (bf16[64,1664]{1,0:T(8,128)(2,1)}, bf16[64,1664]{1,0:T(8,128)(2,1)S(1)}, u32[]{:S(2)}, u32[]{:S(2)}) collective-permute-start(bf16[64,1664]{1,0:T(8,128)(2,1)} %bitcast.66), channel_id=1, source_target_pairs={{0,1},{1,0},{2,3},{3,2},{4,5},{5,4},{6,7},{7,6},{8,9},{9,8},{10,11... | collective-permute-start | bytes 638984 | tf_op jit(solution)/shard_map/ppermute | solution.py:40
  3.0 19.2 %collective-permute-start.2 = (bf16[64,1664]{1,0:T(8,128)(2,1)}, bf16[64,1664]{1,0:T(8,128)(2,1)S(1)}, u32[]{:S(2)}, u32[]{:S(2)}) collective-permute-start(bf16[64,1664]{1,0:T(8,128)(2,1)} %bitcast.67), channel_id=1, source_target_pairs={{0,2},{1,3},{2,4},{3,5},{4,6},{5,7},{6,0},{7,1},{8,10},{9,11},{10,... | collective-permute-start | bytes 638984 | tf_op jit(solution)/shard_map/ppermute | solution.py:44
  5.1 17.1 %collective-permute-start.1 = (bf16[64,1664]{1,0:T(8,128)(2,1)}, bf16[64,1664]{1,0:T(8,128)(2,1)S(1)}, u32[]{:S(2)}, u32[]{:S(2)}) collective-permute-start(bf16[64,1664]{1,0:T(8,128)(2,1)} %bitcast.68), channel_id=1, source_target_pairs={{0,6},{1,7},{2,0},{3,1},{4,2},{5,3},{6,4},{7,5},{8,14},{9,15},{10,... | collective-permute-start | bytes 638984 | tf_op jit(solution)/shard_map/ppermute | solution.py:44
  7.1 18.6 %collective-permute-start = (bf16[64,1664]{1,0:T(8,128)(2,1)}, bf16[64,1664]{1,0:T(8,128)(2,1)S(1)}, u32[]{:S(2)}, u32[]{:S(2)}) collective-permute-start(bf16[64,1664]{1,0:T(8,128)(2,1)} %bitcast.69), channel_id=1, source_target_pairs={{0,4},{1,5},{2,6},{3,7},{4,0},{5,1},{6,2},{7,3},{8,12},{9,13},{10,... | collective-permute-start | bytes 638984 | tf_op jit(solution)/shard_map/ppermute | solution.py:44
  8.1 21.1 %copy-start.17 = (bf16[1,64,1664]{2,1,0:T(8,128)(2,1)S(1)}, bf16[1,64,1664]{2,1,0:T(8,128)(2,1)}, u32[]{:S(2)}) copy-start(bf16[1,64,1664]{2,1,0:T(8,128)(2,1)} %param.13) | copy-start | bytes 638980
  8.1 21.1 %copy-start.24 = (f32[1664]{0:T(1024)S(1)}, f32[1664]{0:T(1024)}, u32[]{:S(2)}) copy-start(f32[1664]{0:T(1024)} %gain.8) | copy-start | bytes 19972
  25.7 15.8 %collective-permute-start.7 = (bf16[192,1664]{1,0:T(8,128)(2,1)S(1)}, bf16[192,1664]{1,0:T(8,128)(2,1)S(1)}, u32[]{:S(2)}, u32[]{:S(2)}) collective-permute-start(bf16[192,1664]{1,0:T(8,128)(2,1)S(1)} %bitcast.75), channel_id=1, source_target_pairs={{0,2},{1,3},{2,4},{3,5},{4,6},{5,7},{8,10},{9,11},{10,12},{11,13},... | collective-permute-start | bytes 1916936 | tf_op jit(solution)/shard_map/ppermute | solution.py:549
  27.1 10.6 %collective-permute-start.5 = (bf16[64,1664]{1,0:T(8,128)(2,1)S(1)}, bf16[64,1664]{1,0:T(8,128)(2,1)S(1)}, u32[]{:S(2)}, u32[]{:S(2)}) collective-permute-start(bf16[64,1664]{1,0:T(8,128)(2,1)S(1)} %collective-permute-done.2.mine), channel_id=1, source_target_pairs={{0,1},{1,0},{2,3},{3,2},{4,5},{5,4},{6,7},{7,6},{8,9},{9,8},{10,11... | collective-permute-start | bytes 638984 | tf_op jit(solution)/shard_map/ppermute | solution.py:40
  28.6 12.9 %collective-permute-start.6 = (bf16[64,1664]{1,0:T(8,128)(2,1)S(1)}, bf16[64,1664]{1,0:T(8,128)(2,1)S(1)}, u32[]{:S(2)}, u32[]{:S(2)}) collective-permute-start(bf16[64,1664]{1,0:T(8,128)(2,1)S(1)} %collective-permute-done.1.mine), channel_id=1, source_target_pairs={{0,1},{1,0},{2,3},{3,2},{4,5},{5,4},{6,7},{7,6},{8,9},{9,8},{10,11... | collective-permute-start | bytes 638984 | tf_op jit(solution)/shard_map/ppermute | solution.py:40
  41.5 16.4 %collective-permute-start.9 = (bf16[80,1664]{1,0:T(8,128)(2,1)S(1)}, bf16[80,1664]{1,0:T(8,128)(2,1)S(1)}, u32[]{:S(2)}, u32[]{:S(2)}) collective-permute-start(bf16[80,1664]{1,0:T(8,128)(2,1)S(1)} %get-tuple-element.96), channel_id=1, source_target_pairs={{0,4},{1,5},{2,6},{3,7},{4,0},{5,1},{6,2},{7,3},{8,12},{9,13},{10,... | collective-permute-start | bytes 798728 | tf_op jit(solution)/shard_map/ppermute | solution.py:44
  44.3 8.2 %collective-permute-start.8 = (bf16[64,1664]{1,0:T(8,128)(2,1)S(1)}, bf16[64,1664]{1,0:T(8,128)(2,1)S(1)}, u32[]{:S(2)}, u32[]{:S(2)}) collective-permute-start(bf16[64,1664]{1,0:T(8,128)(2,1)S(1)} %collective-permute-done.mine), channel_id=1, source_target_pairs={{0,1},{1,0},{2,3},{3,2},{4,5},{5,4},{6,7},{7,6},{8,9},{9,8},{10,11... | collective-permute-start | bytes 638984 | tf_op jit(solution)/shard_map/ppermute | solution.py:40
  45.8 12.1 %collective-permute-start.10 = (bf16[64,1664]{1,0:T(8,128)(2,1)S(1)}, bf16[64,1664]{1,0:T(8,128)(2,1)S(1)}, u32[]{:S(2)}, u32[]{:S(2)}) collective-permute-start(bf16[64,1664]{1,0:T(8,128)(2,1)S(1)} %get-tuple-element.86), channel_id=1, source_target_pairs={{0,1},{1,0},{2,3},{3,2},{4,5},{5,4},{6,7},{7,6},{8,9},{9,8},{10,11... | collective-permute-start | bytes 638984 | tf_op jit(solution)/shard_map/ppermute | solution.py:40
  50.2 10.9 %collective-permute-start.11 = (bf16[64,1664]{1,0:T(8,128)(2,1)S(1)}, bf16[64,1664]{1,0:T(8,128)(2,1)S(1)}, u32[]{:S(2)}, u32[]{:S(2)}) collective-permute-start(bf16[64,1664]{1,0:T(8,128)(2,1)S(1)} %get-tuple-element.91), channel_id=1, source_target_pairs={{0,1},{1,0},{2,3},{3,2},{4,5},{5,4},{6,7},{7,6},{8,9},{9,8},{10,11... | collective-permute-start | bytes 638984 | tf_op jit(solution)/shard_map/ppermute | solution.py:40
  56.3 8.6 %collective-permute-start.12 = (bf16[64,1664]{1,0:T(8,128)(2,1)S(1)}, bf16[64,1664]{1,0:T(8,128)(2,1)S(1)}, u32[]{:S(2)}, u32[]{:S(2)}) collective-permute-start(bf16[64,1664]{1,0:T(8,128)(2,1)S(1)} %get-tuple-element.95), channel_id=1, source_target_pairs={{0,1},{1,0},{2,3},{3,2},{4,5},{5,4},{6,7},{7,6},{8,9},{9,8},{10,11... | collective-permute-start | bytes 638984 | tf_op jit(solution)/shard_map/ppermute | solution.py:40
  61.1 7.9 %collective-permute-start.14 = (bf16[64,1664]{1,0:T(8,128)(2,1)S(1)}, bf16[64,1664]{1,0:T(8,128)(2,1)S(1)}, u32[]{:S(2)}, u32[]{:S(2)}) collective-permute-start(bf16[64,1664]{1,0:T(8,128)(2,1)S(1)} %add_convert_fusion.2), channel_id=1, source_target_pairs={{0,2},{1,3},{2,4},{3,5},{4,6},{5,7},{6,0},{7,1},{8,10},{9,11},{10,... | collective-permute-start | bytes 638984 | tf_op jit(solution)/shard_map/ppermute | solution.py:44
  61.8 8.7 %collective-permute-start.13 = (bf16[64,1664]{1,0:T(8,128)(2,1)S(1)}, bf16[64,1664]{1,0:T(8,128)(2,1)S(1)}, u32[]{:S(2)}, u32[]{:S(2)}) collective-permute-start(bf16[64,1664]{1,0:T(8,128)(2,1)S(1)} %add_convert_fusion.3), channel_id=1, source_target_pairs={{0,6},{1,7},{2,0},{3,1},{4,2},{5,3},{6,4},{7,5},{8,14},{9,15},{10,... | collective-permute-start | bytes 638984 | tf_op jit(solution)/shard_map/ppermute | solution.py:44
  68.9 21.7 %copy-start.40 = (bf16[64,1664]{1,0:T(8,128)(2,1)}, bf16[64,1664]{1,0:T(8,128)(2,1)S(1)}, u32[]{:S(2)}) copy-start(bf16[64,1664]{1,0:T(8,128)(2,1)S(1)} %collective-permute-done.14.refs_4_) | copy-start | bytes 638980
  70.5 20.2 %copy-start.41 = (bf16[64,1664]{1,0:T(8,128)(2,1)}, bf16[64,1664]{1,0:T(8,128)(2,1)S(1)}, u32[]{:S(2)}) copy-start(bf16[64,1664]{1,0:T(8,128)(2,1)S(1)} %collective-permute-done.13.refs_2_) | copy-start | bytes 638980
  70.5 20.1 %collective-permute-start.17 = (bf16[80,1664]{1,0:T(8,128)(2,1)S(1)}, bf16[80,1664]{1,0:T(8,128)(2,1)S(1)}, u32[]{:S(2)}, u32[]{:S(2)}) collective-permute-start(bf16[80,1664]{1,0:T(8,128)(2,1)S(1)} %get-tuple-element.105), channel_id=1, source_target_pairs={{0,4},{1,5},{2,6},{3,7},{4,0},{5,1},{6,2},{7,3},{8,12},{9,13},{10,... | collective-permute-start | bytes 798728 | tf_op jit(solution)/shard_map/ppermute | solution.py:44
  73.8 6.8 %collective-permute-start.15 = (bf16[64,1664]{1,0:T(8,128)(2,1)S(1)}, bf16[64,1664]{1,0:T(8,128)(2,1)S(1)}, u32[]{:S(2)}, u32[]{:S(2)}) collective-permute-start(bf16[64,1664]{1,0:T(8,128)(2,1)S(1)} %get-tuple-element.82), channel_id=1, source_target_pairs={{0,1},{1,0},{2,3},{3,2},{4,5},{5,4},{6,7},{7,6},{8,9},{9,8},{10,11... | collective-permute-start | bytes 638984 | tf_op jit(solution)/shard_map/ppermute | solution.py:40
  75.3 15.3 %collective-permute-start.16 = (bf16[64,1664]{1,0:T(8,128)(2,1)S(1)}, bf16[64,1664]{1,0:T(8,128)(2,1)S(1)}, u32[]{:S(2)}, u32[]{:S(2)}) collective-permute-start(bf16[64,1664]{1,0:T(8,128)(2,1)S(1)} %add_convert_fusion.1), channel_id=1, source_target_pairs={{0,4},{1,5},{2,6},{3,7},{4,0},{5,1},{6,2},{7,3},{8,12},{9,13},{10,... | collective-permute-start | bytes 638984 | tf_op jit(solution)/shard_map/ppermute | solution.py:44
  76.7 20.5 %collective-permute-start.18 = (bf16[192,1664]{1,0:T(8,128)(2,1)S(1)}, bf16[192,1664]{1,0:T(8,128)(2,1)S(1)}, u32[]{:S(2)}, u32[]{:S(2)}) collective-permute-start(bf16[192,1664]{1,0:T(8,128)(2,1)S(1)} %copy-done.37), channel_id=1, source_target_pairs={{0,1},{1,0},{2,3},{3,2},{4,5},{5,4},{6,7},{7,6},{8,9},{9,8},{10,11... | collective-permute-start | bytes 1916936 | tf_op jit(solution)/shard_map/ppermute | solution.py:40
  94.0 14.8 %collective-permute-start.20 = (bf16[160,1664]{1,0:T(8,128)(2,1)S(1)}, bf16[160,1664]{1,0:T(8,128)(2,1)S(1)}, u32[]{:S(2)}, u32[]{:S(2)}) collective-permute-start(bf16[160,1664]{1,0:T(8,128)(2,1)S(1)} %dynamic-slice_bitcast_fusion), channel_id=1, source_target_pairs={{0,2},{1,3},{2,4},{3,5},{4,6},{5,7},{6,0},{7,1},{8,10},{9,11},{10,... | collective-permute-start | bytes 1597448 | tf_op jit(solution)/shard_map/ppermute | solution.py:44
  94.1 14.7 %collective-permute-start.21 = (bf16[160,1664]{1,0:T(8,128)(2,1)S(1)}, bf16[160,1664]{1,0:T(8,128)(2,1)S(1)}, u32[]{:S(2)}, u32[]{:S(2)}) collective-permute-start(bf16[160,1664]{1,0:T(8,128)(2,1)S(1)} %constant_dynamic-update-slice_fusion), channel_id=1, source_target_pairs={{0,16},{8,24},{16,0},{24,8},{1,17},{9,25},{17,1},{25,9},{2,18},{10... | collective-permute-start | bytes 1597448 | tf_op jit(solution)/shard_map/ppermute | solution.py:438
  95.7 8.1 %collective-permute-start.19 = (bf16[4,16,832]{2,1,0:T(8,128)(2,1)S(1)}, bf16[4,16,832]{2,1,0:T(8,128)(2,1)S(1)}, u32[]{:S(2)}, u32[]{:S(2)}) collective-permute-start(bf16[4,16,832]{2,1,0:T(8,128)(2,1)S(1)} %copy-done.49), channel_id=1, source_target_pairs={{0,1},{1,0},{2,3},{3,2},{4,5},{5,4},{6,7},{7,6},{8,9},{9,8},{10,11... | collective-permute-start | bytes 319496 | tf_op jit(solution)/shard_map/ppermute | solution.py:40
  109.0 16.1 %collective-permute-start.25 = (bf16[2,1,160,1664]{3,2,1,0:T(8,128)(2,1)S(1)}, bf16[2,1,160,1664]{3,2,1,0:T(8,128)(2,1)S(1)}, u32[]{:S(2)}, u32[]{:S(2)}) collective-permute-start(bf16[2,1,160,1664]{3,2,1,0:T(8,128)(2,1)S(1)} %maximum_bitcast_fusion.ours.refs_6_), channel_id=1, source_target_pairs={{0,8},{8,0},{16,24},{24,16},{1,9},{9,1},{17,25},{25,17},{2,10},{10... | collective-permute-start | bytes 3194888 | tf_op jit(solution)/shard_map/ppermute | solution.py:438
  109.1 6.7 %collective-permute-start.22 = (bf16[32,832]{1,0:T(8,128)(2,1)S(1)}, bf16[32,832]{1,0:T(8,128)(2,1)S(1)}, u32[]{:S(2)}, u32[]{:S(2)}) collective-permute-start(bf16[32,832]{1,0:T(8,128)(2,1)S(1)} %pad_maximum_fusion.4), channel_id=1, source_target_pairs={{0,2},{1,3},{2,4},{3,5},{4,6},{5,7},{6,0},{7,1},{8,10},{9,11},{10,... | collective-permute-start | bytes 159752 | tf_op jit(solution)/shard_map/ppermute | solution.py:44
  109.2 8.1 %collective-permute-start.23 = (bf16[32,832]{1,0:T(8,128)(2,1)S(1)}, bf16[32,832]{1,0:T(8,128)(2,1)S(1)}, u32[]{:S(2)}, u32[]{:S(2)}) collective-permute-start(bf16[32,832]{1,0:T(8,128)(2,1)S(1)} %pad_maximum_fusion.5), channel_id=1, source_target_pairs={{0,4},{1,5},{2,6},{3,7},{4,0},{5,1},{6,2},{7,3},{8,12},{9,13},{10,... | collective-permute-start | bytes 159752 | tf_op jit(solution)/shard_map/ppermute | solution.py:44
  111.6 5.6 %collective-permute-start.24 = (bf16[32,832]{1,0:T(8,128)(2,1)S(1)}, bf16[32,832]{1,0:T(8,128)(2,1)S(1)}, u32[]{:S(2)}, u32[]{:S(2)}) collective-permute-start(bf16[32,832]{1,0:T(8,128)(2,1)S(1)} %pad_maximum_fusion.6), channel_id=1, source_target_pairs={{0,6},{1,7},{2,0},{3,1},{4,2},{5,3},{6,4},{7,5},{8,14},{9,15},{10,... | collective-permute-start | bytes 159752 | tf_op jit(solution)/shard_map/ppermute | solution.py:44
  119.3 14.9 %collective-permute-start.27 = (bf16[160,1664]{1,0:T(8,128)(2,1)S(1)}, bf16[160,1664]{1,0:T(8,128)(2,1)S(1)}, u32[]{:S(2)}, u32[]{:S(2)}) collective-permute-start(bf16[160,1664]{1,0:T(8,128)(2,1)S(1)} %dynamic-slice_bitcast_fusion), channel_id=1, source_target_pairs={{0,6},{1,7},{2,0},{3,1},{4,2},{5,3},{6,4},{7,5},{8,14},{9,15},{10,... | collective-permute-start | bytes 1597448 | tf_op jit(solution)/shard_map/ppermute | solution.py:44
  122.0 13.7 %collective-permute-start.28 = (bf16[160,1664]{1,0:T(8,128)(2,1)S(1)}, bf16[160,1664]{1,0:T(8,128)(2,1)S(1)}, u32[]{:S(2)}, u32[]{:S(2)}) collective-permute-start(bf16[160,1664]{1,0:T(8,128)(2,1)S(1)} %collective-permute-done.20), channel_id=1, source_target_pairs={{0,16},{8,24},{16,0},{24,8},{1,17},{9,25},{17,1},{25,9},{2,18},{10... | collective-permute-start | bytes 1597448 | tf_op jit(solution)/shard_map/ppermute | solution.py:438
  123.5 8.1 %collective-permute-start.26 = (bf16[128,832]{1,0:T(8,128)(2,1)S(1)}, bf16[128,832]{1,0:T(8,128)(2,1)S(1)}, u32[]{:S(2)}, u32[]{:S(2)}) collective-permute-start(bf16[128,832]{1,0:T(8,128)(2,1)S(1)} %get-tuple-element.125), channel_id=1, source_target_pairs={{0,1},{1,0},{2,3},{3,2},{4,5},{5,4},{6,7},{7,6},{8,9},{9,8},{10,11... | collective-permute-start | bytes 638984 | tf_op jit(solution)/shard_map/ppermute | solution.py:40
  136.8 5.4 %collective-permute-start.29 = (bf16[2,1,160,1664]{3,2,0,1:T(8,128)(2,1)S(1)}, bf16[2,1,160,1664]{3,2,0,1:T(8,128)(2,1)S(1)}, u32[]{:S(2)}, u32[]{:S(2)}) collective-permute-start(bf16[2,1,160,1664]{3,2,0,1:T(8,128)(2,1)S(1)} %get-tuple-element.158), channel_id=1, source_target_pairs={{0,8},{8,0},{16,24},{24,16},{1,9},{9,1},{17,25},{25,17},{2,10},{10... | collective-permute-start | bytes 3194888 | tf_op jit(solution)/shard_map/ppermute | solution.py:438
  136.8 14.5 %collective-permute-start.33 = (bf16[160,1664]{1,0:T(8,128)(2,1)S(1)}, bf16[160,1664]{1,0:T(8,128)(2,1)S(1)}, u32[]{:S(2)}, u32[]{:S(2)}) collective-permute-start(bf16[160,1664]{1,0:T(8,128)(2,1)S(1)} %collective-permute-done.27), channel_id=1, source_target_pairs={{0,16},{8,24},{16,0},{24,8},{1,17},{9,25},{17,1},{25,9},{2,18},{10... | collective-permute-start | bytes 1597448 | tf_op jit(solution)/shard_map/ppermute | solution.py:438
  138.4 10.5 %collective-permute-start.30 = (bf16[64,832]{1,0:T(8,128)(2,1)S(1)}, bf16[64,832]{1,0:T(8,128)(2,1)S(1)}, u32[]{:S(2)}, u32[]{:S(2)}) collective-permute-start(bf16[64,832]{1,0:T(8,128)(2,1)S(1)} %copy-done.48), channel_id=1, source_target_pairs={{0,2},{1,3},{2,4},{3,5},{4,6},{5,7},{6,0},{7,1},{8,10},{9,11},{10,... | collective-permute-start | bytes 319496 | tf_op jit(solution)/shard_map/ppermute | solution.py:44
  138.4 11.9 %collective-permute-start.31 = (bf16[64,832]{1,0:T(8,128)(2,1)S(1)}, bf16[64,832]{1,0:T(8,128)(2,1)S(1)}, u32[]{:S(2)}, u32[]{:S(2)}) collective-permute-start(bf16[64,832]{1,0:T(8,128)(2,1)S(1)} %copy-done.47), channel_id=1, source_target_pairs={{0,4},{1,5},{2,6},{3,7},{4,0},{5,1},{6,2},{7,3},{8,12},{9,13},{10,... | collective-permute-start | bytes 319496 | tf_op jit(solution)/shard_map/ppermute | solution.py:44
  141.0 9.2 %collective-permute-start.32 = (bf16[64,832]{1,0:T(8,128)(2,1)S(1)}, bf16[64,832]{1,0:T(8,128)(2,1)S(1)}, u32[]{:S(2)}, u32[]{:S(2)}) collective-permute-start(bf16[64,832]{1,0:T(8,128)(2,1)S(1)} %copy-done.46), channel_id=1, source_target_pairs={{0,6},{1,7},{2,0},{3,1},{4,2},{5,3},{6,4},{7,5},{8,14},{9,15},{10,... | collective-permute-start | bytes 319496 | tf_op jit(solution)/shard_map/ppermute | solution.py:44
  152.5 5.8 %collective-permute-start.34 = (bf16[2,1,160,1664]{3,2,0,1:T(8,128)(2,1)S(1)}, bf16[2,1,160,1664]{3,2,0,1:T(8,128)(2,1)S(1)}, u32[]{:S(2)}, u32[]{:S(2)}) collective-permute-start(bf16[2,1,160,1664]{3,2,0,1:T(8,128)(2,1)S(1)} %get-tuple-element.156), channel_id=1, source_target_pairs={{0,8},{8,0},{16,24},{24,16},{1,9},{9,1},{17,25},{25,17},{2,10},{10... | collective-permute-start | bytes 3194888 | tf_op jit(solution)/shard_map/ppermute | solution.py:438
  152.5 14.9 %collective-permute-start.38 = (bf16[64,1664]{1,0:T(8,128)(2,1)}, bf16[64,1664]{1,0:T(8,128)(2,1)}, u32[]{:S(2)}, u32[]{:S(2)}) collective-permute-start(bf16[64,1664]{1,0:T(8,128)(2,1)} %constant_dynamic-slice_fusion), channel_id=1, source_target_pairs={{0,4},{1,5},{2,6},{3,7},{4,0},{5,1},{6,2},{7,3},{8,12},{9,13},{10,... | collective-permute-start | bytes 638984 | tf_op jit(solution)/shard_map/ppermute | solution.py:44
  153.4 14.0 %collective-permute-start.37 = (bf16[64,1664]{1,0:T(8,128)(2,1)}, bf16[64,1664]{1,0:T(8,128)(2,1)}, u32[]{:S(2)}, u32[]{:S(2)}) collective-permute-start(bf16[64,1664]{1,0:T(8,128)(2,1)} %constant_dynamic-slice_fusion), channel_id=1, source_target_pairs={{0,6},{1,7},{2,0},{3,1},{4,2},{5,3},{6,4},{7,5},{8,14},{9,15},{10,... | collective-permute-start | bytes 638984 | tf_op jit(solution)/shard_map/ppermute | solution.py:44
  156.8 15.2 %collective-permute-start.36 = (bf16[64,1664]{1,0:T(8,128)(2,1)}, bf16[64,1664]{1,0:T(8,128)(2,1)}, u32[]{:S(2)}, u32[]{:S(2)}) collective-permute-start(bf16[64,1664]{1,0:T(8,128)(2,1)} %constant_dynamic-slice_fusion), channel_id=1, source_target_pairs={{0,2},{1,3},{2,4},{3,5},{4,6},{5,7},{6,0},{7,1},{8,10},{9,11},{10,... | collective-permute-start | bytes 638984 | tf_op jit(solution)/shard_map/ppermute | solution.py:44
  156.8 8.6 %collective-permute-start.35 = (bf16[64,832]{1,0:T(8,128)(2,1)}, bf16[64,832]{1,0:T(8,128)(2,1)}, u32[]{:S(2)}, u32[]{:S(2)}) collective-permute-start(bf16[64,832]{1,0:T(8,128)(2,1)} %add_convert_fusion.4.ours), channel_id=1, source_target_pairs={{0,1},{1,0},{2,3},{3,2},{4,5},{5,4},{6,7},{7,6},{8,9},{9,8},{10,11... | collective-permute-start | bytes 319496 | tf_op jit(solution)/shard_map/ppermute | solution.py:40
  173.2 16.6 %collective-permute-start.39 = (bf16[3,64,1664]{2,1,0:T(8,128)(2,1)S(1)}, bf16[3,64,1664]{2,1,0:T(8,128)(2,1)S(1)}, u32[]{:S(2)}, u32[]{:S(2)}) collective-permute-start(bf16[3,64,1664]{2,1,0:T(8,128)(2,1)S(1)} %pad_maximum_fusion.2.refs_0_), channel_id=1, source_target_pairs={{0,16},{8,24},{16,0},{24,8},{1,17},{9,25},{17,1},{25,9},{2,18},{10... | collective-permute-start | bytes 1916936 | tf_op jit(solution)/shard_map/ppermute | solution.py:438
  173.8 16.6 %collective-permute-start.40 = (bf16[3,64,1664]{2,1,0:T(8,128)(2,1)S(1)}, bf16[3,64,1664]{2,1,0:T(8,128)(2,1)S(1)}, u32[]{:S(2)}, u32[]{:S(2)}) collective-permute-start(bf16[3,64,1664]{2,1,0:T(8,128)(2,1)S(1)} %pad_maximum_fusion.2.refs_0_), channel_id=1, source_target_pairs={{0,8},{8,0},{16,24},{24,16},{1,9},{9,1},{17,25},{25,17},{2,10},{10... | collective-permute-start | bytes 1916936 | tf_op jit(solution)/shard_map/ppermute | solution.py:438
  189.9 2.2 %collective-permute-start.41 = (bf16[3,64,1664]{2,1,0:T(8,128)(2,1)S(1)}, bf16[3,64,1664]{2,1,0:T(8,128)(2,1)S(1)}, u32[]{:S(2)}, u32[]{:S(2)}) collective-permute-start(bf16[3,64,1664]{2,1,0:T(8,128)(2,1)S(1)} %collective-permute-done.39.refs_2_), channel_id=1, source_target_pairs={{0,8},{8,0},{16,24},{24,16},{1,9},{9,1},{17,25},{25,17},{2,10},{10... | collective-permute-start | bytes 1916936 | tf_op jit(solution)/shard_map/ppermute | solution.py:438
  196.8 16.9 %collective-permute-start.42 = (bf16[192,1664]{1,0:T(8,128)(2,1)}, bf16[192,1664]{1,0:T(8,128)(2,1)S(1)}, u32[]{:S(2)}, u32[]{:S(2)}) collective-permute-start(bf16[192,1664]{1,0:T(8,128)(2,1)} %project.2), channel_id=1, source_target_pairs={{0,1},{1,0},{2,3},{3,2},{4,5},{5,4},{6,7},{7,6},{8,9},{9,8},{10,11... | collective-permute-start | bytes 1916936 | tf_op jit(solution)/shard_map/ppermute | solution.py:40
  (45 other events, 286.5 us)

commit v7 on v6

--- a/solution.py
+++ b/solution.py
@@ -661,7 +661,7 @@
             pltpu.VMEM((lines * depth, blk), jnp.float32),
             pltpu.SemaphoreType.DMA((3 * lines,)),
         ],
-        room=32,
+        room=44,
     ))
     out_far = queue.wait(out_far)
     out_across = other_copy(queue.held(out_far), 1)

time: 218 us -> 216 us (level)
    ppermute x9, waiting for transfers between devices: 2.35 us -> 4.63 us  [other_copy(): lax.ppermute(values, 'req', [(i, i ^ flip) for i in range(lax.axis_size('...]
    unnamed x101 -> x99, local copies, waits for them, and re-layouts: 17.6 us -> 15.9 us
  transfers between devices with their start and end apart: 43 -> 43, of which waited for: 17 -> 18; matrix products, arithmetic and copies ran while one was open for 2% -> 2% of each run, Pallas kernels for 31% -> 30%
where the time goes in v7:
time: 216 us; the launch traced here: 215 us
  Pallas kernels  68.9 us (32%)
  waiting for transfers between devices  63.7 us (29%)
  starting transfers between devices  54.9 us (25%)
  local copies, waits for them, and re-layouts  20.2 us (9%)
  other arithmetic  6.76 us (3%)
    pallas_call x11, Pallas kernels, kernel_call(): pl.pallas_call(body, grid=grid, in_specs=[SMEM] + [specs.get(place, whole...  49.8 us
    ppermute x19, waiting for transfers between devices, turned(): return lax.ppermute(values, 'tp', turn_steps(tp_size, turn))  34.1 us
    ppermute x19, starting transfers between devices, turned(): return lax.ppermute(values, 'tp', turn_steps(tp_size, turn))  30.1 us
    ppermute x14, waiting for transfers between devices, swap_pair(): return lax.ppermute(values, 'tp', pair_steps(tp_size))  24.9 us
    ppermute x14, starting transfers between devices, swap_pair(): return lax.ppermute(values, 'tp', pair_steps(tp_size))  18.2 us
    unnamed x99, local copies, waits for them, and re-layouts  15.9 us
    pallas_call x4, Pallas kernels, mlp(): pl.pallas_call(mlp_kernel, grid=(units // step,), in_specs=[whole_block((...  15.2 us
    ppermute x9, starting transfers between devices, other_copy(): lax.ppermute(values, 'req', [(i, i ^ flip) for i in range(lax.axis_size('...  5.27 us
  transfers between devices with their start and end apart: 43, of which 18 were waited for; matrix products, arithmetic and copies ran while one was open for 2% of the time, Pallas kernels for 30%

profile of v7, /device:TPU:0, one launch (start us, length us, event | category | flops | bytes accessed | tf_op | source)
XLA Modules:
  0.0 215.0 jit_solution(6617507666176539578)
XLA Ops:
  0.0 2.9 %collective-permute-start.4 = (bf16[192,1664]{1,0:T(8,128)(2,1)}, bf16[192,1664]{1,0:T(8,128)(2,1)S(1)}, u32[]{:S(2)}, u32[]{:S(2)}) collective-permute-start(bf16[192,1664]{1,0:T(8,128)(2,1)} %bitcast.72), channel_id=1, source_target_pairs={{0,1},{1,0},{2,3},{3,2},{4,5},{5,4},{6,7},{7,6},{8,9},{9,8},{10,11... | collective-permute-start | bytes 1916936 | tf_op jit(solution)/shard_map/ppermute | solution.py:40
  3.0 2.0 collective-permute-start.2
  5.1 2.0 collective-permute-start.1
  9.3 1.7 constant_dynamic-slice_fusion
  11.0 11.2 %collective-permute-done.3.other = bf16[64,1664]{1,0:T(8,128)(2,1)S(1)} collective-permute-done((bf16[64,1664]{1,0:T(8,128)(2,1)}, bf16[64,1664]{1,0:T(8,128)(2,1)S(1)}, u32[]{:S(2)}, u32[]{:S(2)}) %collective-permute-start.3) | collective-permute-done | bytes 213024 | tf_op jit(solution)/shard_map/ppermute | solution.py:40
  22.2 3.5 %collective-permute-done.mine = bf16[64,1664]{1,0:T(8,128)(2,1)S(1)} collective-permute-done((bf16[64,1664]{1,0:T(8,128)(2,1)}, bf16[64,1664]{1,0:T(8,128)(2,1)S(1)}, u32[]{:S(2)}, u32[]{:S(2)}) %collective-permute-start) | collective-permute-done | bytes 213024 | tf_op jit(solution)/shard_map/ppermute | solution.py:44
  27.1 1.6 collective-permute-start.5
  29.2 2.0 copy-done
  31.2 2.0 copy-done.2
  33.1 3.8 %mlp_rows.4 = (bf16[64,1664]{1,0:T(8,128)(2,1)S(1)}, bf16[64,1664]{1,0:T(8,128)(2,1)S(1)}) custom-call(bf16[64,1664]{1,0:T(8,128)(2,1)S(1)} %bitcast.71, bf16[64,1664]{1,0:T(8,128)(2,1)S(1)} %collective-permute-done.3.other, f32[1664]{0:T(1024)S(1)} %copy-done.23, bf16[1664,1024]{1,0:T(8,128)(2,1)S(1)} %copy-done, bf16[1024,1664]{1,0:T(8,128)(2,1)S(1)} %copy-done.2), custom_call_target="tpu_custom_call" | custom-call | flops 1 | bytes 1 | tf_op jit(solution)/shard_map/mlp_rows/pallas_call | solution.py:294
  37.7 3.8 %mlp_rows.5 = (bf16[64,1664]{1,0:T(8,128)(2,1)S(1)}, bf16[64,1664]{1,0:T(8,128)(2,1)S(1)}) custom-call(bf16[64,1664]{1,0:T(8,128)(2,1)S(1)} %collective-permute-done.2.mine, bf16[64,1664]{1,0:T(8,128)(2,1)S(1)} %collective-permute-done.5.other, f32[1664]{0:T(1024)S(1)} %copy-done.23, bf16[1664,1024]{1,0:T(8,128)(2,1)S(1)} %copy-done.1, ...), custom_call_target="tpu_custom_call" | custom-call | flops 1 | bytes 1 | tf_op jit(solution)/shard_map/mlp_rows/pallas_call | solution.py:294
  41.5 2.8 %collective-permute-start.9 = (bf16[80,1664]{1,0:T(8,128)(2,1)S(1)}, bf16[80,1664]{1,0:T(8,128)(2,1)S(1)}, u32[]{:S(2)}, u32[]{:S(2)}) collective-permute-start(bf16[80,1664]{1,0:T(8,128)(2,1)S(1)} %get-tuple-element.96), channel_id=1, source_target_pairs={{0,4},{1,5},{2,6},{3,7},{4,0},{5,1},{6,2},{7,3},{8,12},{9,13},{10,... | collective-permute-start | bytes 798728 | tf_op jit(solution)/shard_map/ppermute | solution.py:44
  46.3 3.8 %mlp_rows.6 = (bf16[64,1664]{1,0:T(8,128)(2,1)S(1)}, bf16[64,1664]{1,0:T(8,128)(2,1)S(1)}) custom-call(bf16[64,1664]{1,0:T(8,128)(2,1)S(1)} %collective-permute-done.1.mine, bf16[64,1664]{1,0:T(8,128)(2,1)S(1)} %collective-permute-done.6.other, f32[1664]{0:T(1024)S(1)} %copy-done.23, bf16[1664,1024]{1,0:T(8,128)(2,1)S(1)} %copy-done.1, ...), custom_call_target="tpu_custom_call" | custom-call | flops 1 | bytes 1 | tf_op jit(solution)/shard_map/mlp_rows/pallas_call | solution.py:294
  50.1 1.6 collective-permute-start.11
  52.5 3.8 %mlp_rows.7 = (bf16[64,1664]{1,0:T(8,128)(2,1)S(1)}, bf16[64,1664]{1,0:T(8,128)(2,1)S(1)}) custom-call(bf16[64,1664]{1,0:T(8,128)(2,1)S(1)} %collective-permute-done.mine, bf16[64,1664]{1,0:T(8,128)(2,1)S(1)} %collective-permute-done.8.other, f32[1664]{0:T(1024)S(1)} %copy-done.23, bf16[1664,1024]{1,0:T(8,128)(2,1)S(1)} %copy-done.1, ...), custom_call_target="tpu_custom_call" | custom-call | flops 1 | bytes 1 | tf_op jit(solution)/shard_map/mlp_rows/pallas_call | solution.py:294
  56.3 1.6 collective-permute-start.12
  57.9 3.1 %collective-permute-done.11 = bf16[64,1664]{1,0:T(8,128)(2,1)S(1)} collective-permute-done((bf16[64,1664]{1,0:T(8,128)(2,1)S(1)}, bf16[64,1664]{1,0:T(8,128)(2,1)S(1)}, u32[]{:S(2)}, u32[]{:S(2)}) %collective-permute-start.11) | collective-permute-done | bytes 213024 | tf_op jit(solution)/shard_map/ppermute | solution.py:40
  61.8 3.2 %collective-permute-start.13 = (bf16[64,1664]{1,0:T(8,128)(2,1)S(1)}, bf16[64,1664]{1,0:T(8,128)(2,1)S(1)}, u32[]{:S(2)}, u32[]{:S(2)}) collective-permute-start(bf16[64,1664]{1,0:T(8,128)(2,1)S(1)} %add_convert_fusion.3), channel_id=1, source_target_pairs={{0,6},{1,7},{2,0},{3,1},{4,2},{5,3},{6,4},{7,5},{8,14},{9,15},{10,... | collective-permute-start | bytes 638984 | tf_op jit(solution)/shard_map/ppermute | solution.py:44
  65.0 4.0 %collective-permute-done.14.refs_4_ = bf16[64,1664]{1,0:T(8,128)(2,1)S(1)} collective-permute-done((bf16[64,1664]{1,0:T(8,128)(2,1)S(1)}, bf16[64,1664]{1,0:T(8,128)(2,1)S(1)}, u32[]{:S(2)}, u32[]{:S(2)}) %collective-permute-start.14) | collective-permute-done | bytes 213024 | tf_op jit(solution)/shard_map/ppermute | solution.py:44
  68.9 1.5 collective-permute-done.13.refs_2_
  70.5 3.3 %collective-permute-start.17 = (bf16[80,1664]{1,0:T(8,128)(2,1)S(1)}, bf16[80,1664]{1,0:T(8,128)(2,1)S(1)}, u32[]{:S(2)}, u32[]{:S(2)}) collective-permute-start(bf16[80,1664]{1,0:T(8,128)(2,1)S(1)} %get-tuple-element.105), channel_id=1, source_target_pairs={{0,4},{1,5},{2,6},{3,7},{4,0},{5,1},{6,2},{7,3},{8,12},{9,13},{10,... | collective-permute-start | bytes 798728 | tf_op jit(solution)/shard_map/ppermute | solution.py:44
  77.3 2.0 masks.1
  80.6 10.0 %collective-permute-done.16.refs_3_ = bf16[64,1664]{1,0:T(8,128)(2,1)S(1)} collective-permute-done((bf16[64,1664]{1,0:T(8,128)(2,1)S(1)}, bf16[64,1664]{1,0:T(8,128)(2,1)S(1)}, u32[]{:S(2)}, u32[]{:S(2)}) %collective-permute-start.16) | collective-permute-done | bytes 213024 | tf_op jit(solution)/shard_map/ppermute | solution.py:44
  91.3 2.7 %spread_rows.1 = (bf16[4,16,832]{2,1,0:T(8,128)(2,1)}, bf16[4,16,832]{2,1,0:T(8,128)(2,1)}) custom-call(s32[16]{0:T(128)} %concatenate.18.starts.place, bf16[64,1664]{1,0:T(8,128)(2,1)} %bitcast.70, bf16[64,1664]{1,0:T(8,128)(2,1)} %copy-done.41, bf16[64,1664]{1,0:T(8,128)(2,1)} %copy-done.21, bf16[64,1664]{1,0:T(8,128)(2,1)} %copy-done.40, ...), custom_call_target="tpu_custom_call" | custom-call | flops 1 | bytes 1 | tf_op jit(solution)/shard_map/spread_rows/pallas_call | solution.py:341
  94.1 1.6 collective-permute-start.21
  98.1 5.7 %text_first.1 = (bf16[768,1664]{1,0:T(8,128)(2,1)}, bf16[4,624,768]{2,1,0:T(8,128)(2,1)}) custom-call(s32[16]{0:T(128)} %concatenate.18.starts.place, f32[1664]{0:T(1024)} %gain.10, bf16[624,1664]{1,0:T(8,128)(2,1)} %bitcast.60, bf16[192,1664]{1,0:T(8,128)(2,1)} %copy-done.35, bf16[192,1664]{1,0:T(8,128)(2,1)} %copy-done.37, bf16[192,1664]{1,0:T(8,128)(2,1)} %bitcast.73, ...), custom_call_target="tpu_custom_call" | custom-call | flops 1 | bytes 1 | tf_op jit(solution)/shard_map/text_first/pallas_call | solution.py:230
  103.8 5.0 %collective-permute-done.20 = bf16[160,1664]{1,0:T(8,128)(2,1)S(1)} collective-permute-done((bf16[160,1664]{1,0:T(8,128)(2,1)S(1)}, bf16[160,1664]{1,0:T(8,128)(2,1)S(1)}, u32[]{:S(2)}, u32[]{:S(2)}) %collective-permute-start.20) | collective-permute-done | bytes 532512 | tf_op jit(solution)/shard_map/ppermute | solution.py:44
  109.2 2.4 %collective-permute-start.23 = (bf16[32,832]{1,0:T(8,128)(2,1)S(1)}, bf16[32,832]{1,0:T(8,128)(2,1)S(1)}, u32[]{:S(2)}, u32[]{:S(2)}) collective-permute-start(bf16[32,832]{1,0:T(8,128)(2,1)S(1)} %pad_maximum_fusion.5), channel_id=1, source_target_pairs={{0,4},{1,5},{2,6},{3,7},{4,0},{5,1},{6,2},{7,3},{8,12},{9,13},{10,... | collective-permute-start | bytes 159752 | tf_op jit(solution)/shard_map/ppermute | solution.py:44
  111.6 1.5 collective-permute-start.24
  113.1 2.6 %collective-permute-done.22.refs_1_ = bf16[32,832]{1,0:T(8,128)(2,1)S(1)} collective-permute-done((bf16[32,832]{1,0:T(8,128)(2,1)S(1)}, bf16[32,832]{1,0:T(8,128)(2,1)S(1)}, u32[]{:S(2)}, u32[]{:S(2)}) %collective-permute-start.22) | collective-permute-done | bytes 53280 | tf_op jit(solution)/shard_map/ppermute | solution.py:44
  119.3 2.7 %collective-permute-start.27 = (bf16[160,1664]{1,0:T(8,128)(2,1)S(1)}, bf16[160,1664]{1,0:T(8,128)(2,1)S(1)}, u32[]{:S(2)}, u32[]{:S(2)}) collective-permute-start(bf16[160,1664]{1,0:T(8,128)(2,1)S(1)} %dynamic-slice_bitcast_fusion), channel_id=1, source_target_pairs={{0,6},{1,7},{2,0},{3,1},{4,2},{5,3},{6,4},{7,5},{8,14},{9,15},{10,... | collective-permute-start | bytes 1597448 | tf_op jit(solution)/shard_map/ppermute | solution.py:44
  122.0 1.5 collective-permute-start.28
  126.0 5.6 %text_next.3.before = bf16[4,624,768]{2,1,0:T(8,128)(2,1)} custom-call(s32[16]{0:T(128)} %concatenate.18.starts.place, bf16[768,1664]{1,0:T(8,128)(2,1)} %get-tuple-element.139.rows, bf16[2,1,160,1664]{3,2,1,0:T(8,128)(2,1)} %copy-done.5, bf16[2,1,160,1664]{3,2,1,0:T(8,128)(2,1)} %copy-done.9, ...), custom_call_target="tpu_custom_call", output_to_operand_aliasing={{}: (4, {})} | custom-call | flops 1 | bytes 1 | tf_op jit(solution)/shard_map/text_next/pallas_call | solution.py:230
  132.3 1.9 image_shares.1
  136.8 1.5 collective-permute-start.33
  138.4 2.6 %collective-permute-start.31 = (bf16[64,832]{1,0:T(8,128)(2,1)S(1)}, bf16[64,832]{1,0:T(8,128)(2,1)S(1)}, u32[]{:S(2)}, u32[]{:S(2)}) collective-permute-start(bf16[64,832]{1,0:T(8,128)(2,1)S(1)} %copy-done.46), channel_id=1, source_target_pairs={{0,4},{1,5},{2,6},{3,7},{4,0},{5,1},{6,2},{7,3},{8,12},{9,13},{10,... | collective-permute-start | bytes 319496 | tf_op jit(solution)/shard_map/ppermute | solution.py:44
  143.2 5.6 %text_next.4.before = bf16[4,624,768]{2,1,0:T(8,128)(2,1)} custom-call(s32[16]{0:T(128)} %concatenate.18.starts.place, bf16[768,1664]{1,0:T(8,128)(2,1)} %get-tuple-element.139.rows, bf16[2,1,160,1664]{3,2,1,0:T(8,128)(2,1)} %get-tuple-element.157.ours.refs_2_, bf16[2,1,160,1664]{3,2,1,0:T(8,128)(2,1)} %bitcast.62, ...), custom_call_target="tpu_custom_call", output_to_operand_aliasing={{}: (4, {})} | custom-call | flops 1 | bytes 1 | tf_op jit(solution)/shard_map/text_next/pallas_call | solution.py:230
  153.4 3.4 %collective-permute-start.37 = (bf16[64,1664]{1,0:T(8,128)(2,1)}, bf16[64,1664]{1,0:T(8,128)(2,1)}, u32[]{:S(2)}, u32[]{:S(2)}) collective-permute-start(bf16[64,1664]{1,0:T(8,128)(2,1)} %constant_dynamic-slice_fusion), channel_id=1, source_target_pairs={{0,6},{1,7},{2,0},{3,1},{4,2},{5,3},{6,4},{7,5},{8,14},{9,15},{10,... | collective-permute-start | bytes 638984 | tf_op jit(solution)/shard_map/ppermute | solution.py:44
  159.4 6.1 %text_next.5.refs_0_ = bf16[4,624,768]{2,1,0:T(8,128)(2,1)} custom-call(s32[16]{0:T(128)} %concatenate.18.starts.place, bf16[768,1664]{1,0:T(8,128)(2,1)} %get-tuple-element.139.rows, bf16[2,1,160,1664]{3,2,1,0:T(8,128)(2,1)} %get-tuple-element.155.ours.refs_4_, bf16[2,1,160,1664]{3,2,1,0:T(8,128)(2,1)} %bitcast.64, ...), custom_call_target="tpu_custom_call", output_to_operand_aliasing={{}: (4, {})} | custom-call | flops 1 | bytes 1 | tf_op jit(solution)/shard_map/text_next/pallas_call | solution.py:230
  165.5 2.0 image_rows.1
  167.4 4.6 %collective-permute-done.36 = bf16[64,1664]{1,0:T(8,128)(2,1)} collective-permute-done((bf16[64,1664]{1,0:T(8,128)(2,1)}, bf16[64,1664]{1,0:T(8,128)(2,1)}, u32[]{:S(2)}, u32[]{:S(2)}) %collective-permute-start.36) | collective-permute-done | bytes 213024 | tf_op jit(solution)/shard_map/ppermute | solution.py:44
  175.1 10.3 %late_attention.1 = (bf16[192,832]{1,0:T(8,128)(2,1)S(1)}, bf16[192,832]{1,0:T(8,128)(2,1)S(1)}) custom-call(s32[16]{0:T(128)S(1)} %copy-done.25, bf16[64,1664]{1,0:T(8,128)(2,1)S(1)} %copy-done.22, bf16[64,768]{1,0:T(8,128)(2,1)S(1)} %copy-done.26, f32[8,768]{1,0:T(8,128)S(1)} %copy-done.27, f32[3,512,128]{2,1,0:T(8,128)S(1)} %copy-done.17, ...), custom_call_target="tpu_custom_call" | custom-call | flops 1 | bytes 1 | tf_op jit(solution)/shard_map/late_attention/pallas_call | solution.py:230
  186.9 2.4 %collective-permute-done.39.refs_2_ = bf16[3,64,1664]{2,1,0:T(8,128)(2,1)S(1)} collective-permute-done((bf16[3,64,1664]{2,1,0:T(8,128)(2,1)S(1)}, bf16[3,64,1664]{2,1,0:T(8,128)(2,1)S(1)}, u32[]{:S(2)}, u32[]{:S(2)}) %collective-permute-start.39) | collective-permute-done | bytes 639008 | tf_op jit(solution)/shard_map/ppermute | solution.py:438
  192.2 3.9 %project.2 = bf16[192,1664]{1,0:T(8,128)(2,1)} custom-call(s32[16]{0:T(128)} %concatenate.18.starts.place, bf16[192,832]{1,0:T(8,128)(2,1)} %copy-done.20, bf16[208,1664]{1,0:T(8,128)(2,1)} %own.3, bf16[3,64,1664]{2,1,0:T(8,128)(2,1)} %copy-done.29, bf16[3,64,1664]{2,1,0:T(8,128)(2,1)} %copy-done.31, bf16[3,64,1664]{2,1,0:T(8,128)(2,1)} %copy-done.30, ...), custom_call_target="tpu_custom_call" | custom-call | flops 1 | bytes 1 | tf_op jit(solution)/shard_map/project/pallas_call | solution.py:230
  197.6 3.9 %project.3.kept = bf16[192,1664]{1,0:T(8,128)(2,1)} custom-call(s32[16]{0:T(128)} %concatenate.18.starts.place, bf16[192,832]{1,0:T(8,128)(2,1)} %copy-done.19, bf16[208,1664]{1,0:T(8,128)(2,1)} %own.3, bf16[3,64,1664]{2,1,0:T(8,128)(2,1)} %copy-done.29, bf16[3,64,1664]{2,1,0:T(8,128)(2,1)} %copy-done.31, bf16[3,64,1664]{2,1,0:T(8,128)(2,1)} %copy-done.30, ...), custom_call_target="tpu_custom_call" | custom-call | flops 1 | bytes 1 | tf_op jit(solution)/shard_map/project/pallas_call | solution.py:230
  201.5 2.7 %out_rows.1 = f32[192,1664]{1,0:T(8,128)} custom-call(s32[16]{0:T(128)} %concatenate.18.starts.place, bf16[192,1664]{1,0:T(8,128)(2,1)} %bitcast.74, s32[8,64]{1,0:T(8,128)} %get-tuple-element.104.slots, bf16[64,1664]{1,0:T(8,128)(2,1)} %get-tuple-element.144.merged, bf16[192,1664]{1,0:T(8,128)(2,1)} %project.3.kept), custom_call_target="tpu_custom_call" | custom-call | flops 1 | bytes 1 | tf_op jit(solution)/shard_map/out_rows/pallas_call | solution.py:230
  204.2 8.5 %collective-permute-done.42 = bf16[192,1664]{1,0:T(8,128)(2,1)S(1)} collective-permute-done((bf16[192,1664]{1,0:T(8,128)(2,1)}, bf16[192,1664]{1,0:T(8,128)(2,1)S(1)}, u32[]{:S(2)}, u32[]{:S(2)}) %collective-permute-start.42) | collective-permute-done | bytes 639008 | tf_op jit(solution)/shard_map/ppermute | solution.py:40
  212.7 2.2 %fusion.4 = bf16[1,192,1664]{2,1,0:T(8,128)(2,1)} fusion(f32[192,1664]{1,0:T(8,128)} %out_rows.1, bf16[192,1664]{1,0:T(8,128)(2,1)S(1)} %collective-permute-done.42), kind=kLoop, calls=%fused_computation.9 | loop fusion | flops 958464 | bytes 2555904 | tf_op jit(solution)/shard_map/broadcast_in_dim | solution.py:677
  (177 shorter events, 44.4 us)
Async XLA Ops:
  0.0 25.7 %copy-start.33 = (bf16[1,192,1664]{2,1,0:T(8,128)(2,1)S(1)}, bf16[1,192,1664]{2,1,0:T(8,128)(2,1)}, u32[]{:S(2)}) copy-start(bf16[1,192,1664]{2,1,0:T(8,128)(2,1)} %param.20) | copy-start | bytes 1916932
  0.0 25.7 %collective-permute-start.4 = (bf16[192,1664]{1,0:T(8,128)(2,1)}, bf16[192,1664]{1,0:T(8,128)(2,1)S(1)}, u32[]{:S(2)}, u32[]{:S(2)}) collective-permute-start(bf16[192,1664]{1,0:T(8,128)(2,1)} %bitcast.72), channel_id=1, source_target_pairs={{0,1},{1,0},{2,3},{3,2},{4,5},{5,4},{6,7},{7,6},{8,9},{9,8},{10,11... | collective-permute-start | bytes 1916936 | tf_op jit(solution)/shard_map/ppermute | solution.py:40
  2.9 19.2 %collective-permute-start.3 = (bf16[64,1664]{1,0:T(8,128)(2,1)}, bf16[64,1664]{1,0:T(8,128)(2,1)S(1)}, u32[]{:S(2)}, u32[]{:S(2)}) collective-permute-start(bf16[64,1664]{1,0:T(8,128)(2,1)} %bitcast.66), channel_id=1, source_target_pairs={{0,1},{1,0},{2,3},{3,2},{4,5},{5,4},{6,7},{7,6},{8,9},{9,8},{10,11... | collective-permute-start | bytes 638984 | tf_op jit(solution)/shard_map/ppermute | solution.py:40
  3.0 19.2 %collective-permute-start.2 = (bf16[64,1664]{1,0:T(8,128)(2,1)}, bf16[64,1664]{1,0:T(8,128)(2,1)S(1)}, u32[]{:S(2)}, u32[]{:S(2)}) collective-permute-start(bf16[64,1664]{1,0:T(8,128)(2,1)} %bitcast.67), channel_id=1, source_target_pairs={{0,2},{1,3},{2,4},{3,5},{4,6},{5,7},{6,0},{7,1},{8,10},{9,11},{10,... | collective-permute-start | bytes 638984 | tf_op jit(solution)/shard_map/ppermute | solution.py:44
  5.1 17.1 %collective-permute-start.1 = (bf16[64,1664]{1,0:T(8,128)(2,1)}, bf16[64,1664]{1,0:T(8,128)(2,1)S(1)}, u32[]{:S(2)}, u32[]{:S(2)}) collective-permute-start(bf16[64,1664]{1,0:T(8,128)(2,1)} %bitcast.68), channel_id=1, source_target_pairs={{0,6},{1,7},{2,0},{3,1},{4,2},{5,3},{6,4},{7,5},{8,14},{9,15},{10,... | collective-permute-start | bytes 638984 | tf_op jit(solution)/shard_map/ppermute | solution.py:44
  7.1 18.6 %collective-permute-start = (bf16[64,1664]{1,0:T(8,128)(2,1)}, bf16[64,1664]{1,0:T(8,128)(2,1)S(1)}, u32[]{:S(2)}, u32[]{:S(2)}) collective-permute-start(bf16[64,1664]{1,0:T(8,128)(2,1)} %bitcast.69), channel_id=1, source_target_pairs={{0,4},{1,5},{2,6},{3,7},{4,0},{5,1},{6,2},{7,3},{8,12},{9,13},{10,... | collective-permute-start | bytes 638984 | tf_op jit(solution)/shard_map/ppermute | solution.py:44
  8.1 21.1 %copy-start.16 = (bf16[1,64,1664]{2,1,0:T(8,128)(2,1)S(1)}, bf16[1,64,1664]{2,1,0:T(8,128)(2,1)}, u32[]{:S(2)}) copy-start(bf16[1,64,1664]{2,1,0:T(8,128)(2,1)} %param.13) | copy-start | bytes 638980
  8.1 21.1 %copy-start.23 = (f32[1664]{0:T(1024)S(1)}, f32[1664]{0:T(1024)}, u32[]{:S(2)}) copy-start(f32[1664]{0:T(1024)} %gain.8) | copy-start | bytes 19972
  25.7 15.8 %collective-permute-start.7 = (bf16[192,1664]{1,0:T(8,128)(2,1)S(1)}, bf16[192,1664]{1,0:T(8,128)(2,1)S(1)}, u32[]{:S(2)}, u32[]{:S(2)}) collective-permute-start(bf16[192,1664]{1,0:T(8,128)(2,1)S(1)} %bitcast.75), channel_id=1, source_target_pairs={{0,2},{1,3},{2,4},{3,5},{4,6},{5,7},{8,10},{9,11},{10,12},{11,13},... | collective-permute-start | bytes 1916936 | tf_op jit(solution)/shard_map/ppermute | solution.py:549
  27.1 10.6 %collective-permute-start.5 = (bf16[64,1664]{1,0:T(8,128)(2,1)S(1)}, bf16[64,1664]{1,0:T(8,128)(2,1)S(1)}, u32[]{:S(2)}, u32[]{:S(2)}) collective-permute-start(bf16[64,1664]{1,0:T(8,128)(2,1)S(1)} %collective-permute-done.2.mine), channel_id=1, source_target_pairs={{0,1},{1,0},{2,3},{3,2},{4,5},{5,4},{6,7},{7,6},{8,9},{9,8},{10,11... | collective-permute-start | bytes 638984 | tf_op jit(solution)/shard_map/ppermute | solution.py:40
  28.6 12.9 %collective-permute-start.6 = (bf16[64,1664]{1,0:T(8,128)(2,1)S(1)}, bf16[64,1664]{1,0:T(8,128)(2,1)S(1)}, u32[]{:S(2)}, u32[]{:S(2)}) collective-permute-start(bf16[64,1664]{1,0:T(8,128)(2,1)S(1)} %collective-permute-done.1.mine), channel_id=1, source_target_pairs={{0,1},{1,0},{2,3},{3,2},{4,5},{5,4},{6,7},{7,6},{8,9},{9,8},{10,11... | collective-permute-start | bytes 638984 | tf_op jit(solution)/shard_map/ppermute | solution.py:40
  41.5 16.4 %collective-permute-start.9 = (bf16[80,1664]{1,0:T(8,128)(2,1)S(1)}, bf16[80,1664]{1,0:T(8,128)(2,1)S(1)}, u32[]{:S(2)}, u32[]{:S(2)}) collective-permute-start(bf16[80,1664]{1,0:T(8,128)(2,1)S(1)} %get-tuple-element.96), channel_id=1, source_target_pairs={{0,4},{1,5},{2,6},{3,7},{4,0},{5,1},{6,2},{7,3},{8,12},{9,13},{10,... | collective-permute-start | bytes 798728 | tf_op jit(solution)/shard_map/ppermute | solution.py:44
  44.3 8.2 %collective-permute-start.8 = (bf16[64,1664]{1,0:T(8,128)(2,1)S(1)}, bf16[64,1664]{1,0:T(8,128)(2,1)S(1)}, u32[]{:S(2)}, u32[]{:S(2)}) collective-permute-start(bf16[64,1664]{1,0:T(8,128)(2,1)S(1)} %collective-permute-done.mine), channel_id=1, source_target_pairs={{0,1},{1,0},{2,3},{3,2},{4,5},{5,4},{6,7},{7,6},{8,9},{9,8},{10,11... | collective-permute-start | bytes 638984 | tf_op jit(solution)/shard_map/ppermute | solution.py:40
  45.8 12.1 %collective-permute-start.10 = (bf16[64,1664]{1,0:T(8,128)(2,1)S(1)}, bf16[64,1664]{1,0:T(8,128)(2,1)S(1)}, u32[]{:S(2)}, u32[]{:S(2)}) collective-permute-start(bf16[64,1664]{1,0:T(8,128)(2,1)S(1)} %get-tuple-element.86), channel_id=1, source_target_pairs={{0,1},{1,0},{2,3},{3,2},{4,5},{5,4},{6,7},{7,6},{8,9},{9,8},{10,11... | collective-permute-start | bytes 638984 | tf_op jit(solution)/shard_map/ppermute | solution.py:40
  50.1 10.9 %collective-permute-start.11 = (bf16[64,1664]{1,0:T(8,128)(2,1)S(1)}, bf16[64,1664]{1,0:T(8,128)(2,1)S(1)}, u32[]{:S(2)}, u32[]{:S(2)}) collective-permute-start(bf16[64,1664]{1,0:T(8,128)(2,1)S(1)} %get-tuple-element.91), channel_id=1, source_target_pairs={{0,1},{1,0},{2,3},{3,2},{4,5},{5,4},{6,7},{7,6},{8,9},{9,8},{10,11... | collective-permute-start | bytes 638984 | tf_op jit(solution)/shard_map/ppermute | solution.py:40
  56.3 8.6 %collective-permute-start.12 = (bf16[64,1664]{1,0:T(8,128)(2,1)S(1)}, bf16[64,1664]{1,0:T(8,128)(2,1)S(1)}, u32[]{:S(2)}, u32[]{:S(2)}) collective-permute-start(bf16[64,1664]{1,0:T(8,128)(2,1)S(1)} %get-tuple-element.95), channel_id=1, source_target_pairs={{0,1},{1,0},{2,3},{3,2},{4,5},{5,4},{6,7},{7,6},{8,9},{9,8},{10,11... | collective-permute-start | bytes 638984 | tf_op jit(solution)/shard_map/ppermute | solution.py:40
  61.1 7.9 %collective-permute-start.14 = (bf16[64,1664]{1,0:T(8,128)(2,1)S(1)}, bf16[64,1664]{1,0:T(8,128)(2,1)S(1)}, u32[]{:S(2)}, u32[]{:S(2)}) collective-permute-start(bf16[64,1664]{1,0:T(8,128)(2,1)S(1)} %add_convert_fusion.2), channel_id=1, source_target_pairs={{0,2},{1,3},{2,4},{3,5},{4,6},{5,7},{6,0},{7,1},{8,10},{9,11},{10,... | collective-permute-start | bytes 638984 | tf_op jit(solution)/shard_map/ppermute | solution.py:44
  61.8 8.7 %collective-permute-start.13 = (bf16[64,1664]{1,0:T(8,128)(2,1)S(1)}, bf16[64,1664]{1,0:T(8,128)(2,1)S(1)}, u32[]{:S(2)}, u32[]{:S(2)}) collective-permute-start(bf16[64,1664]{1,0:T(8,128)(2,1)S(1)} %add_convert_fusion.3), channel_id=1, source_target_pairs={{0,6},{1,7},{2,0},{3,1},{4,2},{5,3},{6,4},{7,5},{8,14},{9,15},{10,... | collective-permute-start | bytes 638984 | tf_op jit(solution)/shard_map/ppermute | solution.py:44
  68.9 21.7 %copy-start.39 = (bf16[64,1664]{1,0:T(8,128)(2,1)}, bf16[64,1664]{1,0:T(8,128)(2,1)S(1)}, u32[]{:S(2)}) copy-start(bf16[64,1664]{1,0:T(8,128)(2,1)S(1)} %collective-permute-done.14.refs_4_) | copy-start | bytes 638980
  70.5 20.2 %copy-start.40 = (bf16[64,1664]{1,0:T(8,128)(2,1)}, bf16[64,1664]{1,0:T(8,128)(2,1)S(1)}, u32[]{:S(2)}) copy-start(bf16[64,1664]{1,0:T(8,128)(2,1)S(1)} %collective-permute-done.13.refs_2_) | copy-start | bytes 638980
  70.5 20.1 %collective-permute-start.17 = (bf16[80,1664]{1,0:T(8,128)(2,1)S(1)}, bf16[80,1664]{1,0:T(8,128)(2,1)S(1)}, u32[]{:S(2)}, u32[]{:S(2)}) collective-permute-start(bf16[80,1664]{1,0:T(8,128)(2,1)S(1)} %get-tuple-element.105), channel_id=1, source_target_pairs={{0,4},{1,5},{2,6},{3,7},{4,0},{5,1},{6,2},{7,3},{8,12},{9,13},{10,... | collective-permute-start | bytes 798728 | tf_op jit(solution)/shard_map/ppermute | solution.py:44
  73.8 6.8 %collective-permute-start.15 = (bf16[64,1664]{1,0:T(8,128)(2,1)S(1)}, bf16[64,1664]{1,0:T(8,128)(2,1)S(1)}, u32[]{:S(2)}, u32[]{:S(2)}) collective-permute-start(bf16[64,1664]{1,0:T(8,128)(2,1)S(1)} %get-tuple-element.82), channel_id=1, source_target_pairs={{0,1},{1,0},{2,3},{3,2},{4,5},{5,4},{6,7},{7,6},{8,9},{9,8},{10,11... | collective-permute-start | bytes 638984 | tf_op jit(solution)/shard_map/ppermute | solution.py:40
  75.3 15.3 %collective-permute-start.16 = (bf16[64,1664]{1,0:T(8,128)(2,1)S(1)}, bf16[64,1664]{1,0:T(8,128)(2,1)S(1)}, u32[]{:S(2)}, u32[]{:S(2)}) collective-permute-start(bf16[64,1664]{1,0:T(8,128)(2,1)S(1)} %add_convert_fusion.1), channel_id=1, source_target_pairs={{0,4},{1,5},{2,6},{3,7},{4,0},{5,1},{6,2},{7,3},{8,12},{9,13},{10,... | collective-permute-start | bytes 638984 | tf_op jit(solution)/shard_map/ppermute | solution.py:44
  76.7 20.4 %collective-permute-start.18 = (bf16[192,1664]{1,0:T(8,128)(2,1)S(1)}, bf16[192,1664]{1,0:T(8,128)(2,1)S(1)}, u32[]{:S(2)}, u32[]{:S(2)}) collective-permute-start(bf16[192,1664]{1,0:T(8,128)(2,1)S(1)} %copy-done.36), channel_id=1, source_target_pairs={{0,1},{1,0},{2,3},{3,2},{4,5},{5,4},{6,7},{7,6},{8,9},{9,8},{10,11... | collective-permute-start | bytes 1916936 | tf_op jit(solution)/shard_map/ppermute | solution.py:40
  94.0 14.8 %collective-permute-start.20 = (bf16[160,1664]{1,0:T(8,128)(2,1)S(1)}, bf16[160,1664]{1,0:T(8,128)(2,1)S(1)}, u32[]{:S(2)}, u32[]{:S(2)}) collective-permute-start(bf16[160,1664]{1,0:T(8,128)(2,1)S(1)} %dynamic-slice_bitcast_fusion), channel_id=1, source_target_pairs={{0,2},{1,3},{2,4},{3,5},{4,6},{5,7},{6,0},{7,1},{8,10},{9,11},{10,... | collective-permute-start | bytes 1597448 | tf_op jit(solution)/shard_map/ppermute | solution.py:44
  94.1 14.7 %collective-permute-start.21 = (bf16[160,1664]{1,0:T(8,128)(2,1)S(1)}, bf16[160,1664]{1,0:T(8,128)(2,1)S(1)}, u32[]{:S(2)}, u32[]{:S(2)}) collective-permute-start(bf16[160,1664]{1,0:T(8,128)(2,1)S(1)} %constant_dynamic-update-slice_fusion), channel_id=1, source_target_pairs={{0,16},{8,24},{16,0},{24,8},{1,17},{9,25},{17,1},{25,9},{2,18},{10... | collective-permute-start | bytes 1597448 | tf_op jit(solution)/shard_map/ppermute | solution.py:438
  95.7 8.1 %collective-permute-start.19 = (bf16[4,16,832]{2,1,0:T(8,128)(2,1)S(1)}, bf16[4,16,832]{2,1,0:T(8,128)(2,1)S(1)}, u32[]{:S(2)}, u32[]{:S(2)}) collective-permute-start(bf16[4,16,832]{2,1,0:T(8,128)(2,1)S(1)} %copy-done.48), channel_id=1, source_target_pairs={{0,1},{1,0},{2,3},{3,2},{4,5},{5,4},{6,7},{7,6},{8,9},{9,8},{10,11... | collective-permute-start | bytes 319496 | tf_op jit(solution)/shard_map/ppermute | solution.py:40
  109.0 16.0 %collective-permute-start.25 = (bf16[2,1,160,1664]{3,2,1,0:T(8,128)(2,1)S(1)}, bf16[2,1,160,1664]{3,2,1,0:T(8,128)(2,1)S(1)}, u32[]{:S(2)}, u32[]{:S(2)}) collective-permute-start(bf16[2,1,160,1664]{3,2,1,0:T(8,128)(2,1)S(1)} %maximum_bitcast_fusion.ours.refs_6_), channel_id=1, source_target_pairs={{0,8},{8,0},{16,24},{24,16},{1,9},{9,1},{17,25},{25,17},{2,10},{10... | collective-permute-start | bytes 3194888 | tf_op jit(solution)/shard_map/ppermute | solution.py:438
  109.1 6.7 %collective-permute-start.22 = (bf16[32,832]{1,0:T(8,128)(2,1)S(1)}, bf16[32,832]{1,0:T(8,128)(2,1)S(1)}, u32[]{:S(2)}, u32[]{:S(2)}) collective-permute-start(bf16[32,832]{1,0:T(8,128)(2,1)S(1)} %pad_maximum_fusion.4), channel_id=1, source_target_pairs={{0,2},{1,3},{2,4},{3,5},{4,6},{5,7},{6,0},{7,1},{8,10},{9,11},{10,... | collective-permute-start | bytes 159752 | tf_op jit(solution)/shard_map/ppermute | solution.py:44
  109.2 8.1 %collective-permute-start.23 = (bf16[32,832]{1,0:T(8,128)(2,1)S(1)}, bf16[32,832]{1,0:T(8,128)(2,1)S(1)}, u32[]{:S(2)}, u32[]{:S(2)}) collective-permute-start(bf16[32,832]{1,0:T(8,128)(2,1)S(1)} %pad_maximum_fusion.5), channel_id=1, source_target_pairs={{0,4},{1,5},{2,6},{3,7},{4,0},{5,1},{6,2},{7,3},{8,12},{9,13},{10,... | collective-permute-start | bytes 159752 | tf_op jit(solution)/shard_map/ppermute | solution.py:44
  111.6 5.6 %collective-permute-start.24 = (bf16[32,832]{1,0:T(8,128)(2,1)S(1)}, bf16[32,832]{1,0:T(8,128)(2,1)S(1)}, u32[]{:S(2)}, u32[]{:S(2)}) collective-permute-start(bf16[32,832]{1,0:T(8,128)(2,1)S(1)} %pad_maximum_fusion.6), channel_id=1, source_target_pairs={{0,6},{1,7},{2,0},{3,1},{4,2},{5,3},{6,4},{7,5},{8,14},{9,15},{10,... | collective-permute-start | bytes 159752 | tf_op jit(solution)/shard_map/ppermute | solution.py:44
  119.3 14.9 %collective-permute-start.27 = (bf16[160,1664]{1,0:T(8,128)(2,1)S(1)}, bf16[160,1664]{1,0:T(8,128)(2,1)S(1)}, u32[]{:S(2)}, u32[]{:S(2)}) collective-permute-start(bf16[160,1664]{1,0:T(8,128)(2,1)S(1)} %dynamic-slice_bitcast_fusion), channel_id=1, source_target_pairs={{0,6},{1,7},{2,0},{3,1},{4,2},{5,3},{6,4},{7,5},{8,14},{9,15},{10,... | collective-permute-start | bytes 1597448 | tf_op jit(solution)/shard_map/ppermute | solution.py:44
  122.0 13.7 %collective-permute-start.28 = (bf16[160,1664]{1,0:T(8,128)(2,1)S(1)}, bf16[160,1664]{1,0:T(8,128)(2,1)S(1)}, u32[]{:S(2)}, u32[]{:S(2)}) collective-permute-start(bf16[160,1664]{1,0:T(8,128)(2,1)S(1)} %collective-permute-done.20), channel_id=1, source_target_pairs={{0,16},{8,24},{16,0},{24,8},{1,17},{9,25},{17,1},{25,9},{2,18},{10... | collective-permute-start | bytes 1597448 | tf_op jit(solution)/shard_map/ppermute | solution.py:438
  123.5 8.1 %collective-permute-start.26 = (bf16[128,832]{1,0:T(8,128)(2,1)S(1)}, bf16[128,832]{1,0:T(8,128)(2,1)S(1)}, u32[]{:S(2)}, u32[]{:S(2)}) collective-permute-start(bf16[128,832]{1,0:T(8,128)(2,1)S(1)} %get-tuple-element.125), channel_id=1, source_target_pairs={{0,1},{1,0},{2,3},{3,2},{4,5},{5,4},{6,7},{7,6},{8,9},{9,8},{10,11... | collective-permute-start | bytes 638984 | tf_op jit(solution)/shard_map/ppermute | solution.py:40
  136.8 5.4 %collective-permute-start.29 = (bf16[2,1,160,1664]{3,2,0,1:T(8,128)(2,1)S(1)}, bf16[2,1,160,1664]{3,2,0,1:T(8,128)(2,1)S(1)}, u32[]{:S(2)}, u32[]{:S(2)}) collective-permute-start(bf16[2,1,160,1664]{3,2,0,1:T(8,128)(2,1)S(1)} %get-tuple-element.158), channel_id=1, source_target_pairs={{0,8},{8,0},{16,24},{24,16},{1,9},{9,1},{17,25},{25,17},{2,10},{10... | collective-permute-start | bytes 3194888 | tf_op jit(solution)/shard_map/ppermute | solution.py:438
  136.8 14.5 %collective-permute-start.33 = (bf16[160,1664]{1,0:T(8,128)(2,1)S(1)}, bf16[160,1664]{1,0:T(8,128)(2,1)S(1)}, u32[]{:S(2)}, u32[]{:S(2)}) collective-permute-start(bf16[160,1664]{1,0:T(8,128)(2,1)S(1)} %collective-permute-done.27), channel_id=1, source_target_pairs={{0,16},{8,24},{16,0},{24,8},{1,17},{9,25},{17,1},{25,9},{2,18},{10... | collective-permute-start | bytes 1597448 | tf_op jit(solution)/shard_map/ppermute | solution.py:438
  138.4 10.5 %collective-permute-start.30 = (bf16[64,832]{1,0:T(8,128)(2,1)S(1)}, bf16[64,832]{1,0:T(8,128)(2,1)S(1)}, u32[]{:S(2)}, u32[]{:S(2)}) collective-permute-start(bf16[64,832]{1,0:T(8,128)(2,1)S(1)} %copy-done.47), channel_id=1, source_target_pairs={{0,2},{1,3},{2,4},{3,5},{4,6},{5,7},{6,0},{7,1},{8,10},{9,11},{10,... | collective-permute-start | bytes 319496 | tf_op jit(solution)/shard_map/ppermute | solution.py:44
  138.4 11.9 %collective-permute-start.31 = (bf16[64,832]{1,0:T(8,128)(2,1)S(1)}, bf16[64,832]{1,0:T(8,128)(2,1)S(1)}, u32[]{:S(2)}, u32[]{:S(2)}) collective-permute-start(bf16[64,832]{1,0:T(8,128)(2,1)S(1)} %copy-done.46), channel_id=1, source_target_pairs={{0,4},{1,5},{2,6},{3,7},{4,0},{5,1},{6,2},{7,3},{8,12},{9,13},{10,... | collective-permute-start | bytes 319496 | tf_op jit(solution)/shard_map/ppermute | solution.py:44
  141.0 9.2 %collective-permute-start.32 = (bf16[64,832]{1,0:T(8,128)(2,1)S(1)}, bf16[64,832]{1,0:T(8,128)(2,1)S(1)}, u32[]{:S(2)}, u32[]{:S(2)}) collective-permute-start(bf16[64,832]{1,0:T(8,128)(2,1)S(1)} %copy-done.45), channel_id=1, source_target_pairs={{0,6},{1,7},{2,0},{3,1},{4,2},{5,3},{6,4},{7,5},{8,14},{9,15},{10,... | collective-permute-start | bytes 319496 | tf_op jit(solution)/shard_map/ppermute | solution.py:44
  152.5 5.8 %collective-permute-start.34 = (bf16[2,1,160,1664]{3,2,0,1:T(8,128)(2,1)S(1)}, bf16[2,1,160,1664]{3,2,0,1:T(8,128)(2,1)S(1)}, u32[]{:S(2)}, u32[]{:S(2)}) collective-permute-start(bf16[2,1,160,1664]{3,2,0,1:T(8,128)(2,1)S(1)} %get-tuple-element.156), channel_id=1, source_target_pairs={{0,8},{8,0},{16,24},{24,16},{1,9},{9,1},{17,25},{25,17},{2,10},{10... | collective-permute-start | bytes 3194888 | tf_op jit(solution)/shard_map/ppermute | solution.py:438
  152.5 15.0 %collective-permute-start.38 = (bf16[64,1664]{1,0:T(8,128)(2,1)}, bf16[64,1664]{1,0:T(8,128)(2,1)}, u32[]{:S(2)}, u32[]{:S(2)}) collective-permute-start(bf16[64,1664]{1,0:T(8,128)(2,1)} %constant_dynamic-slice_fusion), channel_id=1, source_target_pairs={{0,4},{1,5},{2,6},{3,7},{4,0},{5,1},{6,2},{7,3},{8,12},{9,13},{10,... | collective-permute-start | bytes 638984 | tf_op jit(solution)/shard_map/ppermute | solution.py:44
  153.4 14.1 %collective-permute-start.37 = (bf16[64,1664]{1,0:T(8,128)(2,1)}, bf16[64,1664]{1,0:T(8,128)(2,1)}, u32[]{:S(2)}, u32[]{:S(2)}) collective-permute-start(bf16[64,1664]{1,0:T(8,128)(2,1)} %constant_dynamic-slice_fusion), channel_id=1, source_target_pairs={{0,6},{1,7},{2,0},{3,1},{4,2},{5,3},{6,4},{7,5},{8,14},{9,15},{10,... | collective-permute-start | bytes 638984 | tf_op jit(solution)/shard_map/ppermute | solution.py:44
  156.8 15.2 %collective-permute-start.36 = (bf16[64,1664]{1,0:T(8,128)(2,1)}, bf16[64,1664]{1,0:T(8,128)(2,1)}, u32[]{:S(2)}, u32[]{:S(2)}) collective-permute-start(bf16[64,1664]{1,0:T(8,128)(2,1)} %constant_dynamic-slice_fusion), channel_id=1, source_target_pairs={{0,2},{1,3},{2,4},{3,5},{4,6},{5,7},{6,0},{7,1},{8,10},{9,11},{10,... | collective-permute-start | bytes 638984 | tf_op jit(solution)/shard_map/ppermute | solution.py:44
  156.8 8.7 %collective-permute-start.35 = (bf16[64,832]{1,0:T(8,128)(2,1)}, bf16[64,832]{1,0:T(8,128)(2,1)}, u32[]{:S(2)}, u32[]{:S(2)}) collective-permute-start(bf16[64,832]{1,0:T(8,128)(2,1)} %add_convert_fusion.4.ours), channel_id=1, source_target_pairs={{0,1},{1,0},{2,3},{3,2},{4,5},{5,4},{6,7},{7,6},{8,9},{9,8},{10,11... | collective-permute-start | bytes 319496 | tf_op jit(solution)/shard_map/ppermute | solution.py:40
  173.2 16.0 %collective-permute-start.39 = (bf16[3,64,1664]{2,1,0:T(8,128)(2,1)S(1)}, bf16[3,64,1664]{2,1,0:T(8,128)(2,1)S(1)}, u32[]{:S(2)}, u32[]{:S(2)}) collective-permute-start(bf16[3,64,1664]{2,1,0:T(8,128)(2,1)S(1)} %pad_maximum_fusion.2.refs_0_), channel_id=1, source_target_pairs={{0,16},{8,24},{16,0},{24,8},{1,17},{9,25},{17,1},{25,9},{2,18},{10... | collective-permute-start | bytes 1916936 | tf_op jit(solution)/shard_map/ppermute | solution.py:438
  173.8 15.5 %collective-permute-start.40 = (bf16[3,64,1664]{2,1,0:T(8,128)(2,1)S(1)}, bf16[3,64,1664]{2,1,0:T(8,128)(2,1)S(1)}, u32[]{:S(2)}, u32[]{:S(2)}) collective-permute-start(bf16[3,64,1664]{2,1,0:T(8,128)(2,1)S(1)} %pad_maximum_fusion.2.refs_0_), channel_id=1, source_target_pairs={{0,8},{8,0},{16,24},{24,16},{1,9},{9,1},{17,25},{25,17},{2,10},{10... | collective-permute-start | bytes 1916936 | tf_op jit(solution)/shard_map/ppermute | solution.py:438
  189.3 2.1 collective-permute-start.41
  196.1 16.6 %collective-permute-start.42 = (bf16[192,1664]{1,0:T(8,128)(2,1)}, bf16[192,1664]{1,0:T(8,128)(2,1)S(1)}, u32[]{:S(2)}, u32[]{:S(2)}) collective-permute-start(bf16[192,1664]{1,0:T(8,128)(2,1)} %project.2), channel_id=1, source_target_pairs={{0,1},{1,0},{2,3},{3,2},{4,5},{5,4},{6,7},{7,6},{8,9},{9,8},{10,11... | collective-permute-start | bytes 1916936 | tf_op jit(solution)/shard_map/ppermute | solution.py:40
  (44 other events, 281.2 us)
